TPU v7x, 32 devices: a whole 2x2x4 slice. The times are simulated.
32 devices in a mesh: pp: 2 (over x), cp: 4 (over z), tp: 4 (over y, core).
Axes of the slice: x: 2, y: 2, z: 4, core: 2. Of those that a mesh axis runs over, the one named last changes fastest.
Arguments:
- queries: bfloat16 [2, 512, 8192], P('pp', 'cp', 'tp'), may hold values from -9 to 9
- key_vectors: bfloat16 [2, 512, 512], P('pp', 'cp', 'tp'), may hold values from -6 to 6
- value_vectors: bfloat16 [2, 512, 512], P('pp', 'cp', 'tp'), may hold values from -30 to 30
- block_order: int32 [8], replicated, may hold values from 0 to 7, each once
- norm_gain: bfloat16 [2, 8192], P('pp', 'tp'), may hold values from 0.099609375 to 1.8984375
- kv_weight: bfloat16 [2, 8192, 1024], P('pp', 'tp'), may hold values from -0.0625 to 0.0625
Outputs:
- max_logits: float32 [2, 64], P('pp', 'tp')
- kv_next: bfloat16 [2, 512, 1024], P('pp', 'cp', 'tp')
Inputs may be any that keep to these rules, and one draw needn't show every extreme that they name: A permutation; rows 2 c * 64 to (2 c + 2) * 64 - 1 hold the positions of blocks block_order[2 c] and block_order[2 c + 1], in that order.
All inputs are finite; a program needn't handle non-finite values.
Results may differ from a plain program's by a relative error of at most 0.018.
Values may be sent and summed in bfloat16 or wider, within the bound.
No kernel may reach another device: no remote copies, remote signals or barrier semaphores. Data moves between devices by JAX's collectives and lax.ppermute only.
A program may use at most 128 MiB of HBM per device.

v0:
```python
import functools
import math

import jax
import jax.numpy as jnp
from jax import lax
from jax.experimental import pallas as pl
from jax.experimental.pallas import tpu as pltpu
from jax.sharding import PartitionSpec as P

DH = 128
LANES = 128
CHUNKS = 2
SQUARE_ROWS = 16
MASKED = -(2.0**100)
LOG2E = math.log2(math.e)
F32 = jnp.float32
BF16 = jnp.bfloat16
WHOLE = pl.BlockSpec(memory_space=pltpu.VMEM)
OUTSIDE = pl.BlockSpec(memory_space=pl.ANY)
SCALARS = pl.BlockSpec(memory_space=pltpu.SMEM)


def call(kernel, outs, args, specs=None, scratch=(), limit=16, name=None, aliases=None, micros=0):
    return pl.pallas_call(
        kernel,
        out_shape=outs,
        in_specs=specs or [WHOLE] * len(args),
        out_specs=jax.tree.map(lambda _: WHOLE, outs),
        scratch_shapes=scratch,
        name=name,
        input_output_aliases=aliases or {},
        cost_estimate=pl.CostEstimate(flops=int(micros * 1e9), bytes_accessed=0, transcendentals=0) if micros else None,
        compiler_params=pltpu.CompilerParams(vmem_limit_bytes=limit * 2**20),
    )(*args)


def partner(index, step, size):
    return (index + step) % size if size & (size - 1) else index ^ step


def swapped(block, axis, step):
    size = lax.axis_size(axis)
    return lax.ppermute(block, axis, [(i, partner(i, step, size)) for i in range(size)])


def shifted(block, axis, distance):
    size = lax.axis_size(axis)
    return lax.ppermute(block, axis, [((i - distance) % size, i) for i in range(size)])


def prepare(order_ref, q_ref, after, q_out, feature_ref):
    q_out[...] = q_ref[0]
    sources = lax.axis_size("cp")
    me = lax.axis_index("cp")
    block = feature_ref.shape[1] // (2 * sources)
    row = lax.broadcasted_iota(jnp.int32, (block, LANES), 0)
    lane = lax.broadcasted_iota(jnp.int32, (block, LANES), 1)
    for side in range(2):
        mine = order_ref[2 * me + side]
        for d in range(sources):
            source = lax.rem(me - d + sources, sources) if sources & (sources - 1) else me ^ d
            for half in range(2):
                other = order_ref[2 * source + half]
                column = jnp.where(other == mine, row, jnp.where(other > mine, block, -1))
                first = (2 * d + half) * block
                feature_ref[side, first:first + block, :] = jnp.where(lane == column, 1.0, 0.0).astype(BF16)


def attend(first_head, heads, sources, q_ref, feature_ref, *refs):
    pairs = refs[:sources]
    before, (ctx_ref, peak_ref, k_all, vt) = refs[sources:-4], refs[-4:]
    rows = q_ref.shape[0]
    block = rows // 2
    kv_local = pairs[0].shape[1] // (2 * DH)
    count = ctx_ref.shape[1] // DH
    tile = LANES // block
    scale = 1.0 / math.sqrt(DH)
    ahead = lax.rem(lax.broadcasted_iota(jnp.int32, (tile * block, LANES), 0), block)
    lane = lax.broadcasted_iota(jnp.int32, (tile * block, LANES), 1)
    blocked = jnp.where((lane > ahead) & (lane <= block), MASKED, 0.0).astype(BF16)
    if before:
        peak_ref[:, :first_head] = before[0][...]
    vt[kv_local * DH:, :] = jnp.ones((vt.shape[0] - kv_local * DH, vt.shape[1]), BF16)
    for side in range(2):
        k_all[side, :, kv_local * DH:] = feature_ref[side]
    for d in range(sources):
        part = slice(d * rows, (d + 1) * rows)
        for side in range(2):
            k_all[side, part, :kv_local * DH] = pairs[d][:, :kv_local * DH]
        vt[:kv_local * DH, part] = pairs[d][:, kv_local * DH:].astype(F32).T.astype(BF16)

    def scores(i, side):
        tokens = slice(side * block, (side + 1) * block)
        places = [slice((first_head + i + j) * DH, (first_head + i + j + 1) * DH) for j in range(tile)]
        q = jnp.concatenate([q_ref[tokens, place] for place in places], axis=0)
        q = jnp.concatenate([q, blocked], axis=1)
        g = (first_head + i) // (heads // kv_local)
        if kv_local == 1:
            k = k_all[side]
        else:
            k = jnp.concatenate([k_all[side, :, g * DH:(g + 1) * DH], k_all[side, :, kv_local * DH:]], axis=1)
        return lax.dot_general(k, q, (((1,), (1,)), ((), ())), preferred_element_type=F32)

    def context(i, side, s):
        g = (first_head + i) // (heads // kv_local)
        m = jnp.max(s, axis=0, keepdims=True)
        p = jnp.exp2((s - m) * (scale * LOG2E)).astype(BF16)
        if kv_local == 1:
            v = vt[...]
        else:
            v = jnp.concatenate([vt[g * DH:(g + 1) * DH, :], vt[kv_local * DH:, :]], axis=0)
        return m, jnp.dot(v, p, preferred_element_type=F32)

    def store(i, side, o):
        turned = (o[:DH, :] * (1.0 / o[DH:DH + 1, :])).astype(BF16).T
        for j in range(tile):
            ctx_ref[side * block:(side + 1) * block, (i + j) * DH:(i + j + 1) * DH] = turned[j * block:(j + 1) * block, :]

    steps = [(i, side) for i in range(0, count, tile) for side in range(2)]
    peaks = {}
    waiting, unstored = scores(*steps[0]), None
    for n, (i, side) in enumerate(steps):
        s = waiting
        if n + 1 < len(steps):
            waiting = scores(*steps[n + 1])
        m, o = context(i, side, s)
        if unstored:
            store(*unstored)
        unstored = (i, side, o)
        peaks[i] = jnp.maximum(peaks[i], m) if side else m
    store(*unstored)
    for i, peak in peaks.items():
        for j in range(tile):
            h = first_head + i + j
            one = jnp.max(peak[:, j * block:(j + 1) * block], axis=1, keepdims=True)
            peak_ref[:, h:h + 1] = one * scale


def weigh(w_ref, gain_ref, after, out_ref):
    features, columns = w_ref.shape
    for f in range(0, features, LANES):
        gain = jnp.broadcast_to(gain_ref[:, f:f + LANES].astype(F32), (LANES, LANES)).T
        for c in range(0, columns, LANES):
            out_ref[f:f + LANES, c:c + LANES] = (w_ref[f:f + LANES, c:c + LANES].astype(F32) * gain).astype(BF16)


def square_sums(ctx_ref):
    total = None
    for c in range(0, ctx_ref.shape[1], LANES):
        wide = ctx_ref[:, c:c + LANES].astype(F32)
        total = wide * wide if total is None else total + wide * wide
    return jnp.broadcast_to(jnp.sum(total, axis=1, keepdims=True), total.shape)


def project_first(ctx_ref, w_ref, peak_ref, peak_got, sum_ref, square_ref, peak_out):
    peak_out[...] = jnp.maximum(peak_ref[...], peak_got[...])
    square_ref[...] = square_sums(ctx_ref)
    sum_ref[...] = jnp.dot(ctx_ref[...], w_ref[:ctx_ref.shape[1], :], preferred_element_type=F32)


def project_last(ctx_ref, w_ref, sum_ref, square_ref, give_ref, keep_ref):
    rows, width = ctx_ref.shape
    start = w_ref.shape[0] - width
    squares = square_ref[...] + square_sums(ctx_ref)
    lanes = squares.T[:SQUARE_ROWS, :]
    first = lanes.astype(BF16)
    rest = (lanes - first.astype(F32)).astype(BF16)
    groups, cols = give_ref.shape[0], give_ref.shape[2]
    core = lax.rem(lax.axis_index("tp"), 2)
    for ref, side in ((give_ref, 1 - core), (keep_ref, core)):
        for y in range(groups):
            at = pl.ds(pl.multiple_of((2 * y + side) * cols, cols), cols)
            part = sum_ref[:, at] + jnp.dot(ctx_ref[...], w_ref[start:, at], preferred_element_type=F32)
            ref[y, :rows, :] = part.astype(BF16)
            ref[y, rows:, :rows] = first
            ref[y, rows:, rows:2 * rows] = rest
            if cols > 2 * rows:
                ref[y, rows:, 2 * rows:] = jnp.zeros((SQUARE_ROWS, cols - 2 * rows), BF16)


def merge(keep_ref, got_ref, *give_refs):
    groups = keep_ref.shape[0]
    mine = lax.axis_index("tp") // 2
    for step, ref in enumerate(give_refs):
        y = lax.rem(mine + step, groups)
        total = keep_ref[y].astype(F32) + got_ref[y].astype(F32)
        ref[...] = total.astype(ref.dtype)


def finish(features, keep_ref, *refs):
    out_ref = refs[-1]
    rows = out_ref.shape[0]
    total = keep_ref[...]
    for ref in refs[:-1]:
        total = total + ref[...].astype(F32)
    squares = total[rows:rows + 8, :rows] + total[rows:rows + 8, rows:2 * rows]
    inverse = lax.rsqrt(squares / features + 1e-05)
    column = jnp.broadcast_to(inverse[:1, :], (rows, rows)).T[:, :1]
    out_ref[...] = (total[:rows, :] * column).astype(BF16)


def on_device(queries, key_vectors, value_vectors, block_order, norm_gain, kv_weight):
    rows, width = queries.shape[1:]
    heads = width // DH
    peers = lax.axis_size("tp")
    sources = lax.axis_size("cp")
    kv_width = key_vectors.shape[2]
    columns = kv_weight.shape[2]
    out_cols = columns // peers
    shape = jax.ShapeDtypeStruct
    steps = [2**i for i in range((sources - 1).bit_length())]

    pair = jnp.concatenate([key_vectors[0], value_vectors[0]], axis=1)
    pairs = [pair] + [swapped(pair, "cp", d) for d in range(1, sources)]
    q, features = call(
        prepare,
        (shape((rows, width), BF16), shape((2, sources * rows, LANES), BF16)),
        (block_order, queries, pair),
        [SCALARS, WHOLE, OUTSIDE],
        name="prepare",
        micros=1,
    )
    part_heads = heads // CHUNKS
    handed, peaks = [], []
    for c in range(CHUNKS):
        context, peak = call(
            functools.partial(attend, c * part_heads, heads, sources),
            (shape((rows, part_heads * DH), BF16), shape((1, (c + 1) * part_heads), F32)),
            (q, features, *pairs, *peaks[-1:]),
            scratch=[
                pltpu.VMEM((2, sources * rows, kv_width + LANES), BF16),
                pltpu.VMEM((kv_width + 16, sources * rows), BF16),
            ],
            limit=24,
            name="attend",
            micros=1.5,
        )
        handed.append(shifted(context, "pp", 1))
        peaks.append(peak)
    w = call(
        weigh,
        shape((width, columns), BF16),
        (kv_weight[0], norm_gain, context),
        [WHOLE, WHOLE, OUTSIDE],
        name="weigh",
        micros=2,
    )
    peak = peaks[-1]
    for step in steps[:-1]:
        peak = jnp.maximum(peak, swapped(peak, "cp", step))
    total, squares, max_logits = call(
        project_first,
        (shape((rows, columns), F32), shape((rows, LANES), F32), shape((1, heads), F32)),
        (handed[0], w, peak, swapped(peak, "cp", steps[-1])),
        name="project_first",
        micros=0.7,
    )
    slab = shape((peers // 2, rows + SQUARE_ROWS, out_cols), BF16)
    give, keep = call(
        project_last, (slab, slab), (handed[1], w, total, squares), name="project_last", micros=0.5
    )
    got = lax.ppermute(give, "tp", [(i, i ^ 1) for i in range(peers)])
    slab = (rows + SQUARE_ROWS, out_cols)
    mine, *others = call(
        merge,
        [shape(slab, F32)] + [shape(slab, BF16)] * (peers // 2 - 1),
        (keep, got),
        name="merge",
    )
    others = [
        lax.ppermute(block, "tp", [(i, (i + 2 * (step + 1)) % peers) for i in range(peers)])
        for step, block in enumerate(others)
    ]
    kv_next = call(
        functools.partial(finish, width * peers), shape((rows, out_cols), BF16), (mine, *others), name="finish"
    )
    return (max_logits, kv_next[None])


def solution(mesh):
    return jax.shard_map(
        on_device,
        mesh=mesh,
        in_specs=(
            P("pp", "cp", "tp"),
            P("pp", "cp", "tp"),
            P("pp", "cp", "tp"),
            P(),
            P("pp", "tp"),
            P("pp", "tp", None),
        ),
        out_specs=(P("pp", "tp"), P("pp", "cp", "tp")),
        check_vma=False,
    )
```

profile of v0, /device:TPU:0, one launch (start us, length us, event | category | flops | bytes accessed | tf_op | source)
XLA Modules:
  0.0 35.1 jit_solution(1495457556623093184)
XLA Ops:
  0.6 0.8 %pad_maximum_fusion.after.refs_0_ = bf16[128,256]{1,0:T(8,128)(2,1)S(1)} fusion(bf16[128,128]{1,0:T(8,128)(2,1)} %bitcast.6, bf16[128,128]{1,0:T(8,128)(2,1)} %bitcast.7), kind=kLoop, calls=%fused_computation | loop fusion | flops 131072 | bytes 131072 | tf_op jit(solution)/shard_map/concatenate | solution.py:214
  1.4 3.1 %collective-permute-start = (bf16[128,256]{1,0:T(8,128)(2,1)S(1)}, bf16[128,256]{1,0:T(8,128)(2,1)S(1)}, u32[]{:S(2)}, u32[]{:S(2)}) collective-permute-start(bf16[128,256]{1,0:T(8,128)(2,1)S(1)} %pad_maximum_fusion.after.refs_0_), channel_id=1, source_target_pairs={{0,4},{4,0},{8,12},{12,8},{1,5},{5,1},{9,13},{13,9},{2,6},{6,2},{1... | collective-permute-start | bytes 196616 | tf_op jit(solution)/shard_map/ppermute | solution.py:44
  4.5 2.6 %collective-permute-start.1 = (bf16[128,256]{1,0:T(8,128)(2,1)S(1)}, bf16[128,256]{1,0:T(8,128)(2,1)S(1)}, u32[]{:S(2)}, u32[]{:S(2)}) collective-permute-start(bf16[128,256]{1,0:T(8,128)(2,1)S(1)} %pad_maximum_fusion.after.refs_0_), channel_id=1, source_target_pairs={{0,8},{4,12},{8,0},{12,4},{1,9},{5,13},{9,1},{13,5},{2,10},{6,14},... | collective-permute-start | bytes 196616 | tf_op jit(solution)/shard_map/ppermute | solution.py:44
  7.1 0.0 collective-permute-start.2
  7.1 1.0 %copy-done.2 = bf16[1,128,2048]{2,1,0:T(8,128)(2,1)S(1)} copy-done((bf16[1,128,2048]{2,1,0:T(8,128)(2,1)S(1)}, bf16[1,128,2048]{2,1,0:T(8,128)(2,1)}, u32[]{:S(2)}) %copy-start.2) | copy-done | bytes 524312
  8.1 0.7 %copy-done.3 = s32[8]{0:T(128)S(1)} copy-done((s32[8]{0:T(128)S(1)}, s32[8]{0:T(128)}, u32[]{:S(2)}) %copy-start.3) | copy-done | bytes 56
  8.8 0.6 %prepare.1 = (bf16[128,2048]{1,0:T(8,128)(2,1)S(1)}, bf16[2,512,128]{2,1,0:T(8,128)(2,1)S(1)}) custom-call(s32[8]{0:T(128)S(1)} %copy-done.3, bf16[1,128,2048]{2,1,0:T(8,128)(2,1)S(1)} %copy-done.2, bf16[128,256]{1,0:T(8,128)(2,1)S(1)} %pad_maximum_fusion.after.refs_0_), custom_call_target="tpu_custom_call" | custom-call | flops 1000000000 | tf_op jit(solution)/shard_map/prepare/pallas_call | solution.py:25
  9.4 2.3 %collective-permute-done.1.refs_2_ = bf16[128,256]{1,0:T(8,128)(2,1)S(1)} collective-permute-done((bf16[128,256]{1,0:T(8,128)(2,1)S(1)}, bf16[128,256]{1,0:T(8,128)(2,1)S(1)}, u32[]{:S(2)}, u32[]{:S(2)}) %collective-permute-start.1) | collective-permute-done | bytes 65568 | tf_op jit(solution)/shard_map/ppermute | solution.py:44
  11.8 1.4 %collective-permute-done.2.refs_3_ = bf16[128,256]{1,0:T(8,128)(2,1)S(1)} collective-permute-done((bf16[128,256]{1,0:T(8,128)(2,1)S(1)}, bf16[128,256]{1,0:T(8,128)(2,1)S(1)}, u32[]{:S(2)}, u32[]{:S(2)}) %collective-permute-start.2) | collective-permute-done | bytes 65568 | tf_op jit(solution)/shard_map/ppermute | solution.py:44
  13.2 1.8 %attend.2 = (bf16[128,1024]{1,0:T(8,128)(2,1)S(1)}, f32[1,8]{1,0:T(1,128)S(1)}) custom-call(bf16[128,2048]{1,0:T(8,128)(2,1)S(1)} %get-tuple-element.15.q_ref, bf16[2,512,128]{2,1,0:T(8,128)(2,1)S(1)} %get-tuple-element.16.feature_ref, bf16[128,256]{1,0:T(8,128)(2,1)S(1)} %pad_maximum_fusion.after.refs_0_, ...), custom_call_target="tpu_custom_call" | custom-call | flops 1500000000 | tf_op jit(solution)/shard_map/attend/pallas_call | solution.py:25
  15.0 1.6 %collective-permute-start.3 = (bf16[128,1024]{1,0:T(8,128)(2,1)S(1)}, bf16[128,1024]{1,0:T(8,128)(2,1)S(1)}, u32[]{:S(2)}, u32[]{:S(2)}) collective-permute-start(bf16[128,1024]{1,0:T(8,128)(2,1)S(1)} %get-tuple-element.17), channel_id=1, source_target_pairs={{16,0},{0,16},{17,1},{1,17},{18,2},{2,18},{19,3},{3,19},{20,4},{4,... | collective-permute-start | bytes 786440 | tf_op jit(solution)/shard_map/ppermute | solution.py:49
  16.6 1.8 %attend.3 = (bf16[128,1024]{1,0:T(8,128)(2,1)S(1)}, f32[1,16]{1,0:T(1,128)S(1)}) custom-call(bf16[128,2048]{1,0:T(8,128)(2,1)S(1)} %get-tuple-element.15.q_ref, bf16[2,512,128]{2,1,0:T(8,128)(2,1)S(1)} %get-tuple-element.16.feature_ref, bf16[128,256]{1,0:T(8,128)(2,1)S(1)} %pad_maximum_fusion.after.refs_0_, ...), custom_call_target="tpu_custom_call" | custom-call | flops 1500000000 | tf_op jit(solution)/shard_map/attend/pallas_call | solution.py:25
  18.5 0.6 %collective-permute-start.6 = (bf16[128,1024]{1,0:T(8,128)(2,1)S(1)}, bf16[128,1024]{1,0:T(8,128)(2,1)S(1)}, u32[]{:S(2)}, u32[]{:S(2)}) collective-permute-start(bf16[128,1024]{1,0:T(8,128)(2,1)S(1)} %get-tuple-element.19.after), channel_id=1, source_target_pairs={{16,0},{0,16},{17,1},{1,17},{18,2},{2,18},{19,3},{3,19},{20,4},{4,... | collective-permute-start | bytes 786440 | tf_op jit(solution)/shard_map/ppermute | solution.py:49
  19.0 3.5 %collective-permute-done.4 = f32[1,16]{1,0:T(1,128)S(1)} collective-permute-done((f32[1,16]{1,0:T(1,128)S(1)}, f32[1,16]{1,0:T(1,128)S(1)}, u32[]{:S(2)}, u32[]{:S(2)}) %collective-permute-start.4) | collective-permute-done | bytes 96 | tf_op jit(solution)/shard_map/ppermute | solution.py:44
  22.6 1.6 %collective-permute-start.5 = (f32[1,16]{1,0:T(1,128)S(1)}, f32[1,16]{1,0:T(1,128)S(1)}, u32[]{:S(2)}, u32[]{:S(2)}) collective-permute-start(f32[1,16]{1,0:T(1,128)S(1)} %max.3.peak_ref), channel_id=1, source_target_pairs={{0,8},{4,12},{8,0},{12,4},{1,9},{5,13},{9,1},{13,5},{2,10},{6,14},... | collective-permute-start | bytes 200 | tf_op jit(solution)/shard_map/ppermute | solution.py:44
  24.2 0.9 %weigh.1.w_ref = bf16[2048,1024]{1,0:T(8,128)(2,1)S(1)} custom-call(bf16[2048,1024]{1,0:T(8,128)(2,1)S(1)} %bitcast.4, bf16[1,2048]{1,0:T(2,128)(2,1)S(1)} %copy-done.1, bf16[128,1024]{1,0:T(8,128)(2,1)S(1)} %get-tuple-element.19.after), custom_call_target="tpu_custom_call" | custom-call | flops 2000000000 | tf_op jit(solution)/shard_map/weigh/pallas_call | solution.py:25
  25.0 2.0 %collective-permute-done.5.peak_got = f32[1,16]{1,0:T(1,128)S(1)} collective-permute-done((f32[1,16]{1,0:T(1,128)S(1)}, f32[1,16]{1,0:T(1,128)S(1)}, u32[]{:S(2)}, u32[]{:S(2)}) %collective-permute-start.5) | collective-permute-done | bytes 96 | tf_op jit(solution)/shard_map/ppermute | solution.py:44
  27.0 0.8 %project_first.1 = (f32[128,1024]{1,0:T(8,128)S(1)}, f32[128,128]{1,0:T(8,128)S(1)}, f32[1,16]{1,0:T(1,128)}) custom-call(bf16[128,1024]{1,0:T(8,128)(2,1)S(1)} %collective-permute-done.3.ctx_ref, bf16[2048,1024]{1,0:T(8,128)(2,1)S(1)} %weigh.1.w_ref, f32[1,16]{1,0:T(1,128)S(1)} %max.3.peak_ref, f32[1,16]{1,0:T(1,128)S(1)} %collective-permute-done.5.peak_got), custom_call_target="tpu_custom_call" | custom-call | flops 700000000 | tf_op jit(solution)/shard_map/project_first/pallas_call | solution.py:25
  27.9 0.6 %project_last.1 = (bf16[2,144,256]{2,1,0:T(8,128)(2,1)S(1)}, bf16[2,144,256]{2,1,0:T(8,128)(2,1)S(1)}) custom-call(bf16[128,1024]{1,0:T(8,128)(2,1)S(1)} %collective-permute-done.6.ctx_ref, bf16[2048,1024]{1,0:T(8,128)(2,1)S(1)} %weigh.1.w_ref, f32[128,1024]{1,0:T(8,128)S(1)} %get-tuple-element.22.sum_ref, f32[128,128]{1,0:T(8,128)S(1)} %get-tuple-element.23.square_ref), custom_call_target="tpu_custom_call" | custom-call | flops 500000000 | tf_op jit(solution)/shard_map/project_last/pallas_call | solution.py:25
  28.4 0.1 collective-permute-start.7
  28.5 1.4 %collective-permute-done.7.got_ref = bf16[2,144,256]{2,1,0:T(8,128)(2,1)S(1)} collective-permute-done((bf16[2,144,256]{2,1,0:T(8,128)(2,1)S(1)}, bf16[2,144,256]{2,1,0:T(8,128)(2,1)S(1)}, u32[]{:S(2)}, u32[]{:S(2)}) %collective-permute-start.7) | collective-permute-done | bytes 147488 | tf_op jit(solution)/shard_map/ppermute | solution.py:263
  29.9 1.6 %collective-permute-start.8 = (bf16[144,256]{1,0:T(8,128)(2,1)S(1)}, bf16[144,256]{1,0:T(8,128)(2,1)S(1)}, u32[]{:S(2)}, u32[]{:S(2)}) collective-permute-start(bf16[144,256]{1,0:T(8,128)(2,1)S(1)} %get-tuple-element.27), channel_id=1, source_target_pairs={{0,2},{1,3},{2,0},{3,1},{4,6},{5,7},{6,4},{7,5},{8,10},{9,11},{10,... | collective-permute-start | bytes 221192 | tf_op jit(solution)/shard_map/ppermute | solution.py:272
  31.5 2.8 %collective-permute-done.8.refs_0_ = bf16[144,256]{1,0:T(8,128)(2,1)S(1)} collective-permute-done((bf16[144,256]{1,0:T(8,128)(2,1)S(1)}, bf16[144,256]{1,0:T(8,128)(2,1)S(1)}, u32[]{:S(2)}, u32[]{:S(2)}) %collective-permute-start.8) | collective-permute-done | bytes 73760 | tf_op jit(solution)/shard_map/ppermute | solution.py:272
  34.3 0.8 %finish.1 = bf16[128,256]{1,0:T(8,128)(2,1)} custom-call(f32[144,256]{1,0:T(8,128)S(1)} %get-tuple-element.26.keep_ref, bf16[144,256]{1,0:T(8,128)(2,1)S(1)} %collective-permute-done.8.refs_0_), custom_call_target="tpu_custom_call" | custom-call | tf_op jit(solution)/shard_map/finish/pallas_call | solution.py:25
  (12 shorter events, 0.1 us)
Async XLA Ops:
  1.4 8.0 %collective-permute-start = (bf16[128,256]{1,0:T(8,128)(2,1)S(1)}, bf16[128,256]{1,0:T(8,128)(2,1)S(1)}, u32[]{:S(2)}, u32[]{:S(2)}) collective-permute-start(bf16[128,256]{1,0:T(8,128)(2,1)S(1)} %pad_maximum_fusion.after.refs_0_), channel_id=1, source_target_pairs={{0,4},{4,0},{8,12},{12,8},{1,5},{5,1},{9,13},{13,9},{2,6},{6,2},{1... | collective-permute-start | bytes 196616 | tf_op jit(solution)/shard_map/ppermute | solution.py:44
  4.5 7.3 %collective-permute-start.1 = (bf16[128,256]{1,0:T(8,128)(2,1)S(1)}, bf16[128,256]{1,0:T(8,128)(2,1)S(1)}, u32[]{:S(2)}, u32[]{:S(2)}) collective-permute-start(bf16[128,256]{1,0:T(8,128)(2,1)S(1)} %pad_maximum_fusion.after.refs_0_), channel_id=1, source_target_pairs={{0,8},{4,12},{8,0},{12,4},{1,9},{5,13},{9,1},{13,5},{2,10},{6,14},... | collective-permute-start | bytes 196616 | tf_op jit(solution)/shard_map/ppermute | solution.py:44
  7.1 6.1 %collective-permute-start.2 = (bf16[128,256]{1,0:T(8,128)(2,1)S(1)}, bf16[128,256]{1,0:T(8,128)(2,1)S(1)}, u32[]{:S(2)}, u32[]{:S(2)}) collective-permute-start(bf16[128,256]{1,0:T(8,128)(2,1)S(1)} %pad_maximum_fusion.after.refs_0_), channel_id=1, source_target_pairs={{0,12},{4,8},{8,4},{12,0},{1,13},{5,9},{9,5},{13,1},{2,14},{6,10},... | collective-permute-start | bytes 196616 | tf_op jit(solution)/shard_map/ppermute | solution.py:44
  7.1 1.0 %copy-start.2 = (bf16[1,128,2048]{2,1,0:T(8,128)(2,1)S(1)}, bf16[1,128,2048]{2,1,0:T(8,128)(2,1)}, u32[]{:S(2)}) copy-start(bf16[1,128,2048]{2,1,0:T(8,128)(2,1)} %q_ref.1) | copy-start | bytes 1572868
  8.1 0.7 %copy-start.3 = (s32[8]{0:T(128)S(1)}, s32[8]{0:T(128)}, u32[]{:S(2)}) copy-start(s32[8]{0:T(128)} %order_ref.1) | copy-start | bytes 100
  13.2 11.0 %copy-start = (bf16[1,2048,1024]{2,1,0:T(8,128)(2,1)S(1)}, bf16[1,2048,1024]{2,1,0:T(8,128)(2,1)}, u32[]{:S(2)}) copy-start(bf16[1,2048,1024]{2,1,0:T(8,128)(2,1)} %param.11) | copy-start | bytes 12582916
  13.2 11.0 %copy-start.1 = (bf16[1,2048]{1,0:T(2,128)(2,1)S(1)}, bf16[1,2048]{1,0:T(2,128)(2,1)}, u32[]{:S(2)}) copy-start(bf16[1,2048]{1,0:T(2,128)(2,1)} %gain_ref.1) | copy-start | bytes 12292
  15.0 12.0 %collective-permute-start.3 = (bf16[128,1024]{1,0:T(8,128)(2,1)S(1)}, bf16[128,1024]{1,0:T(8,128)(2,1)S(1)}, u32[]{:S(2)}, u32[]{:S(2)}) collective-permute-start(bf16[128,1024]{1,0:T(8,128)(2,1)S(1)} %get-tuple-element.17), channel_id=1, source_target_pairs={{16,0},{0,16},{17,1},{1,17},{18,2},{2,18},{19,3},{3,19},{20,4},{4,... | collective-permute-start | bytes 786440 | tf_op jit(solution)/shard_map/ppermute | solution.py:49
  18.5 9.4 %collective-permute-start.6 = (bf16[128,1024]{1,0:T(8,128)(2,1)S(1)}, bf16[128,1024]{1,0:T(8,128)(2,1)S(1)}, u32[]{:S(2)}, u32[]{:S(2)}) collective-permute-start(bf16[128,1024]{1,0:T(8,128)(2,1)S(1)} %get-tuple-element.19.after), channel_id=1, source_target_pairs={{16,0},{0,16},{17,1},{1,17},{18,2},{2,18},{19,3},{3,19},{20,4},{4,... | collective-permute-start | bytes 786440 | tf_op jit(solution)/shard_map/ppermute | solution.py:49
  19.0 3.5 %collective-permute-start.4 = (f32[1,16]{1,0:T(1,128)S(1)}, f32[1,16]{1,0:T(1,128)S(1)}, u32[]{:S(2)}, u32[]{:S(2)}) collective-permute-start(f32[1,16]{1,0:T(1,128)S(1)} %get-tuple-element.20), channel_id=1, source_target_pairs={{0,4},{4,0},{8,12},{12,8},{1,5},{5,1},{9,13},{13,9},{2,6},{6,2},{1... | collective-permute-start | bytes 200 | tf_op jit(solution)/shard_map/ppermute | solution.py:44
  22.6 4.4 %collective-permute-start.5 = (f32[1,16]{1,0:T(1,128)S(1)}, f32[1,16]{1,0:T(1,128)S(1)}, u32[]{:S(2)}, u32[]{:S(2)}) collective-permute-start(f32[1,16]{1,0:T(1,128)S(1)} %max.3.peak_ref), channel_id=1, source_target_pairs={{0,8},{4,12},{8,0},{12,4},{1,9},{5,13},{9,1},{13,5},{2,10},{6,14},... | collective-permute-start | bytes 200 | tf_op jit(solution)/shard_map/ppermute | solution.py:44
  28.4 1.4 %collective-permute-start.7 = (bf16[2,144,256]{2,1,0:T(8,128)(2,1)S(1)}, bf16[2,144,256]{2,1,0:T(8,128)(2,1)S(1)}, u32[]{:S(2)}, u32[]{:S(2)}) collective-permute-start(bf16[2,144,256]{2,1,0:T(8,128)(2,1)S(1)} %get-tuple-element.25), channel_id=1, source_target_pairs={{0,1},{1,0},{2,3},{3,2},{4,5},{5,4},{6,7},{7,6},{8,9},{9,8},{10,11... | collective-permute-start | bytes 442376 | tf_op jit(solution)/shard_map/ppermute | solution.py:263
  29.9 4.4 %collective-permute-start.8 = (bf16[144,256]{1,0:T(8,128)(2,1)S(1)}, bf16[144,256]{1,0:T(8,128)(2,1)S(1)}, u32[]{:S(2)}, u32[]{:S(2)}) collective-permute-start(bf16[144,256]{1,0:T(8,128)(2,1)S(1)} %get-tuple-element.27), channel_id=1, source_target_pairs={{0,2},{1,3},{2,0},{3,1},{4,6},{5,7},{6,4},{7,5},{8,10},{9,11},{10,... | collective-permute-start | bytes 221192 | tf_op jit(solution)/shard_map/ppermute | solution.py:272
where the time goes:
time: 35.4 us; the launch traced here: 35.1 us
  waiting for transfers between devices  13.4 us (38%)
  starting transfers between devices  11.1 us (31%)
  Pallas kernels  7.46 us (21%)
  local copies, waits for them, and re-layouts  1.7 us (5%)
  other arithmetic  0.79 us (2%)
  between operations  0.7 us (2%)
    ppermute x5, waiting for transfers between devices, swapped(): lax.ppermute(block, axis, [(i, partner(i, step, size)) for i in range(siz...  9.24 us
    pallas_call x8, Pallas kernels, call(): pl.pallas_call(kernel, out_shape=outs, in_specs=specs or [WHOLE] * len(ar...  7.46 us
    ppermute x5, starting transfers between devices, swapped(): lax.ppermute(block, axis, [(i, partner(i, step, size)) for i in range(siz...  7.25 us
    ppermute x1, waiting for transfers between devices, on_device(): lax.ppermute(block, 'tp', [(i, (i + 2 * (step + 1)) % peers) for i in ran...  2.83 us
    ppermute x2, starting transfers between devices, shifted(): lax.ppermute(block, axis, [((i - distance) % size, i) for i in range(size)])  2.16 us
    unnamed x8, local copies, waits for them, and re-layouts  1.7 us
    ppermute x1, starting transfers between devices, on_device(): lax.ppermute(block, 'tp', [(i, (i + 2 * (step + 1)) % peers) for i in ran...  1.58 us
    ppermute x1, waiting for transfers between devices, on_device(): got = lax.ppermute(give, 'tp', [(i, i ^ 1) for i in range(peers)])  1.36 us
  transfers between devices with their start and end apart: 9, of which 6 were waited for; matrix products, arithmetic and copies ran while one was open for 0% of the time, Pallas kernels for 12%

commit v1 on v0

v1 whole, which is shorter than its diff:
```python
import functools
import math

import jax
import jax.numpy as jnp
from jax import lax
from jax.experimental import pallas as pl
from jax.experimental.pallas import tpu as pltpu
from jax.sharding import PartitionSpec as P

DH = 128
LANES = 128
SQUARE_ROWS = 16
MASKED = -(2.0**100)
LOG2E = math.log2(math.e)
F32 = jnp.float32
BF16 = jnp.bfloat16
WHOLE = pl.BlockSpec(memory_space=pltpu.VMEM)
OUTSIDE = pl.BlockSpec(memory_space=pl.ANY)
SCALARS = pl.BlockSpec(memory_space=pltpu.SMEM)


def call(kernel, outs, args, specs=None, scratch=(), limit=16, name=None, aliases=None, micros=0):
    return pl.pallas_call(
        kernel,
        out_shape=outs,
        in_specs=specs or [WHOLE] * len(args),
        out_specs=jax.tree.map(lambda _: WHOLE, outs),
        scratch_shapes=scratch,
        name=name,
        input_output_aliases=aliases or {},
        cost_estimate=pl.CostEstimate(flops=int(micros * 1e9), bytes_accessed=0, transcendentals=0) if micros else None,
        compiler_params=pltpu.CompilerParams(vmem_limit_bytes=limit * 2**20),
    )(*args)


def partner(index, step, size):
    return (index + step) % size if size & (size - 1) else index ^ step


def swapped(block, axis, step):
    size = lax.axis_size(axis)
    return lax.ppermute(block, axis, [(i, partner(i, step, size)) for i in range(size)])


def shifted(block, axis, distance):
    size = lax.axis_size(axis)
    return lax.ppermute(block, axis, [((i - distance) % size, i) for i in range(size)])


def returned(block, step):
    sections, sources = lax.axis_size("pp"), lax.axis_size("cp")
    route = [
        (s * sources + c, (s - 1) % sections * sources + partner(c, step, sources))
        for s in range(sections)
        for c in range(sources)
    ]
    return lax.ppermute(block, ("pp", "cp"), route)


def bind_kernel(block_ref, after, out_ref):
    out_ref[...] = block_ref[...]


def bind(block, after):
    return call(
        bind_kernel, jax.ShapeDtypeStruct(block.shape, block.dtype), (block, after), [WHOLE, OUTSIDE], name="bind"
    )


def source_of(d, me, sources):
    return lax.rem(me - d + sources, sources) if sources & (sources - 1) else me ^ d


def take(first, q_ref, after, part_ref):
    part_ref[...] = q_ref[0, :, first:first + part_ref.shape[1]]


def prepare(order_ref, after, feature_ref):
    sources = lax.axis_size("cp")
    me = lax.axis_index("cp")
    rows = feature_ref.shape[2] // sources
    block = rows // 2
    feature = lax.broadcasted_iota(jnp.int32, (LANES, rows), 0)
    key = lax.broadcasted_iota(jnp.int32, (LANES, rows), 1)
    place = lax.rem(key, block)
    for side in range(2):
        mine = order_ref[2 * me + side]
        for d in range(sources):
            source = source_of(d, me, sources)
            other = jnp.where(key < block, order_ref[2 * source], order_ref[2 * source + 1])
            chosen = jnp.where(other == mine, place, jnp.where(other > mine, block, -1))
            feature_ref[side, :, d * rows:(d + 1) * rows] = jnp.where(feature == chosen, 1.0, 0.0).astype(BF16)


def attend(first_head, heads, sources, q_ref, feature_ref, *refs):
    pairs = refs[:sources]
    before, (ctx_ref, peak_ref, kt, v_all) = refs[sources:-4], refs[-4:]
    rows, width = q_ref.shape
    keys = v_all.shape[0]
    block = rows // 2
    kv_local = pairs[0].shape[1] // (2 * DH)
    group = heads // kv_local
    count = width // DH
    scale = 1.0 / math.sqrt(DH)
    if before:
        peak_ref[:, :first_head] = before[0][...]
    v_all[:, DH:] = jnp.ones((keys, DH), BF16)
    for side in range(2):
        kt[side, DH:, :] = feature_ref[side]
    held = None
    together = max(1, min(count, 12 * 512 // keys))
    peaks = {}
    spans = []
    for i in range(0, count, together):
        while i < count and (not spans or spans[-1][1] < min(i + together, count)):
            start = spans[-1][1] if spans else 0
            limit = ((first_head + start) // group + 1) * group - first_head
            spans.append((start, min(start + together, count, limit)))
    for start, stop in spans:
        g = (first_head + start) // group
        if g != held:
            held = g
            for d, pair in enumerate(pairs):
                part = slice(d * rows, (d + 1) * rows)
                turned = pair[:, g * DH:(g + 1) * DH].astype(F32).T.astype(BF16)
                kt[0, :DH, part] = turned
                kt[1, :DH, part] = turned
                v_all[part, :DH] = pair[:, (kv_local + g) * DH:(kv_local + g + 1) * DH]
        n = stop - start
        token = lax.rem(lax.broadcasted_iota(jnp.int32, (n * block, LANES), 0), block)
        lane = lax.broadcasted_iota(jnp.int32, (n * block, LANES), 1)
        blocked = jnp.where((lane > token) & (lane <= block), MASKED, 0.0).astype(BF16)
        for side in range(2):
            tokens = slice(side * block, (side + 1) * block)
            q = jnp.concatenate([q_ref[tokens, h * DH:(h + 1) * DH] for h in range(start, stop)], axis=0)
            q = jnp.concatenate([q, blocked], axis=1)
            s = jnp.dot(q, kt[side], preferred_element_type=F32)
            m = jnp.max(s, axis=1, keepdims=True)
            p = jnp.exp2((s - m) * (scale * LOG2E)).astype(BF16)
            o = jnp.dot(p, v_all[...], preferred_element_type=F32)
            o = (o[:, :DH] * (1.0 / o[:, DH:])).astype(BF16)
            for j in range(n):
                lines = slice(j * block, (j + 1) * block)
                ctx_ref[tokens, (start + j) * DH:(start + j + 1) * DH] = o[lines, :]
                one = jnp.max(m[lines, :], axis=0, keepdims=True)
                peaks[start + j] = jnp.maximum(peaks[start + j], one) if side else one
    for i, peak in peaks.items():
        peak_ref[:, first_head + i:first_head + i + 1] = peak * scale


def weigh(w_ref, gain_ref, after, out_ref):
    features, columns = w_ref.shape
    for f in range(0, features, LANES):
        gain = jnp.broadcast_to(gain_ref[:, f:f + LANES].astype(F32), (LANES, LANES)).T
        for c in range(0, columns, LANES):
            out_ref[f:f + LANES, c:c + LANES] = (w_ref[f:f + LANES, c:c + LANES].astype(F32) * gain).astype(BF16)


def square_sums(ctx_ref):
    total = None
    for c in range(0, ctx_ref.shape[1], LANES):
        wide = ctx_ref[:, c:c + LANES].astype(F32)
        total = wide * wide if total is None else total + wide * wide
    return jnp.broadcast_to(jnp.sum(total, axis=1, keepdims=True), total.shape)


def project_first(ctx_ref, w_ref, sum_ref, square_ref):
    square_ref[...] = square_sums(ctx_ref)
    sum_ref[...] = jnp.dot(ctx_ref[...], w_ref[:ctx_ref.shape[1], :], preferred_element_type=F32)


def project_last(ctx_ref, w_ref, sum_ref, square_ref, give_ref, keep_ref):
    rows, width = ctx_ref.shape
    start = w_ref.shape[0] - width
    squares = square_ref[...] + square_sums(ctx_ref)
    lanes = squares.T[:SQUARE_ROWS, :]
    first = lanes.astype(BF16)
    rest = (lanes - first.astype(F32)).astype(BF16)
    groups, cols = give_ref.shape[0], give_ref.shape[2]
    core = lax.rem(lax.axis_index("tp"), 2)
    for ref, side in ((give_ref, 1 - core), (keep_ref, core)):
        for y in range(groups):
            at = pl.ds(pl.multiple_of((2 * y + side) * cols, cols), cols)
            part = sum_ref[:, at] + jnp.dot(ctx_ref[...], w_ref[start:, at], preferred_element_type=F32)
            ref[y, :rows, :] = part.astype(BF16)
            ref[y, rows:, :rows] = first
            ref[y, rows:, rows:2 * rows] = rest
            if cols > 2 * rows:
                ref[y, rows:, 2 * rows:] = jnp.zeros((SQUARE_ROWS, cols - 2 * rows), BF16)


def merge(keep_ref, got_ref, peak_ref, peak_got, peak_out, *give_refs):
    peak_out[...] = jnp.maximum(peak_ref[...], peak_got[...])
    groups = keep_ref.shape[0]
    mine = lax.axis_index("tp") // 2
    for step, ref in enumerate(give_refs):
        y = lax.rem(mine + step, groups)
        total = keep_ref[y].astype(F32) + got_ref[y].astype(F32)
        ref[...] = total.astype(ref.dtype)


def finish(features, peak_ref, peak_got, keep_ref, *refs):
    peak_out, out_ref = refs[-2:]
    peak_out[...] = jnp.maximum(peak_ref[...], peak_got[...])
    rows = out_ref.shape[0]
    total = keep_ref[...]
    for ref in refs[:-2]:
        total = total + ref[...].astype(F32)
    squares = total[rows:rows + 8, :rows] + total[rows:rows + 8, rows:2 * rows]
    inverse = lax.rsqrt(squares / features + 1e-05)
    column = jnp.broadcast_to(inverse[:1, :], (rows, rows)).T[:, :1]
    out_ref[...] = (total[:rows, :] * column).astype(BF16)


def on_device(queries, key_vectors, value_vectors, block_order, norm_gain, kv_weight):
    rows, width = queries.shape[1:]
    heads = width // DH
    peers = lax.axis_size("tp")
    sources = lax.axis_size("cp")
    kv_width = key_vectors.shape[2]
    columns = kv_weight.shape[2]
    out_cols = columns // peers
    shape = jax.ShapeDtypeStruct
    steps = [2**i for i in range((sources - 1).bit_length())]

    pair_here = jnp.concatenate([key_vectors[0], value_vectors[0]], axis=1)
    pair = shifted(pair_here, "pp", 1)
    cut = heads * 3 // 4
    counts = [cut, heads - cut]
    starts = [0, cut]
    crossed = []
    for start, count, after in zip(starts, counts, [pair_here, pair]):
        part = call(
            functools.partial(take, start * DH),
            shape((rows, count * DH), BF16),
            (queries, after),
            [WHOLE, OUTSIDE],
            name="take",
            micros=3,
        )
        crossed.append(shifted(part, "pp", 1))
    moved = {d: swapped(pair, "cp", d) for d in reversed(range(1, sources))}
    pairs = [pair] + [moved[d] for d in range(1, sources)]
    features = call(
        prepare,
        shape((2, LANES, sources * rows), BF16),
        (block_order, pair),
        [SCALARS, OUTSIDE],
        name="prepare",
        micros=0.5,
    )
    contexts, peaks = [], []
    for start, count, part in zip(starts, counts, crossed):
        context, peak = call(
            functools.partial(attend, start, heads, sources),
            (shape((rows, count * DH), BF16), shape((1, start + count), F32)),
            (part, features, *pairs, *peaks[-1:]),
            scratch=[
                pltpu.VMEM((2, DH + LANES, sources * rows), BF16),
                pltpu.VMEM((sources * rows, 2 * DH), BF16),
            ],
            limit=32,
            name="attend",
            micros=count * 0.14,
        )
        contexts.append(context)
        peaks.append(peak)
        if start == 0:
            w = call(
                weigh,
                shape((width, columns), BF16),
                (kv_weight[0], norm_gain, context),
                [WHOLE, WHOLE, OUTSIDE],
                name="weigh",
                micros=1,
            )
            total, squares = call(
                project_first,
                (shape((rows, columns), F32), shape((rows, LANES), F32)),
                (context, w),
                name="project_first",
                micros=0.7,
            )
    slab = shape((peers // 2, rows + SQUARE_ROWS, out_cols), BF16)
    give, keep = call(
        project_last, (slab, slab), (contexts[-1], w, total, squares), name="project_last", micros=0.5
    )
    got = lax.ppermute(give, "tp", [(i, i ^ 1) for i in range(peers)])
    peak = bind(peaks[-1], give)
    slab = (rows + SQUARE_ROWS, out_cols)
    peak, mine, *others = call(
        merge,
        [shape((1, heads), F32), shape(slab, F32)] + [shape(slab, BF16)] * (peers // 2 - 1),
        (keep, got, shifted(peak, "pp", -1), returned(peak, steps[0])),
        name="merge",
    )
    for step in steps[1:-1]:
        peak = jnp.maximum(peak, swapped(peak, "cp", step))
    others = [
        lax.ppermute(block, "tp", [(i, (i + 2 * (step + 1)) % peers) for i in range(peers)])
        for step, block in enumerate(others)
    ]
    max_logits, kv_next = call(
        functools.partial(finish, width * peers),
        (shape((1, heads), F32), shape((rows, out_cols), BF16)),
        (peak, swapped(peak, "cp", steps[-1]), mine, *others),
        name="finish",
    )
    return (max_logits, kv_next[None])


def solution(mesh):
    return jax.shard_map(
        on_device,
        mesh=mesh,
        in_specs=(
            P("pp", "cp", "tp"),
            P("pp", "cp", "tp"),
            P("pp", "cp", "tp"),
            P(),
            P("pp", "tp"),
            P("pp", "tp", None),
        ),
        out_specs=(P("pp", "tp"), P("pp", "cp", "tp")),
        check_vma=False,
    )
```

time: 35.4 us -> 34.3 us (0.969)
  starting transfers between devices: 11.1 us -> 17.4 us
  waiting for transfers between devices: 13.4 us -> 8.32 us
  Pallas kernels: 7.46 us -> 5.74 us
  local copies, waits for them, and re-layouts: 1.7 us -> 1.06 us
    ppermute x5 -> x4, waiting for transfers between devices: 9.24 us -> 3.36 us  [swapped(): lax.ppermute(block, axis, [(i, partner(i, step, size)) for i in range(siz...]
    ppermute x2 -> x4, starting transfers between devices: 2.16 us -> 6.96 us  [shifted(): lax.ppermute(block, axis, [((i - distance) % size, i) for i in range(size)])]
    ppermute x2 -> x4, waiting for transfers between devices: 0.01 us -> 3.56 us  [shifted(): lax.ppermute(block, axis, [((i - distance) % size, i) for i in range(size)])]
    ppermute x1, waiting for transfers between devices: 2.83 us -> 0.01 us  [on_device(): lax.ppermute(block, 'tp', [(i, (i + 2 * (step + 1)) % peers) for i in ran...]
    pallas_call x8 -> x11, Pallas kernels: 7.46 us -> 5.74 us  [call(): pl.pallas_call(kernel, out_shape=outs, in_specs=specs or [WHOLE] * len(ar...]
    ppermute x0 -> x1, starting transfers between devices: none -> 1.68 us  [returned(): return lax.ppermute(block, ('pp', 'cp'), route)]
    ppermute x0 -> x1, waiting for transfers between devices: none -> 1.39 us  [returned(): return lax.ppermute(block, ('pp', 'cp'), route)]
    ppermute x1, waiting for transfers between devices: 1.36 us -> 0.01 us  [on_device(): got = lax.ppermute(give, 'tp', [(i, i ^ 1) for i in range(peers)])]
  transfers between devices with their start and end apart: 9 -> 11, of which waited for: 6 -> 6; matrix products, arithmetic and copies ran while one was open for 0% -> 0% of each run, Pallas kernels for 12% -> 11%
where the time goes in v1:
time: 34.3 us; the launch traced here: 34 us
  starting transfers between devices  17.4 us (51%)
  waiting for transfers between devices  8.32 us (24%)
  Pallas kernels  5.74 us (17%)
  local copies, waits for them, and re-layouts  1.06 us (3%)
  other arithmetic  0.78 us (2%)
  between operations  0.76 us (2%)
    ppermute x4, starting transfers between devices, swapped(): lax.ppermute(block, axis, [(i, partner(i, step, size)) for i in range(siz...  7.08 us
    ppermute x4, starting transfers between devices, shifted(): lax.ppermute(block, axis, [((i - distance) % size, i) for i in range(size)])  6.96 us
    pallas_call x11, Pallas kernels, call(): pl.pallas_call(kernel, out_shape=outs, in_specs=specs or [WHOLE] * len(ar...  5.74 us
    ppermute x4, waiting for transfers between devices, shifted(): lax.ppermute(block, axis, [((i - distance) % size, i) for i in range(size)])  3.56 us
    ppermute x4, waiting for transfers between devices, swapped(): lax.ppermute(block, axis, [(i, partner(i, step, size)) for i in range(siz...  3.36 us
    ppermute x1, starting transfers between devices, returned(): return lax.ppermute(block, ('pp', 'cp'), route)  1.68 us
    ppermute x1, starting transfers between devices, on_device(): lax.ppermute(block, 'tp', [(i, (i + 2 * (step + 1)) % peers) for i in ran...  1.59 us
    ppermute x1, waiting for transfers between devices, returned(): return lax.ppermute(block, ('pp', 'cp'), route)  1.39 us
  transfers between devices with their start and end apart: 11, of which 6 were waited for; matrix products, arithmetic and copies ran while one was open for 0% of the time, Pallas kernels for 11%

profile of v1, /device:TPU:0, one launch (start us, length us, event | category | flops | bytes accessed | tf_op | source)
XLA Modules:
  0.0 34.0 jit_solution(3520580532491732027)
XLA Ops:
  0.6 0.8 %pad_maximum_fusion.after = bf16[128,256]{1,0:T(8,128)(2,1)S(1)} fusion(bf16[128,128]{1,0:T(8,128)(2,1)} %bitcast.5, bf16[128,128]{1,0:T(8,128)(2,1)} %bitcast.6), kind=kLoop, calls=%fused_computation | loop fusion | flops 131072 | bytes 131072 | tf_op jit(solution)/shard_map/concatenate | solution.py:227
  1.4 3.0 %collective-permute-start = (bf16[128,256]{1,0:T(8,128)(2,1)S(1)}, bf16[128,256]{1,0:T(8,128)(2,1)S(1)}, u32[]{:S(2)}, u32[]{:S(2)}) collective-permute-start(bf16[128,256]{1,0:T(8,128)(2,1)S(1)} %pad_maximum_fusion.after), channel_id=1, source_target_pairs={{16,0},{0,16},{17,1},{1,17},{18,2},{2,18},{19,3},{3,19},{20,4},{4,... | collective-permute-start | bytes 196616 | tf_op jit(solution)/shard_map/ppermute | solution.py:48
  4.4 1.0 %copy-done.2 = bf16[1,128,2048]{2,1,0:T(8,128)(2,1)S(1)} copy-done((bf16[1,128,2048]{2,1,0:T(8,128)(2,1)S(1)}, bf16[1,128,2048]{2,1,0:T(8,128)(2,1)}, u32[]{:S(2)}) %copy-start.2) | copy-done | bytes 524312
  5.5 0.1 collective-permute-start.5
  5.6 1.3 %collective-permute-done.after.refs_0_ = bf16[128,256]{1,0:T(8,128)(2,1)S(1)} collective-permute-done((bf16[128,256]{1,0:T(8,128)(2,1)S(1)}, bf16[128,256]{1,0:T(8,128)(2,1)S(1)}, u32[]{:S(2)}, u32[]{:S(2)}) %collective-permute-start) | collective-permute-done | bytes 65568 | tf_op jit(solution)/shard_map/ppermute | solution.py:48
  6.9 3.9 %collective-permute-start.4 = (bf16[128,256]{1,0:T(8,128)(2,1)S(1)}, bf16[128,256]{1,0:T(8,128)(2,1)S(1)}, u32[]{:S(2)}, u32[]{:S(2)}) collective-permute-start(bf16[128,256]{1,0:T(8,128)(2,1)S(1)} %collective-permute-done.after.refs_0_), channel_id=1, source_target_pairs={{0,12},{4,8},{8,4},{12,0},{1,13},{5,9},{9,5},{13,1},{2,14},{6,10},... | collective-permute-start | bytes 196616 | tf_op jit(solution)/shard_map/ppermute | solution.py:43
  10.8 0.6 %collective-permute-start.2 = (bf16[128,256]{1,0:T(8,128)(2,1)S(1)}, bf16[128,256]{1,0:T(8,128)(2,1)S(1)}, u32[]{:S(2)}, u32[]{:S(2)}) collective-permute-start(bf16[128,256]{1,0:T(8,128)(2,1)S(1)} %collective-permute-done.after.refs_0_), channel_id=1, source_target_pairs={{0,4},{4,0},{8,12},{12,8},{1,5},{5,1},{9,13},{13,9},{2,6},{6,2},{1... | collective-permute-start | bytes 196616 | tf_op jit(solution)/shard_map/ppermute | solution.py:43
  11.4 2.4 %collective-permute-start.1 = (bf16[128,512]{1,0:T(8,128)(2,1)S(1)}, bf16[128,512]{1,0:T(8,128)(2,1)S(1)}, u32[]{:S(2)}, u32[]{:S(2)}) collective-permute-start(bf16[128,512]{1,0:T(8,128)(2,1)S(1)} %take.2), channel_id=1, source_target_pairs={{16,0},{0,16},{17,1},{1,17},{18,2},{2,18},{19,3},{3,19},{20,4},{4,... | collective-permute-start | bytes 393224 | tf_op jit(solution)/shard_map/ppermute | solution.py:48
  13.8 0.6 %prepare.1.feature_ref = bf16[2,128,512]{2,1,0:T(8,128)(2,1)S(1)} custom-call(s32[8]{0:T(128)S(1)} %copy-done.3, bf16[128,256]{1,0:T(8,128)(2,1)S(1)} %collective-permute-done.after.refs_0_), custom_call_target="tpu_custom_call" | custom-call | flops 500000000 | tf_op jit(solution)/shard_map/prepare/pallas_call | solution.py:24
  14.5 1.5 %collective-permute-done.3.refs_2_ = bf16[128,256]{1,0:T(8,128)(2,1)S(1)} collective-permute-done((bf16[128,256]{1,0:T(8,128)(2,1)S(1)}, bf16[128,256]{1,0:T(8,128)(2,1)S(1)}, u32[]{:S(2)}, u32[]{:S(2)}) %collective-permute-start.3) | collective-permute-done | bytes 65568 | tf_op jit(solution)/shard_map/ppermute | solution.py:43
  16.0 1.6 %collective-permute-done.5.q_ref = bf16[128,1536]{1,0:T(8,128)(2,1)S(1)} collective-permute-done((bf16[128,1536]{1,0:T(8,128)(2,1)S(1)}, bf16[128,1536]{1,0:T(8,128)(2,1)S(1)}, u32[]{:S(2)}, u32[]{:S(2)}) %collective-permute-start.5) | collective-permute-done | bytes 393248 | tf_op jit(solution)/shard_map/ppermute | solution.py:48
  17.5 1.6 %attend.2 = (bf16[128,1536]{1,0:T(8,128)(2,1)S(1)}, f32[1,12]{1,0:T(1,128)S(1)}) custom-call(bf16[128,1536]{1,0:T(8,128)(2,1)S(1)} %collective-permute-done.5.q_ref, bf16[2,128,512]{2,1,0:T(8,128)(2,1)S(1)} %prepare.1.feature_ref, bf16[128,256]{1,0:T(8,128)(2,1)S(1)} %collective-permute-done.after.refs_0_, ...), custom_call_target="tpu_custom_call" | custom-call | flops 1680000000 | tf_op jit(solution)/shard_map/attend/pallas_call | solution.py:24
  19.1 0.9 %weigh.1.w_ref = bf16[2048,1024]{1,0:T(8,128)(2,1)S(1)} custom-call(bf16[2048,1024]{1,0:T(8,128)(2,1)S(1)} %bitcast.4, bf16[1,2048]{1,0:T(2,128)(2,1)S(1)} %copy-done.1, bf16[128,1536]{1,0:T(8,128)(2,1)S(1)} %get-tuple-element.17.after.ctx_ref), custom_call_target="tpu_custom_call" | custom-call | flops 1000000000 | tf_op jit(solution)/shard_map/weigh/pallas_call | solution.py:24
  20.0 0.6 %project_first.1 = (f32[128,1024]{1,0:T(8,128)S(1)}, f32[128,128]{1,0:T(8,128)S(1)}) custom-call(bf16[128,1536]{1,0:T(8,128)(2,1)S(1)} %get-tuple-element.17.after.ctx_ref, bf16[2048,1024]{1,0:T(8,128)(2,1)S(1)} %weigh.1.w_ref), custom_call_target="tpu_custom_call" | custom-call | flops 700000000 | tf_op jit(solution)/shard_map/project_first/pallas_call | solution.py:24
  20.6 0.8 %attend.3 = (bf16[128,512]{1,0:T(8,128)(2,1)S(1)}, f32[1,16]{1,0:T(1,128)S(1)}) custom-call(bf16[128,512]{1,0:T(8,128)(2,1)S(1)} %collective-permute-done.1.q_ref, bf16[2,128,512]{2,1,0:T(8,128)(2,1)S(1)} %prepare.1.feature_ref, bf16[128,256]{1,0:T(8,128)(2,1)S(1)} %collective-permute-done.after.refs_0_, ...), custom_call_target="tpu_custom_call" | custom-call | flops 560000000 | tf_op jit(solution)/shard_map/attend/pallas_call | solution.py:24
  21.5 0.4 %project_last.1 = (bf16[2,144,256]{2,1,0:T(8,128)(2,1)S(1)}, bf16[2,144,256]{2,1,0:T(8,128)(2,1)S(1)}) custom-call(bf16[128,512]{1,0:T(8,128)(2,1)S(1)} %get-tuple-element.16.ctx_ref, bf16[2048,1024]{1,0:T(8,128)(2,1)S(1)} %weigh.1.w_ref, f32[128,1024]{1,0:T(8,128)S(1)} %get-tuple-element.18.sum_ref, f32[128,128]{1,0:T(8,128)S(1)} %get-tuple-element.19.square_ref), custom_call_target="tpu_custom_call" | custom-call | flops 500000000 | tf_op jit(solution)/shard_map/project_last/pallas_call | solution.py:24
  21.9 1.7 %collective-permute-start.8 = (f32[1,16]{1,0:T(1,128)S(1)}, f32[1,16]{1,0:T(1,128)S(1)}, u32[]{:S(2)}, u32[]{:S(2)}) collective-permute-start(f32[1,16]{1,0:T(1,128)S(1)} %bind.1), channel_id=1, source_target_pairs={{0,20},{4,16},{8,28},{12,24},{16,4},{20,0},{24,12},{28,8},{1,21},{... | collective-permute-start | bytes 200 | tf_op jit(solution)/shard_map/ppermute | solution.py:58
  23.6 1.4 %collective-permute-start.7 = (f32[1,16]{1,0:T(1,128)S(1)}, f32[1,16]{1,0:T(1,128)S(1)}, u32[]{:S(2)}, u32[]{:S(2)}) collective-permute-start(f32[1,16]{1,0:T(1,128)S(1)} %bind.1), channel_id=1, source_target_pairs={{16,0},{0,16},{17,1},{1,17},{18,2},{2,18},{19,3},{3,19},{20,4},{4,... | collective-permute-start | bytes 200 | tf_op jit(solution)/shard_map/ppermute | solution.py:48
  25.0 1.4 %collective-permute-done.8.peak_got = f32[1,16]{1,0:T(1,128)S(1)} collective-permute-done((f32[1,16]{1,0:T(1,128)S(1)}, f32[1,16]{1,0:T(1,128)S(1)}, u32[]{:S(2)}, u32[]{:S(2)}) %collective-permute-start.8) | collective-permute-done | bytes 96 | tf_op jit(solution)/shard_map/ppermute | solution.py:58
  26.4 0.7 %collective-permute-done.7.peak_ref = f32[1,16]{1,0:T(1,128)S(1)} collective-permute-done((f32[1,16]{1,0:T(1,128)S(1)}, f32[1,16]{1,0:T(1,128)S(1)}, u32[]{:S(2)}, u32[]{:S(2)}) %collective-permute-start.7) | collective-permute-done | bytes 96 | tf_op jit(solution)/shard_map/ppermute | solution.py:48
  27.2 1.6 %collective-permute-start.10 = (bf16[144,256]{1,0:T(8,128)(2,1)S(1)}, bf16[144,256]{1,0:T(8,128)(2,1)S(1)}, u32[]{:S(2)}, u32[]{:S(2)}) collective-permute-start(bf16[144,256]{1,0:T(8,128)(2,1)S(1)} %get-tuple-element.25), channel_id=1, source_target_pairs={{0,2},{1,3},{2,0},{3,1},{4,6},{5,7},{6,4},{7,5},{8,10},{9,11},{10,... | collective-permute-start | bytes 221192 | tf_op jit(solution)/shard_map/ppermute | solution.py:301
  28.8 2.6 %collective-permute-start.9 = (f32[1,16]{1,0:T(1,128)S(1)}, f32[1,16]{1,0:T(1,128)S(1)}, u32[]{:S(2)}, u32[]{:S(2)}) collective-permute-start(f32[1,16]{1,0:T(1,128)S(1)} %get-tuple-element.23.peak_ref), channel_id=1, source_target_pairs={{0,8},{4,12},{8,0},{12,4},{1,9},{5,13},{9,1},{13,5},{2,10},{6,14},... | collective-permute-start | bytes 200 | tf_op jit(solution)/shard_map/ppermute | solution.py:43
  31.4 1.9 %collective-permute-done.9.peak_got = f32[1,16]{1,0:T(1,128)S(1)} collective-permute-done((f32[1,16]{1,0:T(1,128)S(1)}, f32[1,16]{1,0:T(1,128)S(1)}, u32[]{:S(2)}, u32[]{:S(2)}) %collective-permute-start.9) | collective-permute-done | bytes 96 | tf_op jit(solution)/shard_map/ppermute | solution.py:43
  33.2 0.8 %finish.1 = (f32[1,16]{1,0:T(1,128)}, bf16[128,256]{1,0:T(8,128)(2,1)}) custom-call(f32[1,16]{1,0:T(1,128)S(1)} %get-tuple-element.23.peak_ref, f32[1,16]{1,0:T(1,128)S(1)} %collective-permute-done.9.peak_got, f32[144,256]{1,0:T(8,128)S(1)} %get-tuple-element.24.keep_ref, bf16[144,256]{1,0:T(8,128)(2,1)S(1)} %collective-permute-done.10.refs_0_), custom_call_target="tpu_custom_call" | custom-call | tf_op jit(solution)/shard_map/finish/pallas_call | solution.py:24
  (18 shorter events, 0.2 us)
Async XLA Ops:
  1.4 5.5 %collective-permute-start = (bf16[128,256]{1,0:T(8,128)(2,1)S(1)}, bf16[128,256]{1,0:T(8,128)(2,1)S(1)}, u32[]{:S(2)}, u32[]{:S(2)}) collective-permute-start(bf16[128,256]{1,0:T(8,128)(2,1)S(1)} %pad_maximum_fusion.after), channel_id=1, source_target_pairs={{16,0},{0,16},{17,1},{1,17},{18,2},{2,18},{19,3},{3,19},{20,4},{4,... | collective-permute-start | bytes 196616 | tf_op jit(solution)/shard_map/ppermute | solution.py:48
  4.4 1.0 %copy-start.2 = (bf16[1,128,2048]{2,1,0:T(8,128)(2,1)S(1)}, bf16[1,128,2048]{2,1,0:T(8,128)(2,1)}, u32[]{:S(2)}) copy-start(bf16[1,128,2048]{2,1,0:T(8,128)(2,1)} %q_ref.3) | copy-start | bytes 1572868
  5.5 8.4 %copy-start.3 = (s32[8]{0:T(128)S(1)}, s32[8]{0:T(128)}, u32[]{:S(2)}) copy-start(s32[8]{0:T(128)} %order_ref.1) | copy-start | bytes 100
  5.5 12.0 %collective-permute-start.5 = (bf16[128,1536]{1,0:T(8,128)(2,1)S(1)}, bf16[128,1536]{1,0:T(8,128)(2,1)S(1)}, u32[]{:S(2)}, u32[]{:S(2)}) collective-permute-start(bf16[128,1536]{1,0:T(8,128)(2,1)S(1)} %take.3), channel_id=1, source_target_pairs={{16,0},{0,16},{17,1},{1,17},{18,2},{2,18},{19,3},{3,19},{20,4},{4,... | collective-permute-start | bytes 1179656 | tf_op jit(solution)/shard_map/ppermute | solution.py:48
  6.9 7.6 %collective-permute-start.4 = (bf16[128,256]{1,0:T(8,128)(2,1)S(1)}, bf16[128,256]{1,0:T(8,128)(2,1)S(1)}, u32[]{:S(2)}, u32[]{:S(2)}) collective-permute-start(bf16[128,256]{1,0:T(8,128)(2,1)S(1)} %collective-permute-done.after.refs_0_), channel_id=1, source_target_pairs={{0,12},{4,8},{8,4},{12,0},{1,13},{5,9},{9,5},{13,1},{2,14},{6,10},... | collective-permute-start | bytes 196616 | tf_op jit(solution)/shard_map/ppermute | solution.py:43
  10.8 5.2 %collective-permute-start.3 = (bf16[128,256]{1,0:T(8,128)(2,1)S(1)}, bf16[128,256]{1,0:T(8,128)(2,1)S(1)}, u32[]{:S(2)}, u32[]{:S(2)}) collective-permute-start(bf16[128,256]{1,0:T(8,128)(2,1)S(1)} %collective-permute-done.after.refs_0_), channel_id=1, source_target_pairs={{0,8},{4,12},{8,0},{12,4},{1,9},{5,13},{9,1},{13,5},{2,10},{6,14},... | collective-permute-start | bytes 196616 | tf_op jit(solution)/shard_map/ppermute | solution.py:43
  10.8 5.2 %collective-permute-start.2 = (bf16[128,256]{1,0:T(8,128)(2,1)S(1)}, bf16[128,256]{1,0:T(8,128)(2,1)S(1)}, u32[]{:S(2)}, u32[]{:S(2)}) collective-permute-start(bf16[128,256]{1,0:T(8,128)(2,1)S(1)} %collective-permute-done.after.refs_0_), channel_id=1, source_target_pairs={{0,4},{4,0},{8,12},{12,8},{1,5},{5,1},{9,13},{13,9},{2,6},{6,2},{1... | collective-permute-start | bytes 196616 | tf_op jit(solution)/shard_map/ppermute | solution.py:43
  11.4 7.7 %copy-start = (bf16[1,2048,1024]{2,1,0:T(8,128)(2,1)S(1)}, bf16[1,2048,1024]{2,1,0:T(8,128)(2,1)}, u32[]{:S(2)}) copy-start(bf16[1,2048,1024]{2,1,0:T(8,128)(2,1)} %param.11) | copy-start | bytes 12582916
  11.4 7.7 %copy-start.1 = (bf16[1,2048]{1,0:T(2,128)(2,1)S(1)}, bf16[1,2048]{1,0:T(2,128)(2,1)}, u32[]{:S(2)}) copy-start(bf16[1,2048]{1,0:T(2,128)(2,1)} %gain_ref.1) | copy-start | bytes 12292
  11.4 9.2 %collective-permute-start.1 = (bf16[128,512]{1,0:T(8,128)(2,1)S(1)}, bf16[128,512]{1,0:T(8,128)(2,1)S(1)}, u32[]{:S(2)}, u32[]{:S(2)}) collective-permute-start(bf16[128,512]{1,0:T(8,128)(2,1)S(1)} %take.2), channel_id=1, source_target_pairs={{16,0},{0,16},{17,1},{1,17},{18,2},{2,18},{19,3},{3,19},{20,4},{4,... | collective-permute-start | bytes 393224 | tf_op jit(solution)/shard_map/ppermute | solution.py:48
  21.8 5.3 %collective-permute-start.6 = (bf16[2,144,256]{2,1,0:T(8,128)(2,1)S(1)}, bf16[2,144,256]{2,1,0:T(8,128)(2,1)S(1)}, u32[]{:S(2)}, u32[]{:S(2)}) collective-permute-start(bf16[2,144,256]{2,1,0:T(8,128)(2,1)S(1)} %get-tuple-element.21.after), channel_id=1, source_target_pairs={{0,1},{1,0},{2,3},{3,2},{4,5},{5,4},{6,7},{7,6},{8,9},{9,8},{10,11... | collective-permute-start | bytes 442376 | tf_op jit(solution)/shard_map/ppermute | solution.py:289
  21.9 4.5 %collective-permute-start.8 = (f32[1,16]{1,0:T(1,128)S(1)}, f32[1,16]{1,0:T(1,128)S(1)}, u32[]{:S(2)}, u32[]{:S(2)}) collective-permute-start(f32[1,16]{1,0:T(1,128)S(1)} %bind.1), channel_id=1, source_target_pairs={{0,20},{4,16},{8,28},{12,24},{16,4},{20,0},{24,12},{28,8},{1,21},{... | collective-permute-start | bytes 200 | tf_op jit(solution)/shard_map/ppermute | solution.py:58
  23.6 3.5 %collective-permute-start.7 = (f32[1,16]{1,0:T(1,128)S(1)}, f32[1,16]{1,0:T(1,128)S(1)}, u32[]{:S(2)}, u32[]{:S(2)}) collective-permute-start(f32[1,16]{1,0:T(1,128)S(1)} %bind.1), channel_id=1, source_target_pairs={{16,0},{0,16},{17,1},{1,17},{18,2},{2,18},{19,3},{3,19},{20,4},{4,... | collective-permute-start | bytes 200 | tf_op jit(solution)/shard_map/ppermute | solution.py:48
  27.2 6.0 %collective-permute-start.10 = (bf16[144,256]{1,0:T(8,128)(2,1)S(1)}, bf16[144,256]{1,0:T(8,128)(2,1)S(1)}, u32[]{:S(2)}, u32[]{:S(2)}) collective-permute-start(bf16[144,256]{1,0:T(8,128)(2,1)S(1)} %get-tuple-element.25), channel_id=1, source_target_pairs={{0,2},{1,3},{2,0},{3,1},{4,6},{5,7},{6,4},{7,5},{8,10},{9,11},{10,... | collective-permute-start | bytes 221192 | tf_op jit(solution)/shard_map/ppermute | solution.py:301
  28.8 4.4 %collective-permute-start.9 = (f32[1,16]{1,0:T(1,128)S(1)}, f32[1,16]{1,0:T(1,128)S(1)}, u32[]{:S(2)}, u32[]{:S(2)}) collective-permute-start(f32[1,16]{1,0:T(1,128)S(1)} %get-tuple-element.23.peak_ref), channel_id=1, source_target_pairs={{0,8},{4,12},{8,0},{12,4},{1,9},{5,13},{9,1},{13,5},{2,10},{6,14},... | collective-permute-start | bytes 200 | tf_op jit(solution)/shard_map/ppermute | solution.py:43

commit v2 on v1

--- a/solution.py
+++ b/solution.py
@@ -93,40 +93,42 @@
             feature_ref[side, :, d * rows:(d + 1) * rows] = jnp.where(feature == chosen, 1.0, 0.0).astype(BF16)
 
 
-def attend(first_head, heads, sources, q_ref, feature_ref, *refs):
-    pairs = refs[:sources]
-    before, (ctx_ref, peak_ref, kt, v_all) = refs[sources:-4], refs[-4:]
+def touch(block_ref, out_ref):
+    out_ref[...] = jnp.zeros(out_ref.shape, F32)
+
+
+def arrange(feature_ref, *refs):
+    pairs, (kt_ref, v_ref) = refs[:-2], refs[-2:]
+    rows = pairs[0].shape[0]
+    for g in range(v_ref.shape[0]):
+        v_ref[g, :, DH:] = jnp.ones((v_ref.shape[1], DH), BF16)
+        for side in range(2):
+            kt_ref[g, side, DH:, :] = feature_ref[side]
+        for d, pair in enumerate(pairs):
+            part = slice(d * rows, (d + 1) * rows)
+            turned = pair[:, g * DH:(g + 1) * DH].astype(F32).T.astype(BF16)
+            for side in range(2):
+                kt_ref[g, side, :DH, part] = turned
+            first = (v_ref.shape[0] + g) * DH
+            v_ref[g, part, :DH] = pair[:, first:first + DH]
+
+
+def attend(first_head, heads, q_ref, kt_ref, v_ref, *refs):
+    before, (ctx_ref, peak_ref) = refs[:-2], refs[-2:]
     rows, width = q_ref.shape
-    keys = v_all.shape[0]
+    keys = v_ref.shape[1]
     block = rows // 2
-    kv_local = pairs[0].shape[1] // (2 * DH)
-    group = heads // kv_local
+    group = heads // v_ref.shape[0]
     count = width // DH
     scale = 1.0 / math.sqrt(DH)
     if before:
         peak_ref[:, :first_head] = before[0][...]
-    v_all[:, DH:] = jnp.ones((keys, DH), BF16)
-    for side in range(2):
-        kt[side, DH:, :] = feature_ref[side]
-    held = None
     together = max(1, min(count, 12 * 512 // keys))
     peaks = {}
-    spans = []
-    for i in range(0, count, together):
-        while i < count and (not spans or spans[-1][1] < min(i + together, count)):
-            start = spans[-1][1] if spans else 0
-            limit = ((first_head + start) // group + 1) * group - first_head
-            spans.append((start, min(start + together, count, limit)))
-    for start, stop in spans:
+    start = 0
+    while start < count:
         g = (first_head + start) // group
-        if g != held:
-            held = g
-            for d, pair in enumerate(pairs):
-                part = slice(d * rows, (d + 1) * rows)
-                turned = pair[:, g * DH:(g + 1) * DH].astype(F32).T.astype(BF16)
-                kt[0, :DH, part] = turned
-                kt[1, :DH, part] = turned
-                v_all[part, :DH] = pair[:, (kv_local + g) * DH:(kv_local + g + 1) * DH]
+        stop = min(start + together, count, (g + 1) * group - first_head)
         n = stop - start
         token = lax.rem(lax.broadcasted_iota(jnp.int32, (n * block, LANES), 0), block)
         lane = lax.broadcasted_iota(jnp.int32, (n * block, LANES), 1)
@@ -135,16 +137,17 @@
             tokens = slice(side * block, (side + 1) * block)
             q = jnp.concatenate([q_ref[tokens, h * DH:(h + 1) * DH] for h in range(start, stop)], axis=0)
             q = jnp.concatenate([q, blocked], axis=1)
-            s = jnp.dot(q, kt[side], preferred_element_type=F32)
+            s = jnp.dot(q, kt_ref[g, side], preferred_element_type=F32)
             m = jnp.max(s, axis=1, keepdims=True)
             p = jnp.exp2((s - m) * (scale * LOG2E)).astype(BF16)
-            o = jnp.dot(p, v_all[...], preferred_element_type=F32)
+            o = jnp.dot(p, v_ref[g], preferred_element_type=F32)
             o = (o[:, :DH] * (1.0 / o[:, DH:])).astype(BF16)
             for j in range(n):
                 lines = slice(j * block, (j + 1) * block)
                 ctx_ref[tokens, (start + j) * DH:(start + j + 1) * DH] = o[lines, :]
                 one = jnp.max(m[lines, :], axis=0, keepdims=True)
                 peaks[start + j] = jnp.maximum(peaks[start + j], one) if side else one
+        start = stop
     for i, peak in peaks.items():
         peak_ref[:, first_head + i:first_head + i + 1] = peak * scale
 
@@ -230,51 +233,60 @@
     counts = [cut, heads - cut]
     starts = [0, cut]
     crossed = []
-    for start, count, after in zip(starts, counts, [pair_here, pair]):
+
+    def cross(start, count, after, micros):
         part = call(
             functools.partial(take, start * DH),
             shape((rows, count * DH), BF16),
             (queries, after),
             [WHOLE, OUTSIDE],
             name="take",
-            micros=3,
+            micros=micros,
         )
         crossed.append(shifted(part, "pp", 1))
+
+    mark = call(touch, shape((8, LANES), F32), (pair_here,), [OUTSIDE], name="touch", micros=3)
+    cross(starts[0], counts[0], mark, 3)
     moved = {d: swapped(pair, "cp", d) for d in reversed(range(1, sources))}
     pairs = [pair] + [moved[d] for d in range(1, sources)]
+    cross(starts[1], counts[1], moved[1], 0)
     features = call(
         prepare,
         shape((2, LANES, sources * rows), BF16),
         (block_order, pair),
         [SCALARS, OUTSIDE],
         name="prepare",
-        micros=0.5,
+        micros=2,
+    )
+    kv_local = kv_width // DH
+    kt, v_all = call(
+        arrange,
+        (shape((kv_local, 2, DH + LANES, sources * rows), BF16), shape((kv_local, sources * rows, 2 * DH), BF16)),
+        (features, *pairs),
+        name="arrange",
+        micros=2,
+    )
+    w = call(
+        weigh,
+        shape((width, columns), BF16),
+        (kv_weight[0], norm_gain, kt),
+        [WHOLE, WHOLE, OUTSIDE],
+        name="weigh",
+        micros=1,
     )
     contexts, peaks = [], []
     for start, count, part in zip(starts, counts, crossed):
         context, peak = call(
-            functools.partial(attend, start, heads, sources),
+            functools.partial(attend, start, heads),
             (shape((rows, count * DH), BF16), shape((1, start + count), F32)),
-            (part, features, *pairs, *peaks[-1:]),
-            scratch=[
-                pltpu.VMEM((2, DH + LANES, sources * rows), BF16),
-                pltpu.VMEM((sources * rows, 2 * DH), BF16),
-            ],
+            (part, kt, v_all, *peaks[-1:]),
             limit=32,
             name="attend",
-            micros=count * 0.14,
+            micros=count * 0.12,
         )
         contexts.append(context)
         peaks.append(peak)
         if start == 0:
-            w = call(
-                weigh,
-                shape((width, columns), BF16),
-                (kv_weight[0], norm_gain, context),
-                [WHOLE, WHOLE, OUTSIDE],
-                name="weigh",
-                micros=1,
-            )
             total, squares = call(
                 project_first,
                 (shape((rows, columns), F32), shape((rows, LANES), F32)),

time: 34.3 us -> 35 us (1.020)
  waiting for transfers between devices: 8.32 us -> 10.6 us
  local copies, waits for them, and re-layouts: 1.06 us -> 0.02 us
  starting transfers between devices: 17.4 us -> 17 us
    ppermute x4, waiting for transfers between devices: 3.36 us -> 5.82 us  [swapped(): lax.ppermute(block, axis, [(i, partner(i, step, size)) for i in range(siz...]
    unnamed x8, local copies, waits for them, and re-layouts: 1.06 us -> 0.02 us
    ppermute x1, starting transfers between devices: 1.68 us -> 2.58 us  [returned(): return lax.ppermute(block, ('pp', 'cp'), route)]
    ppermute x4, starting transfers between devices: 6.96 us -> 6.12 us  [shifted(): lax.ppermute(block, axis, [((i - distance) % size, i) for i in range(size)])]
    ppermute x4, starting transfers between devices: 7.08 us -> 6.66 us  [swapped(): lax.ppermute(block, axis, [(i, partner(i, step, size)) for i in range(siz...]
    ppermute x4, waiting for transfers between devices: 3.56 us -> 3.18 us  [shifted(): lax.ppermute(block, axis, [((i - distance) % size, i) for i in range(size)])]
    pallas_call x11 -> x13, Pallas kernels: 5.74 us -> 5.66 us  [call(): pl.pallas_call(kernel, out_shape=outs, in_specs=specs or [WHOLE] * len(ar...]
where the time goes in v2:
time: 35 us; the launch traced here: 34.8 us
  starting transfers between devices  17 us (49%)
  waiting for transfers between devices  10.6 us (30%)
  Pallas kernels  5.66 us (16%)
  other arithmetic  0.78 us (2%)
  between operations  0.76 us (2%)
    ppermute x4, starting transfers between devices, swapped(): lax.ppermute(block, axis, [(i, partner(i, step, size)) for i in range(siz...  6.66 us
    ppermute x4, starting transfers between devices, shifted(): lax.ppermute(block, axis, [((i - distance) % size, i) for i in range(size)])  6.12 us
    ppermute x4, waiting for transfers between devices, swapped(): lax.ppermute(block, axis, [(i, partner(i, step, size)) for i in range(siz...  5.82 us
    pallas_call x13, Pallas kernels, call(): pl.pallas_call(kernel, out_shape=outs, in_specs=specs or [WHOLE] * len(ar...  5.66 us
    ppermute x4, waiting for transfers between devices, shifted(): lax.ppermute(block, axis, [((i - distance) % size, i) for i in range(size)])  3.18 us
    ppermute x1, starting transfers between devices, returned(): return lax.ppermute(block, ('pp', 'cp'), route)  2.58 us
    ppermute x1, starting transfers between devices, on_device(): lax.ppermute(block, 'tp', [(i, (i + 2 * (step + 1)) % peers) for i in ran...  1.58 us
    ppermute x1, waiting for transfers between devices, returned(): return lax.ppermute(block, ('pp', 'cp'), route)  1.58 us
  transfers between devices with their start and end apart: 11, of which 6 were waited for; matrix products, arithmetic and copies ran while one was open for 0% of the time, Pallas kernels for 11%

profile of v2, /device:TPU:0, one launch (start us, length us, event | category | flops | bytes accessed | tf_op | source)
XLA Modules:
  0.0 34.8 jit_solution(13337931024554822011)
XLA Ops:
  0.6 0.8 %pad_maximum_fusion.block_ref = bf16[128,256]{1,0:T(8,128)(2,1)S(1)} fusion(bf16[128,128]{1,0:T(8,128)(2,1)} %bitcast.5, bf16[128,128]{1,0:T(8,128)(2,1)} %bitcast.6), kind=kLoop, calls=%fused_computation | loop fusion | flops 131072 | bytes 131072 | tf_op jit(solution)/shard_map/concatenate | solution.py:230
  1.4 3.0 %collective-permute-start = (bf16[128,256]{1,0:T(8,128)(2,1)S(1)}, bf16[128,256]{1,0:T(8,128)(2,1)S(1)}, u32[]{:S(2)}, u32[]{:S(2)}) collective-permute-start(bf16[128,256]{1,0:T(8,128)(2,1)S(1)} %pad_maximum_fusion.block_ref), channel_id=1, source_target_pairs={{16,0},{0,16},{17,1},{1,17},{18,2},{2,18},{19,3},{3,19},{20,4},{4,... | collective-permute-start | bytes 196616 | tf_op jit(solution)/shard_map/ppermute | solution.py:48
  4.5 1.0 %collective-permute-start.5 = (bf16[128,1536]{1,0:T(8,128)(2,1)S(1)}, bf16[128,1536]{1,0:T(8,128)(2,1)S(1)}, u32[]{:S(2)}, u32[]{:S(2)}) collective-permute-start(bf16[128,1536]{1,0:T(8,128)(2,1)S(1)} %take.3), channel_id=1, source_target_pairs={{16,0},{0,16},{17,1},{1,17},{18,2},{2,18},{19,3},{3,19},{20,4},{4,... | collective-permute-start | bytes 1179656 | tf_op jit(solution)/shard_map/ppermute | solution.py:48
  5.5 1.4 %collective-permute-done.after.refs_0_ = bf16[128,256]{1,0:T(8,128)(2,1)S(1)} collective-permute-done((bf16[128,256]{1,0:T(8,128)(2,1)S(1)}, bf16[128,256]{1,0:T(8,128)(2,1)S(1)}, u32[]{:S(2)}, u32[]{:S(2)}) %collective-permute-start) | collective-permute-done | bytes 65568 | tf_op jit(solution)/shard_map/ppermute | solution.py:48
  6.9 4.4 %collective-permute-start.4 = (bf16[128,256]{1,0:T(8,128)(2,1)S(1)}, bf16[128,256]{1,0:T(8,128)(2,1)S(1)}, u32[]{:S(2)}, u32[]{:S(2)}) collective-permute-start(bf16[128,256]{1,0:T(8,128)(2,1)S(1)} %collective-permute-done.after.refs_0_), channel_id=1, source_target_pairs={{0,12},{4,8},{8,4},{12,0},{1,13},{5,9},{9,5},{13,1},{2,14},{6,10},... | collective-permute-start | bytes 196616 | tf_op jit(solution)/shard_map/ppermute | solution.py:43
  11.3 0.6 %collective-permute-start.1 = (bf16[128,256]{1,0:T(8,128)(2,1)S(1)}, bf16[128,256]{1,0:T(8,128)(2,1)S(1)}, u32[]{:S(2)}, u32[]{:S(2)}) collective-permute-start(bf16[128,256]{1,0:T(8,128)(2,1)S(1)} %collective-permute-done.after.refs_0_), channel_id=1, source_target_pairs={{0,4},{4,0},{8,12},{12,8},{1,5},{5,1},{9,13},{13,9},{2,6},{6,2},{1... | collective-permute-start | bytes 196616 | tf_op jit(solution)/shard_map/ppermute | solution.py:43
  11.9 0.6 %prepare.1.feature_ref = bf16[2,128,512]{2,1,0:T(8,128)(2,1)S(1)} custom-call(s32[8]{0:T(128)S(1)} %copy-done.3, bf16[128,256]{1,0:T(8,128)(2,1)S(1)} %collective-permute-done.after.refs_0_), custom_call_target="tpu_custom_call" | custom-call | flops 2000000000 | tf_op jit(solution)/shard_map/prepare/pallas_call | solution.py:24
  12.5 3.1 %collective-permute-done.1.after.refs_1_ = bf16[128,256]{1,0:T(8,128)(2,1)S(1)} collective-permute-done((bf16[128,256]{1,0:T(8,128)(2,1)S(1)}, bf16[128,256]{1,0:T(8,128)(2,1)S(1)}, u32[]{:S(2)}, u32[]{:S(2)}) %collective-permute-start.1) | collective-permute-done | bytes 65568 | tf_op jit(solution)/shard_map/ppermute | solution.py:43
  15.6 1.7 %collective-permute-start.2 = (bf16[128,512]{1,0:T(8,128)(2,1)S(1)}, bf16[128,512]{1,0:T(8,128)(2,1)S(1)}, u32[]{:S(2)}, u32[]{:S(2)}) collective-permute-start(bf16[128,512]{1,0:T(8,128)(2,1)S(1)} %take.2), channel_id=1, source_target_pairs={{16,0},{0,16},{17,1},{1,17},{18,2},{2,18},{19,3},{3,19},{20,4},{4,... | collective-permute-start | bytes 393224 | tf_op jit(solution)/shard_map/ppermute | solution.py:48
  17.3 0.1 arrange.1
  17.5 0.9 %weigh.1.w_ref = bf16[2048,1024]{1,0:T(8,128)(2,1)S(1)} custom-call(bf16[2048,1024]{1,0:T(8,128)(2,1)S(1)} %bitcast.4, bf16[1,2048]{1,0:T(2,128)(2,1)S(1)} %copy-done.2, bf16[1,2,256,512]{3,2,1,0:T(8,128)(2,1)S(1)} %get-tuple-element.17.kt_ref.after), custom_call_target="tpu_custom_call" | custom-call | flops 1000000000 | tf_op jit(solution)/shard_map/weigh/pallas_call | solution.py:24
  18.4 1.4 %attend.2 = (bf16[128,1536]{1,0:T(8,128)(2,1)S(1)}, f32[1,12]{1,0:T(1,128)S(1)}) custom-call(bf16[128,1536]{1,0:T(8,128)(2,1)S(1)} %collective-permute-done.5.q_ref, bf16[1,2,256,512]{3,2,1,0:T(8,128)(2,1)S(1)} %get-tuple-element.17.kt_ref.after, bf16[1,512,256]{2,1,0:T(8,128)(2,1)S(1)} %get-tuple-element.18.v_ref), custom_call_target="tpu_custom_call" | custom-call | flops 1440000000 | tf_op jit(solution)/shard_map/attend/pallas_call | solution.py:24
  19.9 0.6 %project_first.1 = (f32[128,1024]{1,0:T(8,128)S(1)}, f32[128,128]{1,0:T(8,128)S(1)}) custom-call(bf16[128,1536]{1,0:T(8,128)(2,1)S(1)} %get-tuple-element.21.ctx_ref, bf16[2048,1024]{1,0:T(8,128)(2,1)S(1)} %weigh.1.w_ref), custom_call_target="tpu_custom_call" | custom-call | flops 700000000 | tf_op jit(solution)/shard_map/project_first/pallas_call | solution.py:24
  20.5 0.1 collective-permute-done.2.q_ref
  20.6 0.7 %attend.3 = (bf16[128,512]{1,0:T(8,128)(2,1)S(1)}, f32[1,16]{1,0:T(1,128)S(1)}) custom-call(bf16[128,512]{1,0:T(8,128)(2,1)S(1)} %collective-permute-done.2.q_ref, bf16[1,2,256,512]{3,2,1,0:T(8,128)(2,1)S(1)} %get-tuple-element.17.kt_ref.after, bf16[1,512,256]{2,1,0:T(8,128)(2,1)S(1)} %get-tuple-element.18.v_ref, f32[1,12]{1,0:T(1,128)S(1)} %get-tuple-element.19.refs_0_), custom_call_target="tpu_custom_call" | custom-call | flops 480000000 | tf_op jit(solution)/shard_map/attend/pallas_call | solution.py:24
  21.4 0.3 project_last.1
  21.8 2.6 %collective-permute-start.8 = (f32[1,16]{1,0:T(1,128)S(1)}, f32[1,16]{1,0:T(1,128)S(1)}, u32[]{:S(2)}, u32[]{:S(2)}) collective-permute-start(f32[1,16]{1,0:T(1,128)S(1)} %bind.1), channel_id=1, source_target_pairs={{0,20},{4,16},{8,28},{12,24},{16,4},{20,0},{24,12},{28,8},{1,21},{... | collective-permute-start | bytes 200 | tf_op jit(solution)/shard_map/ppermute | solution.py:58
  24.4 0.3 %collective-permute-start.7 = (f32[1,16]{1,0:T(1,128)S(1)}, f32[1,16]{1,0:T(1,128)S(1)}, u32[]{:S(2)}, u32[]{:S(2)}) collective-permute-start(f32[1,16]{1,0:T(1,128)S(1)} %bind.1), channel_id=1, source_target_pairs={{16,0},{0,16},{17,1},{1,17},{18,2},{2,18},{19,3},{3,19},{20,4},{4,... | collective-permute-start | bytes 200 | tf_op jit(solution)/shard_map/ppermute | solution.py:48
  24.7 1.6 %collective-permute-done.8.peak_got = f32[1,16]{1,0:T(1,128)S(1)} collective-permute-done((f32[1,16]{1,0:T(1,128)S(1)}, f32[1,16]{1,0:T(1,128)S(1)}, u32[]{:S(2)}, u32[]{:S(2)}) %collective-permute-start.8) | collective-permute-done | bytes 96 | tf_op jit(solution)/shard_map/ppermute | solution.py:58
  26.3 1.6 %collective-permute-done.7.peak_ref = f32[1,16]{1,0:T(1,128)S(1)} collective-permute-done((f32[1,16]{1,0:T(1,128)S(1)}, f32[1,16]{1,0:T(1,128)S(1)}, u32[]{:S(2)}, u32[]{:S(2)}) %collective-permute-start.7) | collective-permute-done | bytes 96 | tf_op jit(solution)/shard_map/ppermute | solution.py:48
  28.0 1.6 %collective-permute-start.10 = (bf16[144,256]{1,0:T(8,128)(2,1)S(1)}, bf16[144,256]{1,0:T(8,128)(2,1)S(1)}, u32[]{:S(2)}, u32[]{:S(2)}) collective-permute-start(bf16[144,256]{1,0:T(8,128)(2,1)S(1)} %get-tuple-element.29), channel_id=1, source_target_pairs={{0,2},{1,3},{2,0},{3,1},{4,6},{5,7},{6,4},{7,5},{8,10},{9,11},{10,... | collective-permute-start | bytes 221192 | tf_op jit(solution)/shard_map/ppermute | solution.py:313
  29.6 1.7 %collective-permute-start.9 = (f32[1,16]{1,0:T(1,128)S(1)}, f32[1,16]{1,0:T(1,128)S(1)}, u32[]{:S(2)}, u32[]{:S(2)}) collective-permute-start(f32[1,16]{1,0:T(1,128)S(1)} %get-tuple-element.27.peak_ref), channel_id=1, source_target_pairs={{0,8},{4,12},{8,0},{12,4},{1,9},{5,13},{9,1},{13,5},{2,10},{6,14},... | collective-permute-start | bytes 200 | tf_op jit(solution)/shard_map/ppermute | solution.py:43
  31.2 2.8 %collective-permute-done.9.peak_got = f32[1,16]{1,0:T(1,128)S(1)} collective-permute-done((f32[1,16]{1,0:T(1,128)S(1)}, f32[1,16]{1,0:T(1,128)S(1)}, u32[]{:S(2)}, u32[]{:S(2)}) %collective-permute-start.9) | collective-permute-done | bytes 96 | tf_op jit(solution)/shard_map/ppermute | solution.py:43
  34.0 0.8 %finish.1 = (f32[1,16]{1,0:T(1,128)}, bf16[128,256]{1,0:T(8,128)(2,1)}) custom-call(f32[1,16]{1,0:T(1,128)S(1)} %get-tuple-element.27.peak_ref, f32[1,16]{1,0:T(1,128)S(1)} %collective-permute-done.9.peak_got, f32[144,256]{1,0:T(8,128)S(1)} %get-tuple-element.28.keep_ref, bf16[144,256]{1,0:T(8,128)(2,1)S(1)} %collective-permute-done.10.refs_0_), custom_call_target="tpu_custom_call" | custom-call | tf_op jit(solution)/shard_map/finish/pallas_call | solution.py:24
  (20 shorter events, 0.2 us)
Async XLA Ops:
  1.4 3.0 %copy-start.1 = (bf16[1,128,2048]{2,1,0:T(8,128)(2,1)S(1)}, bf16[1,128,2048]{2,1,0:T(8,128)(2,1)}, u32[]{:S(2)}) copy-start(bf16[1,128,2048]{2,1,0:T(8,128)(2,1)} %q_ref.3) | copy-start | bytes 1572868
  1.4 5.5 %collective-permute-start = (bf16[128,256]{1,0:T(8,128)(2,1)S(1)}, bf16[128,256]{1,0:T(8,128)(2,1)S(1)}, u32[]{:S(2)}, u32[]{:S(2)}) collective-permute-start(bf16[128,256]{1,0:T(8,128)(2,1)S(1)} %pad_maximum_fusion.block_ref), channel_id=1, source_target_pairs={{16,0},{0,16},{17,1},{1,17},{18,2},{2,18},{19,3},{3,19},{20,4},{4,... | collective-permute-start | bytes 196616 | tf_op jit(solution)/shard_map/ppermute | solution.py:48
  4.4 7.5 %copy-start.3 = (s32[8]{0:T(128)S(1)}, s32[8]{0:T(128)}, u32[]{:S(2)}) copy-start(s32[8]{0:T(128)} %order_ref.1) | copy-start | bytes 100
  4.5 13.9 %collective-permute-start.5 = (bf16[128,1536]{1,0:T(8,128)(2,1)S(1)}, bf16[128,1536]{1,0:T(8,128)(2,1)S(1)}, u32[]{:S(2)}, u32[]{:S(2)}) collective-permute-start(bf16[128,1536]{1,0:T(8,128)(2,1)S(1)} %take.3), channel_id=1, source_target_pairs={{16,0},{0,16},{17,1},{1,17},{18,2},{2,18},{19,3},{3,19},{20,4},{4,... | collective-permute-start | bytes 1179656 | tf_op jit(solution)/shard_map/ppermute | solution.py:48
  6.9 10.4 %collective-permute-start.4 = (bf16[128,256]{1,0:T(8,128)(2,1)S(1)}, bf16[128,256]{1,0:T(8,128)(2,1)S(1)}, u32[]{:S(2)}, u32[]{:S(2)}) collective-permute-start(bf16[128,256]{1,0:T(8,128)(2,1)S(1)} %collective-permute-done.after.refs_0_), channel_id=1, source_target_pairs={{0,12},{4,8},{8,4},{12,0},{1,13},{5,9},{9,5},{13,1},{2,14},{6,10},... | collective-permute-start | bytes 196616 | tf_op jit(solution)/shard_map/ppermute | solution.py:43
  11.3 6.0 %collective-permute-start.3 = (bf16[128,256]{1,0:T(8,128)(2,1)S(1)}, bf16[128,256]{1,0:T(8,128)(2,1)S(1)}, u32[]{:S(2)}, u32[]{:S(2)}) collective-permute-start(bf16[128,256]{1,0:T(8,128)(2,1)S(1)} %collective-permute-done.after.refs_0_), channel_id=1, source_target_pairs={{0,8},{4,12},{8,0},{12,4},{1,9},{5,13},{9,1},{13,5},{2,10},{6,14},... | collective-permute-start | bytes 196616 | tf_op jit(solution)/shard_map/ppermute | solution.py:43
  11.3 4.3 %collective-permute-start.1 = (bf16[128,256]{1,0:T(8,128)(2,1)S(1)}, bf16[128,256]{1,0:T(8,128)(2,1)S(1)}, u32[]{:S(2)}, u32[]{:S(2)}) collective-permute-start(bf16[128,256]{1,0:T(8,128)(2,1)S(1)} %collective-permute-done.after.refs_0_), channel_id=1, source_target_pairs={{0,4},{4,0},{8,12},{12,8},{1,5},{5,1},{9,13},{13,9},{2,6},{6,2},{1... | collective-permute-start | bytes 196616 | tf_op jit(solution)/shard_map/ppermute | solution.py:43
  12.5 5.0 %copy-start = (bf16[1,2048,1024]{2,1,0:T(8,128)(2,1)S(1)}, bf16[1,2048,1024]{2,1,0:T(8,128)(2,1)}, u32[]{:S(2)}) copy-start(bf16[1,2048,1024]{2,1,0:T(8,128)(2,1)} %param.11) | copy-start | bytes 12582916
  12.5 5.0 %copy-start.2 = (bf16[1,2048]{1,0:T(2,128)(2,1)S(1)}, bf16[1,2048]{1,0:T(2,128)(2,1)}, u32[]{:S(2)}) copy-start(bf16[1,2048]{1,0:T(2,128)(2,1)} %gain_ref.1) | copy-start | bytes 12292
  15.6 5.0 %collective-permute-start.2 = (bf16[128,512]{1,0:T(8,128)(2,1)S(1)}, bf16[128,512]{1,0:T(8,128)(2,1)S(1)}, u32[]{:S(2)}, u32[]{:S(2)}) collective-permute-start(bf16[128,512]{1,0:T(8,128)(2,1)S(1)} %take.2), channel_id=1, source_target_pairs={{16,0},{0,16},{17,1},{1,17},{18,2},{2,18},{19,3},{3,19},{20,4},{4,... | collective-permute-start | bytes 393224 | tf_op jit(solution)/shard_map/ppermute | solution.py:48
  21.7 6.2 %collective-permute-start.6 = (bf16[2,144,256]{2,1,0:T(8,128)(2,1)S(1)}, bf16[2,144,256]{2,1,0:T(8,128)(2,1)S(1)}, u32[]{:S(2)}, u32[]{:S(2)}) collective-permute-start(bf16[2,144,256]{2,1,0:T(8,128)(2,1)S(1)} %get-tuple-element.25.after), channel_id=1, source_target_pairs={{0,1},{1,0},{2,3},{3,2},{4,5},{5,4},{6,7},{7,6},{8,9},{9,8},{10,11... | collective-permute-start | bytes 442376 | tf_op jit(solution)/shard_map/ppermute | solution.py:301
  21.8 4.5 %collective-permute-start.8 = (f32[1,16]{1,0:T(1,128)S(1)}, f32[1,16]{1,0:T(1,128)S(1)}, u32[]{:S(2)}, u32[]{:S(2)}) collective-permute-start(f32[1,16]{1,0:T(1,128)S(1)} %bind.1), channel_id=1, source_target_pairs={{0,20},{4,16},{8,28},{12,24},{16,4},{20,0},{24,12},{28,8},{1,21},{... | collective-permute-start | bytes 200 | tf_op jit(solution)/shard_map/ppermute | solution.py:58
  24.4 3.5 %collective-permute-start.7 = (f32[1,16]{1,0:T(1,128)S(1)}, f32[1,16]{1,0:T(1,128)S(1)}, u32[]{:S(2)}, u32[]{:S(2)}) collective-permute-start(f32[1,16]{1,0:T(1,128)S(1)} %bind.1), channel_id=1, source_target_pairs={{16,0},{0,16},{17,1},{1,17},{18,2},{2,18},{19,3},{3,19},{20,4},{4,... | collective-permute-start | bytes 200 | tf_op jit(solution)/shard_map/ppermute | solution.py:48
  28.0 6.0 %collective-permute-start.10 = (bf16[144,256]{1,0:T(8,128)(2,1)S(1)}, bf16[144,256]{1,0:T(8,128)(2,1)S(1)}, u32[]{:S(2)}, u32[]{:S(2)}) collective-permute-start(bf16[144,256]{1,0:T(8,128)(2,1)S(1)} %get-tuple-element.29), channel_id=1, source_target_pairs={{0,2},{1,3},{2,0},{3,1},{4,6},{5,7},{6,4},{7,5},{8,10},{9,11},{10,... | collective-permute-start | bytes 221192 | tf_op jit(solution)/shard_map/ppermute | solution.py:313
  29.6 4.4 %collective-permute-start.9 = (f32[1,16]{1,0:T(1,128)S(1)}, f32[1,16]{1,0:T(1,128)S(1)}, u32[]{:S(2)}, u32[]{:S(2)}) collective-permute-start(f32[1,16]{1,0:T(1,128)S(1)} %get-tuple-element.27.peak_ref), channel_id=1, source_target_pairs={{0,8},{4,12},{8,0},{12,4},{1,9},{5,13},{9,1},{13,5},{2,10},{6,14},... | collective-permute-start | bytes 200 | tf_op jit(solution)/shard_map/ppermute | solution.py:43

commit v3 on v2

--- a/solution.py
+++ b/solution.py
@@ -46,16 +46,6 @@
 def shifted(block, axis, distance):
     size = lax.axis_size(axis)
     return lax.ppermute(block, axis, [((i - distance) % size, i) for i in range(size)])
-
-
-def returned(block, step):
-    sections, sources = lax.axis_size("pp"), lax.axis_size("cp")
-    route = [
-        (s * sources + c, (s - 1) % sections * sources + partner(c, step, sources))
-        for s in range(sections)
-        for c in range(sources)
-    ]
-    return lax.ppermute(block, ("pp", "cp"), route)
 
 
 def bind_kernel(block_ref, after, out_ref):
@@ -97,59 +87,92 @@
     out_ref[...] = jnp.zeros(out_ref.shape, F32)
 
 
+def join(pair_ref, here_ref, out_ref):
+    width = pair_ref.shape[1]
+    out_ref[:, :width] = pair_ref[...]
+    out_ref[:, width:] = here_ref[:, :width // 2]
+
+
 def arrange(feature_ref, *refs):
-    pairs, (kt_ref, v_ref) = refs[:-2], refs[-2:]
-    rows = pairs[0].shape[0]
-    for g in range(v_ref.shape[0]):
+    triples, (kt_ref, v_ref, own_ref) = refs[:-3], refs[-3:]
+    rows = triples[0].shape[0]
+    kv_local = v_ref.shape[0]
+    for g in range(kv_local):
         v_ref[g, :, DH:] = jnp.ones((v_ref.shape[1], DH), BF16)
-        for side in range(2):
-            kt_ref[g, side, DH:, :] = feature_ref[side]
-        for d, pair in enumerate(pairs):
+        for ref in (kt_ref, own_ref):
+            for side in range(2):
+                ref[g, side, DH:, :] = feature_ref[side]
+        for d, triple in enumerate(triples):
             part = slice(d * rows, (d + 1) * rows)
-            turned = pair[:, g * DH:(g + 1) * DH].astype(F32).T.astype(BF16)
-            for side in range(2):
-                kt_ref[g, side, :DH, part] = turned
-            first = (v_ref.shape[0] + g) * DH
-            v_ref[g, part, :DH] = pair[:, first:first + DH]
-
-
-def attend(first_head, heads, q_ref, kt_ref, v_ref, *refs):
-    before, (ctx_ref, peak_ref) = refs[:-2], refs[-2:]
-    rows, width = q_ref.shape
-    keys = v_ref.shape[1]
-    block = rows // 2
-    group = heads // v_ref.shape[0]
-    count = width // DH
-    scale = 1.0 / math.sqrt(DH)
-    if before:
-        peak_ref[:, :first_head] = before[0][...]
-    together = max(1, min(count, 12 * 512 // keys))
-    peaks = {}
+            for ref, first in ((kt_ref, g * DH), (own_ref, (2 * kv_local + g) * DH)):
+                turned = triple[:, first:first + DH].astype(F32).T.astype(BF16)
+                for side in range(2):
+                    ref[g, side, :DH, part] = turned
+            first = (kv_local + g) * DH
+            v_ref[g, part, :DH] = triple[:, first:first + DH]
+
+
+def spans(first_head, count, group, together):
     start = 0
     while start < count:
         g = (first_head + start) // group
         stop = min(start + together, count, (g + 1) * group - first_head)
-        n = stop - start
-        token = lax.rem(lax.broadcasted_iota(jnp.int32, (n * block, LANES), 0), block)
-        lane = lax.broadcasted_iota(jnp.int32, (n * block, LANES), 1)
-        blocked = jnp.where((lane > token) & (lane <= block), MASKED, 0.0).astype(BF16)
+        yield g, start, stop
+        start = stop
+
+
+def stacked(q_ref, start, stop, side):
+    block = q_ref.shape[0] // 2
+    shape = ((stop - start) * block, LANES)
+    token = lax.rem(lax.broadcasted_iota(jnp.int32, shape, 0), block)
+    lane = lax.broadcasted_iota(jnp.int32, shape, 1)
+    blocked = jnp.where((lane > token) & (lane <= block), MASKED, 0.0).astype(BF16)
+    tokens = slice(side * block, (side + 1) * block)
+    q = jnp.concatenate([q_ref[tokens, h * DH:(h + 1) * DH] for h in range(start, stop)], axis=0)
+    return jnp.concatenate([q, blocked], axis=1)
+
+
+def maxima(q_ref, own_ref, peak_ref):
+    q_ref = q_ref.at[0]
+    block = q_ref.shape[0] // 2
+    heads = q_ref.shape[1] // DH
+    keys = own_ref.shape[3]
+    for g, start, stop in spans(0, heads, heads // own_ref.shape[0], max(1, 8 * 512 // keys)):
+        tops = []
         for side in range(2):
-            tokens = slice(side * block, (side + 1) * block)
-            q = jnp.concatenate([q_ref[tokens, h * DH:(h + 1) * DH] for h in range(start, stop)], axis=0)
-            q = jnp.concatenate([q, blocked], axis=1)
-            s = jnp.dot(q, kt_ref[g, side], preferred_element_type=F32)
+            s = jnp.dot(stacked(q_ref, start, stop, side), own_ref[g, side], preferred_element_type=F32)
+            top = s[:, :LANES]
+            for c in range(LANES, keys, LANES):
+                top = jnp.maximum(top, s[:, c:c + LANES])
+            tops.append(top)
+        top = jnp.maximum(*tops)
+        for j in range(stop - start):
+            one = jnp.max(top[j * block:(j + 1) * block, :], axis=0, keepdims=True)
+            h = start + j
+            peak_ref[:, h:h + 1] = jnp.max(one, axis=1, keepdims=True) * (1.0 / math.sqrt(DH))
+
+
+def attend(first_head, heads, q_ref, kt_ref, v_ref, after, ctx_ref):
+    rows, width = q_ref.shape
+    keys = v_ref.shape[1]
+    block = rows // 2
+    count = width // DH
+    scale = 1.0 / math.sqrt(DH)
+    for g, start, stop in spans(first_head, count, heads // v_ref.shape[0], max(1, 12 * 512 // keys)):
+        scores = [
+            jnp.dot(stacked(q_ref, start, stop, side), kt_ref[g, side], preferred_element_type=F32) for side in range(2)
+        ]
+        probs = []
+        for s in scores:
             m = jnp.max(s, axis=1, keepdims=True)
-            p = jnp.exp2((s - m) * (scale * LOG2E)).astype(BF16)
-            o = jnp.dot(p, v_ref[g], preferred_element_type=F32)
+            probs.append(jnp.exp2((s - m) * (scale * LOG2E)).astype(BF16))
+        for side in range(2):
+            o = jnp.dot(probs[side], v_ref[g], preferred_element_type=F32)
             o = (o[:, :DH] * (1.0 / o[:, DH:])).astype(BF16)
-            for j in range(n):
-                lines = slice(j * block, (j + 1) * block)
-                ctx_ref[tokens, (start + j) * DH:(start + j + 1) * DH] = o[lines, :]
-                one = jnp.max(m[lines, :], axis=0, keepdims=True)
-                peaks[start + j] = jnp.maximum(peaks[start + j], one) if side else one
-        start = stop
-    for i, peak in peaks.items():
-        peak_ref[:, first_head + i:first_head + i + 1] = peak * scale
+            for j in range(stop - start):
+                ctx_ref[side * block:(side + 1) * block, (start + j) * DH:(start + j + 1) * DH] = o[
+                    j * block:(j + 1) * block, :
+                ]
 
 
 def weigh(w_ref, gain_ref, after, out_ref):
@@ -247,45 +270,48 @@
 
     mark = call(touch, shape((8, LANES), F32), (pair_here,), [OUTSIDE], name="touch", micros=3)
     cross(starts[0], counts[0], mark, 3)
-    moved = {d: swapped(pair, "cp", d) for d in reversed(range(1, sources))}
-    pairs = [pair] + [moved[d] for d in range(1, sources)]
-    cross(starts[1], counts[1], moved[1], 0)
+    triple = call(join, shape((rows, 3 * kv_width), BF16), (pair, pair_here), name="join")
+    moved = {d: swapped(triple, "cp", d) for d in reversed(range(1, sources))}
+    triples = [triple] + [moved[d] for d in range(1, sources)]
+    cross(starts[1], counts[1], triple, 0)
     features = call(
         prepare,
         shape((2, LANES, sources * rows), BF16),
-        (block_order, pair),
+        (block_order, triple),
         [SCALARS, OUTSIDE],
         name="prepare",
-        micros=2,
-    )
-    kv_local = kv_width // DH
-    kt, v_all = call(
-        arrange,
-        (shape((kv_local, 2, DH + LANES, sources * rows), BF16), shape((kv_local, sources * rows, 2 * DH), BF16)),
-        (features, *pairs),
-        name="arrange",
-        micros=2,
+        micros=3,
     )
     w = call(
         weigh,
         shape((width, columns), BF16),
-        (kv_weight[0], norm_gain, kt),
+        (kv_weight[0], norm_gain, features),
         [WHOLE, WHOLE, OUTSIDE],
         name="weigh",
         micros=1,
     )
-    contexts, peaks = [], []
+    kv_local = kv_width // DH
+    turned = shape((kv_local, 2, DH + LANES, sources * rows), BF16)
+    kt, v_all, own = call(
+        arrange,
+        (turned, shape((kv_local, sources * rows, 2 * DH), BF16), turned),
+        (features, *triples),
+        name="arrange",
+        micros=0.2,
+    )
+    peak = call(maxima, shape((1, heads), F32), (queries, own), limit=32, name="maxima", micros=0.7)
+    contexts, after = [], peak
     for start, count, part in zip(starts, counts, crossed):
-        context, peak = call(
+        context = call(
             functools.partial(attend, start, heads),
-            (shape((rows, count * DH), BF16), shape((1, start + count), F32)),
-            (part, kt, v_all, *peaks[-1:]),
+            shape((rows, count * DH), BF16),
+            (part, kt, v_all, after),
+            [WHOLE, WHOLE, WHOLE, OUTSIDE],
             limit=32,
             name="attend",
             micros=count * 0.12,
         )
         contexts.append(context)
-        peaks.append(peak)
         if start == 0:
             total, squares = call(
                 project_first,
@@ -294,17 +320,18 @@
                 name="project_first",
                 micros=0.7,
             )
+            after = squares
     slab = shape((peers // 2, rows + SQUARE_ROWS, out_cols), BF16)
     give, keep = call(
         project_last, (slab, slab), (contexts[-1], w, total, squares), name="project_last", micros=0.5
     )
     got = lax.ppermute(give, "tp", [(i, i ^ 1) for i in range(peers)])
-    peak = bind(peaks[-1], give)
+    peak = bind(peak, give)
     slab = (rows + SQUARE_ROWS, out_cols)
     peak, mine, *others = call(
         merge,
         [shape((1, heads), F32), shape(slab, F32)] + [shape(slab, BF16)] * (peers // 2 - 1),
-        (keep, got, shifted(peak, "pp", -1), returned(peak, steps[0])),
+        (keep, got, peak, swapped(peak, "cp", steps[0])),
         name="merge",
     )
     for step in steps[1:-1]:

time: 35 us -> 33.1 us (0.946)
  waiting for transfers between devices: 10.6 us -> 8.9 us
  starting transfers between devices: 17 us -> 16.3 us
  Pallas kernels: 5.66 us -> 6.16 us
    ppermute x1 -> x0, starting transfers between devices: 2.58 us -> none  [returned(): return lax.ppermute(block, ('pp', 'cp'), route)]
    ppermute x4 -> x5, starting transfers between devices: 6.66 us -> 8.63 us  [swapped(): lax.ppermute(block, axis, [(i, partner(i, step, size)) for i in range(siz...]
    ppermute x4 -> x3, waiting for transfers between devices: 3.18 us -> 1.42 us  [shifted(): lax.ppermute(block, axis, [((i - distance) % size, i) for i in range(size)])]
    ppermute x4 -> x5, waiting for transfers between devices: 5.82 us -> 7.48 us  [swapped(): lax.ppermute(block, axis, [(i, partner(i, step, size)) for i in range(siz...]
    ppermute x1 -> x0, waiting for transfers between devices: 1.58 us -> none  [returned(): return lax.ppermute(block, ('pp', 'cp'), route)]
    pallas_call x13 -> x15, Pallas kernels: 5.66 us -> 6.16 us  [call(): pl.pallas_call(kernel, out_shape=outs, in_specs=specs or [WHOLE] * len(ar...]
    ppermute x4 -> x3, starting transfers between devices: 6.12 us -> 5.99 us  [shifted(): lax.ppermute(block, axis, [((i - distance) % size, i) for i in range(size)])]
  transfers between devices with their start and end apart: 11 -> 10, of which waited for: 6 -> 5; matrix products, arithmetic and copies ran while one was open for 0% -> 0% of each run, Pallas kernels for 11% -> 13%
where the time goes in v3:
time: 33.1 us; the launch traced here: 32.9 us
  starting transfers between devices  16.3 us (49%)
  waiting for transfers between devices  8.9 us (27%)
  Pallas kernels  6.16 us (19%)
  other arithmetic  0.78 us (2%)
  between operations  0.76 us (2%)
    ppermute x5, starting transfers between devices, swapped(): lax.ppermute(block, axis, [(i, partner(i, step, size)) for i in range(siz...  8.63 us
    ppermute x5, waiting for transfers between devices, swapped(): lax.ppermute(block, axis, [(i, partner(i, step, size)) for i in range(siz...  7.48 us
    pallas_call x15, Pallas kernels, call(): pl.pallas_call(kernel, out_shape=outs, in_specs=specs or [WHOLE] * len(ar...  6.16 us
    ppermute x3, starting transfers between devices, shifted(): lax.ppermute(block, axis, [((i - distance) % size, i) for i in range(size)])  5.99 us
    ppermute x1, starting transfers between devices, on_device(): lax.ppermute(block, 'tp', [(i, (i + 2 * (step + 1)) % peers) for i in ran...  1.59 us
    ppermute x3, waiting for transfers between devices, shifted(): lax.ppermute(block, axis, [((i - distance) % size, i) for i in range(size)])  1.42 us
    concatenate x1, other arithmetic, on_device(): pair_here = jnp.concatenate([key_vectors[0], value_vectors[0]], axis=1)  0.78 us
  transfers between devices with their start and end apart: 10, of which 5 were waited for; matrix products, arithmetic and copies ran while one was open for 0% of the time, Pallas kernels for 13%

profile of v3, /device:TPU:0, one launch (start us, length us, event | category | flops | bytes accessed | tf_op | source)
XLA Modules:
  0.0 32.9 jit_solution(5960874865420785275)
XLA Ops:
  0.6 0.8 %pad_maximum_fusion.here_ref.block_ref = bf16[128,256]{1,0:T(8,128)(2,1)S(1)} fusion(bf16[128,128]{1,0:T(8,128)(2,1)} %bitcast.5, bf16[128,128]{1,0:T(8,128)(2,1)} %bitcast.6), kind=kLoop, calls=%fused_computation | loop fusion | flops 131072 | bytes 131072 | tf_op jit(solution)/shard_map/concatenate | solution.py:253
  1.4 3.0 %collective-permute-start = (bf16[128,256]{1,0:T(8,128)(2,1)S(1)}, bf16[128,256]{1,0:T(8,128)(2,1)S(1)}, u32[]{:S(2)}, u32[]{:S(2)}) collective-permute-start(bf16[128,256]{1,0:T(8,128)(2,1)S(1)} %pad_maximum_fusion.here_ref.block_ref), channel_id=1, source_target_pairs={{16,0},{0,16},{17,1},{1,17},{18,2},{2,18},{19,3},{3,19},{20,4},{4,... | collective-permute-start | bytes 196616 | tf_op jit(solution)/shard_map/ppermute | solution.py:48
  4.5 1.0 %collective-permute-start.5 = (bf16[128,1536]{1,0:T(8,128)(2,1)S(1)}, bf16[128,1536]{1,0:T(8,128)(2,1)S(1)}, u32[]{:S(2)}, u32[]{:S(2)}) collective-permute-start(bf16[128,1536]{1,0:T(8,128)(2,1)S(1)} %take.3), channel_id=1, source_target_pairs={{16,0},{0,16},{17,1},{1,17},{18,2},{2,18},{19,3},{3,19},{20,4},{4,... | collective-permute-start | bytes 1179656 | tf_op jit(solution)/shard_map/ppermute | solution.py:48
  5.5 1.4 %collective-permute-done.pair_ref = bf16[128,256]{1,0:T(8,128)(2,1)S(1)} collective-permute-done((bf16[128,256]{1,0:T(8,128)(2,1)S(1)}, bf16[128,256]{1,0:T(8,128)(2,1)S(1)}, u32[]{:S(2)}, u32[]{:S(2)}) %collective-permute-start) | collective-permute-done | bytes 65568 | tf_op jit(solution)/shard_map/ppermute | solution.py:48
  6.9 2.5 %collective-permute-start.2 = (bf16[128,384]{1,0:T(8,128)(2,1)S(1)}, bf16[128,384]{1,0:T(8,128)(2,1)S(1)}, u32[]{:S(2)}, u32[]{:S(2)}) collective-permute-start(bf16[128,384]{1,0:T(8,128)(2,1)S(1)} %join.1.after.refs_0_), channel_id=1, source_target_pairs={{0,4},{4,0},{8,12},{12,8},{1,5},{5,1},{9,13},{13,9},{2,6},{6,2},{1... | collective-permute-start | bytes 294920 | tf_op jit(solution)/shard_map/ppermute | solution.py:43
  9.4 2.6 %collective-permute-start.3 = (bf16[128,384]{1,0:T(8,128)(2,1)S(1)}, bf16[128,384]{1,0:T(8,128)(2,1)S(1)}, u32[]{:S(2)}, u32[]{:S(2)}) collective-permute-start(bf16[128,384]{1,0:T(8,128)(2,1)S(1)} %join.1.after.refs_0_), channel_id=1, source_target_pairs={{0,8},{4,12},{8,0},{12,4},{1,9},{5,13},{9,1},{13,5},{2,10},{6,14},... | collective-permute-start | bytes 294920 | tf_op jit(solution)/shard_map/ppermute | solution.py:43
  12.0 0.6 %prepare.1.feature_ref.after = bf16[2,128,512]{2,1,0:T(8,128)(2,1)S(1)} custom-call(s32[8]{0:T(128)S(1)} %copy-done.3, bf16[128,384]{1,0:T(8,128)(2,1)S(1)} %join.1.after.refs_0_), custom_call_target="tpu_custom_call" | custom-call | flops 3000000000 | tf_op jit(solution)/shard_map/prepare/pallas_call | solution.py:24
  12.6 2.0 %collective-permute-start.1 = (bf16[128,512]{1,0:T(8,128)(2,1)S(1)}, bf16[128,512]{1,0:T(8,128)(2,1)S(1)}, u32[]{:S(2)}, u32[]{:S(2)}) collective-permute-start(bf16[128,512]{1,0:T(8,128)(2,1)S(1)} %take.2), channel_id=1, source_target_pairs={{16,0},{0,16},{17,1},{1,17},{18,2},{2,18},{19,3},{3,19},{20,4},{4,... | collective-permute-start | bytes 393224 | tf_op jit(solution)/shard_map/ppermute | solution.py:48
  14.6 0.9 %weigh.1.w_ref = bf16[2048,1024]{1,0:T(8,128)(2,1)S(1)} custom-call(bf16[2048,1024]{1,0:T(8,128)(2,1)S(1)} %bitcast.4, bf16[1,2048]{1,0:T(2,128)(2,1)S(1)} %copy-done.2, bf16[2,128,512]{2,1,0:T(8,128)(2,1)S(1)} %prepare.1.feature_ref.after), custom_call_target="tpu_custom_call" | custom-call | flops 1000000000 | tf_op jit(solution)/shard_map/weigh/pallas_call | solution.py:24
  15.5 1.6 %collective-permute-done.3.refs_2_ = bf16[128,384]{1,0:T(8,128)(2,1)S(1)} collective-permute-done((bf16[128,384]{1,0:T(8,128)(2,1)S(1)}, bf16[128,384]{1,0:T(8,128)(2,1)S(1)}, u32[]{:S(2)}, u32[]{:S(2)}) %collective-permute-start.3) | collective-permute-done | bytes 98336 | tf_op jit(solution)/shard_map/ppermute | solution.py:43
  17.1 1.4 %collective-permute-done.4.refs_3_ = bf16[128,384]{1,0:T(8,128)(2,1)S(1)} collective-permute-done((bf16[128,384]{1,0:T(8,128)(2,1)S(1)}, bf16[128,384]{1,0:T(8,128)(2,1)S(1)}, u32[]{:S(2)}, u32[]{:S(2)}) %collective-permute-start.4) | collective-permute-done | bytes 98336 | tf_op jit(solution)/shard_map/ppermute | solution.py:43
  18.5 0.2 arrange.1
  18.7 0.8 %maxima.1.after.block_ref = f32[1,16]{1,0:T(1,128)S(1)} custom-call(bf16[1,128,2048]{2,1,0:T(8,128)(2,1)S(1)} %copy-done.1, bf16[1,2,256,512]{3,2,1,0:T(8,128)(2,1)S(1)} %get-tuple-element.16.own_ref), custom_call_target="tpu_custom_call" | custom-call | flops 700000000 | tf_op jit(solution)/shard_map/maxima/pallas_call | solution.py:24
  19.5 1.2 %attend.2.ctx_ref = bf16[128,1536]{1,0:T(8,128)(2,1)S(1)} custom-call(bf16[128,1536]{1,0:T(8,128)(2,1)S(1)} %collective-permute-done.5.q_ref, bf16[1,2,256,512]{3,2,1,0:T(8,128)(2,1)S(1)} %get-tuple-element.14.kt_ref, bf16[1,512,256]{2,1,0:T(8,128)(2,1)S(1)} %get-tuple-element.15.v_ref, f32[1,16]{1,0:T(1,128)S(1)} %maxima.1.after.block_ref), custom_call_target="tpu_custom_call" | custom-call | flops 1440000000 | tf_op jit(solution)/shard_map/attend/pallas_call | solution.py:24
  20.7 0.6 %project_first.1 = (f32[128,1024]{1,0:T(8,128)S(1)}, f32[128,128]{1,0:T(8,128)S(1)}) custom-call(bf16[128,1536]{1,0:T(8,128)(2,1)S(1)} %attend.2.ctx_ref, bf16[2048,1024]{1,0:T(8,128)(2,1)S(1)} %weigh.1.w_ref), custom_call_target="tpu_custom_call" | custom-call | flops 700000000 | tf_op jit(solution)/shard_map/project_first/pallas_call | solution.py:24
  21.3 0.7 %attend.3.ctx_ref = bf16[128,512]{1,0:T(8,128)(2,1)S(1)} custom-call(bf16[128,512]{1,0:T(8,128)(2,1)S(1)} %collective-permute-done.1.q_ref, bf16[1,2,256,512]{3,2,1,0:T(8,128)(2,1)S(1)} %get-tuple-element.14.kt_ref, bf16[1,512,256]{2,1,0:T(8,128)(2,1)S(1)} %get-tuple-element.15.v_ref, f32[128,128]{1,0:T(8,128)S(1)} %get-tuple-element.17.after.square_ref), custom_call_target="tpu_custom_call" | custom-call | flops 480000000 | tf_op jit(solution)/shard_map/attend/pallas_call | solution.py:24
  22.0 0.4 %project_last.1 = (bf16[2,144,256]{2,1,0:T(8,128)(2,1)S(1)}, bf16[2,144,256]{2,1,0:T(8,128)(2,1)S(1)}) custom-call(bf16[128,512]{1,0:T(8,128)(2,1)S(1)} %attend.3.ctx_ref, bf16[2048,1024]{1,0:T(8,128)(2,1)S(1)} %weigh.1.w_ref, f32[128,1024]{1,0:T(8,128)S(1)} %get-tuple-element.18.sum_ref, f32[128,128]{1,0:T(8,128)S(1)} %get-tuple-element.17.after.square_ref), custom_call_target="tpu_custom_call" | custom-call | flops 500000000 | tf_op jit(solution)/shard_map/project_last/pallas_call | solution.py:24
  22.3 0.1 collective-permute-start.6
  22.4 1.3 %collective-permute-start.7 = (f32[1,16]{1,0:T(1,128)S(1)}, f32[1,16]{1,0:T(1,128)S(1)}, u32[]{:S(2)}, u32[]{:S(2)}) collective-permute-start(f32[1,16]{1,0:T(1,128)S(1)} %bind.1.peak_ref), channel_id=1, source_target_pairs={{0,4},{4,0},{8,12},{12,8},{1,5},{5,1},{9,13},{13,9},{2,6},{6,2},{1... | collective-permute-start | bytes 200 | tf_op jit(solution)/shard_map/ppermute | solution.py:43
  23.7 2.3 %collective-permute-done.7.peak_got = f32[1,16]{1,0:T(1,128)S(1)} collective-permute-done((f32[1,16]{1,0:T(1,128)S(1)}, f32[1,16]{1,0:T(1,128)S(1)}, u32[]{:S(2)}, u32[]{:S(2)}) %collective-permute-start.7) | collective-permute-done | bytes 96 | tf_op jit(solution)/shard_map/ppermute | solution.py:43
  26.1 1.6 %collective-permute-start.9 = (bf16[144,256]{1,0:T(8,128)(2,1)S(1)}, bf16[144,256]{1,0:T(8,128)(2,1)S(1)}, u32[]{:S(2)}, u32[]{:S(2)}) collective-permute-start(bf16[144,256]{1,0:T(8,128)(2,1)S(1)} %get-tuple-element.23), channel_id=1, source_target_pairs={{0,2},{1,3},{2,0},{3,1},{4,6},{5,7},{6,4},{7,5},{8,10},{9,11},{10,... | collective-permute-start | bytes 221192 | tf_op jit(solution)/shard_map/ppermute | solution.py:340
  27.6 2.3 %collective-permute-start.8 = (f32[1,16]{1,0:T(1,128)S(1)}, f32[1,16]{1,0:T(1,128)S(1)}, u32[]{:S(2)}, u32[]{:S(2)}) collective-permute-start(f32[1,16]{1,0:T(1,128)S(1)} %get-tuple-element.21.peak_ref), channel_id=1, source_target_pairs={{0,8},{4,12},{8,0},{12,4},{1,9},{5,13},{9,1},{13,5},{2,10},{6,14},... | collective-permute-start | bytes 200 | tf_op jit(solution)/shard_map/ppermute | solution.py:43
  29.9 2.2 %collective-permute-done.8.peak_got = f32[1,16]{1,0:T(1,128)S(1)} collective-permute-done((f32[1,16]{1,0:T(1,128)S(1)}, f32[1,16]{1,0:T(1,128)S(1)}, u32[]{:S(2)}, u32[]{:S(2)}) %collective-permute-start.8) | collective-permute-done | bytes 96 | tf_op jit(solution)/shard_map/ppermute | solution.py:43
  32.1 0.8 %finish.1 = (f32[1,16]{1,0:T(1,128)}, bf16[128,256]{1,0:T(8,128)(2,1)}) custom-call(f32[1,16]{1,0:T(1,128)S(1)} %get-tuple-element.21.peak_ref, f32[1,16]{1,0:T(1,128)S(1)} %collective-permute-done.8.peak_got, f32[144,256]{1,0:T(8,128)S(1)} %get-tuple-element.22.keep_ref, bf16[144,256]{1,0:T(8,128)(2,1)S(1)} %collective-permute-done.9.refs_0_), custom_call_target="tpu_custom_call" | custom-call | tf_op jit(solution)/shard_map/finish/pallas_call | solution.py:24
  (20 shorter events, 0.1 us)
Async XLA Ops:
  1.4 3.0 %copy-start.1 = (bf16[1,128,2048]{2,1,0:T(8,128)(2,1)S(1)}, bf16[1,128,2048]{2,1,0:T(8,128)(2,1)}, u32[]{:S(2)}) copy-start(bf16[1,128,2048]{2,1,0:T(8,128)(2,1)} %q_ref.5) | copy-start | bytes 1572868
  1.4 5.5 %collective-permute-start = (bf16[128,256]{1,0:T(8,128)(2,1)S(1)}, bf16[128,256]{1,0:T(8,128)(2,1)S(1)}, u32[]{:S(2)}, u32[]{:S(2)}) collective-permute-start(bf16[128,256]{1,0:T(8,128)(2,1)S(1)} %pad_maximum_fusion.here_ref.block_ref), channel_id=1, source_target_pairs={{16,0},{0,16},{17,1},{1,17},{18,2},{2,18},{19,3},{3,19},{20,4},{4,... | collective-permute-start | bytes 196616 | tf_op jit(solution)/shard_map/ppermute | solution.py:48
  4.4 7.6 %copy-start.3 = (s32[8]{0:T(128)S(1)}, s32[8]{0:T(128)}, u32[]{:S(2)}) copy-start(s32[8]{0:T(128)} %order_ref.1) | copy-start | bytes 100
  4.5 15.0 %collective-permute-start.5 = (bf16[128,1536]{1,0:T(8,128)(2,1)S(1)}, bf16[128,1536]{1,0:T(8,128)(2,1)S(1)}, u32[]{:S(2)}, u32[]{:S(2)}) collective-permute-start(bf16[128,1536]{1,0:T(8,128)(2,1)S(1)} %take.3), channel_id=1, source_target_pairs={{16,0},{0,16},{17,1},{1,17},{18,2},{2,18},{19,3},{3,19},{20,4},{4,... | collective-permute-start | bytes 1179656 | tf_op jit(solution)/shard_map/ppermute | solution.py:48
  6.9 7.7 %copy-start = (bf16[1,2048,1024]{2,1,0:T(8,128)(2,1)S(1)}, bf16[1,2048,1024]{2,1,0:T(8,128)(2,1)}, u32[]{:S(2)}) copy-start(bf16[1,2048,1024]{2,1,0:T(8,128)(2,1)} %param.11) | copy-start | bytes 12582916
  6.9 7.7 %copy-start.2 = (bf16[1,2048]{1,0:T(2,128)(2,1)S(1)}, bf16[1,2048]{1,0:T(2,128)(2,1)}, u32[]{:S(2)}) copy-start(bf16[1,2048]{1,0:T(2,128)(2,1)} %gain_ref.1) | copy-start | bytes 12292
  6.9 8.5 %collective-permute-start.2 = (bf16[128,384]{1,0:T(8,128)(2,1)S(1)}, bf16[128,384]{1,0:T(8,128)(2,1)S(1)}, u32[]{:S(2)}, u32[]{:S(2)}) collective-permute-start(bf16[128,384]{1,0:T(8,128)(2,1)S(1)} %join.1.after.refs_0_), channel_id=1, source_target_pairs={{0,4},{4,0},{8,12},{12,8},{1,5},{5,1},{9,13},{13,9},{2,6},{6,2},{1... | collective-permute-start | bytes 294920 | tf_op jit(solution)/shard_map/ppermute | solution.py:43
  9.4 7.7 %collective-permute-start.3 = (bf16[128,384]{1,0:T(8,128)(2,1)S(1)}, bf16[128,384]{1,0:T(8,128)(2,1)S(1)}, u32[]{:S(2)}, u32[]{:S(2)}) collective-permute-start(bf16[128,384]{1,0:T(8,128)(2,1)S(1)} %join.1.after.refs_0_), channel_id=1, source_target_pairs={{0,8},{4,12},{8,0},{12,4},{1,9},{5,13},{9,1},{13,5},{2,10},{6,14},... | collective-permute-start | bytes 294920 | tf_op jit(solution)/shard_map/ppermute | solution.py:43
  12.0 6.5 %collective-permute-start.4 = (bf16[128,384]{1,0:T(8,128)(2,1)S(1)}, bf16[128,384]{1,0:T(8,128)(2,1)S(1)}, u32[]{:S(2)}, u32[]{:S(2)}) collective-permute-start(bf16[128,384]{1,0:T(8,128)(2,1)S(1)} %join.1.after.refs_0_), channel_id=1, source_target_pairs={{0,12},{4,8},{8,4},{12,0},{1,13},{5,9},{9,5},{13,1},{2,14},{6,10},... | collective-permute-start | bytes 294920 | tf_op jit(solution)/shard_map/ppermute | solution.py:43
  12.6 8.6 %collective-permute-start.1 = (bf16[128,512]{1,0:T(8,128)(2,1)S(1)}, bf16[128,512]{1,0:T(8,128)(2,1)S(1)}, u32[]{:S(2)}, u32[]{:S(2)}) collective-permute-start(bf16[128,512]{1,0:T(8,128)(2,1)S(1)} %take.2), channel_id=1, source_target_pairs={{16,0},{0,16},{17,1},{1,17},{18,2},{2,18},{19,3},{3,19},{20,4},{4,... | collective-permute-start | bytes 393224 | tf_op jit(solution)/shard_map/ppermute | solution.py:48
  22.3 3.7 %collective-permute-start.6 = (bf16[2,144,256]{2,1,0:T(8,128)(2,1)S(1)}, bf16[2,144,256]{2,1,0:T(8,128)(2,1)S(1)}, u32[]{:S(2)}, u32[]{:S(2)}) collective-permute-start(bf16[2,144,256]{2,1,0:T(8,128)(2,1)S(1)} %get-tuple-element.20.after), channel_id=1, source_target_pairs={{0,1},{1,0},{2,3},{3,2},{4,5},{5,4},{6,7},{7,6},{8,9},{9,8},{10,11... | collective-permute-start | bytes 442376 | tf_op jit(solution)/shard_map/ppermute | solution.py:328
  22.4 3.6 %collective-permute-start.7 = (f32[1,16]{1,0:T(1,128)S(1)}, f32[1,16]{1,0:T(1,128)S(1)}, u32[]{:S(2)}, u32[]{:S(2)}) collective-permute-start(f32[1,16]{1,0:T(1,128)S(1)} %bind.1.peak_ref), channel_id=1, source_target_pairs={{0,4},{4,0},{8,12},{12,8},{1,5},{5,1},{9,13},{13,9},{2,6},{6,2},{1... | collective-permute-start | bytes 200 | tf_op jit(solution)/shard_map/ppermute | solution.py:43
  26.1 6.0 %collective-permute-start.9 = (bf16[144,256]{1,0:T(8,128)(2,1)S(1)}, bf16[144,256]{1,0:T(8,128)(2,1)S(1)}, u32[]{:S(2)}, u32[]{:S(2)}) collective-permute-start(bf16[144,256]{1,0:T(8,128)(2,1)S(1)} %get-tuple-element.23), channel_id=1, source_target_pairs={{0,2},{1,3},{2,0},{3,1},{4,6},{5,7},{6,4},{7,5},{8,10},{9,11},{10,... | collective-permute-start | bytes 221192 | tf_op jit(solution)/shard_map/ppermute | solution.py:340
  27.6 4.4 %collective-permute-start.8 = (f32[1,16]{1,0:T(1,128)S(1)}, f32[1,16]{1,0:T(1,128)S(1)}, u32[]{:S(2)}, u32[]{:S(2)}) collective-permute-start(f32[1,16]{1,0:T(1,128)S(1)} %get-tuple-element.21.peak_ref), channel_id=1, source_target_pairs={{0,8},{4,12},{8,0},{12,4},{1,9},{5,13},{9,1},{13,5},{2,10},{6,14},... | collective-permute-start | bytes 200 | tf_op jit(solution)/shard_map/ppermute | solution.py:43

commit v4 on v3

--- a/solution.py
+++ b/solution.py
@@ -93,7 +93,7 @@
     out_ref[:, width:] = here_ref[:, :width // 2]
 
 
-def arrange(feature_ref, *refs):
+def arrange(after, feature_ref, *refs):
     triples, (kt_ref, v_ref, own_ref) = refs[:-3], refs[-3:]
     rows = triples[0].shape[0]
     kv_local = v_ref.shape[0]
@@ -196,7 +196,7 @@
     sum_ref[...] = jnp.dot(ctx_ref[...], w_ref[:ctx_ref.shape[1], :], preferred_element_type=F32)
 
 
-def project_last(ctx_ref, w_ref, sum_ref, square_ref, give_ref, keep_ref):
+def project_last(ctx_ref, w_ref, sum_ref, square_ref, after, give_ref, keep_ref):
     rows, width = ctx_ref.shape
     start = w_ref.shape[0] - width
     squares = square_ref[...] + square_sums(ctx_ref)
@@ -216,8 +216,11 @@
                 ref[y, rows:, 2 * rows:] = jnp.zeros((SQUARE_ROWS, cols - 2 * rows), BF16)
 
 
-def merge(keep_ref, got_ref, peak_ref, peak_got, peak_out, *give_refs):
-    peak_out[...] = jnp.maximum(peak_ref[...], peak_got[...])
+def larger(left_ref, right_ref, after, out_ref):
+    out_ref[...] = jnp.maximum(left_ref[...], right_ref[...])
+
+
+def merge(keep_ref, got_ref, *give_refs):
     groups = keep_ref.shape[0]
     mine = lax.axis_index("tp") // 2
     for step, ref in enumerate(give_refs):
@@ -277,7 +280,7 @@
     features = call(
         prepare,
         shape((2, LANES, sources * rows), BF16),
-        (block_order, triple),
+        (block_order, mark),
         [SCALARS, OUTSIDE],
         name="prepare",
         micros=3,
@@ -285,7 +288,7 @@
     w = call(
         weigh,
         shape((width, columns), BF16),
-        (kv_weight[0], norm_gain, features),
+        (kv_weight[0], norm_gain, moved[sources - 1]),
         [WHOLE, WHOLE, OUTSIDE],
         name="weigh",
         micros=1,
@@ -295,7 +298,8 @@
     kt, v_all, own = call(
         arrange,
         (turned, shape((kv_local, sources * rows, 2 * DH), BF16), turned),
-        (features, *triples),
+        (w, features, *triples),
+        [OUTSIDE] + [WHOLE] * (1 + sources),
         name="arrange",
         micros=0.2,
     )
@@ -321,21 +325,29 @@
                 micros=0.7,
             )
             after = squares
+    for step in steps[:-1]:
+        peak = call(
+            larger,
+            shape((1, heads), F32),
+            (peak, swapped(peak, "cp", step), squares),
+            [WHOLE, WHOLE, OUTSIDE],
+            name="larger",
+        )
     slab = shape((peers // 2, rows + SQUARE_ROWS, out_cols), BF16)
     give, keep = call(
-        project_last, (slab, slab), (contexts[-1], w, total, squares), name="project_last", micros=0.5
+        project_last,
+        (slab, slab),
+        (contexts[-1], w, total, squares, peak),
+        [WHOLE] * 4 + [OUTSIDE],
+        name="project_last",
+        micros=0.5,
     )
     got = lax.ppermute(give, "tp", [(i, i ^ 1) for i in range(peers)])
     peak = bind(peak, give)
     slab = (rows + SQUARE_ROWS, out_cols)
-    peak, mine, *others = call(
-        merge,
-        [shape((1, heads), F32), shape(slab, F32)] + [shape(slab, BF16)] * (peers // 2 - 1),
-        (keep, got, peak, swapped(peak, "cp", steps[0])),
-        name="merge",
-    )
-    for step in steps[1:-1]:
-        peak = jnp.maximum(peak, swapped(peak, "cp", step))
+    mine, *others = call(
+        merge, [shape(slab, F32)] + [shape(slab, BF16)] * (peers // 2 - 1), (keep, got), name="merge"
+    )
     others = [
         lax.ppermute(block, "tp", [(i, (i + 2 * (step + 1)) % peers) for i in range(peers)])
         for step, block in enumerate(others)

time: 33.1 us -> 32.1 us (0.970)
  starting transfers between devices: 16.3 us -> 15.2 us
    ppermute x1, waiting for transfers between devices: 0.01 us -> 1.36 us  [on_device(): got = lax.ppermute(give, 'tp', [(i, i ^ 1) for i in range(peers)])]
    ppermute x5, waiting for transfers between devices: 7.48 us -> 6.26 us  [swapped(): lax.ppermute(block, axis, [(i, partner(i, step, size)) for i in range(siz...]
    ppermute x5, starting transfers between devices: 8.63 us -> 7.62 us  [swapped(): lax.ppermute(block, axis, [(i, partner(i, step, size)) for i in range(siz...]
    pallas_call x15 -> x16, Pallas kernels: 6.16 us -> 6.14 us  [call(): pl.pallas_call(kernel, out_shape=outs, in_specs=specs or [WHOLE] * len(ar...]
  transfers between devices with their start and end apart: 10 -> 10, of which waited for: 5 -> 6; matrix products, arithmetic and copies ran while one was open for 0% -> 0% of each run, Pallas kernels for 13% -> 15%
where the time goes in v4:
time: 32.1 us; the launch traced here: 31.9 us
  starting transfers between devices  15.2 us (47%)
  waiting for transfers between devices  9.04 us (28%)
  Pallas kernels  6.14 us (19%)
  other arithmetic  0.78 us (2%)
  between operations  0.75 us (2%)
    ppermute x5, starting transfers between devices, swapped(): lax.ppermute(block, axis, [(i, partner(i, step, size)) for i in range(siz...  7.62 us
    ppermute x5, waiting for transfers between devices, swapped(): lax.ppermute(block, axis, [(i, partner(i, step, size)) for i in range(siz...  6.26 us
    pallas_call x16, Pallas kernels, call(): pl.pallas_call(kernel, out_shape=outs, in_specs=specs or [WHOLE] * len(ar...  6.14 us
    ppermute x3, starting transfers between devices, shifted(): lax.ppermute(block, axis, [((i - distance) % size, i) for i in range(size)])  5.91 us
    ppermute x1, starting transfers between devices, on_device(): lax.ppermute(block, 'tp', [(i, (i + 2 * (step + 1)) % peers) for i in ran...  1.59 us
    ppermute x3, waiting for transfers between devices, shifted(): lax.ppermute(block, axis, [((i - distance) % size, i) for i in range(size)])  1.42 us
    ppermute x1, waiting for transfers between devices, on_device(): got = lax.ppermute(give, 'tp', [(i, i ^ 1) for i in range(peers)])  1.36 us
    concatenate x1, other arithmetic, on_device(): pair_here = jnp.concatenate([key_vectors[0], value_vectors[0]], axis=1)  0.78 us
  transfers between devices with their start and end apart: 10, of which 6 were waited for; matrix products, arithmetic and copies ran while one was open for 0% of the time, Pallas kernels for 15%

profile of v4, /device:TPU:0, one launch (start us, length us, event | category | flops | bytes accessed | tf_op | source)
XLA Modules:
  0.0 31.9 jit_solution(8402191426589271924)
XLA Ops:
  0.6 0.8 %pad_maximum_fusion.here_ref.block_ref = bf16[128,256]{1,0:T(8,128)(2,1)S(1)} fusion(bf16[128,128]{1,0:T(8,128)(2,1)} %bitcast.5, bf16[128,128]{1,0:T(8,128)(2,1)} %bitcast.6), kind=kLoop, calls=%fused_computation | loop fusion | flops 131072 | bytes 131072 | tf_op jit(solution)/shard_map/concatenate | solution.py:256
  1.4 3.0 %collective-permute-start = (bf16[128,256]{1,0:T(8,128)(2,1)S(1)}, bf16[128,256]{1,0:T(8,128)(2,1)S(1)}, u32[]{:S(2)}, u32[]{:S(2)}) collective-permute-start(bf16[128,256]{1,0:T(8,128)(2,1)S(1)} %pad_maximum_fusion.here_ref.block_ref), channel_id=1, source_target_pairs={{16,0},{0,16},{17,1},{1,17},{18,2},{2,18},{19,3},{3,19},{20,4},{4,... | collective-permute-start | bytes 196616 | tf_op jit(solution)/shard_map/ppermute | solution.py:48
  4.5 1.0 %collective-permute-start.5 = (bf16[128,1536]{1,0:T(8,128)(2,1)S(1)}, bf16[128,1536]{1,0:T(8,128)(2,1)S(1)}, u32[]{:S(2)}, u32[]{:S(2)}) collective-permute-start(bf16[128,1536]{1,0:T(8,128)(2,1)S(1)} %take.2), channel_id=1, source_target_pairs={{16,0},{0,16},{17,1},{1,17},{18,2},{2,18},{19,3},{3,19},{20,4},{4,... | collective-permute-start | bytes 1179656 | tf_op jit(solution)/shard_map/ppermute | solution.py:48
  5.5 1.4 %collective-permute-done.pair_ref = bf16[128,256]{1,0:T(8,128)(2,1)S(1)} collective-permute-done((bf16[128,256]{1,0:T(8,128)(2,1)S(1)}, bf16[128,256]{1,0:T(8,128)(2,1)S(1)}, u32[]{:S(2)}, u32[]{:S(2)}) %collective-permute-start) | collective-permute-done | bytes 65568 | tf_op jit(solution)/shard_map/ppermute | solution.py:48
  6.9 4.5 %collective-permute-start.1 = (bf16[128,384]{1,0:T(8,128)(2,1)S(1)}, bf16[128,384]{1,0:T(8,128)(2,1)S(1)}, u32[]{:S(2)}, u32[]{:S(2)}) collective-permute-start(bf16[128,384]{1,0:T(8,128)(2,1)S(1)} %join.1.refs_0_.after), channel_id=1, source_target_pairs={{0,12},{4,8},{8,4},{12,0},{1,13},{5,9},{9,5},{13,1},{2,14},{6,10},... | collective-permute-start | bytes 294920 | tf_op jit(solution)/shard_map/ppermute | solution.py:43
  11.4 0.6 %collective-permute-start.3 = (bf16[128,384]{1,0:T(8,128)(2,1)S(1)}, bf16[128,384]{1,0:T(8,128)(2,1)S(1)}, u32[]{:S(2)}, u32[]{:S(2)}) collective-permute-start(bf16[128,384]{1,0:T(8,128)(2,1)S(1)} %join.1.refs_0_.after), channel_id=1, source_target_pairs={{0,8},{4,12},{8,0},{12,4},{1,9},{5,13},{9,1},{13,5},{2,10},{6,14},... | collective-permute-start | bytes 294920 | tf_op jit(solution)/shard_map/ppermute | solution.py:43
  12.1 0.6 %prepare.1.feature_ref = bf16[2,128,512]{2,1,0:T(8,128)(2,1)S(1)} custom-call(s32[8]{0:T(128)S(1)} %copy-done.3, f32[8,128]{1,0:T(8,128)S(1)} %touch.1.after), custom_call_target="tpu_custom_call" | custom-call | flops 3000000000 | tf_op jit(solution)/shard_map/prepare/pallas_call | solution.py:24
  12.7 1.9 %collective-permute-start.6 = (bf16[128,512]{1,0:T(8,128)(2,1)S(1)}, bf16[128,512]{1,0:T(8,128)(2,1)S(1)}, u32[]{:S(2)}, u32[]{:S(2)}) collective-permute-start(bf16[128,512]{1,0:T(8,128)(2,1)S(1)} %take.3), channel_id=1, source_target_pairs={{16,0},{0,16},{17,1},{1,17},{18,2},{2,18},{19,3},{3,19},{20,4},{4,... | collective-permute-start | bytes 393224 | tf_op jit(solution)/shard_map/ppermute | solution.py:48
  14.6 0.9 %weigh.1.after.w_ref = bf16[2048,1024]{1,0:T(8,128)(2,1)S(1)} custom-call(bf16[2048,1024]{1,0:T(8,128)(2,1)S(1)} %bitcast.4, bf16[1,2048]{1,0:T(2,128)(2,1)S(1)} %copy-done.2, bf16[128,384]{1,0:T(8,128)(2,1)S(1)} %collective-permute-done.1.after.refs_3_), custom_call_target="tpu_custom_call" | custom-call | flops 1000000000 | tf_op jit(solution)/shard_map/weigh/pallas_call | solution.py:24
  15.5 2.1 %collective-permute-done.2.refs_1_ = bf16[128,384]{1,0:T(8,128)(2,1)S(1)} collective-permute-done((bf16[128,384]{1,0:T(8,128)(2,1)S(1)}, bf16[128,384]{1,0:T(8,128)(2,1)S(1)}, u32[]{:S(2)}, u32[]{:S(2)}) %collective-permute-start.2) | collective-permute-done | bytes 98336 | tf_op jit(solution)/shard_map/ppermute | solution.py:43
  17.6 1.1 %collective-permute-done.3.refs_2_ = bf16[128,384]{1,0:T(8,128)(2,1)S(1)} collective-permute-done((bf16[128,384]{1,0:T(8,128)(2,1)S(1)}, bf16[128,384]{1,0:T(8,128)(2,1)S(1)}, u32[]{:S(2)}, u32[]{:S(2)}) %collective-permute-start.3) | collective-permute-done | bytes 98336 | tf_op jit(solution)/shard_map/ppermute | solution.py:43
  18.7 0.2 arrange.1
  18.9 0.8 %maxima.1.after.left_ref = f32[1,16]{1,0:T(1,128)S(1)} custom-call(bf16[1,128,2048]{2,1,0:T(8,128)(2,1)S(1)} %copy-done.1, bf16[1,2,256,512]{3,2,1,0:T(8,128)(2,1)S(1)} %get-tuple-element.13.own_ref), custom_call_target="tpu_custom_call" | custom-call | flops 700000000 | tf_op jit(solution)/shard_map/maxima/pallas_call | solution.py:24
  19.7 0.4 %collective-permute-start.4 = (f32[1,16]{1,0:T(1,128)S(1)}, f32[1,16]{1,0:T(1,128)S(1)}, u32[]{:S(2)}, u32[]{:S(2)}) collective-permute-start(f32[1,16]{1,0:T(1,128)S(1)} %maxima.1.after.left_ref), channel_id=1, source_target_pairs={{0,4},{4,0},{8,12},{12,8},{1,5},{5,1},{9,13},{13,9},{2,6},{6,2},{1... | collective-permute-start | bytes 200 | tf_op jit(solution)/shard_map/ppermute | solution.py:43
  20.1 1.2 %attend.2.ctx_ref = bf16[128,1536]{1,0:T(8,128)(2,1)S(1)} custom-call(bf16[128,1536]{1,0:T(8,128)(2,1)S(1)} %collective-permute-done.5.q_ref, bf16[1,2,256,512]{3,2,1,0:T(8,128)(2,1)S(1)} %get-tuple-element.14.kt_ref, bf16[1,512,256]{2,1,0:T(8,128)(2,1)S(1)} %get-tuple-element.15.v_ref, f32[1,16]{1,0:T(1,128)S(1)} %maxima.1.after.left_ref), custom_call_target="tpu_custom_call" | custom-call | flops 1440000000 | tf_op jit(solution)/shard_map/attend/pallas_call | solution.py:24
  21.2 0.6 %project_first.1 = (f32[128,1024]{1,0:T(8,128)S(1)}, f32[128,128]{1,0:T(8,128)S(1)}) custom-call(bf16[128,1536]{1,0:T(8,128)(2,1)S(1)} %attend.2.ctx_ref, bf16[2048,1024]{1,0:T(8,128)(2,1)S(1)} %weigh.1.after.w_ref), custom_call_target="tpu_custom_call" | custom-call | flops 700000000 | tf_op jit(solution)/shard_map/project_first/pallas_call | solution.py:24
  21.9 0.7 %attend.3.ctx_ref = bf16[128,512]{1,0:T(8,128)(2,1)S(1)} custom-call(bf16[128,512]{1,0:T(8,128)(2,1)S(1)} %collective-permute-done.6.q_ref, bf16[1,2,256,512]{3,2,1,0:T(8,128)(2,1)S(1)} %get-tuple-element.14.kt_ref, bf16[1,512,256]{2,1,0:T(8,128)(2,1)S(1)} %get-tuple-element.15.v_ref, f32[128,128]{1,0:T(8,128)S(1)} %get-tuple-element.16.after.square_ref), custom_call_target="tpu_custom_call" | custom-call | flops 480000000 | tf_op jit(solution)/shard_map/attend/pallas_call | solution.py:24
  22.5 0.7 %collective-permute-done.4.right_ref = f32[1,16]{1,0:T(1,128)S(1)} collective-permute-done((f32[1,16]{1,0:T(1,128)S(1)}, f32[1,16]{1,0:T(1,128)S(1)}, u32[]{:S(2)}, u32[]{:S(2)}) %collective-permute-start.4) | collective-permute-done | bytes 96 | tf_op jit(solution)/shard_map/ppermute | solution.py:43
  23.2 0.3 %project_last.1 = (bf16[2,144,256]{2,1,0:T(8,128)(2,1)S(1)}, bf16[2,144,256]{2,1,0:T(8,128)(2,1)S(1)}) custom-call(bf16[128,512]{1,0:T(8,128)(2,1)S(1)} %attend.3.ctx_ref, bf16[2048,1024]{1,0:T(8,128)(2,1)S(1)} %weigh.1.after.w_ref, f32[128,1024]{1,0:T(8,128)S(1)} %get-tuple-element.17.sum_ref, f32[128,128]{1,0:T(8,128)S(1)} %get-tuple-element.16.after.square_ref, ...), custom_call_target="tpu_custom_call" | custom-call | flops 500000000 | tf_op jit(solution)/shard_map/project_last/pallas_call | solution.py:24
  23.7 1.4 %collective-permute-done.8.got_ref = bf16[2,144,256]{2,1,0:T(8,128)(2,1)S(1)} collective-permute-done((bf16[2,144,256]{2,1,0:T(8,128)(2,1)S(1)}, bf16[2,144,256]{2,1,0:T(8,128)(2,1)S(1)}, u32[]{:S(2)}, u32[]{:S(2)}) %collective-permute-start.8) | collective-permute-done | bytes 147488 | tf_op jit(solution)/shard_map/ppermute | solution.py:345
  25.1 1.6 %collective-permute-start.9 = (bf16[144,256]{1,0:T(8,128)(2,1)S(1)}, bf16[144,256]{1,0:T(8,128)(2,1)S(1)}, u32[]{:S(2)}, u32[]{:S(2)}) collective-permute-start(bf16[144,256]{1,0:T(8,128)(2,1)S(1)} %get-tuple-element.21), channel_id=1, source_target_pairs={{0,2},{1,3},{2,0},{3,1},{4,6},{5,7},{6,4},{7,5},{8,10},{9,11},{10,... | collective-permute-start | bytes 221192 | tf_op jit(solution)/shard_map/ppermute | solution.py:352
  26.7 2.1 %collective-permute-start.7 = (f32[1,16]{1,0:T(1,128)S(1)}, f32[1,16]{1,0:T(1,128)S(1)}, u32[]{:S(2)}, u32[]{:S(2)}) collective-permute-start(f32[1,16]{1,0:T(1,128)S(1)} %bind.1.peak_ref), channel_id=1, source_target_pairs={{0,8},{4,12},{8,0},{12,4},{1,9},{5,13},{9,1},{13,5},{2,10},{6,14},... | collective-permute-start | bytes 200 | tf_op jit(solution)/shard_map/ppermute | solution.py:43
  28.8 2.3 %collective-permute-done.7.peak_got = f32[1,16]{1,0:T(1,128)S(1)} collective-permute-done((f32[1,16]{1,0:T(1,128)S(1)}, f32[1,16]{1,0:T(1,128)S(1)}, u32[]{:S(2)}, u32[]{:S(2)}) %collective-permute-start.7) | collective-permute-done | bytes 96 | tf_op jit(solution)/shard_map/ppermute | solution.py:43
  31.1 0.8 %finish.1 = (f32[1,16]{1,0:T(1,128)}, bf16[128,256]{1,0:T(8,128)(2,1)}) custom-call(f32[1,16]{1,0:T(1,128)S(1)} %bind.1.peak_ref, f32[1,16]{1,0:T(1,128)S(1)} %collective-permute-done.7.peak_got, f32[144,256]{1,0:T(8,128)S(1)} %get-tuple-element.20.keep_ref, bf16[144,256]{1,0:T(8,128)(2,1)S(1)} %collective-permute-done.9.refs_0_), custom_call_target="tpu_custom_call" | custom-call | tf_op jit(solution)/shard_map/finish/pallas_call | solution.py:24
  (21 shorter events, 0.2 us)
Async XLA Ops:
  1.4 3.0 %copy-start.1 = (bf16[1,128,2048]{2,1,0:T(8,128)(2,1)S(1)}, bf16[1,128,2048]{2,1,0:T(8,128)(2,1)}, u32[]{:S(2)}) copy-start(bf16[1,128,2048]{2,1,0:T(8,128)(2,1)} %q_ref.5) | copy-start | bytes 1572868
  1.4 5.5 %collective-permute-start = (bf16[128,256]{1,0:T(8,128)(2,1)S(1)}, bf16[128,256]{1,0:T(8,128)(2,1)S(1)}, u32[]{:S(2)}, u32[]{:S(2)}) collective-permute-start(bf16[128,256]{1,0:T(8,128)(2,1)S(1)} %pad_maximum_fusion.here_ref.block_ref), channel_id=1, source_target_pairs={{16,0},{0,16},{17,1},{1,17},{18,2},{2,18},{19,3},{3,19},{20,4},{4,... | collective-permute-start | bytes 196616 | tf_op jit(solution)/shard_map/ppermute | solution.py:48
  4.4 7.6 %copy-start.3 = (s32[8]{0:T(128)S(1)}, s32[8]{0:T(128)}, u32[]{:S(2)}) copy-start(s32[8]{0:T(128)} %order_ref.1) | copy-start | bytes 100
  4.5 15.6 %collective-permute-start.5 = (bf16[128,1536]{1,0:T(8,128)(2,1)S(1)}, bf16[128,1536]{1,0:T(8,128)(2,1)S(1)}, u32[]{:S(2)}, u32[]{:S(2)}) collective-permute-start(bf16[128,1536]{1,0:T(8,128)(2,1)S(1)} %take.2), channel_id=1, source_target_pairs={{16,0},{0,16},{17,1},{1,17},{18,2},{2,18},{19,3},{3,19},{20,4},{4,... | collective-permute-start | bytes 1179656 | tf_op jit(solution)/shard_map/ppermute | solution.py:48
  6.9 7.7 %copy-start = (bf16[1,2048,1024]{2,1,0:T(8,128)(2,1)S(1)}, bf16[1,2048,1024]{2,1,0:T(8,128)(2,1)}, u32[]{:S(2)}) copy-start(bf16[1,2048,1024]{2,1,0:T(8,128)(2,1)} %param.11) | copy-start | bytes 12582916
  6.9 7.7 %copy-start.2 = (bf16[1,2048]{1,0:T(2,128)(2,1)S(1)}, bf16[1,2048]{1,0:T(2,128)(2,1)}, u32[]{:S(2)}) copy-start(bf16[1,2048]{1,0:T(2,128)(2,1)} %gain_ref.1) | copy-start | bytes 12292
  6.9 7.6 %collective-permute-start.1 = (bf16[128,384]{1,0:T(8,128)(2,1)S(1)}, bf16[128,384]{1,0:T(8,128)(2,1)S(1)}, u32[]{:S(2)}, u32[]{:S(2)}) collective-permute-start(bf16[128,384]{1,0:T(8,128)(2,1)S(1)} %join.1.refs_0_.after), channel_id=1, source_target_pairs={{0,12},{4,8},{8,4},{12,0},{1,13},{5,9},{9,5},{13,1},{2,14},{6,10},... | collective-permute-start | bytes 294920 | tf_op jit(solution)/shard_map/ppermute | solution.py:43
  11.4 6.1 %collective-permute-start.2 = (bf16[128,384]{1,0:T(8,128)(2,1)S(1)}, bf16[128,384]{1,0:T(8,128)(2,1)S(1)}, u32[]{:S(2)}, u32[]{:S(2)}) collective-permute-start(bf16[128,384]{1,0:T(8,128)(2,1)S(1)} %join.1.refs_0_.after), channel_id=1, source_target_pairs={{0,4},{4,0},{8,12},{12,8},{1,5},{5,1},{9,13},{13,9},{2,6},{6,2},{1... | collective-permute-start | bytes 294920 | tf_op jit(solution)/shard_map/ppermute | solution.py:43
  11.4 7.3 %collective-permute-start.3 = (bf16[128,384]{1,0:T(8,128)(2,1)S(1)}, bf16[128,384]{1,0:T(8,128)(2,1)S(1)}, u32[]{:S(2)}, u32[]{:S(2)}) collective-permute-start(bf16[128,384]{1,0:T(8,128)(2,1)S(1)} %join.1.refs_0_.after), channel_id=1, source_target_pairs={{0,8},{4,12},{8,0},{12,4},{1,9},{5,13},{9,1},{13,5},{2,10},{6,14},... | collective-permute-start | bytes 294920 | tf_op jit(solution)/shard_map/ppermute | solution.py:43
  12.7 9.1 %collective-permute-start.6 = (bf16[128,512]{1,0:T(8,128)(2,1)S(1)}, bf16[128,512]{1,0:T(8,128)(2,1)S(1)}, u32[]{:S(2)}, u32[]{:S(2)}) collective-permute-start(bf16[128,512]{1,0:T(8,128)(2,1)S(1)} %take.3), channel_id=1, source_target_pairs={{16,0},{0,16},{17,1},{1,17},{18,2},{2,18},{19,3},{3,19},{20,4},{4,... | collective-permute-start | bytes 393224 | tf_op jit(solution)/shard_map/ppermute | solution.py:48
  19.7 3.5 %collective-permute-start.4 = (f32[1,16]{1,0:T(1,128)S(1)}, f32[1,16]{1,0:T(1,128)S(1)}, u32[]{:S(2)}, u32[]{:S(2)}) collective-permute-start(f32[1,16]{1,0:T(1,128)S(1)} %maxima.1.after.left_ref), channel_id=1, source_target_pairs={{0,4},{4,0},{8,12},{12,8},{1,5},{5,1},{9,13},{13,9},{2,6},{6,2},{1... | collective-permute-start | bytes 200 | tf_op jit(solution)/shard_map/ppermute | solution.py:43
  23.6 1.4 %collective-permute-start.8 = (bf16[2,144,256]{2,1,0:T(8,128)(2,1)S(1)}, bf16[2,144,256]{2,1,0:T(8,128)(2,1)S(1)}, u32[]{:S(2)}, u32[]{:S(2)}) collective-permute-start(bf16[2,144,256]{2,1,0:T(8,128)(2,1)S(1)} %get-tuple-element.18.after), channel_id=1, source_target_pairs={{0,1},{1,0},{2,3},{3,2},{4,5},{5,4},{6,7},{7,6},{8,9},{9,8},{10,11... | collective-permute-start | bytes 442376 | tf_op jit(solution)/shard_map/ppermute | solution.py:345
  25.1 6.0 %collective-permute-start.9 = (bf16[144,256]{1,0:T(8,128)(2,1)S(1)}, bf16[144,256]{1,0:T(8,128)(2,1)S(1)}, u32[]{:S(2)}, u32[]{:S(2)}) collective-permute-start(bf16[144,256]{1,0:T(8,128)(2,1)S(1)} %get-tuple-element.21), channel_id=1, source_target_pairs={{0,2},{1,3},{2,0},{3,1},{4,6},{5,7},{6,4},{7,5},{8,10},{9,11},{10,... | collective-permute-start | bytes 221192 | tf_op jit(solution)/shard_map/ppermute | solution.py:352
  26.7 4.4 %collective-permute-start.7 = (f32[1,16]{1,0:T(1,128)S(1)}, f32[1,16]{1,0:T(1,128)S(1)}, u32[]{:S(2)}, u32[]{:S(2)}) collective-permute-start(f32[1,16]{1,0:T(1,128)S(1)} %bind.1.peak_ref), channel_id=1, source_target_pairs={{0,8},{4,12},{8,0},{12,4},{1,9},{5,13},{9,1},{13,5},{2,10},{6,14},... | collective-permute-start | bytes 200 | tf_op jit(solution)/shard_map/ppermute | solution.py:43

commit v5 on v4

--- a/solution.py
+++ b/solution.py
@@ -66,7 +66,8 @@
     part_ref[...] = q_ref[0, :, first:first + part_ref.shape[1]]
 
 
-def prepare(order_ref, after, feature_ref):
+def prepare(order_ref, *refs):
+    feature_ref = refs[-1]
     sources = lax.axis_size("cp")
     me = lax.axis_index("cp")
     rows = feature_ref.shape[2] // sources
@@ -87,29 +88,34 @@
     out_ref[...] = jnp.zeros(out_ref.shape, F32)
 
 
+def first_part(block_ref, after, out_ref):
+    out_ref[...] = block_ref[:, :out_ref.shape[1]]
+
+
 def join(pair_ref, here_ref, out_ref):
     width = pair_ref.shape[1]
     out_ref[:, :width] = pair_ref[...]
     out_ref[:, width:] = here_ref[:, :width // 2]
 
 
-def arrange(after, feature_ref, *refs):
-    triples, (kt_ref, v_ref, own_ref) = refs[:-3], refs[-3:]
-    rows = triples[0].shape[0]
+def arrange(sources, after, feature_ref, *refs):
+    pairs, owns, (kt_ref, v_ref, own_ref) = refs[:sources], refs[sources:-3], refs[-3:]
+    rows = pairs[0].shape[0]
     kv_local = v_ref.shape[0]
+    width = kv_local * DH
     for g in range(kv_local):
         v_ref[g, :, DH:] = jnp.ones((v_ref.shape[1], DH), BF16)
         for ref in (kt_ref, own_ref):
             for side in range(2):
                 ref[g, side, DH:, :] = feature_ref[side]
-        for d, triple in enumerate(triples):
+        for d, (pair, own) in enumerate(zip(pairs, owns)):
             part = slice(d * rows, (d + 1) * rows)
-            for ref, first in ((kt_ref, g * DH), (own_ref, (2 * kv_local + g) * DH)):
-                turned = triple[:, first:first + DH].astype(F32).T.astype(BF16)
+            column = slice(g * DH, (g + 1) * DH)
+            for ref, keys in ((kt_ref, pair[:, column]), (own_ref, own[:, own.shape[1] - width:][:, column])):
+                turned = keys.astype(F32).T.astype(BF16)
                 for side in range(2):
                     ref[g, side, :DH, part] = turned
-            first = (kv_local + g) * DH
-            v_ref[g, part, :DH] = triple[:, first:first + DH]
+            v_ref[g, part, :DH] = pair[:, width + g * DH:width + (g + 1) * DH]
 
 
 def spans(first_head, count, group, together):
@@ -270,36 +276,42 @@
             micros=micros,
         )
         crossed.append(shifted(part, "pp", 1))
+        return part
 
     mark = call(touch, shape((8, LANES), F32), (pair_here,), [OUTSIDE], name="touch", micros=3)
-    cross(starts[0], counts[0], mark, 3)
-    triple = call(join, shape((rows, 3 * kv_width), BF16), (pair, pair_here), name="join")
-    moved = {d: swapped(triple, "cp", d) for d in reversed(range(1, sources))}
-    triples = [triple] + [moved[d] for d in range(1, sources)]
-    cross(starts[1], counts[1], triple, 0)
+    first_queries = cross(starts[0], counts[0], mark, 3)
+    own_here = call(
+        first_part, shape((rows, kv_width), BF16), (pair_here, first_queries), [WHOLE, OUTSIDE], name="own_keys", micros=3
+    )
+    own_moved = {d: swapped(own_here, "cp", d) for d in reversed(range(2, sources))}
     features = call(
         prepare,
         shape((2, LANES, sources * rows), BF16),
-        (block_order, mark),
-        [SCALARS, OUTSIDE],
+        (block_order, mark, *own_moved.values()),
+        [SCALARS] + [OUTSIDE] * (1 + len(own_moved)),
         name="prepare",
         micros=3,
     )
+    triple = call(join, shape((rows, 3 * kv_width), BF16), (pair, pair_here), name="join")
+    moved = {d: swapped(pair, "cp", d) for d in reversed(range(2, sources))}
+    moved[1] = swapped(triple, "cp", 1)
+    pairs = [pair] + [moved[d] for d in range(1, sources)]
+    owns = [own_here, moved[1]] + [own_moved[d] for d in range(2, sources)]
+    cross(starts[1], counts[1], features, 0)
     w = call(
         weigh,
         shape((width, columns), BF16),
         (kv_weight[0], norm_gain, moved[sources - 1]),
         [WHOLE, WHOLE, OUTSIDE],
         name="weigh",
-        micros=1,
     )
     kv_local = kv_width // DH
     turned = shape((kv_local, 2, DH + LANES, sources * rows), BF16)
     kt, v_all, own = call(
-        arrange,
+        functools.partial(arrange, sources),
         (turned, shape((kv_local, sources * rows, 2 * DH), BF16), turned),
-        (w, features, *triples),
-        [OUTSIDE] + [WHOLE] * (1 + sources),
+        (w, features, *pairs, *owns),
+        [OUTSIDE] + [WHOLE] * (1 + 2 * sources),
         name="arrange",
         micros=0.2,
     )

time: 32.1 us -> 32.6 us (1.016)
  starting transfers between devices: 15.2 us -> 16.8 us
  waiting for transfers between devices: 9.04 us -> 7.84 us
    ppermute x5 -> x7, starting transfers between devices: 7.62 us -> 10 us  [swapped(): lax.ppermute(block, axis, [(i, partner(i, step, size)) for i in range(siz...]
    ppermute x3, waiting for transfers between devices: 1.42 us -> 0.01 us  [shifted(): lax.ppermute(block, axis, [((i - distance) % size, i) for i in range(size)])]
    ppermute x3, starting transfers between devices: 5.91 us -> 5.09 us  [shifted(): lax.ppermute(block, axis, [((i - distance) % size, i) for i in range(size)])]
    ppermute x5 -> x7, waiting for transfers between devices: 6.26 us -> 6.47 us  [swapped(): lax.ppermute(block, axis, [(i, partner(i, step, size)) for i in range(siz...]
    pallas_call x16 -> x17, Pallas kernels: 6.14 us -> 6.2 us  [call(): pl.pallas_call(kernel, out_shape=outs, in_specs=specs or [WHOLE] * len(ar...]
  transfers between devices with their start and end apart: 10 -> 12, of which waited for: 6 -> 5; matrix products, arithmetic and copies ran while one was open for 0% -> 0% of each run, Pallas kernels for 15% -> 15%
where the time goes in v5:
time: 32.6 us; the launch traced here: 32.4 us
  starting transfers between devices  16.8 us (52%)
  waiting for transfers between devices  7.84 us (24%)
  Pallas kernels  6.2 us (19%)
  other arithmetic  0.78 us (2%)
  between operations  0.77 us (2%)
    ppermute x7, starting transfers between devices, swapped(): lax.ppermute(block, axis, [(i, partner(i, step, size)) for i in range(siz...  10 us
    ppermute x7, waiting for transfers between devices, swapped(): lax.ppermute(block, axis, [(i, partner(i, step, size)) for i in range(siz...  6.47 us
    pallas_call x17, Pallas kernels, call(): pl.pallas_call(kernel, out_shape=outs, in_specs=specs or [WHOLE] * len(ar...  6.2 us
    ppermute x3, starting transfers between devices, shifted(): lax.ppermute(block, axis, [((i - distance) % size, i) for i in range(size)])  5.09 us
    ppermute x1, starting transfers between devices, on_device(): lax.ppermute(block, 'tp', [(i, (i + 2 * (step + 1)) % peers) for i in ran...  1.58 us
    ppermute x1, waiting for transfers between devices, on_device(): got = lax.ppermute(give, 'tp', [(i, i ^ 1) for i in range(peers)])  1.36 us
    concatenate x1, other arithmetic, on_device(): pair_here = jnp.concatenate([key_vectors[0], value_vectors[0]], axis=1)  0.78 us
  transfers between devices with their start and end apart: 12, of which 5 were waited for; matrix products, arithmetic and copies ran while one was open for 0% of the time, Pallas kernels for 15%

profile of v5, /device:TPU:0, one launch (start us, length us, event | category | flops | bytes accessed | tf_op | source)
XLA Modules:
  0.0 32.4 jit_solution(16701156369551695248)
XLA Ops:
  0.6 0.8 %pad_maximum_fusion.block_ref.here_ref = bf16[128,256]{1,0:T(8,128)(2,1)S(1)} fusion(bf16[128,128]{1,0:T(8,128)(2,1)} %bitcast.5, bf16[128,128]{1,0:T(8,128)(2,1)} %bitcast.6), kind=kLoop, calls=%fused_computation | loop fusion | flops 131072 | bytes 131072 | tf_op jit(solution)/shard_map/concatenate | solution.py:262
  1.4 3.0 %collective-permute-start = (bf16[128,256]{1,0:T(8,128)(2,1)S(1)}, bf16[128,256]{1,0:T(8,128)(2,1)S(1)}, u32[]{:S(2)}, u32[]{:S(2)}) collective-permute-start(bf16[128,256]{1,0:T(8,128)(2,1)S(1)} %pad_maximum_fusion.block_ref.here_ref), channel_id=1, source_target_pairs={{16,0},{0,16},{17,1},{1,17},{18,2},{2,18},{19,3},{3,19},{20,4},{4,... | collective-permute-start | bytes 196616 | tf_op jit(solution)/shard_map/ppermute | solution.py:48
  4.5 3.7 %collective-permute-start.2 = (bf16[128,128]{1,0:T(8,128)(2,1)S(1)}, bf16[128,128]{1,0:T(8,128)(2,1)S(1)}, u32[]{:S(2)}, u32[]{:S(2)}) collective-permute-start(bf16[128,128]{1,0:T(8,128)(2,1)S(1)} %own_keys.1.refs_4_), channel_id=1, source_target_pairs={{0,12},{4,8},{8,4},{12,0},{1,13},{5,9},{9,5},{13,1},{2,14},{6,10},... | collective-permute-start | bytes 98312 | tf_op jit(solution)/shard_map/ppermute | solution.py:43
  8.2 1.0 %collective-permute-start.7 = (bf16[128,1536]{1,0:T(8,128)(2,1)S(1)}, bf16[128,1536]{1,0:T(8,128)(2,1)S(1)}, u32[]{:S(2)}, u32[]{:S(2)}) collective-permute-start(bf16[128,1536]{1,0:T(8,128)(2,1)S(1)} %take.2.after), channel_id=1, source_target_pairs={{16,0},{0,16},{17,1},{1,17},{18,2},{2,18},{19,3},{3,19},{20,4},{4,... | collective-permute-start | bytes 1179656 | tf_op jit(solution)/shard_map/ppermute | solution.py:48
  9.2 0.8 %collective-permute-start.4 = (bf16[128,384]{1,0:T(8,128)(2,1)S(1)}, bf16[128,384]{1,0:T(8,128)(2,1)S(1)}, u32[]{:S(2)}, u32[]{:S(2)}) collective-permute-start(bf16[128,384]{1,0:T(8,128)(2,1)S(1)} %join.1), channel_id=1, source_target_pairs={{0,4},{4,0},{8,12},{12,8},{1,5},{5,1},{9,13},{13,9},{2,6},{6,2},{1... | collective-permute-start | bytes 294920 | tf_op jit(solution)/shard_map/ppermute | solution.py:43
  10.0 3.6 %collective-permute-start.1 = (bf16[128,256]{1,0:T(8,128)(2,1)S(1)}, bf16[128,256]{1,0:T(8,128)(2,1)S(1)}, u32[]{:S(2)}, u32[]{:S(2)}) collective-permute-start(bf16[128,256]{1,0:T(8,128)(2,1)S(1)} %collective-permute-done.pair_ref.refs_0_), channel_id=1, source_target_pairs={{0,12},{4,8},{8,4},{12,0},{1,13},{5,9},{9,5},{13,1},{2,14},{6,10},... | collective-permute-start | bytes 196616 | tf_op jit(solution)/shard_map/ppermute | solution.py:43
  13.6 0.6 %prepare.1.feature_ref.after = bf16[2,128,512]{2,1,0:T(8,128)(2,1)S(1)} custom-call(s32[8]{0:T(128)S(1)} %copy-done.3, f32[8,128]{1,0:T(8,128)S(1)} %touch.1.after.refs_0_, bf16[128,128]{1,0:T(8,128)(2,1)S(1)} %collective-permute-done.2.refs_1_.refs_7_, bf16[128,128]{1,0:T(8,128)(2,1)S(1)} %collective-permute-done.3.refs_2_.refs_6_), custom_call_target="tpu_custom_call" | custom-call | flops 3000000000 | tf_op jit(solution)/shard_map/prepare/pallas_call | solution.py:24
  14.3 1.1 %collective-permute-start.8 = (bf16[128,512]{1,0:T(8,128)(2,1)S(1)}, bf16[128,512]{1,0:T(8,128)(2,1)S(1)}, u32[]{:S(2)}, u32[]{:S(2)}) collective-permute-start(bf16[128,512]{1,0:T(8,128)(2,1)S(1)} %take.3), channel_id=1, source_target_pairs={{16,0},{0,16},{17,1},{1,17},{18,2},{2,18},{19,3},{3,19},{20,4},{4,... | collective-permute-start | bytes 393224 | tf_op jit(solution)/shard_map/ppermute | solution.py:48
  15.4 2.1 %collective-permute-done.1.after.refs_3_ = bf16[128,256]{1,0:T(8,128)(2,1)S(1)} collective-permute-done((bf16[128,256]{1,0:T(8,128)(2,1)S(1)}, bf16[128,256]{1,0:T(8,128)(2,1)S(1)}, u32[]{:S(2)}, u32[]{:S(2)}) %collective-permute-start.1) | collective-permute-done | bytes 65568 | tf_op jit(solution)/shard_map/ppermute | solution.py:43
  17.5 0.9 %weigh.1.after.w_ref = bf16[2048,1024]{1,0:T(8,128)(2,1)S(1)} custom-call(bf16[2048,1024]{1,0:T(8,128)(2,1)S(1)} %bitcast.4, bf16[1,2048]{1,0:T(2,128)(2,1)S(1)} %copy-done.2, bf16[128,256]{1,0:T(8,128)(2,1)S(1)} %collective-permute-done.1.after.refs_3_), custom_call_target="tpu_custom_call" | custom-call | tf_op jit(solution)/shard_map/weigh/pallas_call | solution.py:24
  18.4 0.8 %collective-permute-done.5.refs_2_ = bf16[128,256]{1,0:T(8,128)(2,1)S(1)} collective-permute-done((bf16[128,256]{1,0:T(8,128)(2,1)S(1)}, bf16[128,256]{1,0:T(8,128)(2,1)S(1)}, u32[]{:S(2)}, u32[]{:S(2)}) %collective-permute-start.5) | collective-permute-done | bytes 65568 | tf_op jit(solution)/shard_map/ppermute | solution.py:43
  19.1 0.2 arrange.1
  19.4 0.8 %maxima.1.after.left_ref = f32[1,16]{1,0:T(1,128)S(1)} custom-call(bf16[1,128,2048]{2,1,0:T(8,128)(2,1)S(1)} %copy-done.1, bf16[1,2,256,512]{3,2,1,0:T(8,128)(2,1)S(1)} %get-tuple-element.13.own_ref), custom_call_target="tpu_custom_call" | custom-call | flops 700000000 | tf_op jit(solution)/shard_map/maxima/pallas_call | solution.py:24
  20.2 0.6 %collective-permute-start.6 = (f32[1,16]{1,0:T(1,128)S(1)}, f32[1,16]{1,0:T(1,128)S(1)}, u32[]{:S(2)}, u32[]{:S(2)}) collective-permute-start(f32[1,16]{1,0:T(1,128)S(1)} %maxima.1.after.left_ref), channel_id=1, source_target_pairs={{0,4},{4,0},{8,12},{12,8},{1,5},{5,1},{9,13},{13,9},{2,6},{6,2},{1... | collective-permute-start | bytes 200 | tf_op jit(solution)/shard_map/ppermute | solution.py:43
  20.8 1.2 %attend.2.ctx_ref = bf16[128,1536]{1,0:T(8,128)(2,1)S(1)} custom-call(bf16[128,1536]{1,0:T(8,128)(2,1)S(1)} %collective-permute-done.7.q_ref, bf16[1,2,256,512]{3,2,1,0:T(8,128)(2,1)S(1)} %get-tuple-element.14.kt_ref, bf16[1,512,256]{2,1,0:T(8,128)(2,1)S(1)} %get-tuple-element.15.v_ref, f32[1,16]{1,0:T(1,128)S(1)} %maxima.1.after.left_ref), custom_call_target="tpu_custom_call" | custom-call | flops 1440000000 | tf_op jit(solution)/shard_map/attend/pallas_call | solution.py:24
  22.0 0.6 %project_first.1 = (f32[128,1024]{1,0:T(8,128)S(1)}, f32[128,128]{1,0:T(8,128)S(1)}) custom-call(bf16[128,1536]{1,0:T(8,128)(2,1)S(1)} %attend.2.ctx_ref, bf16[2048,1024]{1,0:T(8,128)(2,1)S(1)} %weigh.1.after.w_ref), custom_call_target="tpu_custom_call" | custom-call | flops 700000000 | tf_op jit(solution)/shard_map/project_first/pallas_call | solution.py:24
  22.6 0.7 %attend.3.ctx_ref = bf16[128,512]{1,0:T(8,128)(2,1)S(1)} custom-call(bf16[128,512]{1,0:T(8,128)(2,1)S(1)} %collective-permute-done.8.q_ref, bf16[1,2,256,512]{3,2,1,0:T(8,128)(2,1)S(1)} %get-tuple-element.14.kt_ref, bf16[1,512,256]{2,1,0:T(8,128)(2,1)S(1)} %get-tuple-element.15.v_ref, f32[128,128]{1,0:T(8,128)S(1)} %get-tuple-element.16.after.square_ref), custom_call_target="tpu_custom_call" | custom-call | flops 480000000 | tf_op jit(solution)/shard_map/attend/pallas_call | solution.py:24
  23.2 0.5 %collective-permute-done.6.right_ref = f32[1,16]{1,0:T(1,128)S(1)} collective-permute-done((f32[1,16]{1,0:T(1,128)S(1)}, f32[1,16]{1,0:T(1,128)S(1)}, u32[]{:S(2)}, u32[]{:S(2)}) %collective-permute-start.6) | collective-permute-done | bytes 96 | tf_op jit(solution)/shard_map/ppermute | solution.py:43
  23.7 0.3 %project_last.1 = (bf16[2,144,256]{2,1,0:T(8,128)(2,1)S(1)}, bf16[2,144,256]{2,1,0:T(8,128)(2,1)S(1)}) custom-call(bf16[128,512]{1,0:T(8,128)(2,1)S(1)} %attend.3.ctx_ref, bf16[2048,1024]{1,0:T(8,128)(2,1)S(1)} %weigh.1.after.w_ref, f32[128,1024]{1,0:T(8,128)S(1)} %get-tuple-element.17.sum_ref, f32[128,128]{1,0:T(8,128)S(1)} %get-tuple-element.16.after.square_ref, ...), custom_call_target="tpu_custom_call" | custom-call | flops 500000000 | tf_op jit(solution)/shard_map/project_last/pallas_call | solution.py:24
  24.1 1.4 %collective-permute-done.10.got_ref = bf16[2,144,256]{2,1,0:T(8,128)(2,1)S(1)} collective-permute-done((bf16[2,144,256]{2,1,0:T(8,128)(2,1)S(1)}, bf16[2,144,256]{2,1,0:T(8,128)(2,1)S(1)}, u32[]{:S(2)}, u32[]{:S(2)}) %collective-permute-start.10) | collective-permute-done | bytes 147488 | tf_op jit(solution)/shard_map/ppermute | solution.py:357
  25.5 1.6 %collective-permute-start.11 = (bf16[144,256]{1,0:T(8,128)(2,1)S(1)}, bf16[144,256]{1,0:T(8,128)(2,1)S(1)}, u32[]{:S(2)}, u32[]{:S(2)}) collective-permute-start(bf16[144,256]{1,0:T(8,128)(2,1)S(1)} %get-tuple-element.21), channel_id=1, source_target_pairs={{0,2},{1,3},{2,0},{3,1},{4,6},{5,7},{6,4},{7,5},{8,10},{9,11},{10,... | collective-permute-start | bytes 221192 | tf_op jit(solution)/shard_map/ppermute | solution.py:364
  27.1 1.3 %collective-permute-start.9 = (f32[1,16]{1,0:T(1,128)S(1)}, f32[1,16]{1,0:T(1,128)S(1)}, u32[]{:S(2)}, u32[]{:S(2)}) collective-permute-start(f32[1,16]{1,0:T(1,128)S(1)} %bind.1.peak_ref), channel_id=1, source_target_pairs={{0,8},{4,12},{8,0},{12,4},{1,9},{5,13},{9,1},{13,5},{2,10},{6,14},... | collective-permute-start | bytes 200 | tf_op jit(solution)/shard_map/ppermute | solution.py:43
  28.4 3.2 %collective-permute-done.9.peak_got = f32[1,16]{1,0:T(1,128)S(1)} collective-permute-done((f32[1,16]{1,0:T(1,128)S(1)}, f32[1,16]{1,0:T(1,128)S(1)}, u32[]{:S(2)}, u32[]{:S(2)}) %collective-permute-start.9) | collective-permute-done | bytes 96 | tf_op jit(solution)/shard_map/ppermute | solution.py:43
  31.6 0.8 %finish.1 = (f32[1,16]{1,0:T(1,128)}, bf16[128,256]{1,0:T(8,128)(2,1)}) custom-call(f32[1,16]{1,0:T(1,128)S(1)} %bind.1.peak_ref, f32[1,16]{1,0:T(1,128)S(1)} %collective-permute-done.9.peak_got, f32[144,256]{1,0:T(8,128)S(1)} %get-tuple-element.20.keep_ref, bf16[144,256]{1,0:T(8,128)(2,1)S(1)} %collective-permute-done.11.refs_0_), custom_call_target="tpu_custom_call" | custom-call | tf_op jit(solution)/shard_map/finish/pallas_call | solution.py:24
  (26 shorter events, 0.2 us)
Async XLA Ops:
  1.4 3.0 %copy-start.1 = (bf16[1,128,2048]{2,1,0:T(8,128)(2,1)S(1)}, bf16[1,128,2048]{2,1,0:T(8,128)(2,1)}, u32[]{:S(2)}) copy-start(bf16[1,128,2048]{2,1,0:T(8,128)(2,1)} %q_ref.5) | copy-start | bytes 1572868
  1.4 7.7 %collective-permute-start = (bf16[128,256]{1,0:T(8,128)(2,1)S(1)}, bf16[128,256]{1,0:T(8,128)(2,1)S(1)}, u32[]{:S(2)}, u32[]{:S(2)}) collective-permute-start(bf16[128,256]{1,0:T(8,128)(2,1)S(1)} %pad_maximum_fusion.block_ref.here_ref), channel_id=1, source_target_pairs={{16,0},{0,16},{17,1},{1,17},{18,2},{2,18},{19,3},{3,19},{20,4},{4,... | collective-permute-start | bytes 196616 | tf_op jit(solution)/shard_map/ppermute | solution.py:48
  4.5 9.2 %copy-start.3 = (s32[8]{0:T(128)S(1)}, s32[8]{0:T(128)}, u32[]{:S(2)}) copy-start(s32[8]{0:T(128)} %order_ref.1) | copy-start | bytes 100
  4.5 9.1 %collective-permute-start.2 = (bf16[128,128]{1,0:T(8,128)(2,1)S(1)}, bf16[128,128]{1,0:T(8,128)(2,1)S(1)}, u32[]{:S(2)}, u32[]{:S(2)}) collective-permute-start(bf16[128,128]{1,0:T(8,128)(2,1)S(1)} %own_keys.1.refs_4_), channel_id=1, source_target_pairs={{0,12},{4,8},{8,4},{12,0},{1,13},{5,9},{9,5},{13,1},{2,14},{6,10},... | collective-permute-start | bytes 98312 | tf_op jit(solution)/shard_map/ppermute | solution.py:43
  8.2 5.5 %collective-permute-start.3 = (bf16[128,128]{1,0:T(8,128)(2,1)S(1)}, bf16[128,128]{1,0:T(8,128)(2,1)S(1)}, u32[]{:S(2)}, u32[]{:S(2)}) collective-permute-start(bf16[128,128]{1,0:T(8,128)(2,1)S(1)} %own_keys.1.refs_4_), channel_id=1, source_target_pairs={{0,8},{4,12},{8,0},{12,4},{1,9},{5,13},{9,1},{13,5},{2,10},{6,14},... | collective-permute-start | bytes 98312 | tf_op jit(solution)/shard_map/ppermute | solution.py:43
  8.2 12.6 %collective-permute-start.7 = (bf16[128,1536]{1,0:T(8,128)(2,1)S(1)}, bf16[128,1536]{1,0:T(8,128)(2,1)S(1)}, u32[]{:S(2)}, u32[]{:S(2)}) collective-permute-start(bf16[128,1536]{1,0:T(8,128)(2,1)S(1)} %take.2.after), channel_id=1, source_target_pairs={{16,0},{0,16},{17,1},{1,17},{18,2},{2,18},{19,3},{3,19},{20,4},{4,... | collective-permute-start | bytes 1179656 | tf_op jit(solution)/shard_map/ppermute | solution.py:48
  9.1 8.4 %copy-start = (bf16[1,2048,1024]{2,1,0:T(8,128)(2,1)S(1)}, bf16[1,2048,1024]{2,1,0:T(8,128)(2,1)}, u32[]{:S(2)}) copy-start(bf16[1,2048,1024]{2,1,0:T(8,128)(2,1)} %param.11) | copy-start | bytes 12582916
  9.2 8.3 %copy-start.2 = (bf16[1,2048]{1,0:T(2,128)(2,1)S(1)}, bf16[1,2048]{1,0:T(2,128)(2,1)}, u32[]{:S(2)}) copy-start(bf16[1,2048]{1,0:T(2,128)(2,1)} %gain_ref.1) | copy-start | bytes 12292
  9.2 10.0 %collective-permute-start.4 = (bf16[128,384]{1,0:T(8,128)(2,1)S(1)}, bf16[128,384]{1,0:T(8,128)(2,1)S(1)}, u32[]{:S(2)}, u32[]{:S(2)}) collective-permute-start(bf16[128,384]{1,0:T(8,128)(2,1)S(1)} %join.1), channel_id=1, source_target_pairs={{0,4},{4,0},{8,12},{12,8},{1,5},{5,1},{9,13},{13,9},{2,6},{6,2},{1... | collective-permute-start | bytes 294920 | tf_op jit(solution)/shard_map/ppermute | solution.py:43
  10.0 7.5 %collective-permute-start.1 = (bf16[128,256]{1,0:T(8,128)(2,1)S(1)}, bf16[128,256]{1,0:T(8,128)(2,1)S(1)}, u32[]{:S(2)}, u32[]{:S(2)}) collective-permute-start(bf16[128,256]{1,0:T(8,128)(2,1)S(1)} %collective-permute-done.pair_ref.refs_0_), channel_id=1, source_target_pairs={{0,12},{4,8},{8,4},{12,0},{1,13},{5,9},{9,5},{13,1},{2,14},{6,10},... | collective-permute-start | bytes 196616 | tf_op jit(solution)/shard_map/ppermute | solution.py:43
  13.6 5.5 %collective-permute-start.5 = (bf16[128,256]{1,0:T(8,128)(2,1)S(1)}, bf16[128,256]{1,0:T(8,128)(2,1)S(1)}, u32[]{:S(2)}, u32[]{:S(2)}) collective-permute-start(bf16[128,256]{1,0:T(8,128)(2,1)S(1)} %collective-permute-done.pair_ref.refs_0_), channel_id=1, source_target_pairs={{0,8},{4,12},{8,0},{12,4},{1,9},{5,13},{9,1},{13,5},{2,10},{6,14},... | collective-permute-start | bytes 196616 | tf_op jit(solution)/shard_map/ppermute | solution.py:43
  14.3 8.3 %collective-permute-start.8 = (bf16[128,512]{1,0:T(8,128)(2,1)S(1)}, bf16[128,512]{1,0:T(8,128)(2,1)S(1)}, u32[]{:S(2)}, u32[]{:S(2)}) collective-permute-start(bf16[128,512]{1,0:T(8,128)(2,1)S(1)} %take.3), channel_id=1, source_target_pairs={{16,0},{0,16},{17,1},{1,17},{18,2},{2,18},{19,3},{3,19},{20,4},{4,... | collective-permute-start | bytes 393224 | tf_op jit(solution)/shard_map/ppermute | solution.py:48
  20.2 3.5 %collective-permute-start.6 = (f32[1,16]{1,0:T(1,128)S(1)}, f32[1,16]{1,0:T(1,128)S(1)}, u32[]{:S(2)}, u32[]{:S(2)}) collective-permute-start(f32[1,16]{1,0:T(1,128)S(1)} %maxima.1.after.left_ref), channel_id=1, source_target_pairs={{0,4},{4,0},{8,12},{12,8},{1,5},{5,1},{9,13},{13,9},{2,6},{6,2},{1... | collective-permute-start | bytes 200 | tf_op jit(solution)/shard_map/ppermute | solution.py:43
  24.1 1.4 %collective-permute-start.10 = (bf16[2,144,256]{2,1,0:T(8,128)(2,1)S(1)}, bf16[2,144,256]{2,1,0:T(8,128)(2,1)S(1)}, u32[]{:S(2)}, u32[]{:S(2)}) collective-permute-start(bf16[2,144,256]{2,1,0:T(8,128)(2,1)S(1)} %get-tuple-element.18.after), channel_id=1, source_target_pairs={{0,1},{1,0},{2,3},{3,2},{4,5},{5,4},{6,7},{7,6},{8,9},{9,8},{10,11... | collective-permute-start | bytes 442376 | tf_op jit(solution)/shard_map/ppermute | solution.py:357
  25.5 6.0 %collective-permute-start.11 = (bf16[144,256]{1,0:T(8,128)(2,1)S(1)}, bf16[144,256]{1,0:T(8,128)(2,1)S(1)}, u32[]{:S(2)}, u32[]{:S(2)}) collective-permute-start(bf16[144,256]{1,0:T(8,128)(2,1)S(1)} %get-tuple-element.21), channel_id=1, source_target_pairs={{0,2},{1,3},{2,0},{3,1},{4,6},{5,7},{6,4},{7,5},{8,10},{9,11},{10,... | collective-permute-start | bytes 221192 | tf_op jit(solution)/shard_map/ppermute | solution.py:364
  27.1 4.4 %collective-permute-start.9 = (f32[1,16]{1,0:T(1,128)S(1)}, f32[1,16]{1,0:T(1,128)S(1)}, u32[]{:S(2)}, u32[]{:S(2)}) collective-permute-start(f32[1,16]{1,0:T(1,128)S(1)} %bind.1.peak_ref), channel_id=1, source_target_pairs={{0,8},{4,12},{8,0},{12,4},{1,9},{5,13},{9,1},{13,5},{2,10},{6,14},... | collective-permute-start | bytes 200 | tf_op jit(solution)/shard_map/ppermute | solution.py:43

commit v6 on v4

--- a/solution.py
+++ b/solution.py
@@ -94,7 +94,7 @@
 
 
 def arrange(after, feature_ref, *refs):
-    triples, (kt_ref, v_ref, own_ref) = refs[:-3], refs[-3:]
+    triples, (kt_ref, v_ref, own_ref) = refs[-4::-1], refs[-3:]
     rows = triples[0].shape[0]
     kv_local = v_ref.shape[0]
     for g in range(kv_local):
@@ -255,7 +255,7 @@
 
     pair_here = jnp.concatenate([key_vectors[0], value_vectors[0]], axis=1)
     pair = shifted(pair_here, "pp", 1)
-    cut = heads * 3 // 4
+    cut = heads // 2
     counts = [cut, heads - cut]
     starts = [0, cut]
     crossed = []
@@ -298,7 +298,7 @@
     kt, v_all, own = call(
         arrange,
         (turned, shape((kv_local, sources * rows, 2 * DH), BF16), turned),
-        (w, features, *triples),
+        (w, features, *reversed(triples)),
         [OUTSIDE] + [WHOLE] * (1 + sources),
         name="arrange",
         micros=0.2,

time: 32.1 us -> 32.7 us (1.019)
  waiting for transfers between devices: 9.04 us -> 10.1 us
  starting transfers between devices: 15.2 us -> 14.6 us
    ppermute x5, waiting for transfers between devices: 6.26 us -> 7.31 us  [swapped(): lax.ppermute(block, axis, [(i, partner(i, step, size)) for i in range(siz...]
    ppermute x5, starting transfers between devices: 7.62 us -> 7 us  [swapped(): lax.ppermute(block, axis, [(i, partner(i, step, size)) for i in range(siz...]
  transfers between devices with their start and end apart: 10 -> 10, of which waited for: 6 -> 5; matrix products, arithmetic and copies ran while one was open for 0% -> 0% of each run, Pallas kernels for 15% -> 12%
where the time goes in v6:
time: 32.7 us; the launch traced here: 32.5 us
  starting transfers between devices  14.6 us (45%)
  waiting for transfers between devices  10.1 us (31%)
  Pallas kernels  6.27 us (19%)
  other arithmetic  0.78 us (2%)
  between operations  0.74 us (2%)
    ppermute x5, waiting for transfers between devices, swapped(): lax.ppermute(block, axis, [(i, partner(i, step, size)) for i in range(siz...  7.31 us
    ppermute x5, starting transfers between devices, swapped(): lax.ppermute(block, axis, [(i, partner(i, step, size)) for i in range(siz...  7 us
    pallas_call x16, Pallas kernels, call(): pl.pallas_call(kernel, out_shape=outs, in_specs=specs or [WHOLE] * len(ar...  6.27 us
    ppermute x3, starting transfers between devices, shifted(): lax.ppermute(block, axis, [((i - distance) % size, i) for i in range(size)])  5.9 us
    ppermute x1, starting transfers between devices, on_device(): lax.ppermute(block, 'tp', [(i, (i + 2 * (step + 1)) % peers) for i in ran...  1.58 us
    ppermute x3, waiting for transfers between devices, shifted(): lax.ppermute(block, axis, [((i - distance) % size, i) for i in range(size)])  1.43 us
    ppermute x1, waiting for transfers between devices, on_device(): got = lax.ppermute(give, 'tp', [(i, i ^ 1) for i in range(peers)])  1.36 us
    concatenate x1, other arithmetic, on_device(): pair_here = jnp.concatenate([key_vectors[0], value_vectors[0]], axis=1)  0.78 us
  transfers between devices with their start and end apart: 10, of which 5 were waited for; matrix products, arithmetic and copies ran while one was open for 0% of the time, Pallas kernels for 12%

profile of v6, /device:TPU:0, one launch (start us, length us, event | category | flops | bytes accessed | tf_op | source)
XLA Modules:
  0.0 32.5 jit_solution(12275932509133429681)
XLA Ops:
  0.6 0.8 %pad_maximum_fusion.here_ref.block_ref = bf16[128,256]{1,0:T(8,128)(2,1)S(1)} fusion(bf16[128,128]{1,0:T(8,128)(2,1)} %bitcast.5, bf16[128,128]{1,0:T(8,128)(2,1)} %bitcast.6), kind=kLoop, calls=%fused_computation | loop fusion | flops 131072 | bytes 131072 | tf_op jit(solution)/shard_map/concatenate | solution.py:256
  1.4 3.0 %collective-permute-start = (bf16[128,256]{1,0:T(8,128)(2,1)S(1)}, bf16[128,256]{1,0:T(8,128)(2,1)S(1)}, u32[]{:S(2)}, u32[]{:S(2)}) collective-permute-start(bf16[128,256]{1,0:T(8,128)(2,1)S(1)} %pad_maximum_fusion.here_ref.block_ref), channel_id=1, source_target_pairs={{16,0},{0,16},{17,1},{1,17},{18,2},{2,18},{19,3},{3,19},{20,4},{4,... | collective-permute-start | bytes 196616 | tf_op jit(solution)/shard_map/ppermute | solution.py:48
  4.5 1.0 %collective-permute-start.5 = (bf16[128,1024]{1,0:T(8,128)(2,1)S(1)}, bf16[128,1024]{1,0:T(8,128)(2,1)S(1)}, u32[]{:S(2)}, u32[]{:S(2)}) collective-permute-start(bf16[128,1024]{1,0:T(8,128)(2,1)S(1)} %take.2), channel_id=1, source_target_pairs={{16,0},{0,16},{17,1},{1,17},{18,2},{2,18},{19,3},{3,19},{20,4},{4,... | collective-permute-start | bytes 786440 | tf_op jit(solution)/shard_map/ppermute | solution.py:48
  5.5 1.4 %collective-permute-done.pair_ref = bf16[128,256]{1,0:T(8,128)(2,1)S(1)} collective-permute-done((bf16[128,256]{1,0:T(8,128)(2,1)S(1)}, bf16[128,256]{1,0:T(8,128)(2,1)S(1)}, u32[]{:S(2)}, u32[]{:S(2)}) %collective-permute-start) | collective-permute-done | bytes 65568 | tf_op jit(solution)/shard_map/ppermute | solution.py:48
  7.0 4.5 %collective-permute-start.1 = (bf16[128,384]{1,0:T(8,128)(2,1)S(1)}, bf16[128,384]{1,0:T(8,128)(2,1)S(1)}, u32[]{:S(2)}, u32[]{:S(2)}) collective-permute-start(bf16[128,384]{1,0:T(8,128)(2,1)S(1)} %join.1.refs_3_.after), channel_id=1, source_target_pairs={{0,12},{4,8},{8,4},{12,0},{1,13},{5,9},{9,5},{13,1},{2,14},{6,10},... | collective-permute-start | bytes 294920 | tf_op jit(solution)/shard_map/ppermute | solution.py:43
  11.4 0.6 %collective-permute-start.3 = (bf16[128,384]{1,0:T(8,128)(2,1)S(1)}, bf16[128,384]{1,0:T(8,128)(2,1)S(1)}, u32[]{:S(2)}, u32[]{:S(2)}) collective-permute-start(bf16[128,384]{1,0:T(8,128)(2,1)S(1)} %join.1.refs_3_.after), channel_id=1, source_target_pairs={{0,4},{4,0},{8,12},{12,8},{1,5},{5,1},{9,13},{13,9},{2,6},{6,2},{1... | collective-permute-start | bytes 294920 | tf_op jit(solution)/shard_map/ppermute | solution.py:43
  12.1 0.6 %prepare.1.feature_ref = bf16[2,128,512]{2,1,0:T(8,128)(2,1)S(1)} custom-call(s32[8]{0:T(128)S(1)} %copy-done.3, f32[8,128]{1,0:T(8,128)S(1)} %touch.1.after), custom_call_target="tpu_custom_call" | custom-call | flops 3000000000 | tf_op jit(solution)/shard_map/prepare/pallas_call | solution.py:24
  12.7 1.9 %collective-permute-start.6 = (bf16[128,1024]{1,0:T(8,128)(2,1)S(1)}, bf16[128,1024]{1,0:T(8,128)(2,1)S(1)}, u32[]{:S(2)}, u32[]{:S(2)}) collective-permute-start(bf16[128,1024]{1,0:T(8,128)(2,1)S(1)} %take.3), channel_id=1, source_target_pairs={{16,0},{0,16},{17,1},{1,17},{18,2},{2,18},{19,3},{3,19},{20,4},{4,... | collective-permute-start | bytes 786440 | tf_op jit(solution)/shard_map/ppermute | solution.py:48
  14.6 0.9 %weigh.1.after.w_ref = bf16[2048,1024]{1,0:T(8,128)(2,1)S(1)} custom-call(bf16[2048,1024]{1,0:T(8,128)(2,1)S(1)} %bitcast.4, bf16[1,2048]{1,0:T(2,128)(2,1)S(1)} %copy-done.2, bf16[128,384]{1,0:T(8,128)(2,1)S(1)} %collective-permute-done.1.after.refs_0_), custom_call_target="tpu_custom_call" | custom-call | flops 1000000000 | tf_op jit(solution)/shard_map/weigh/pallas_call | solution.py:24
  15.5 2.6 %collective-permute-done.2.refs_1_ = bf16[128,384]{1,0:T(8,128)(2,1)S(1)} collective-permute-done((bf16[128,384]{1,0:T(8,128)(2,1)S(1)}, bf16[128,384]{1,0:T(8,128)(2,1)S(1)}, u32[]{:S(2)}, u32[]{:S(2)}) %collective-permute-start.2) | collective-permute-done | bytes 98336 | tf_op jit(solution)/shard_map/ppermute | solution.py:43
  18.1 0.2 arrange.1
  18.3 0.8 %maxima.1.after.left_ref = f32[1,16]{1,0:T(1,128)S(1)} custom-call(bf16[1,128,2048]{2,1,0:T(8,128)(2,1)S(1)} %copy-done.1, bf16[1,2,256,512]{3,2,1,0:T(8,128)(2,1)S(1)} %get-tuple-element.13.own_ref), custom_call_target="tpu_custom_call" | custom-call | flops 700000000 | tf_op jit(solution)/shard_map/maxima/pallas_call | solution.py:24
  19.1 0.5 %collective-permute-start.4 = (f32[1,16]{1,0:T(1,128)S(1)}, f32[1,16]{1,0:T(1,128)S(1)}, u32[]{:S(2)}, u32[]{:S(2)}) collective-permute-start(f32[1,16]{1,0:T(1,128)S(1)} %maxima.1.after.left_ref), channel_id=1, source_target_pairs={{0,4},{4,0},{8,12},{12,8},{1,5},{5,1},{9,13},{13,9},{2,6},{6,2},{1... | collective-permute-start | bytes 200 | tf_op jit(solution)/shard_map/ppermute | solution.py:43
  19.6 0.9 %attend.2.ctx_ref = bf16[128,1024]{1,0:T(8,128)(2,1)S(1)} custom-call(bf16[128,1024]{1,0:T(8,128)(2,1)S(1)} %collective-permute-done.5.q_ref, bf16[1,2,256,512]{3,2,1,0:T(8,128)(2,1)S(1)} %get-tuple-element.14.kt_ref, bf16[1,512,256]{2,1,0:T(8,128)(2,1)S(1)} %get-tuple-element.15.v_ref, f32[1,16]{1,0:T(1,128)S(1)} %maxima.1.after.left_ref), custom_call_target="tpu_custom_call" | custom-call | flops 960000000 | tf_op jit(solution)/shard_map/attend/pallas_call | solution.py:24
  20.5 0.5 %project_first.1 = (f32[128,1024]{1,0:T(8,128)S(1)}, f32[128,128]{1,0:T(8,128)S(1)}) custom-call(bf16[128,1024]{1,0:T(8,128)(2,1)S(1)} %attend.2.ctx_ref, bf16[2048,1024]{1,0:T(8,128)(2,1)S(1)} %weigh.1.after.w_ref), custom_call_target="tpu_custom_call" | custom-call | flops 700000000 | tf_op jit(solution)/shard_map/project_first/pallas_call | solution.py:24
  21.0 1.6 %collective-permute-done.4.right_ref = f32[1,16]{1,0:T(1,128)S(1)} collective-permute-done((f32[1,16]{1,0:T(1,128)S(1)}, f32[1,16]{1,0:T(1,128)S(1)}, u32[]{:S(2)}, u32[]{:S(2)}) %collective-permute-start.4) | collective-permute-done | bytes 96 | tf_op jit(solution)/shard_map/ppermute | solution.py:43
  22.6 0.9 %attend.3.ctx_ref = bf16[128,1024]{1,0:T(8,128)(2,1)S(1)} custom-call(bf16[128,1024]{1,0:T(8,128)(2,1)S(1)} %collective-permute-done.6.q_ref, bf16[1,2,256,512]{3,2,1,0:T(8,128)(2,1)S(1)} %get-tuple-element.14.kt_ref, bf16[1,512,256]{2,1,0:T(8,128)(2,1)S(1)} %get-tuple-element.15.v_ref, f32[128,128]{1,0:T(8,128)S(1)} %get-tuple-element.16.after.square_ref), custom_call_target="tpu_custom_call" | custom-call | flops 960000000 | tf_op jit(solution)/shard_map/attend/pallas_call | solution.py:24
  23.6 0.6 %project_last.1 = (bf16[2,144,256]{2,1,0:T(8,128)(2,1)S(1)}, bf16[2,144,256]{2,1,0:T(8,128)(2,1)S(1)}) custom-call(bf16[128,1024]{1,0:T(8,128)(2,1)S(1)} %attend.3.ctx_ref, bf16[2048,1024]{1,0:T(8,128)(2,1)S(1)} %weigh.1.after.w_ref, f32[128,1024]{1,0:T(8,128)S(1)} %get-tuple-element.17.sum_ref, f32[128,128]{1,0:T(8,128)S(1)} %get-tuple-element.16.after.square_ref, ...), custom_call_target="tpu_custom_call" | custom-call | flops 500000000 | tf_op jit(solution)/shard_map/project_last/pallas_call | solution.py:24
  24.2 0.1 collective-permute-start.8
  24.2 1.4 %collective-permute-done.8.got_ref = bf16[2,144,256]{2,1,0:T(8,128)(2,1)S(1)} collective-permute-done((bf16[2,144,256]{2,1,0:T(8,128)(2,1)S(1)}, bf16[2,144,256]{2,1,0:T(8,128)(2,1)S(1)}, u32[]{:S(2)}, u32[]{:S(2)}) %collective-permute-start.8) | collective-permute-done | bytes 147488 | tf_op jit(solution)/shard_map/ppermute | solution.py:345
  25.6 1.6 %collective-permute-start.9 = (bf16[144,256]{1,0:T(8,128)(2,1)S(1)}, bf16[144,256]{1,0:T(8,128)(2,1)S(1)}, u32[]{:S(2)}, u32[]{:S(2)}) collective-permute-start(bf16[144,256]{1,0:T(8,128)(2,1)S(1)} %get-tuple-element.21), channel_id=1, source_target_pairs={{0,2},{1,3},{2,0},{3,1},{4,6},{5,7},{6,4},{7,5},{8,10},{9,11},{10,... | collective-permute-start | bytes 221192 | tf_op jit(solution)/shard_map/ppermute | solution.py:352
  27.2 1.4 %collective-permute-start.7 = (f32[1,16]{1,0:T(1,128)S(1)}, f32[1,16]{1,0:T(1,128)S(1)}, u32[]{:S(2)}, u32[]{:S(2)}) collective-permute-start(f32[1,16]{1,0:T(1,128)S(1)} %bind.1.peak_ref), channel_id=1, source_target_pairs={{0,8},{4,12},{8,0},{12,4},{1,9},{5,13},{9,1},{13,5},{2,10},{6,14},... | collective-permute-start | bytes 200 | tf_op jit(solution)/shard_map/ppermute | solution.py:43
  28.6 3.1 %collective-permute-done.7.peak_got = f32[1,16]{1,0:T(1,128)S(1)} collective-permute-done((f32[1,16]{1,0:T(1,128)S(1)}, f32[1,16]{1,0:T(1,128)S(1)}, u32[]{:S(2)}, u32[]{:S(2)}) %collective-permute-start.7) | collective-permute-done | bytes 96 | tf_op jit(solution)/shard_map/ppermute | solution.py:43
  31.7 0.8 %finish.1 = (f32[1,16]{1,0:T(1,128)}, bf16[128,256]{1,0:T(8,128)(2,1)}) custom-call(f32[1,16]{1,0:T(1,128)S(1)} %bind.1.peak_ref, f32[1,16]{1,0:T(1,128)S(1)} %collective-permute-done.7.peak_got, f32[144,256]{1,0:T(8,128)S(1)} %get-tuple-element.20.keep_ref, bf16[144,256]{1,0:T(8,128)(2,1)S(1)} %collective-permute-done.9.refs_0_), custom_call_target="tpu_custom_call" | custom-call | tf_op jit(solution)/shard_map/finish/pallas_call | solution.py:24
  (21 shorter events, 0.1 us)
Async XLA Ops:
  1.4 3.0 %copy-start.1 = (bf16[1,128,2048]{2,1,0:T(8,128)(2,1)S(1)}, bf16[1,128,2048]{2,1,0:T(8,128)(2,1)}, u32[]{:S(2)}) copy-start(bf16[1,128,2048]{2,1,0:T(8,128)(2,1)} %q_ref.5) | copy-start | bytes 1572868
  1.4 5.5 %collective-permute-start = (bf16[128,256]{1,0:T(8,128)(2,1)S(1)}, bf16[128,256]{1,0:T(8,128)(2,1)S(1)}, u32[]{:S(2)}, u32[]{:S(2)}) collective-permute-start(bf16[128,256]{1,0:T(8,128)(2,1)S(1)} %pad_maximum_fusion.here_ref.block_ref), channel_id=1, source_target_pairs={{16,0},{0,16},{17,1},{1,17},{18,2},{2,18},{19,3},{3,19},{20,4},{4,... | collective-permute-start | bytes 196616 | tf_op jit(solution)/shard_map/ppermute | solution.py:48
  4.4 7.7 %copy-start.3 = (s32[8]{0:T(128)S(1)}, s32[8]{0:T(128)}, u32[]{:S(2)}) copy-start(s32[8]{0:T(128)} %order_ref.1) | copy-start | bytes 100
  4.5 15.1 %collective-permute-start.5 = (bf16[128,1024]{1,0:T(8,128)(2,1)S(1)}, bf16[128,1024]{1,0:T(8,128)(2,1)S(1)}, u32[]{:S(2)}, u32[]{:S(2)}) collective-permute-start(bf16[128,1024]{1,0:T(8,128)(2,1)S(1)} %take.2), channel_id=1, source_target_pairs={{16,0},{0,16},{17,1},{1,17},{18,2},{2,18},{19,3},{3,19},{20,4},{4,... | collective-permute-start | bytes 786440 | tf_op jit(solution)/shard_map/ppermute | solution.py:48
  6.9 7.7 %copy-start = (bf16[1,2048,1024]{2,1,0:T(8,128)(2,1)S(1)}, bf16[1,2048,1024]{2,1,0:T(8,128)(2,1)}, u32[]{:S(2)}) copy-start(bf16[1,2048,1024]{2,1,0:T(8,128)(2,1)} %param.11) | copy-start | bytes 12582916
  6.9 7.7 %copy-start.2 = (bf16[1,2048]{1,0:T(2,128)(2,1)S(1)}, bf16[1,2048]{1,0:T(2,128)(2,1)}, u32[]{:S(2)}) copy-start(bf16[1,2048]{1,0:T(2,128)(2,1)} %gain_ref.1) | copy-start | bytes 12292
  7.0 7.7 %collective-permute-start.1 = (bf16[128,384]{1,0:T(8,128)(2,1)S(1)}, bf16[128,384]{1,0:T(8,128)(2,1)S(1)}, u32[]{:S(2)}, u32[]{:S(2)}) collective-permute-start(bf16[128,384]{1,0:T(8,128)(2,1)S(1)} %join.1.refs_3_.after), channel_id=1, source_target_pairs={{0,12},{4,8},{8,4},{12,0},{1,13},{5,9},{9,5},{13,1},{2,14},{6,10},... | collective-permute-start | bytes 294920 | tf_op jit(solution)/shard_map/ppermute | solution.py:43
  11.4 6.7 %collective-permute-start.2 = (bf16[128,384]{1,0:T(8,128)(2,1)S(1)}, bf16[128,384]{1,0:T(8,128)(2,1)S(1)}, u32[]{:S(2)}, u32[]{:S(2)}) collective-permute-start(bf16[128,384]{1,0:T(8,128)(2,1)S(1)} %join.1.refs_3_.after), channel_id=1, source_target_pairs={{0,8},{4,12},{8,0},{12,4},{1,9},{5,13},{9,1},{13,5},{2,10},{6,14},... | collective-permute-start | bytes 294920 | tf_op jit(solution)/shard_map/ppermute | solution.py:43
  11.4 6.7 %collective-permute-start.3 = (bf16[128,384]{1,0:T(8,128)(2,1)S(1)}, bf16[128,384]{1,0:T(8,128)(2,1)S(1)}, u32[]{:S(2)}, u32[]{:S(2)}) collective-permute-start(bf16[128,384]{1,0:T(8,128)(2,1)S(1)} %join.1.refs_3_.after), channel_id=1, source_target_pairs={{0,4},{4,0},{8,12},{12,8},{1,5},{5,1},{9,13},{13,9},{2,6},{6,2},{1... | collective-permute-start | bytes 294920 | tf_op jit(solution)/shard_map/ppermute | solution.py:43
  12.7 9.9 %collective-permute-start.6 = (bf16[128,1024]{1,0:T(8,128)(2,1)S(1)}, bf16[128,1024]{1,0:T(8,128)(2,1)S(1)}, u32[]{:S(2)}, u32[]{:S(2)}) collective-permute-start(bf16[128,1024]{1,0:T(8,128)(2,1)S(1)} %take.3), channel_id=1, source_target_pairs={{16,0},{0,16},{17,1},{1,17},{18,2},{2,18},{19,3},{3,19},{20,4},{4,... | collective-permute-start | bytes 786440 | tf_op jit(solution)/shard_map/ppermute | solution.py:48
  19.1 3.5 %collective-permute-start.4 = (f32[1,16]{1,0:T(1,128)S(1)}, f32[1,16]{1,0:T(1,128)S(1)}, u32[]{:S(2)}, u32[]{:S(2)}) collective-permute-start(f32[1,16]{1,0:T(1,128)S(1)} %maxima.1.after.left_ref), channel_id=1, source_target_pairs={{0,4},{4,0},{8,12},{12,8},{1,5},{5,1},{9,13},{13,9},{2,6},{6,2},{1... | collective-permute-start | bytes 200 | tf_op jit(solution)/shard_map/ppermute | solution.py:43
  24.2 1.4 %collective-permute-start.8 = (bf16[2,144,256]{2,1,0:T(8,128)(2,1)S(1)}, bf16[2,144,256]{2,1,0:T(8,128)(2,1)S(1)}, u32[]{:S(2)}, u32[]{:S(2)}) collective-permute-start(bf16[2,144,256]{2,1,0:T(8,128)(2,1)S(1)} %get-tuple-element.18.after), channel_id=1, source_target_pairs={{0,1},{1,0},{2,3},{3,2},{4,5},{5,4},{6,7},{7,6},{8,9},{9,8},{10,11... | collective-permute-start | bytes 442376 | tf_op jit(solution)/shard_map/ppermute | solution.py:345
  25.6 6.0 %collective-permute-start.9 = (bf16[144,256]{1,0:T(8,128)(2,1)S(1)}, bf16[144,256]{1,0:T(8,128)(2,1)S(1)}, u32[]{:S(2)}, u32[]{:S(2)}) collective-permute-start(bf16[144,256]{1,0:T(8,128)(2,1)S(1)} %get-tuple-element.21), channel_id=1, source_target_pairs={{0,2},{1,3},{2,0},{3,1},{4,6},{5,7},{6,4},{7,5},{8,10},{9,11},{10,... | collective-permute-start | bytes 221192 | tf_op jit(solution)/shard_map/ppermute | solution.py:352
  27.2 4.4 %collective-permute-start.7 = (f32[1,16]{1,0:T(1,128)S(1)}, f32[1,16]{1,0:T(1,128)S(1)}, u32[]{:S(2)}, u32[]{:S(2)}) collective-permute-start(f32[1,16]{1,0:T(1,128)S(1)} %bind.1.peak_ref), channel_id=1, source_target_pairs={{0,8},{4,12},{8,0},{12,4},{1,9},{5,13},{9,1},{13,5},{2,10},{6,14},... | collective-permute-start | bytes 200 | tf_op jit(solution)/shard_map/ppermute | solution.py:43

commit v7 on v6

--- a/solution.py
+++ b/solution.py
@@ -191,29 +191,48 @@
     return jnp.broadcast_to(jnp.sum(total, axis=1, keepdims=True), total.shape)
 
 
-def project_first(ctx_ref, w_ref, sum_ref, square_ref):
-    square_ref[...] = square_sums(ctx_ref)
-    sum_ref[...] = jnp.dot(ctx_ref[...], w_ref[:ctx_ref.shape[1], :], preferred_element_type=F32)
-
-
-def project_last(ctx_ref, w_ref, sum_ref, square_ref, after, give_ref, keep_ref):
-    rows, width = ctx_ref.shape
-    start = w_ref.shape[0] - width
-    squares = square_ref[...] + square_sums(ctx_ref)
+def columns_of(y, side, cols):
+    return pl.ds(pl.multiple_of((2 * y + side) * cols, cols), cols)
+
+
+def fill(ref, y, part, squares):
+    rows, cols = part.shape
     lanes = squares.T[:SQUARE_ROWS, :]
     first = lanes.astype(BF16)
     rest = (lanes - first.astype(F32)).astype(BF16)
-    groups, cols = give_ref.shape[0], give_ref.shape[2]
+    ref[y, :rows, :] = part.astype(BF16)
+    ref[y, rows:, :rows] = first
+    ref[y, rows:, rows:2 * rows] = rest
+    if cols > 2 * rows:
+        ref[y, rows:, 2 * rows:] = jnp.zeros((SQUARE_ROWS, cols - 2 * rows), BF16)
+
+
+def project_first(ctx_ref, w_ref, sum_ref, square_ref):
+    other = 1 - lax.rem(lax.axis_index("tp"), 2)
+    square_ref[...] = square_sums(ctx_ref)
+    for y in range(sum_ref.shape[0]):
+        w = w_ref[:ctx_ref.shape[1], columns_of(y, other, sum_ref.shape[2])]
+        sum_ref[y] = jnp.dot(ctx_ref[...], w, preferred_element_type=F32)
+
+
+def project_give(ctx_ref, w_ref, sum_ref, square_ref, after, give_ref, square_out):
+    other = 1 - lax.rem(lax.axis_index("tp"), 2)
+    start = w_ref.shape[0] - ctx_ref.shape[1]
+    squares = square_ref[...] + square_sums(ctx_ref)
+    square_out[...] = squares
+    for y in range(give_ref.shape[0]):
+        w = w_ref[start:, columns_of(y, other, give_ref.shape[2])]
+        fill(give_ref, y, sum_ref[y] + jnp.dot(ctx_ref[...], w, preferred_element_type=F32), squares)
+
+
+def project_keep(first_ref, last_ref, w_ref, square_ref, keep_ref):
     core = lax.rem(lax.axis_index("tp"), 2)
-    for ref, side in ((give_ref, 1 - core), (keep_ref, core)):
-        for y in range(groups):
-            at = pl.ds(pl.multiple_of((2 * y + side) * cols, cols), cols)
-            part = sum_ref[:, at] + jnp.dot(ctx_ref[...], w_ref[start:, at], preferred_element_type=F32)
-            ref[y, :rows, :] = part.astype(BF16)
-            ref[y, rows:, :rows] = first
-            ref[y, rows:, rows:2 * rows] = rest
-            if cols > 2 * rows:
-                ref[y, rows:, 2 * rows:] = jnp.zeros((SQUARE_ROWS, cols - 2 * rows), BF16)
+    cut = first_ref.shape[1]
+    for y in range(keep_ref.shape[0]):
+        at = columns_of(y, core, keep_ref.shape[2])
+        part = jnp.dot(first_ref[...], w_ref[:cut, at], preferred_element_type=F32)
+        part += jnp.dot(last_ref[...], w_ref[cut:, at], preferred_element_type=F32)
+        fill(keep_ref, y, part, square_ref[...])
 
 
 def larger(left_ref, right_ref, after, out_ref):
@@ -319,7 +338,7 @@
         if start == 0:
             total, squares = call(
                 project_first,
-                (shape((rows, columns), F32), shape((rows, LANES), F32)),
+                (shape((peers // 2, rows, out_cols), F32), shape((rows, LANES), F32)),
                 (context, w),
                 name="project_first",
                 micros=0.7,
@@ -329,19 +348,20 @@
         peak = call(
             larger,
             shape((1, heads), F32),
-            (peak, swapped(peak, "cp", step), squares),
+            (peak, swapped(peak, "cp", step), contexts[-1]),
             [WHOLE, WHOLE, OUTSIDE],
             name="larger",
         )
     slab = shape((peers // 2, rows + SQUARE_ROWS, out_cols), BF16)
-    give, keep = call(
-        project_last,
-        (slab, slab),
+    give, squares = call(
+        project_give,
+        (slab, shape((rows, LANES), F32)),
         (contexts[-1], w, total, squares, peak),
         [WHOLE] * 4 + [OUTSIDE],
-        name="project_last",
-        micros=0.5,
-    )
+        name="project_give",
+        micros=0.4,
+    )
+    keep = call(project_keep, slab, (*contexts, w, squares), name="project_keep", micros=0.6)
     got = lax.ppermute(give, "tp", [(i, i ^ 1) for i in range(peers)])
     peak = bind(peak, give)
     slab = (rows + SQUARE_ROWS, out_cols)

time: 32.7 us -> 31.6 us (0.966)
  waiting for transfers between devices: 10.1 us -> 8.35 us
    ppermute x5, waiting for transfers between devices: 7.31 us -> 6.05 us  [swapped(): lax.ppermute(block, axis, [(i, partner(i, step, size)) for i in range(siz...]
    ppermute x1, waiting for transfers between devices: 1.36 us -> 0.87 us  [on_device(): got = lax.ppermute(give, 'tp', [(i, i ^ 1) for i in range(peers)])]
    ppermute x5, starting transfers between devices: 7 us -> 7.38 us  [swapped(): lax.ppermute(block, axis, [(i, partner(i, step, size)) for i in range(siz...]
    pallas_call x16 -> x17, Pallas kernels: 6.27 us -> 6.5 us  [call(): pl.pallas_call(kernel, out_shape=outs, in_specs=specs or [WHOLE] * len(ar...]
  transfers between devices with their start and end apart: 10 -> 10, of which waited for: 5 -> 5; matrix products, arithmetic and copies ran while one was open for 0% -> 0% of each run, Pallas kernels for 12% -> 17%
where the time goes in v7:
time: 31.6 us; the launch traced here: 31.4 us
  starting transfers between devices  14.9 us (47%)
  waiting for transfers between devices  8.35 us (26%)
  Pallas kernels  6.5 us (21%)
  other arithmetic  0.78 us (2%)
  between operations  0.76 us (2%)
    ppermute x5, starting transfers between devices, swapped(): lax.ppermute(block, axis, [(i, partner(i, step, size)) for i in range(siz...  7.38 us
    pallas_call x17, Pallas kernels, call(): pl.pallas_call(kernel, out_shape=outs, in_specs=specs or [WHOLE] * len(ar...  6.5 us
    ppermute x5, waiting for transfers between devices, swapped(): lax.ppermute(block, axis, [(i, partner(i, step, size)) for i in range(siz...  6.05 us
    ppermute x3, starting transfers between devices, shifted(): lax.ppermute(block, axis, [((i - distance) % size, i) for i in range(size)])  5.9 us
    ppermute x1, starting transfers between devices, on_device(): lax.ppermute(block, 'tp', [(i, (i + 2 * (step + 1)) % peers) for i in ran...  1.59 us
    ppermute x3, waiting for transfers between devices, shifted(): lax.ppermute(block, axis, [((i - distance) % size, i) for i in range(size)])  1.43 us
    ppermute x1, waiting for transfers between devices, on_device(): got = lax.ppermute(give, 'tp', [(i, i ^ 1) for i in range(peers)])  0.87 us
    concatenate x1, other arithmetic, on_device(): pair_here = jnp.concatenate([key_vectors[0], value_vectors[0]], axis=1)  0.78 us
  transfers between devices with their start and end apart: 10, of which 5 were waited for; matrix products, arithmetic and copies ran while one was open for 0% of the time, Pallas kernels for 17%

profile of v7, /device:TPU:0, one launch (start us, length us, event | category | flops | bytes accessed | tf_op | source)
XLA Modules:
  0.0 31.4 jit_solution(9666014194919447362)
XLA Ops:
  0.6 0.8 %pad_maximum_fusion.here_ref.block_ref = bf16[128,256]{1,0:T(8,128)(2,1)S(1)} fusion(bf16[128,128]{1,0:T(8,128)(2,1)} %bitcast.5, bf16[128,128]{1,0:T(8,128)(2,1)} %bitcast.6), kind=kLoop, calls=%fused_computation | loop fusion | flops 131072 | bytes 131072 | tf_op jit(solution)/shard_map/concatenate | solution.py:275
  1.4 3.0 %collective-permute-start = (bf16[128,256]{1,0:T(8,128)(2,1)S(1)}, bf16[128,256]{1,0:T(8,128)(2,1)S(1)}, u32[]{:S(2)}, u32[]{:S(2)}) collective-permute-start(bf16[128,256]{1,0:T(8,128)(2,1)S(1)} %pad_maximum_fusion.here_ref.block_ref), channel_id=1, source_target_pairs={{16,0},{0,16},{17,1},{1,17},{18,2},{2,18},{19,3},{3,19},{20,4},{4,... | collective-permute-start | bytes 196616 | tf_op jit(solution)/shard_map/ppermute | solution.py:48
  4.5 1.0 %collective-permute-start.6 = (bf16[128,1024]{1,0:T(8,128)(2,1)S(1)}, bf16[128,1024]{1,0:T(8,128)(2,1)S(1)}, u32[]{:S(2)}, u32[]{:S(2)}) collective-permute-start(bf16[128,1024]{1,0:T(8,128)(2,1)S(1)} %take.3), channel_id=1, source_target_pairs={{16,0},{0,16},{17,1},{1,17},{18,2},{2,18},{19,3},{3,19},{20,4},{4,... | collective-permute-start | bytes 786440 | tf_op jit(solution)/shard_map/ppermute | solution.py:48
  5.5 1.4 %collective-permute-done.pair_ref = bf16[128,256]{1,0:T(8,128)(2,1)S(1)} collective-permute-done((bf16[128,256]{1,0:T(8,128)(2,1)S(1)}, bf16[128,256]{1,0:T(8,128)(2,1)S(1)}, u32[]{:S(2)}, u32[]{:S(2)}) %collective-permute-start) | collective-permute-done | bytes 65568 | tf_op jit(solution)/shard_map/ppermute | solution.py:48
  7.0 4.5 %collective-permute-start.1 = (bf16[128,384]{1,0:T(8,128)(2,1)S(1)}, bf16[128,384]{1,0:T(8,128)(2,1)S(1)}, u32[]{:S(2)}, u32[]{:S(2)}) collective-permute-start(bf16[128,384]{1,0:T(8,128)(2,1)S(1)} %join.1.refs_3_.after), channel_id=1, source_target_pairs={{0,12},{4,8},{8,4},{12,0},{1,13},{5,9},{9,5},{13,1},{2,14},{6,10},... | collective-permute-start | bytes 294920 | tf_op jit(solution)/shard_map/ppermute | solution.py:43
  11.4 0.6 %collective-permute-start.3 = (bf16[128,384]{1,0:T(8,128)(2,1)S(1)}, bf16[128,384]{1,0:T(8,128)(2,1)S(1)}, u32[]{:S(2)}, u32[]{:S(2)}) collective-permute-start(bf16[128,384]{1,0:T(8,128)(2,1)S(1)} %join.1.refs_3_.after), channel_id=1, source_target_pairs={{0,4},{4,0},{8,12},{12,8},{1,5},{5,1},{9,13},{13,9},{2,6},{6,2},{1... | collective-permute-start | bytes 294920 | tf_op jit(solution)/shard_map/ppermute | solution.py:43
  12.1 0.6 %prepare.1.feature_ref = bf16[2,128,512]{2,1,0:T(8,128)(2,1)S(1)} custom-call(s32[8]{0:T(128)S(1)} %copy-done.3, f32[8,128]{1,0:T(8,128)S(1)} %touch.1.after), custom_call_target="tpu_custom_call" | custom-call | flops 3000000000 | tf_op jit(solution)/shard_map/prepare/pallas_call | solution.py:24
  12.7 1.9 %collective-permute-start.5 = (bf16[128,1024]{1,0:T(8,128)(2,1)S(1)}, bf16[128,1024]{1,0:T(8,128)(2,1)S(1)}, u32[]{:S(2)}, u32[]{:S(2)}) collective-permute-start(bf16[128,1024]{1,0:T(8,128)(2,1)S(1)} %take.2), channel_id=1, source_target_pairs={{16,0},{0,16},{17,1},{1,17},{18,2},{2,18},{19,3},{3,19},{20,4},{4,... | collective-permute-start | bytes 786440 | tf_op jit(solution)/shard_map/ppermute | solution.py:48
  14.6 0.9 %weigh.1.after.w_ref = bf16[2048,1024]{1,0:T(8,128)(2,1)S(1)} custom-call(bf16[2048,1024]{1,0:T(8,128)(2,1)S(1)} %bitcast.4, bf16[1,2048]{1,0:T(2,128)(2,1)S(1)} %copy-done.2, bf16[128,384]{1,0:T(8,128)(2,1)S(1)} %collective-permute-done.1.after.refs_0_), custom_call_target="tpu_custom_call" | custom-call | flops 1000000000 | tf_op jit(solution)/shard_map/weigh/pallas_call | solution.py:24
  15.5 2.6 %collective-permute-done.2.refs_1_ = bf16[128,384]{1,0:T(8,128)(2,1)S(1)} collective-permute-done((bf16[128,384]{1,0:T(8,128)(2,1)S(1)}, bf16[128,384]{1,0:T(8,128)(2,1)S(1)}, u32[]{:S(2)}, u32[]{:S(2)}) %collective-permute-start.2) | collective-permute-done | bytes 98336 | tf_op jit(solution)/shard_map/ppermute | solution.py:43
  18.1 0.2 arrange.1
  18.3 0.8 %maxima.1.after.left_ref = f32[1,16]{1,0:T(1,128)S(1)} custom-call(bf16[1,128,2048]{2,1,0:T(8,128)(2,1)S(1)} %copy-done.1, bf16[1,2,256,512]{3,2,1,0:T(8,128)(2,1)S(1)} %get-tuple-element.13.own_ref), custom_call_target="tpu_custom_call" | custom-call | flops 700000000 | tf_op jit(solution)/shard_map/maxima/pallas_call | solution.py:24
  19.1 0.5 %collective-permute-start.4 = (f32[1,16]{1,0:T(1,128)S(1)}, f32[1,16]{1,0:T(1,128)S(1)}, u32[]{:S(2)}, u32[]{:S(2)}) collective-permute-start(f32[1,16]{1,0:T(1,128)S(1)} %maxima.1.after.left_ref), channel_id=1, source_target_pairs={{0,4},{4,0},{8,12},{12,8},{1,5},{5,1},{9,13},{13,9},{2,6},{6,2},{1... | collective-permute-start | bytes 200 | tf_op jit(solution)/shard_map/ppermute | solution.py:43
  19.6 0.9 %attend.2.ctx_ref.first_ref = bf16[128,1024]{1,0:T(8,128)(2,1)S(1)} custom-call(bf16[128,1024]{1,0:T(8,128)(2,1)S(1)} %collective-permute-done.6.q_ref, bf16[1,2,256,512]{3,2,1,0:T(8,128)(2,1)S(1)} %get-tuple-element.14.kt_ref, bf16[1,512,256]{2,1,0:T(8,128)(2,1)S(1)} %get-tuple-element.15.v_ref, f32[1,16]{1,0:T(1,128)S(1)} %maxima.1.after.left_ref), custom_call_target="tpu_custom_call" | custom-call | flops 960000000 | tf_op jit(solution)/shard_map/attend/pallas_call | solution.py:24
  20.5 0.4 %project_first.1 = (f32[2,128,256]{2,1,0:T(8,128)S(1)}, f32[128,128]{1,0:T(8,128)S(1)}) custom-call(bf16[128,1024]{1,0:T(8,128)(2,1)S(1)} %attend.2.ctx_ref.first_ref, bf16[2048,1024]{1,0:T(8,128)(2,1)S(1)} %weigh.1.after.w_ref), custom_call_target="tpu_custom_call" | custom-call | flops 700000000 | tf_op jit(solution)/shard_map/project_first/pallas_call | solution.py:24
  20.9 0.9 %attend.3.after.ctx_ref.last_ref = bf16[128,1024]{1,0:T(8,128)(2,1)S(1)} custom-call(bf16[128,1024]{1,0:T(8,128)(2,1)S(1)} %collective-permute-done.5.q_ref, bf16[1,2,256,512]{3,2,1,0:T(8,128)(2,1)S(1)} %get-tuple-element.14.kt_ref, bf16[1,512,256]{2,1,0:T(8,128)(2,1)S(1)} %get-tuple-element.15.v_ref, f32[128,128]{1,0:T(8,128)S(1)} %get-tuple-element.16.after.square_ref), custom_call_target="tpu_custom_call" | custom-call | flops 960000000 | tf_op jit(solution)/shard_map/attend/pallas_call | solution.py:24
  21.9 0.8 %collective-permute-done.4.right_ref = f32[1,16]{1,0:T(1,128)S(1)} collective-permute-done((f32[1,16]{1,0:T(1,128)S(1)}, f32[1,16]{1,0:T(1,128)S(1)}, u32[]{:S(2)}, u32[]{:S(2)}) %collective-permute-start.4) | collective-permute-done | bytes 96 | tf_op jit(solution)/shard_map/ppermute | solution.py:43
  22.6 0.4 %project_give.1 = (bf16[2,144,256]{2,1,0:T(8,128)(2,1)S(1)}, f32[128,128]{1,0:T(8,128)S(1)}) custom-call(bf16[128,1024]{1,0:T(8,128)(2,1)S(1)} %attend.3.after.ctx_ref.last_ref, bf16[2048,1024]{1,0:T(8,128)(2,1)S(1)} %weigh.1.after.w_ref, f32[2,128,256]{2,1,0:T(8,128)S(1)} %get-tuple-element.17.sum_ref, f32[128,128]{1,0:T(8,128)S(1)} %get-tuple-element.16.after.square_ref, ...), custom_call_target="tpu_custom_call" | custom-call | flops 400000000 | tf_op jit(solution)/shard_map/project_give/pallas_call | solution.py:24
  23.1 0.5 %project_keep.1.keep_ref = bf16[2,144,256]{2,1,0:T(8,128)(2,1)S(1)} custom-call(bf16[128,1024]{1,0:T(8,128)(2,1)S(1)} %attend.2.ctx_ref.first_ref, bf16[128,1024]{1,0:T(8,128)(2,1)S(1)} %attend.3.after.ctx_ref.last_ref, bf16[2048,1024]{1,0:T(8,128)(2,1)S(1)} %weigh.1.after.w_ref, f32[128,128]{1,0:T(8,128)S(1)} %get-tuple-element.19.square_ref), custom_call_target="tpu_custom_call" | custom-call | flops 600000000 | tf_op jit(solution)/shard_map/project_keep/pallas_call | solution.py:24
  23.6 0.9 %collective-permute-done.8.got_ref = bf16[2,144,256]{2,1,0:T(8,128)(2,1)S(1)} collective-permute-done((bf16[2,144,256]{2,1,0:T(8,128)(2,1)S(1)}, bf16[2,144,256]{2,1,0:T(8,128)(2,1)S(1)}, u32[]{:S(2)}, u32[]{:S(2)}) %collective-permute-start.8) | collective-permute-done | bytes 147488 | tf_op jit(solution)/shard_map/ppermute | solution.py:365
  24.5 1.6 %collective-permute-start.9 = (bf16[144,256]{1,0:T(8,128)(2,1)S(1)}, bf16[144,256]{1,0:T(8,128)(2,1)S(1)}, u32[]{:S(2)}, u32[]{:S(2)}) collective-permute-start(bf16[144,256]{1,0:T(8,128)(2,1)S(1)} %get-tuple-element.21), channel_id=1, source_target_pairs={{0,2},{1,3},{2,0},{3,1},{4,6},{5,7},{6,4},{7,5},{8,10},{9,11},{10,... | collective-permute-start | bytes 221192 | tf_op jit(solution)/shard_map/ppermute | solution.py:372
  26.1 1.8 %collective-permute-start.7 = (f32[1,16]{1,0:T(1,128)S(1)}, f32[1,16]{1,0:T(1,128)S(1)}, u32[]{:S(2)}, u32[]{:S(2)}) collective-permute-start(f32[1,16]{1,0:T(1,128)S(1)} %bind.1.peak_ref), channel_id=1, source_target_pairs={{0,8},{4,12},{8,0},{12,4},{1,9},{5,13},{9,1},{13,5},{2,10},{6,14},... | collective-permute-start | bytes 200 | tf_op jit(solution)/shard_map/ppermute | solution.py:43
  27.9 2.7 %collective-permute-done.7.peak_got = f32[1,16]{1,0:T(1,128)S(1)} collective-permute-done((f32[1,16]{1,0:T(1,128)S(1)}, f32[1,16]{1,0:T(1,128)S(1)}, u32[]{:S(2)}, u32[]{:S(2)}) %collective-permute-start.7) | collective-permute-done | bytes 96 | tf_op jit(solution)/shard_map/ppermute | solution.py:43
  30.6 0.8 %finish.1 = (f32[1,16]{1,0:T(1,128)}, bf16[128,256]{1,0:T(8,128)(2,1)}) custom-call(f32[1,16]{1,0:T(1,128)S(1)} %bind.1.peak_ref, f32[1,16]{1,0:T(1,128)S(1)} %collective-permute-done.7.peak_got, f32[144,256]{1,0:T(8,128)S(1)} %get-tuple-element.20.keep_ref, bf16[144,256]{1,0:T(8,128)(2,1)S(1)} %collective-permute-done.9.refs_0_), custom_call_target="tpu_custom_call" | custom-call | tf_op jit(solution)/shard_map/finish/pallas_call | solution.py:24
  (22 shorter events, 0.2 us)
Async XLA Ops:
  1.4 3.0 %copy-start.1 = (bf16[1,128,2048]{2,1,0:T(8,128)(2,1)S(1)}, bf16[1,128,2048]{2,1,0:T(8,128)(2,1)}, u32[]{:S(2)}) copy-start(bf16[1,128,2048]{2,1,0:T(8,128)(2,1)} %q_ref.5) | copy-start | bytes 1572868
  1.4 5.5 %collective-permute-start = (bf16[128,256]{1,0:T(8,128)(2,1)S(1)}, bf16[128,256]{1,0:T(8,128)(2,1)S(1)}, u32[]{:S(2)}, u32[]{:S(2)}) collective-permute-start(bf16[128,256]{1,0:T(8,128)(2,1)S(1)} %pad_maximum_fusion.here_ref.block_ref), channel_id=1, source_target_pairs={{16,0},{0,16},{17,1},{1,17},{18,2},{2,18},{19,3},{3,19},{20,4},{4,... | collective-permute-start | bytes 196616 | tf_op jit(solution)/shard_map/ppermute | solution.py:48
  4.4 7.7 %copy-start.3 = (s32[8]{0:T(128)S(1)}, s32[8]{0:T(128)}, u32[]{:S(2)}) copy-start(s32[8]{0:T(128)} %order_ref.1) | copy-start | bytes 100
  4.5 15.1 %collective-permute-start.6 = (bf16[128,1024]{1,0:T(8,128)(2,1)S(1)}, bf16[128,1024]{1,0:T(8,128)(2,1)S(1)}, u32[]{:S(2)}, u32[]{:S(2)}) collective-permute-start(bf16[128,1024]{1,0:T(8,128)(2,1)S(1)} %take.3), channel_id=1, source_target_pairs={{16,0},{0,16},{17,1},{1,17},{18,2},{2,18},{19,3},{3,19},{20,4},{4,... | collective-permute-start | bytes 786440 | tf_op jit(solution)/shard_map/ppermute | solution.py:48
  6.9 7.7 %copy-start = (bf16[1,2048,1024]{2,1,0:T(8,128)(2,1)S(1)}, bf16[1,2048,1024]{2,1,0:T(8,128)(2,1)}, u32[]{:S(2)}) copy-start(bf16[1,2048,1024]{2,1,0:T(8,128)(2,1)} %param.11) | copy-start | bytes 12582916
  6.9 7.7 %copy-start.2 = (bf16[1,2048]{1,0:T(2,128)(2,1)S(1)}, bf16[1,2048]{1,0:T(2,128)(2,1)}, u32[]{:S(2)}) copy-start(bf16[1,2048]{1,0:T(2,128)(2,1)} %gain_ref.1) | copy-start | bytes 12292
  7.0 7.7 %collective-permute-start.1 = (bf16[128,384]{1,0:T(8,128)(2,1)S(1)}, bf16[128,384]{1,0:T(8,128)(2,1)S(1)}, u32[]{:S(2)}, u32[]{:S(2)}) collective-permute-start(bf16[128,384]{1,0:T(8,128)(2,1)S(1)} %join.1.refs_3_.after), channel_id=1, source_target_pairs={{0,12},{4,8},{8,4},{12,0},{1,13},{5,9},{9,5},{13,1},{2,14},{6,10},... | collective-permute-start | bytes 294920 | tf_op jit(solution)/shard_map/ppermute | solution.py:43
  11.4 6.7 %collective-permute-start.2 = (bf16[128,384]{1,0:T(8,128)(2,1)S(1)}, bf16[128,384]{1,0:T(8,128)(2,1)S(1)}, u32[]{:S(2)}, u32[]{:S(2)}) collective-permute-start(bf16[128,384]{1,0:T(8,128)(2,1)S(1)} %join.1.refs_3_.after), channel_id=1, source_target_pairs={{0,8},{4,12},{8,0},{12,4},{1,9},{5,13},{9,1},{13,5},{2,10},{6,14},... | collective-permute-start | bytes 294920 | tf_op jit(solution)/shard_map/ppermute | solution.py:43
  11.4 6.7 %collective-permute-start.3 = (bf16[128,384]{1,0:T(8,128)(2,1)S(1)}, bf16[128,384]{1,0:T(8,128)(2,1)S(1)}, u32[]{:S(2)}, u32[]{:S(2)}) collective-permute-start(bf16[128,384]{1,0:T(8,128)(2,1)S(1)} %join.1.refs_3_.after), channel_id=1, source_target_pairs={{0,4},{4,0},{8,12},{12,8},{1,5},{5,1},{9,13},{13,9},{2,6},{6,2},{1... | collective-permute-start | bytes 294920 | tf_op jit(solution)/shard_map/ppermute | solution.py:43
  12.7 8.2 %collective-permute-start.5 = (bf16[128,1024]{1,0:T(8,128)(2,1)S(1)}, bf16[128,1024]{1,0:T(8,128)(2,1)S(1)}, u32[]{:S(2)}, u32[]{:S(2)}) collective-permute-start(bf16[128,1024]{1,0:T(8,128)(2,1)S(1)} %take.2), channel_id=1, source_target_pairs={{16,0},{0,16},{17,1},{1,17},{18,2},{2,18},{19,3},{3,19},{20,4},{4,... | collective-permute-start | bytes 786440 | tf_op jit(solution)/shard_map/ppermute | solution.py:48
  19.1 3.5 %collective-permute-start.4 = (f32[1,16]{1,0:T(1,128)S(1)}, f32[1,16]{1,0:T(1,128)S(1)}, u32[]{:S(2)}, u32[]{:S(2)}) collective-permute-start(f32[1,16]{1,0:T(1,128)S(1)} %maxima.1.after.left_ref), channel_id=1, source_target_pairs={{0,4},{4,0},{8,12},{12,8},{1,5},{5,1},{9,13},{13,9},{2,6},{6,2},{1... | collective-permute-start | bytes 200 | tf_op jit(solution)/shard_map/ppermute | solution.py:43
  23.0 1.4 %collective-permute-start.8 = (bf16[2,144,256]{2,1,0:T(8,128)(2,1)S(1)}, bf16[2,144,256]{2,1,0:T(8,128)(2,1)S(1)}, u32[]{:S(2)}, u32[]{:S(2)}) collective-permute-start(bf16[2,144,256]{2,1,0:T(8,128)(2,1)S(1)} %get-tuple-element.18.after), channel_id=1, source_target_pairs={{0,1},{1,0},{2,3},{3,2},{4,5},{5,4},{6,7},{7,6},{8,9},{9,8},{10,11... | collective-permute-start | bytes 442376 | tf_op jit(solution)/shard_map/ppermute | solution.py:365
  24.5 6.0 %collective-permute-start.9 = (bf16[144,256]{1,0:T(8,128)(2,1)S(1)}, bf16[144,256]{1,0:T(8,128)(2,1)S(1)}, u32[]{:S(2)}, u32[]{:S(2)}) collective-permute-start(bf16[144,256]{1,0:T(8,128)(2,1)S(1)} %get-tuple-element.21), channel_id=1, source_target_pairs={{0,2},{1,3},{2,0},{3,1},{4,6},{5,7},{6,4},{7,5},{8,10},{9,11},{10,... | collective-permute-start | bytes 221192 | tf_op jit(solution)/shard_map/ppermute | solution.py:372
  26.1 4.4 %collective-permute-start.7 = (f32[1,16]{1,0:T(1,128)S(1)}, f32[1,16]{1,0:T(1,128)S(1)}, u32[]{:S(2)}, u32[]{:S(2)}) collective-permute-start(f32[1,16]{1,0:T(1,128)S(1)} %bind.1.peak_ref), channel_id=1, source_target_pairs={{0,8},{4,12},{8,0},{12,4},{1,9},{5,13},{9,1},{13,5},{2,10},{6,14},... | collective-permute-start | bytes 200 | tf_op jit(solution)/shard_map/ppermute | solution.py:43

commit v8 on v7

--- a/solution.py
+++ b/solution.py
@@ -93,21 +93,35 @@
     out_ref[:, width:] = here_ref[:, :width // 2]
 
 
-def arrange(after, feature_ref, *refs):
-    triples, (kt_ref, v_ref, own_ref) = refs[-4::-1], refs[-3:]
+def turn(triple, first, block):
+    return triple[:, first:first + block].astype(F32).T.astype(BF16)
+
+
+def arrange_own(distances, after, feature_ref, *refs):
+    triples, own_ref = refs[:-1], refs[-1]
+    kv_local, rows = own_ref.shape[0], triples[0].shape[0]
+    for g in range(kv_local):
+        for n, (d, triple) in enumerate(zip(distances, triples)):
+            part = slice(n * rows, (n + 1) * rows)
+            turned = turn(triple, (2 * kv_local + g) * DH, DH)
+            for side in range(2):
+                own_ref[g, side, DH:, part] = feature_ref[side, :, d * rows:(d + 1) * rows]
+                own_ref[g, side, :DH, part] = turned
+
+
+def arrange(distances, after, feature_ref, *refs):
+    triples, (kt_ref, v_ref) = refs[:-2], refs[-2:]
     rows = triples[0].shape[0]
     kv_local = v_ref.shape[0]
     for g in range(kv_local):
         v_ref[g, :, DH:] = jnp.ones((v_ref.shape[1], DH), BF16)
-        for ref in (kt_ref, own_ref):
+        for side in range(2):
+            kt_ref[g, side, DH:, :] = feature_ref[side]
+        for d, triple in zip(distances, triples):
+            part = slice(d * rows, (d + 1) * rows)
+            turned = turn(triple, g * DH, DH)
             for side in range(2):
-                ref[g, side, DH:, :] = feature_ref[side]
-        for d, triple in enumerate(triples):
-            part = slice(d * rows, (d + 1) * rows)
-            for ref, first in ((kt_ref, g * DH), (own_ref, (2 * kv_local + g) * DH)):
-                turned = triple[:, first:first + DH].astype(F32).T.astype(BF16)
-                for side in range(2):
-                    ref[g, side, :DH, part] = turned
+                kt_ref[g, side, :DH, part] = turned
             first = (kv_local + g) * DH
             v_ref[g, part, :DH] = triple[:, first:first + DH]
 
@@ -132,7 +146,8 @@
     return jnp.concatenate([q, blocked], axis=1)
 
 
-def maxima(q_ref, own_ref, peak_ref):
+def maxima(q_ref, own_ref, *refs):
+    before, peak_ref = refs[:-1], refs[-1]
     q_ref = q_ref.at[0]
     block = q_ref.shape[0] // 2
     heads = q_ref.shape[1] // DH
@@ -149,7 +164,8 @@
         for j in range(stop - start):
             one = jnp.max(top[j * block:(j + 1) * block, :], axis=0, keepdims=True)
             h = start + j
-            peak_ref[:, h:h + 1] = jnp.max(one, axis=1, keepdims=True) * (1.0 / math.sqrt(DH))
+            one = jnp.max(one, axis=1, keepdims=True) * (1.0 / math.sqrt(DH))
+            peak_ref[:, h:h + 1] = jnp.maximum(one, before[0][:, h:h + 1]) if before else one
 
 
 def attend(first_head, heads, q_ref, kt_ref, v_ref, after, ctx_ref):
@@ -158,21 +174,29 @@
     block = rows // 2
     count = width // DH
     scale = 1.0 / math.sqrt(DH)
-    for g, start, stop in spans(first_head, count, heads // v_ref.shape[0], max(1, 12 * 512 // keys)):
-        scores = [
-            jnp.dot(stacked(q_ref, start, stop, side), kt_ref[g, side], preferred_element_type=F32) for side in range(2)
-        ]
-        probs = []
-        for s in scores:
-            m = jnp.max(s, axis=1, keepdims=True)
-            probs.append(jnp.exp2((s - m) * (scale * LOG2E)).astype(BF16))
-        for side in range(2):
-            o = jnp.dot(probs[side], v_ref[g], preferred_element_type=F32)
-            o = (o[:, :DH] * (1.0 / o[:, DH:])).astype(BF16)
-            for j in range(stop - start):
-                ctx_ref[side * block:(side + 1) * block, (start + j) * DH:(start + j + 1) * DH] = o[
-                    j * block:(j + 1) * block, :
-                ]
+    together = max(1, min(4, 4 * 512 // keys))
+    units = [
+        (g, start, stop, side)
+        for g, start, stop in spans(first_head, count, heads // v_ref.shape[0], together)
+        for side in range(2)
+    ]
+
+    def scores(g, start, stop, side):
+        return jnp.dot(stacked(q_ref, start, stop, side), kt_ref[g, side], preferred_element_type=F32)
+
+    ahead = [scores(*unit) for unit in units[:2]]
+    for n, (g, start, stop, side) in enumerate(units):
+        s = ahead.pop(0)
+        m = jnp.max(s, axis=1, keepdims=True)
+        p = jnp.exp2((s - m) * (scale * LOG2E)).astype(BF16)
+        if n + 2 < len(units):
+            ahead.append(scores(*units[n + 2]))
+        o = jnp.dot(p, v_ref[g], preferred_element_type=F32)
+        o = (o[:, :DH] * (1.0 / o[:, DH:])).astype(BF16)
+        for j in range(stop - start):
+            ctx_ref[side * block:(side + 1) * block, (start + j) * DH:(start + j + 1) * DH] = o[
+                j * block:(j + 1) * block, :
+            ]
 
 
 def weigh(w_ref, gain_ref, after, out_ref):
@@ -193,6 +217,12 @@
 
 def columns_of(y, side, cols):
     return pl.ds(pl.multiple_of((2 * y + side) * cols, cols), cols)
+
+
+def product(first_ref, last_ref, w_ref, at):
+    cut = first_ref.shape[1]
+    part = jnp.dot(first_ref[...], w_ref[:cut, at], preferred_element_type=F32)
+    return part + jnp.dot(last_ref[...], w_ref[cut:, at], preferred_element_type=F32)
 
 
 def fill(ref, y, part, squares):
@@ -207,32 +237,19 @@
         ref[y, rows:, 2 * rows:] = jnp.zeros((SQUARE_ROWS, cols - 2 * rows), BF16)
 
 
-def project_first(ctx_ref, w_ref, sum_ref, square_ref):
+def project_give(first_ref, last_ref, w_ref, after, give_ref, square_ref):
     other = 1 - lax.rem(lax.axis_index("tp"), 2)
-    square_ref[...] = square_sums(ctx_ref)
-    for y in range(sum_ref.shape[0]):
-        w = w_ref[:ctx_ref.shape[1], columns_of(y, other, sum_ref.shape[2])]
-        sum_ref[y] = jnp.dot(ctx_ref[...], w, preferred_element_type=F32)
-
-
-def project_give(ctx_ref, w_ref, sum_ref, square_ref, after, give_ref, square_out):
-    other = 1 - lax.rem(lax.axis_index("tp"), 2)
-    start = w_ref.shape[0] - ctx_ref.shape[1]
-    squares = square_ref[...] + square_sums(ctx_ref)
-    square_out[...] = squares
+    squares = square_sums(first_ref) + square_sums(last_ref)
+    square_ref[...] = squares
     for y in range(give_ref.shape[0]):
-        w = w_ref[start:, columns_of(y, other, give_ref.shape[2])]
-        fill(give_ref, y, sum_ref[y] + jnp.dot(ctx_ref[...], w, preferred_element_type=F32), squares)
+        fill(give_ref, y, product(first_ref, last_ref, w_ref, columns_of(y, other, give_ref.shape[2])), squares)
 
 
 def project_keep(first_ref, last_ref, w_ref, square_ref, keep_ref):
     core = lax.rem(lax.axis_index("tp"), 2)
-    cut = first_ref.shape[1]
     for y in range(keep_ref.shape[0]):
         at = columns_of(y, core, keep_ref.shape[2])
-        part = jnp.dot(first_ref[...], w_ref[:cut, at], preferred_element_type=F32)
-        part += jnp.dot(last_ref[...], w_ref[cut:, at], preferred_element_type=F32)
-        fill(keep_ref, y, part, square_ref[...])
+        fill(keep_ref, y, product(first_ref, last_ref, w_ref, at), square_ref[...])
 
 
 def larger(left_ref, right_ref, after, out_ref):
@@ -302,27 +319,53 @@
         (block_order, mark),
         [SCALARS, OUTSIDE],
         name="prepare",
-        micros=3,
+        micros=0.5,
     )
     w = call(
         weigh,
         shape((width, columns), BF16),
-        (kv_weight[0], norm_gain, moved[sources - 1]),
+        (kv_weight[0], norm_gain, features),
         [WHOLE, WHOLE, OUTSIDE],
         name="weigh",
         micros=1,
     )
     kv_local = kv_width // DH
-    turned = shape((kv_local, 2, DH + LANES, sources * rows), BF16)
-    kt, v_all, own = call(
-        arrange,
-        (turned, shape((kv_local, sources * rows, 2 * DH), BF16), turned),
-        (w, features, *reversed(triples)),
+    near = sorted({0, sources - 1})
+    far = list(reversed(range(1, sources - 1)))
+    peaks, after = [], w
+    for distances in [near, far] if far else [near]:
+        own = call(
+            functools.partial(arrange_own, distances),
+            shape((kv_local, 2, DH + LANES, len(distances) * rows), BF16),
+            (after, features, *[triples[d] for d in distances]),
+            [OUTSIDE] + [WHOLE] * (1 + len(distances)),
+            name="arrange_own",
+            micros=0.2,
+        )
+        peaks.append(
+            call(
+                maxima,
+                shape((1, heads), F32),
+                (queries, own, *peaks[-1:]),
+                limit=32,
+                name="maxima",
+                micros=0.5,
+            )
+        )
+        after = peaks[-1]
+    peak = peaks[-1]
+    distances = list(reversed(range(sources)))
+    kt, v_all = call(
+        functools.partial(arrange, distances),
+        (
+            shape((kv_local, 2, DH + LANES, sources * rows), BF16),
+            shape((kv_local, sources * rows, 2 * DH), BF16),
+        ),
+        (w, features, *[triples[d] for d in distances]),
         [OUTSIDE] + [WHOLE] * (1 + sources),
         name="arrange",
         micros=0.2,
     )
-    peak = call(maxima, shape((1, heads), F32), (queries, own), limit=32, name="maxima", micros=0.7)
     contexts, after = [], peak
     for start, count, part in zip(starts, counts, crossed):
         context = call(
@@ -335,15 +378,7 @@
             micros=count * 0.12,
         )
         contexts.append(context)
-        if start == 0:
-            total, squares = call(
-                project_first,
-                (shape((peers // 2, rows, out_cols), F32), shape((rows, LANES), F32)),
-                (context, w),
-                name="project_first",
-                micros=0.7,
-            )
-            after = squares
+        after = context
     for step in steps[:-1]:
         peak = call(
             larger,
@@ -356,8 +391,8 @@
     give, squares = call(
         project_give,
         (slab, shape((rows, LANES), F32)),
-        (contexts[-1], w, total, squares, peak),
-        [WHOLE] * 4 + [OUTSIDE],
+        (*contexts, w, peak),
+        [WHOLE] * 3 + [OUTSIDE],
         name="project_give",
         micros=0.4,
     )

time: 31.6 us -> 32 us (1.013)
  waiting for transfers between devices: 8.35 us -> 9.09 us
  starting transfers between devices: 14.9 us -> 14.4 us
    ppermute x5, waiting for transfers between devices: 6.05 us -> 6.79 us  [swapped(): lax.ppermute(block, axis, [(i, partner(i, step, size)) for i in range(siz...]
    ppermute x5, starting transfers between devices: 7.38 us -> 6.73 us  [swapped(): lax.ppermute(block, axis, [(i, partner(i, step, size)) for i in range(siz...]
    pallas_call x17 -> x19, Pallas kernels: 6.5 us -> 6.79 us  [call(): pl.pallas_call(kernel, out_shape=outs, in_specs=specs or [WHOLE] * len(ar...]
where the time goes in v8:
time: 32 us; the launch traced here: 31.8 us
  starting transfers between devices  14.4 us (45%)
  waiting for transfers between devices  9.09 us (28%)
  Pallas kernels  6.79 us (21%)
  between operations  0.79 us (2%)
  other arithmetic  0.78 us (2%)
    ppermute x5, waiting for transfers between devices, swapped(): lax.ppermute(block, axis, [(i, partner(i, step, size)) for i in range(siz...  6.79 us
    pallas_call x19, Pallas kernels, call(): pl.pallas_call(kernel, out_shape=outs, in_specs=specs or [WHOLE] * len(ar...  6.79 us
    ppermute x5, starting transfers between devices, swapped(): lax.ppermute(block, axis, [(i, partner(i, step, size)) for i in range(siz...  6.73 us
    ppermute x3, starting transfers between devices, shifted(): lax.ppermute(block, axis, [((i - distance) % size, i) for i in range(size)])  5.97 us
    ppermute x1, starting transfers between devices, on_device(): lax.ppermute(block, 'tp', [(i, (i + 2 * (step + 1)) % peers) for i in ran...  1.58 us
    ppermute x3, waiting for transfers between devices, shifted(): lax.ppermute(block, axis, [((i - distance) % size, i) for i in range(size)])  1.43 us
    ppermute x1, waiting for transfers between devices, on_device(): got = lax.ppermute(give, 'tp', [(i, i ^ 1) for i in range(peers)])  0.87 us
    concatenate x1, other arithmetic, on_device(): pair_here = jnp.concatenate([key_vectors[0], value_vectors[0]], axis=1)  0.78 us
  transfers between devices with their start and end apart: 10, of which 5 were waited for; matrix products, arithmetic and copies ran while one was open for 0% of the time, Pallas kernels for 17%

profile of v8, /device:TPU:0, one launch (start us, length us, event | category | flops | bytes accessed | tf_op | source)
XLA Modules:
  0.0 31.8 jit_solution(17864188810009032534)
XLA Ops:
  0.6 0.8 %pad_maximum_fusion.block_ref.here_ref = bf16[128,256]{1,0:T(8,128)(2,1)S(1)} fusion(bf16[128,128]{1,0:T(8,128)(2,1)} %bitcast.5, bf16[128,128]{1,0:T(8,128)(2,1)} %bitcast.6), kind=kLoop, calls=%fused_computation | loop fusion | flops 131072 | bytes 131072 | tf_op jit(solution)/shard_map/concatenate | solution.py:292
  1.4 3.0 %collective-permute-start = (bf16[128,256]{1,0:T(8,128)(2,1)S(1)}, bf16[128,256]{1,0:T(8,128)(2,1)S(1)}, u32[]{:S(2)}, u32[]{:S(2)}) collective-permute-start(bf16[128,256]{1,0:T(8,128)(2,1)S(1)} %pad_maximum_fusion.block_ref.here_ref), channel_id=1, source_target_pairs={{16,0},{0,16},{17,1},{1,17},{18,2},{2,18},{19,3},{3,19},{20,4},{4,... | collective-permute-start | bytes 196616 | tf_op jit(solution)/shard_map/ppermute | solution.py:48
  4.5 1.0 %collective-permute-start.6 = (bf16[128,1024]{1,0:T(8,128)(2,1)S(1)}, bf16[128,1024]{1,0:T(8,128)(2,1)S(1)}, u32[]{:S(2)}, u32[]{:S(2)}) collective-permute-start(bf16[128,1024]{1,0:T(8,128)(2,1)S(1)} %take.3), channel_id=1, source_target_pairs={{16,0},{0,16},{17,1},{1,17},{18,2},{2,18},{19,3},{3,19},{20,4},{4,... | collective-permute-start | bytes 786440 | tf_op jit(solution)/shard_map/ppermute | solution.py:48
  5.5 1.4 %collective-permute-done.pair_ref = bf16[128,256]{1,0:T(8,128)(2,1)S(1)} collective-permute-done((bf16[128,256]{1,0:T(8,128)(2,1)S(1)}, bf16[128,256]{1,0:T(8,128)(2,1)S(1)}, u32[]{:S(2)}, u32[]{:S(2)}) %collective-permute-start) | collective-permute-done | bytes 65568 | tf_op jit(solution)/shard_map/ppermute | solution.py:48
  6.9 4.5 %collective-permute-start.1 = (bf16[128,384]{1,0:T(8,128)(2,1)S(1)}, bf16[128,384]{1,0:T(8,128)(2,1)S(1)}, u32[]{:S(2)}, u32[]{:S(2)}) collective-permute-start(bf16[128,384]{1,0:T(8,128)(2,1)S(1)} %join.1.refs_0_.after.refs_3_), channel_id=1, source_target_pairs={{0,12},{4,8},{8,4},{12,0},{1,13},{5,9},{9,5},{13,1},{2,14},{6,10},... | collective-permute-start | bytes 294920 | tf_op jit(solution)/shard_map/ppermute | solution.py:43
  11.4 0.6 %prepare.1.after.feature_ref = bf16[2,128,512]{2,1,0:T(8,128)(2,1)S(1)} custom-call(s32[8]{0:T(128)S(1)} %copy-done.3, f32[8,128]{1,0:T(8,128)S(1)} %touch.1.after), custom_call_target="tpu_custom_call" | custom-call | flops 500000000 | tf_op jit(solution)/shard_map/prepare/pallas_call | solution.py:24
  12.1 0.6 %collective-permute-start.3 = (bf16[128,384]{1,0:T(8,128)(2,1)S(1)}, bf16[128,384]{1,0:T(8,128)(2,1)S(1)}, u32[]{:S(2)}, u32[]{:S(2)}) collective-permute-start(bf16[128,384]{1,0:T(8,128)(2,1)S(1)} %join.1.refs_0_.after.refs_3_), channel_id=1, source_target_pairs={{0,4},{4,0},{8,12},{12,8},{1,5},{5,1},{9,13},{13,9},{2,6},{6,2},{1... | collective-permute-start | bytes 294920 | tf_op jit(solution)/shard_map/ppermute | solution.py:43
  12.7 2.0 %collective-permute-start.5 = (bf16[128,1024]{1,0:T(8,128)(2,1)S(1)}, bf16[128,1024]{1,0:T(8,128)(2,1)S(1)}, u32[]{:S(2)}, u32[]{:S(2)}) collective-permute-start(bf16[128,1024]{1,0:T(8,128)(2,1)S(1)} %take.2), channel_id=1, source_target_pairs={{16,0},{0,16},{17,1},{1,17},{18,2},{2,18},{19,3},{3,19},{20,4},{4,... | collective-permute-start | bytes 786440 | tf_op jit(solution)/shard_map/ppermute | solution.py:48
  14.6 0.9 %weigh.1.after.w_ref = bf16[2048,1024]{1,0:T(8,128)(2,1)S(1)} custom-call(bf16[2048,1024]{1,0:T(8,128)(2,1)S(1)} %bitcast.4, bf16[1,2048]{1,0:T(2,128)(2,1)S(1)} %copy-done.2, bf16[2,128,512]{2,1,0:T(8,128)(2,1)S(1)} %prepare.1.after.feature_ref), custom_call_target="tpu_custom_call" | custom-call | flops 1000000000 | tf_op jit(solution)/shard_map/weigh/pallas_call | solution.py:24
  15.5 0.1 arrange_own.2.own_ref
  15.7 0.5 %maxima.2.after.refs_0_ = f32[1,16]{1,0:T(1,128)S(1)} custom-call(bf16[1,128,2048]{2,1,0:T(8,128)(2,1)S(1)} %copy-done.1, bf16[1,2,256,256]{3,2,1,0:T(8,128)(2,1)S(1)} %arrange_own.2.own_ref), custom_call_target="tpu_custom_call" | custom-call | flops 500000000 | tf_op jit(solution)/shard_map/maxima/pallas_call | solution.py:24
  16.2 2.5 %collective-permute-done.2.refs_0_.refs_1_ = bf16[128,384]{1,0:T(8,128)(2,1)S(1)} collective-permute-done((bf16[128,384]{1,0:T(8,128)(2,1)S(1)}, bf16[128,384]{1,0:T(8,128)(2,1)S(1)}, u32[]{:S(2)}, u32[]{:S(2)}) %collective-permute-start.2) | collective-permute-done | bytes 98336 | tf_op jit(solution)/shard_map/ppermute | solution.py:43
  18.8 0.5 %maxima.3.after.left_ref = f32[1,16]{1,0:T(1,128)S(1)} custom-call(bf16[1,128,2048]{2,1,0:T(8,128)(2,1)S(1)} %copy-done.1, bf16[1,2,256,256]{3,2,1,0:T(8,128)(2,1)S(1)} %arrange_own.3.own_ref, f32[1,16]{1,0:T(1,128)S(1)} %maxima.2.after.refs_0_), custom_call_target="tpu_custom_call" | custom-call | flops 500000000 | tf_op jit(solution)/shard_map/maxima/pallas_call | solution.py:24
  19.3 0.1 arrange.1
  19.5 1.0 %attend.2.after.first_ref = bf16[128,1024]{1,0:T(8,128)(2,1)S(1)} custom-call(bf16[128,1024]{1,0:T(8,128)(2,1)S(1)} %collective-permute-done.6.q_ref, bf16[1,2,256,512]{3,2,1,0:T(8,128)(2,1)S(1)} %get-tuple-element.10.kt_ref, bf16[1,512,256]{2,1,0:T(8,128)(2,1)S(1)} %get-tuple-element.11.v_ref, f32[1,16]{1,0:T(1,128)S(1)} %maxima.3.after.left_ref), custom_call_target="tpu_custom_call" | custom-call | flops 960000000 | tf_op jit(solution)/shard_map/attend/pallas_call | solution.py:24
  20.5 1.0 %attend.3.after.last_ref = bf16[128,1024]{1,0:T(8,128)(2,1)S(1)} custom-call(bf16[128,1024]{1,0:T(8,128)(2,1)S(1)} %collective-permute-done.5.q_ref, bf16[1,2,256,512]{3,2,1,0:T(8,128)(2,1)S(1)} %get-tuple-element.10.kt_ref, bf16[1,512,256]{2,1,0:T(8,128)(2,1)S(1)} %get-tuple-element.11.v_ref, bf16[128,1024]{1,0:T(8,128)(2,1)S(1)} %attend.2.after.first_ref), custom_call_target="tpu_custom_call" | custom-call | flops 960000000 | tf_op jit(solution)/shard_map/attend/pallas_call | solution.py:24
  21.4 1.4 %collective-permute-done.4.right_ref = f32[1,16]{1,0:T(1,128)S(1)} collective-permute-done((f32[1,16]{1,0:T(1,128)S(1)}, f32[1,16]{1,0:T(1,128)S(1)}, u32[]{:S(2)}, u32[]{:S(2)}) %collective-permute-start.4) | collective-permute-done | bytes 96 | tf_op jit(solution)/shard_map/ppermute | solution.py:43
  22.9 0.6 %project_give.1 = (bf16[2,144,256]{2,1,0:T(8,128)(2,1)S(1)}, f32[128,128]{1,0:T(8,128)S(1)}) custom-call(bf16[128,1024]{1,0:T(8,128)(2,1)S(1)} %attend.2.after.first_ref, bf16[128,1024]{1,0:T(8,128)(2,1)S(1)} %attend.3.after.last_ref, bf16[2048,1024]{1,0:T(8,128)(2,1)S(1)} %weigh.1.after.w_ref, f32[1,16]{1,0:T(1,128)S(1)} %larger.1.after.block_ref), custom_call_target="tpu_custom_call" | custom-call | flops 400000000 | tf_op jit(solution)/shard_map/project_give/pallas_call | solution.py:24
  23.6 0.5 %project_keep.1.keep_ref = bf16[2,144,256]{2,1,0:T(8,128)(2,1)S(1)} custom-call(bf16[128,1024]{1,0:T(8,128)(2,1)S(1)} %attend.2.after.first_ref, bf16[128,1024]{1,0:T(8,128)(2,1)S(1)} %attend.3.after.last_ref, bf16[2048,1024]{1,0:T(8,128)(2,1)S(1)} %weigh.1.after.w_ref, f32[128,128]{1,0:T(8,128)S(1)} %get-tuple-element.13.square_ref), custom_call_target="tpu_custom_call" | custom-call | flops 600000000 | tf_op jit(solution)/shard_map/project_keep/pallas_call | solution.py:24
  24.1 0.9 %collective-permute-done.8.got_ref = bf16[2,144,256]{2,1,0:T(8,128)(2,1)S(1)} collective-permute-done((bf16[2,144,256]{2,1,0:T(8,128)(2,1)S(1)}, bf16[2,144,256]{2,1,0:T(8,128)(2,1)S(1)}, u32[]{:S(2)}, u32[]{:S(2)}) %collective-permute-start.8) | collective-permute-done | bytes 147488 | tf_op jit(solution)/shard_map/ppermute | solution.py:400
  25.0 1.6 %collective-permute-start.9 = (bf16[144,256]{1,0:T(8,128)(2,1)S(1)}, bf16[144,256]{1,0:T(8,128)(2,1)S(1)}, u32[]{:S(2)}, u32[]{:S(2)}) collective-permute-start(bf16[144,256]{1,0:T(8,128)(2,1)S(1)} %get-tuple-element.15), channel_id=1, source_target_pairs={{0,2},{1,3},{2,0},{3,1},{4,6},{5,7},{6,4},{7,5},{8,10},{9,11},{10,... | collective-permute-start | bytes 221192 | tf_op jit(solution)/shard_map/ppermute | solution.py:407
  26.6 1.6 %collective-permute-start.7 = (f32[1,16]{1,0:T(1,128)S(1)}, f32[1,16]{1,0:T(1,128)S(1)}, u32[]{:S(2)}, u32[]{:S(2)}) collective-permute-start(f32[1,16]{1,0:T(1,128)S(1)} %bind.1.peak_ref), channel_id=1, source_target_pairs={{0,8},{4,12},{8,0},{12,4},{1,9},{5,13},{9,1},{13,5},{2,10},{6,14},... | collective-permute-start | bytes 200 | tf_op jit(solution)/shard_map/ppermute | solution.py:43
  28.2 2.8 %collective-permute-done.7.peak_got = f32[1,16]{1,0:T(1,128)S(1)} collective-permute-done((f32[1,16]{1,0:T(1,128)S(1)}, f32[1,16]{1,0:T(1,128)S(1)}, u32[]{:S(2)}, u32[]{:S(2)}) %collective-permute-start.7) | collective-permute-done | bytes 96 | tf_op jit(solution)/shard_map/ppermute | solution.py:43
  31.0 0.8 %finish.1 = (f32[1,16]{1,0:T(1,128)}, bf16[128,256]{1,0:T(8,128)(2,1)}) custom-call(f32[1,16]{1,0:T(1,128)S(1)} %bind.1.peak_ref, f32[1,16]{1,0:T(1,128)S(1)} %collective-permute-done.7.peak_got, f32[144,256]{1,0:T(8,128)S(1)} %get-tuple-element.14.keep_ref, bf16[144,256]{1,0:T(8,128)(2,1)S(1)} %collective-permute-done.9.refs_0_), custom_call_target="tpu_custom_call" | custom-call | tf_op jit(solution)/shard_map/finish/pallas_call | solution.py:24
  (24 shorter events, 0.4 us)
Async XLA Ops:
  1.4 3.0 %copy-start.1 = (bf16[1,128,2048]{2,1,0:T(8,128)(2,1)S(1)}, bf16[1,128,2048]{2,1,0:T(8,128)(2,1)}, u32[]{:S(2)}) copy-start(bf16[1,128,2048]{2,1,0:T(8,128)(2,1)} %q_ref.7) | copy-start | bytes 1572868
  1.4 5.5 %collective-permute-start = (bf16[128,256]{1,0:T(8,128)(2,1)S(1)}, bf16[128,256]{1,0:T(8,128)(2,1)S(1)}, u32[]{:S(2)}, u32[]{:S(2)}) collective-permute-start(bf16[128,256]{1,0:T(8,128)(2,1)S(1)} %pad_maximum_fusion.block_ref.here_ref), channel_id=1, source_target_pairs={{16,0},{0,16},{17,1},{1,17},{18,2},{2,18},{19,3},{3,19},{20,4},{4,... | collective-permute-start | bytes 196616 | tf_op jit(solution)/shard_map/ppermute | solution.py:48
  4.4 7.0 %copy-start.3 = (s32[8]{0:T(128)S(1)}, s32[8]{0:T(128)}, u32[]{:S(2)}) copy-start(s32[8]{0:T(128)} %order_ref.1) | copy-start | bytes 100
  4.4 10.2 %copy-start = (bf16[1,2048,1024]{2,1,0:T(8,128)(2,1)S(1)}, bf16[1,2048,1024]{2,1,0:T(8,128)(2,1)}, u32[]{:S(2)}) copy-start(bf16[1,2048,1024]{2,1,0:T(8,128)(2,1)} %param.11) | copy-start | bytes 12582916
  4.4 10.2 %copy-start.2 = (bf16[1,2048]{1,0:T(2,128)(2,1)S(1)}, bf16[1,2048]{1,0:T(2,128)(2,1)}, u32[]{:S(2)}) copy-start(bf16[1,2048]{1,0:T(2,128)(2,1)} %gain_ref.1) | copy-start | bytes 12292
  4.5 15.0 %collective-permute-start.6 = (bf16[128,1024]{1,0:T(8,128)(2,1)S(1)}, bf16[128,1024]{1,0:T(8,128)(2,1)S(1)}, u32[]{:S(2)}, u32[]{:S(2)}) collective-permute-start(bf16[128,1024]{1,0:T(8,128)(2,1)S(1)} %take.3), channel_id=1, source_target_pairs={{16,0},{0,16},{17,1},{1,17},{18,2},{2,18},{19,3},{3,19},{20,4},{4,... | collective-permute-start | bytes 786440 | tf_op jit(solution)/shard_map/ppermute | solution.py:48
  6.9 8.6 %collective-permute-start.1 = (bf16[128,384]{1,0:T(8,128)(2,1)S(1)}, bf16[128,384]{1,0:T(8,128)(2,1)S(1)}, u32[]{:S(2)}, u32[]{:S(2)}) collective-permute-start(bf16[128,384]{1,0:T(8,128)(2,1)S(1)} %join.1.refs_0_.after.refs_3_), channel_id=1, source_target_pairs={{0,12},{4,8},{8,4},{12,0},{1,13},{5,9},{9,5},{13,1},{2,14},{6,10},... | collective-permute-start | bytes 294920 | tf_op jit(solution)/shard_map/ppermute | solution.py:43
  12.0 6.7 %collective-permute-start.2 = (bf16[128,384]{1,0:T(8,128)(2,1)S(1)}, bf16[128,384]{1,0:T(8,128)(2,1)S(1)}, u32[]{:S(2)}, u32[]{:S(2)}) collective-permute-start(bf16[128,384]{1,0:T(8,128)(2,1)S(1)} %join.1.refs_0_.after.refs_3_), channel_id=1, source_target_pairs={{0,8},{4,12},{8,0},{12,4},{1,9},{5,13},{9,1},{13,5},{2,10},{6,14},... | collective-permute-start | bytes 294920 | tf_op jit(solution)/shard_map/ppermute | solution.py:43
  12.1 6.6 %collective-permute-start.3 = (bf16[128,384]{1,0:T(8,128)(2,1)S(1)}, bf16[128,384]{1,0:T(8,128)(2,1)S(1)}, u32[]{:S(2)}, u32[]{:S(2)}) collective-permute-start(bf16[128,384]{1,0:T(8,128)(2,1)S(1)} %join.1.refs_0_.after.refs_3_), channel_id=1, source_target_pairs={{0,4},{4,0},{8,12},{12,8},{1,5},{5,1},{9,13},{13,9},{2,6},{6,2},{1... | collective-permute-start | bytes 294920 | tf_op jit(solution)/shard_map/ppermute | solution.py:43
  12.7 7.8 %collective-permute-start.5 = (bf16[128,1024]{1,0:T(8,128)(2,1)S(1)}, bf16[128,1024]{1,0:T(8,128)(2,1)S(1)}, u32[]{:S(2)}, u32[]{:S(2)}) collective-permute-start(bf16[128,1024]{1,0:T(8,128)(2,1)S(1)} %take.2), channel_id=1, source_target_pairs={{16,0},{0,16},{17,1},{1,17},{18,2},{2,18},{19,3},{3,19},{20,4},{4,... | collective-permute-start | bytes 786440 | tf_op jit(solution)/shard_map/ppermute | solution.py:48
  19.3 3.6 %collective-permute-start.4 = (f32[1,16]{1,0:T(1,128)S(1)}, f32[1,16]{1,0:T(1,128)S(1)}, u32[]{:S(2)}, u32[]{:S(2)}) collective-permute-start(f32[1,16]{1,0:T(1,128)S(1)} %maxima.3.after.left_ref), channel_id=1, source_target_pairs={{0,4},{4,0},{8,12},{12,8},{1,5},{5,1},{9,13},{13,9},{2,6},{6,2},{1... | collective-permute-start | bytes 200 | tf_op jit(solution)/shard_map/ppermute | solution.py:43
  23.5 1.4 %collective-permute-start.8 = (bf16[2,144,256]{2,1,0:T(8,128)(2,1)S(1)}, bf16[2,144,256]{2,1,0:T(8,128)(2,1)S(1)}, u32[]{:S(2)}, u32[]{:S(2)}) collective-permute-start(bf16[2,144,256]{2,1,0:T(8,128)(2,1)S(1)} %get-tuple-element.12.after), channel_id=1, source_target_pairs={{0,1},{1,0},{2,3},{3,2},{4,5},{5,4},{6,7},{7,6},{8,9},{9,8},{10,11... | collective-permute-start | bytes 442376 | tf_op jit(solution)/shard_map/ppermute | solution.py:400
  25.0 6.0 %collective-permute-start.9 = (bf16[144,256]{1,0:T(8,128)(2,1)S(1)}, bf16[144,256]{1,0:T(8,128)(2,1)S(1)}, u32[]{:S(2)}, u32[]{:S(2)}) collective-permute-start(bf16[144,256]{1,0:T(8,128)(2,1)S(1)} %get-tuple-element.15), channel_id=1, source_target_pairs={{0,2},{1,3},{2,0},{3,1},{4,6},{5,7},{6,4},{7,5},{8,10},{9,11},{10,... | collective-permute-start | bytes 221192 | tf_op jit(solution)/shard_map/ppermute | solution.py:407
  26.6 4.4 %collective-permute-start.7 = (f32[1,16]{1,0:T(1,128)S(1)}, f32[1,16]{1,0:T(1,128)S(1)}, u32[]{:S(2)}, u32[]{:S(2)}) collective-permute-start(f32[1,16]{1,0:T(1,128)S(1)} %bind.1.peak_ref), channel_id=1, source_target_pairs={{0,8},{4,12},{8,0},{12,4},{1,9},{5,13},{9,1},{13,5},{2,10},{6,14},... | collective-permute-start | bytes 200 | tf_op jit(solution)/shard_map/ppermute | solution.py:43

commit v9 on v7

--- a/solution.py
+++ b/solution.py
@@ -207,35 +207,28 @@
         ref[y, rows:, 2 * rows:] = jnp.zeros((SQUARE_ROWS, cols - 2 * rows), BF16)
 
 
-def project_first(ctx_ref, w_ref, sum_ref, square_ref):
+def product(first_ref, last_ref, w_ref, at):
+    cut = first_ref.shape[1]
+    part = jnp.dot(first_ref[...], w_ref[:cut, at], preferred_element_type=F32)
+    return part + jnp.dot(last_ref[...], w_ref[cut:, at], preferred_element_type=F32)
+
+
+def project_give(first_ref, last_ref, w_ref, give_ref, square_ref):
     other = 1 - lax.rem(lax.axis_index("tp"), 2)
-    square_ref[...] = square_sums(ctx_ref)
-    for y in range(sum_ref.shape[0]):
-        w = w_ref[:ctx_ref.shape[1], columns_of(y, other, sum_ref.shape[2])]
-        sum_ref[y] = jnp.dot(ctx_ref[...], w, preferred_element_type=F32)
-
-
-def project_give(ctx_ref, w_ref, sum_ref, square_ref, after, give_ref, square_out):
-    other = 1 - lax.rem(lax.axis_index("tp"), 2)
-    start = w_ref.shape[0] - ctx_ref.shape[1]
-    squares = square_ref[...] + square_sums(ctx_ref)
-    square_out[...] = squares
+    squares = square_sums(first_ref) + square_sums(last_ref)
+    square_ref[...] = squares
     for y in range(give_ref.shape[0]):
-        w = w_ref[start:, columns_of(y, other, give_ref.shape[2])]
-        fill(give_ref, y, sum_ref[y] + jnp.dot(ctx_ref[...], w, preferred_element_type=F32), squares)
+        fill(give_ref, y, product(first_ref, last_ref, w_ref, columns_of(y, other, give_ref.shape[2])), squares)
 
 
 def project_keep(first_ref, last_ref, w_ref, square_ref, keep_ref):
     core = lax.rem(lax.axis_index("tp"), 2)
-    cut = first_ref.shape[1]
     for y in range(keep_ref.shape[0]):
         at = columns_of(y, core, keep_ref.shape[2])
-        part = jnp.dot(first_ref[...], w_ref[:cut, at], preferred_element_type=F32)
-        part += jnp.dot(last_ref[...], w_ref[cut:, at], preferred_element_type=F32)
-        fill(keep_ref, y, part, square_ref[...])
-
-
-def larger(left_ref, right_ref, after, out_ref):
+        fill(keep_ref, y, product(first_ref, last_ref, w_ref, at), square_ref[...])
+
+
+def larger(left_ref, right_ref, out_ref):
     out_ref[...] = jnp.maximum(left_ref[...], right_ref[...])
 
 
@@ -335,35 +328,26 @@
             micros=count * 0.12,
         )
         contexts.append(context)
-        if start == 0:
-            total, squares = call(
-                project_first,
-                (shape((peers // 2, rows, out_cols), F32), shape((rows, LANES), F32)),
-                (context, w),
-                name="project_first",
-                micros=0.7,
-            )
-            after = squares
-    for step in steps[:-1]:
-        peak = call(
-            larger,
-            shape((1, heads), F32),
-            (peak, swapped(peak, "cp", step), contexts[-1]),
-            [WHOLE, WHOLE, OUTSIDE],
-            name="larger",
-        )
+        after = context
     slab = shape((peers // 2, rows + SQUARE_ROWS, out_cols), BF16)
     give, squares = call(
         project_give,
         (slab, shape((rows, LANES), F32)),
-        (contexts[-1], w, total, squares, peak),
-        [WHOLE] * 4 + [OUTSIDE],
+        (*contexts, w),
         name="project_give",
         micros=0.4,
     )
     keep = call(project_keep, slab, (*contexts, w, squares), name="project_keep", micros=0.6)
     got = lax.ppermute(give, "tp", [(i, i ^ 1) for i in range(peers)])
     peak = bind(peak, give)
+    for step in reversed(steps[1:]):
+        peak = call(
+            larger,
+            shape((1, heads), F32),
+            (peak, swapped(peak, "cp", step)),
+            name="larger",
+            micros=5,
+        )
     slab = (rows + SQUARE_ROWS, out_cols)
     mine, *others = call(
         merge, [shape(slab, F32)] + [shape(slab, BF16)] * (peers // 2 - 1), (keep, got), name="merge"
@@ -375,7 +359,7 @@
     max_logits, kv_next = call(
         functools.partial(finish, width * peers),
         (shape((1, heads), F32), shape((rows, out_cols), BF16)),
-        (peak, swapped(peak, "cp", steps[-1]), mine, *others),
+        (peak, swapped(peak, "cp", steps[0]), mine, *others),
         name="finish",
     )
     return (max_logits, kv_next[None])

time: 31.6 us -> 30.7 us (0.972)
  waiting for transfers between devices: 8.35 us -> 7.34 us
  starting transfers between devices: 14.9 us -> 15.3 us
    ppermute x1, waiting for transfers between devices: 0.87 us -> 0.01 us  [on_device(): got = lax.ppermute(give, 'tp', [(i, i ^ 1) for i in range(peers)])]
    ppermute x5, starting transfers between devices: 7.38 us -> 7.75 us  [swapped(): lax.ppermute(block, axis, [(i, partner(i, step, size)) for i in range(siz...]
    pallas_call x17 -> x16, Pallas kernels: 6.5 us -> 6.33 us  [call(): pl.pallas_call(kernel, out_shape=outs, in_specs=specs or [WHOLE] * len(ar...]
  transfers between devices with their start and end apart: 10 -> 10, of which waited for: 5 -> 4; matrix products, arithmetic and copies ran while one was open for 0% -> 0% of each run, Pallas kernels for 17% -> 13%
where the time goes in v9:
time: 30.7 us; the launch traced here: 30.6 us
  starting transfers between devices  15.3 us (50%)
  waiting for transfers between devices  7.34 us (24%)
  Pallas kernels  6.33 us (21%)
  other arithmetic  0.78 us (3%)
  between operations  0.77 us (3%)
    ppermute x5, starting transfers between devices, swapped(): lax.ppermute(block, axis, [(i, partner(i, step, size)) for i in range(siz...  7.75 us
    pallas_call x16, Pallas kernels, call(): pl.pallas_call(kernel, out_shape=outs, in_specs=specs or [WHOLE] * len(ar...  6.33 us
    ppermute x3, starting transfers between devices, shifted(): lax.ppermute(block, axis, [((i - distance) % size, i) for i in range(size)])  5.9 us
    ppermute x5, waiting for transfers between devices, swapped(): lax.ppermute(block, axis, [(i, partner(i, step, size)) for i in range(siz...  5.9 us
    ppermute x1, starting transfers between devices, on_device(): lax.ppermute(block, 'tp', [(i, (i + 2 * (step + 1)) % peers) for i in ran...  1.58 us
    ppermute x3, waiting for transfers between devices, shifted(): lax.ppermute(block, axis, [((i - distance) % size, i) for i in range(size)])  1.43 us
    concatenate x1, other arithmetic, on_device(): pair_here = jnp.concatenate([key_vectors[0], value_vectors[0]], axis=1)  0.78 us
  transfers between devices with their start and end apart: 10, of which 4 were waited for; matrix products, arithmetic and copies ran while one was open for 0% of the time, Pallas kernels for 13%

profile of v9, /device:TPU:0, one launch (start us, length us, event | category | flops | bytes accessed | tf_op | source)
XLA Modules:
  0.0 30.6 jit_solution(758193562126939067)
XLA Ops:
  0.6 0.8 %pad_maximum_fusion.here_ref.block_ref = bf16[128,256]{1,0:T(8,128)(2,1)S(1)} fusion(bf16[128,128]{1,0:T(8,128)(2,1)} %bitcast.5, bf16[128,128]{1,0:T(8,128)(2,1)} %bitcast.6), kind=kLoop, calls=%fused_computation | loop fusion | flops 131072 | bytes 131072 | tf_op jit(solution)/shard_map/concatenate | solution.py:268
  1.4 3.0 %collective-permute-start = (bf16[128,256]{1,0:T(8,128)(2,1)S(1)}, bf16[128,256]{1,0:T(8,128)(2,1)S(1)}, u32[]{:S(2)}, u32[]{:S(2)}) collective-permute-start(bf16[128,256]{1,0:T(8,128)(2,1)S(1)} %pad_maximum_fusion.here_ref.block_ref), channel_id=1, source_target_pairs={{16,0},{0,16},{17,1},{1,17},{18,2},{2,18},{19,3},{3,19},{20,4},{4,... | collective-permute-start | bytes 196616 | tf_op jit(solution)/shard_map/ppermute | solution.py:48
  4.5 1.0 %collective-permute-start.4 = (bf16[128,1024]{1,0:T(8,128)(2,1)S(1)}, bf16[128,1024]{1,0:T(8,128)(2,1)S(1)}, u32[]{:S(2)}, u32[]{:S(2)}) collective-permute-start(bf16[128,1024]{1,0:T(8,128)(2,1)S(1)} %take.2), channel_id=1, source_target_pairs={{16,0},{0,16},{17,1},{1,17},{18,2},{2,18},{19,3},{3,19},{20,4},{4,... | collective-permute-start | bytes 786440 | tf_op jit(solution)/shard_map/ppermute | solution.py:48
  5.5 1.4 %collective-permute-done.pair_ref = bf16[128,256]{1,0:T(8,128)(2,1)S(1)} collective-permute-done((bf16[128,256]{1,0:T(8,128)(2,1)S(1)}, bf16[128,256]{1,0:T(8,128)(2,1)S(1)}, u32[]{:S(2)}, u32[]{:S(2)}) %collective-permute-start) | collective-permute-done | bytes 65568 | tf_op jit(solution)/shard_map/ppermute | solution.py:48
  7.0 4.5 %collective-permute-start.1 = (bf16[128,384]{1,0:T(8,128)(2,1)S(1)}, bf16[128,384]{1,0:T(8,128)(2,1)S(1)}, u32[]{:S(2)}, u32[]{:S(2)}) collective-permute-start(bf16[128,384]{1,0:T(8,128)(2,1)S(1)} %join.1.refs_3_.after), channel_id=1, source_target_pairs={{0,12},{4,8},{8,4},{12,0},{1,13},{5,9},{9,5},{13,1},{2,14},{6,10},... | collective-permute-start | bytes 294920 | tf_op jit(solution)/shard_map/ppermute | solution.py:43
  11.4 0.6 %collective-permute-start.3 = (bf16[128,384]{1,0:T(8,128)(2,1)S(1)}, bf16[128,384]{1,0:T(8,128)(2,1)S(1)}, u32[]{:S(2)}, u32[]{:S(2)}) collective-permute-start(bf16[128,384]{1,0:T(8,128)(2,1)S(1)} %join.1.refs_3_.after), channel_id=1, source_target_pairs={{0,4},{4,0},{8,12},{12,8},{1,5},{5,1},{9,13},{13,9},{2,6},{6,2},{1... | collective-permute-start | bytes 294920 | tf_op jit(solution)/shard_map/ppermute | solution.py:43
  12.1 0.6 %prepare.1.feature_ref = bf16[2,128,512]{2,1,0:T(8,128)(2,1)S(1)} custom-call(s32[8]{0:T(128)S(1)} %copy-done.3, f32[8,128]{1,0:T(8,128)S(1)} %touch.1.after), custom_call_target="tpu_custom_call" | custom-call | flops 3000000000 | tf_op jit(solution)/shard_map/prepare/pallas_call | solution.py:24
  12.7 1.9 %collective-permute-start.5 = (bf16[128,1024]{1,0:T(8,128)(2,1)S(1)}, bf16[128,1024]{1,0:T(8,128)(2,1)S(1)}, u32[]{:S(2)}, u32[]{:S(2)}) collective-permute-start(bf16[128,1024]{1,0:T(8,128)(2,1)S(1)} %take.3), channel_id=1, source_target_pairs={{16,0},{0,16},{17,1},{1,17},{18,2},{2,18},{19,3},{3,19},{20,4},{4,... | collective-permute-start | bytes 786440 | tf_op jit(solution)/shard_map/ppermute | solution.py:48
  14.6 0.9 %weigh.1.after.w_ref = bf16[2048,1024]{1,0:T(8,128)(2,1)S(1)} custom-call(bf16[2048,1024]{1,0:T(8,128)(2,1)S(1)} %bitcast.4, bf16[1,2048]{1,0:T(2,128)(2,1)S(1)} %copy-done.2, bf16[128,384]{1,0:T(8,128)(2,1)S(1)} %collective-permute-done.1.after.refs_0_), custom_call_target="tpu_custom_call" | custom-call | flops 1000000000 | tf_op jit(solution)/shard_map/weigh/pallas_call | solution.py:24
  15.5 2.6 %collective-permute-done.2.refs_1_ = bf16[128,384]{1,0:T(8,128)(2,1)S(1)} collective-permute-done((bf16[128,384]{1,0:T(8,128)(2,1)S(1)}, bf16[128,384]{1,0:T(8,128)(2,1)S(1)}, u32[]{:S(2)}, u32[]{:S(2)}) %collective-permute-start.2) | collective-permute-done | bytes 98336 | tf_op jit(solution)/shard_map/ppermute | solution.py:43
  18.1 0.2 arrange.1
  18.3 0.8 %maxima.1.after.block_ref = f32[1,16]{1,0:T(1,128)S(1)} custom-call(bf16[1,128,2048]{2,1,0:T(8,128)(2,1)S(1)} %copy-done.1, bf16[1,2,256,512]{3,2,1,0:T(8,128)(2,1)S(1)} %get-tuple-element.11.own_ref), custom_call_target="tpu_custom_call" | custom-call | flops 700000000 | tf_op jit(solution)/shard_map/maxima/pallas_call | solution.py:24
  19.1 0.9 %attend.2.after.first_ref = bf16[128,1024]{1,0:T(8,128)(2,1)S(1)} custom-call(bf16[128,1024]{1,0:T(8,128)(2,1)S(1)} %collective-permute-done.4.q_ref, bf16[1,2,256,512]{3,2,1,0:T(8,128)(2,1)S(1)} %get-tuple-element.12.kt_ref, bf16[1,512,256]{2,1,0:T(8,128)(2,1)S(1)} %get-tuple-element.13.v_ref, f32[1,16]{1,0:T(1,128)S(1)} %maxima.1.after.block_ref), custom_call_target="tpu_custom_call" | custom-call | flops 960000000 | tf_op jit(solution)/shard_map/attend/pallas_call | solution.py:24
  20.0 0.9 %attend.3.last_ref = bf16[128,1024]{1,0:T(8,128)(2,1)S(1)} custom-call(bf16[128,1024]{1,0:T(8,128)(2,1)S(1)} %collective-permute-done.5.q_ref, bf16[1,2,256,512]{3,2,1,0:T(8,128)(2,1)S(1)} %get-tuple-element.12.kt_ref, bf16[1,512,256]{2,1,0:T(8,128)(2,1)S(1)} %get-tuple-element.13.v_ref, bf16[128,1024]{1,0:T(8,128)(2,1)S(1)} %attend.2.after.first_ref), custom_call_target="tpu_custom_call" | custom-call | flops 960000000 | tf_op jit(solution)/shard_map/attend/pallas_call | solution.py:24
  21.0 0.6 %project_give.1 = (bf16[2,144,256]{2,1,0:T(8,128)(2,1)S(1)}, f32[128,128]{1,0:T(8,128)S(1)}) custom-call(bf16[128,1024]{1,0:T(8,128)(2,1)S(1)} %attend.2.after.first_ref, bf16[128,1024]{1,0:T(8,128)(2,1)S(1)} %attend.3.last_ref, bf16[2048,1024]{1,0:T(8,128)(2,1)S(1)} %weigh.1.after.w_ref), custom_call_target="tpu_custom_call" | custom-call | flops 400000000 | tf_op jit(solution)/shard_map/project_give/pallas_call | solution.py:24
  21.6 0.1 collective-permute-start.8
  21.7 1.5 %collective-permute-start.6 = (f32[1,16]{1,0:T(1,128)S(1)}, f32[1,16]{1,0:T(1,128)S(1)}, u32[]{:S(2)}, u32[]{:S(2)}) collective-permute-start(f32[1,16]{1,0:T(1,128)S(1)} %bind.1.left_ref), channel_id=1, source_target_pairs={{0,8},{4,12},{8,0},{12,4},{1,9},{5,13},{9,1},{13,5},{2,10},{6,14},... | collective-permute-start | bytes 200 | tf_op jit(solution)/shard_map/ppermute | solution.py:43
  23.2 0.5 %project_keep.1.keep_ref = bf16[2,144,256]{2,1,0:T(8,128)(2,1)S(1)} custom-call(bf16[128,1024]{1,0:T(8,128)(2,1)S(1)} %attend.2.after.first_ref, bf16[128,1024]{1,0:T(8,128)(2,1)S(1)} %attend.3.last_ref, bf16[2048,1024]{1,0:T(8,128)(2,1)S(1)} %weigh.1.after.w_ref, f32[128,128]{1,0:T(8,128)S(1)} %get-tuple-element.15.square_ref), custom_call_target="tpu_custom_call" | custom-call | flops 600000000 | tf_op jit(solution)/shard_map/project_keep/pallas_call | solution.py:24
  23.7 0.1 merge.1
  23.7 1.6 %collective-permute-start.9 = (bf16[144,256]{1,0:T(8,128)(2,1)S(1)}, bf16[144,256]{1,0:T(8,128)(2,1)S(1)}, u32[]{:S(2)}, u32[]{:S(2)}) collective-permute-start(bf16[144,256]{1,0:T(8,128)(2,1)S(1)} %get-tuple-element.17), channel_id=1, source_target_pairs={{0,2},{1,3},{2,0},{3,1},{4,6},{5,7},{6,4},{7,5},{8,10},{9,11},{10,... | collective-permute-start | bytes 221192 | tf_op jit(solution)/shard_map/ppermute | solution.py:356
  25.3 0.9 %collective-permute-done.6.right_ref = f32[1,16]{1,0:T(1,128)S(1)} collective-permute-done((f32[1,16]{1,0:T(1,128)S(1)}, f32[1,16]{1,0:T(1,128)S(1)}, u32[]{:S(2)}, u32[]{:S(2)}) %collective-permute-start.6) | collective-permute-done | bytes 96 | tf_op jit(solution)/shard_map/ppermute | solution.py:43
  26.2 1.1 %collective-permute-start.7 = (f32[1,16]{1,0:T(1,128)S(1)}, f32[1,16]{1,0:T(1,128)S(1)}, u32[]{:S(2)}, u32[]{:S(2)}) collective-permute-start(f32[1,16]{1,0:T(1,128)S(1)} %larger.1.peak_ref), channel_id=1, source_target_pairs={{0,4},{4,0},{8,12},{12,8},{1,5},{5,1},{9,13},{13,9},{2,6},{6,2},{1... | collective-permute-start | bytes 200 | tf_op jit(solution)/shard_map/ppermute | solution.py:43
  27.3 2.4 %collective-permute-done.7.peak_got = f32[1,16]{1,0:T(1,128)S(1)} collective-permute-done((f32[1,16]{1,0:T(1,128)S(1)}, f32[1,16]{1,0:T(1,128)S(1)}, u32[]{:S(2)}, u32[]{:S(2)}) %collective-permute-start.7) | collective-permute-done | bytes 96 | tf_op jit(solution)/shard_map/ppermute | solution.py:43
  29.7 0.8 %finish.1 = (f32[1,16]{1,0:T(1,128)}, bf16[128,256]{1,0:T(8,128)(2,1)}) custom-call(f32[1,16]{1,0:T(1,128)S(1)} %larger.1.peak_ref, f32[1,16]{1,0:T(1,128)S(1)} %collective-permute-done.7.peak_got, f32[144,256]{1,0:T(8,128)S(1)} %get-tuple-element.16.keep_ref, bf16[144,256]{1,0:T(8,128)(2,1)S(1)} %collective-permute-done.9.refs_0_), custom_call_target="tpu_custom_call" | custom-call | tf_op jit(solution)/shard_map/finish/pallas_call | solution.py:24
  (21 shorter events, 0.1 us)
Async XLA Ops:
  1.4 3.0 %copy-start.1 = (bf16[1,128,2048]{2,1,0:T(8,128)(2,1)S(1)}, bf16[1,128,2048]{2,1,0:T(8,128)(2,1)}, u32[]{:S(2)}) copy-start(bf16[1,128,2048]{2,1,0:T(8,128)(2,1)} %q_ref.5) | copy-start | bytes 1572868
  1.4 5.5 %collective-permute-start = (bf16[128,256]{1,0:T(8,128)(2,1)S(1)}, bf16[128,256]{1,0:T(8,128)(2,1)S(1)}, u32[]{:S(2)}, u32[]{:S(2)}) collective-permute-start(bf16[128,256]{1,0:T(8,128)(2,1)S(1)} %pad_maximum_fusion.here_ref.block_ref), channel_id=1, source_target_pairs={{16,0},{0,16},{17,1},{1,17},{18,2},{2,18},{19,3},{3,19},{20,4},{4,... | collective-permute-start | bytes 196616 | tf_op jit(solution)/shard_map/ppermute | solution.py:48
  4.4 7.7 %copy-start.3 = (s32[8]{0:T(128)S(1)}, s32[8]{0:T(128)}, u32[]{:S(2)}) copy-start(s32[8]{0:T(128)} %order_ref.1) | copy-start | bytes 100
  4.5 14.6 %collective-permute-start.4 = (bf16[128,1024]{1,0:T(8,128)(2,1)S(1)}, bf16[128,1024]{1,0:T(8,128)(2,1)S(1)}, u32[]{:S(2)}, u32[]{:S(2)}) collective-permute-start(bf16[128,1024]{1,0:T(8,128)(2,1)S(1)} %take.2), channel_id=1, source_target_pairs={{16,0},{0,16},{17,1},{1,17},{18,2},{2,18},{19,3},{3,19},{20,4},{4,... | collective-permute-start | bytes 786440 | tf_op jit(solution)/shard_map/ppermute | solution.py:48
  6.9 7.7 %copy-start = (bf16[1,2048,1024]{2,1,0:T(8,128)(2,1)S(1)}, bf16[1,2048,1024]{2,1,0:T(8,128)(2,1)}, u32[]{:S(2)}) copy-start(bf16[1,2048,1024]{2,1,0:T(8,128)(2,1)} %param.11) | copy-start | bytes 12582916
  6.9 7.7 %copy-start.2 = (bf16[1,2048]{1,0:T(2,128)(2,1)S(1)}, bf16[1,2048]{1,0:T(2,128)(2,1)}, u32[]{:S(2)}) copy-start(bf16[1,2048]{1,0:T(2,128)(2,1)} %gain_ref.1) | copy-start | bytes 12292
  7.0 7.7 %collective-permute-start.1 = (bf16[128,384]{1,0:T(8,128)(2,1)S(1)}, bf16[128,384]{1,0:T(8,128)(2,1)S(1)}, u32[]{:S(2)}, u32[]{:S(2)}) collective-permute-start(bf16[128,384]{1,0:T(8,128)(2,1)S(1)} %join.1.refs_3_.after), channel_id=1, source_target_pairs={{0,12},{4,8},{8,4},{12,0},{1,13},{5,9},{9,5},{13,1},{2,14},{6,10},... | collective-permute-start | bytes 294920 | tf_op jit(solution)/shard_map/ppermute | solution.py:43
  11.4 6.7 %collective-permute-start.2 = (bf16[128,384]{1,0:T(8,128)(2,1)S(1)}, bf16[128,384]{1,0:T(8,128)(2,1)S(1)}, u32[]{:S(2)}, u32[]{:S(2)}) collective-permute-start(bf16[128,384]{1,0:T(8,128)(2,1)S(1)} %join.1.refs_3_.after), channel_id=1, source_target_pairs={{0,8},{4,12},{8,0},{12,4},{1,9},{5,13},{9,1},{13,5},{2,10},{6,14},... | collective-permute-start | bytes 294920 | tf_op jit(solution)/shard_map/ppermute | solution.py:43
  11.4 6.7 %collective-permute-start.3 = (bf16[128,384]{1,0:T(8,128)(2,1)S(1)}, bf16[128,384]{1,0:T(8,128)(2,1)S(1)}, u32[]{:S(2)}, u32[]{:S(2)}) collective-permute-start(bf16[128,384]{1,0:T(8,128)(2,1)S(1)} %join.1.refs_3_.after), channel_id=1, source_target_pairs={{0,4},{4,0},{8,12},{12,8},{1,5},{5,1},{9,13},{13,9},{2,6},{6,2},{1... | collective-permute-start | bytes 294920 | tf_op jit(solution)/shard_map/ppermute | solution.py:43
  12.7 7.3 %collective-permute-start.5 = (bf16[128,1024]{1,0:T(8,128)(2,1)S(1)}, bf16[128,1024]{1,0:T(8,128)(2,1)S(1)}, u32[]{:S(2)}, u32[]{:S(2)}) collective-permute-start(bf16[128,1024]{1,0:T(8,128)(2,1)S(1)} %take.3), channel_id=1, source_target_pairs={{16,0},{0,16},{17,1},{1,17},{18,2},{2,18},{19,3},{3,19},{20,4},{4,... | collective-permute-start | bytes 786440 | tf_op jit(solution)/shard_map/ppermute | solution.py:48
  21.6 2.1 %collective-permute-start.8 = (bf16[2,144,256]{2,1,0:T(8,128)(2,1)S(1)}, bf16[2,144,256]{2,1,0:T(8,128)(2,1)S(1)}, u32[]{:S(2)}, u32[]{:S(2)}) collective-permute-start(bf16[2,144,256]{2,1,0:T(8,128)(2,1)S(1)} %get-tuple-element.14.after), channel_id=1, source_target_pairs={{0,1},{1,0},{2,3},{3,2},{4,5},{5,4},{6,7},{7,6},{8,9},{9,8},{10,11... | collective-permute-start | bytes 442376 | tf_op jit(solution)/shard_map/ppermute | solution.py:341
  21.7 4.5 %collective-permute-start.6 = (f32[1,16]{1,0:T(1,128)S(1)}, f32[1,16]{1,0:T(1,128)S(1)}, u32[]{:S(2)}, u32[]{:S(2)}) collective-permute-start(f32[1,16]{1,0:T(1,128)S(1)} %bind.1.left_ref), channel_id=1, source_target_pairs={{0,8},{4,12},{8,0},{12,4},{1,9},{5,13},{9,1},{13,5},{2,10},{6,14},... | collective-permute-start | bytes 200 | tf_op jit(solution)/shard_map/ppermute | solution.py:43
  23.7 6.0 %collective-permute-start.9 = (bf16[144,256]{1,0:T(8,128)(2,1)S(1)}, bf16[144,256]{1,0:T(8,128)(2,1)S(1)}, u32[]{:S(2)}, u32[]{:S(2)}) collective-permute-start(bf16[144,256]{1,0:T(8,128)(2,1)S(1)} %get-tuple-element.17), channel_id=1, source_target_pairs={{0,2},{1,3},{2,0},{3,1},{4,6},{5,7},{6,4},{7,5},{8,10},{9,11},{10,... | collective-permute-start | bytes 221192 | tf_op jit(solution)/shard_map/ppermute | solution.py:356
  26.2 3.5 %collective-permute-start.7 = (f32[1,16]{1,0:T(1,128)S(1)}, f32[1,16]{1,0:T(1,128)S(1)}, u32[]{:S(2)}, u32[]{:S(2)}) collective-permute-start(f32[1,16]{1,0:T(1,128)S(1)} %larger.1.peak_ref), channel_id=1, source_target_pairs={{0,4},{4,0},{8,12},{12,8},{1,5},{5,1},{9,13},{13,9},{2,6},{6,2},{1... | collective-permute-start | bytes 200 | tf_op jit(solution)/shard_map/ppermute | solution.py:43

commit v10 on v9

--- a/solution.py
+++ b/solution.py
@@ -337,9 +337,9 @@
         name="project_give",
         micros=0.4,
     )
-    keep = call(project_keep, slab, (*contexts, w, squares), name="project_keep", micros=0.6)
+    keep = call(project_keep, slab, (*contexts, w, squares), name="project_keep", micros=3)
     got = lax.ppermute(give, "tp", [(i, i ^ 1) for i in range(peers)])
-    peak = bind(peak, give)
+    peak = bind(peak, contexts[0])
     for step in reversed(steps[1:]):
         peak = call(
             larger,

time: 30.7 us -> 30.7 us (level)
  starting transfers between devices: 15.3 us -> 15.8 us
  waiting for transfers between devices: 7.34 us -> 6.85 us
    ppermute x5, waiting for transfers between devices: 5.9 us -> 4.55 us  [swapped(): lax.ppermute(block, axis, [(i, partner(i, step, size)) for i in range(siz...]
    ppermute x1, waiting for transfers between devices: 0.01 us -> 0.87 us  [on_device(): got = lax.ppermute(give, 'tp', [(i, i ^ 1) for i in range(peers)])]
    ppermute x5, starting transfers between devices: 7.75 us -> 8.19 us  [swapped(): lax.ppermute(block, axis, [(i, partner(i, step, size)) for i in range(siz...]
  transfers between devices with their start and end apart: 10 -> 10, of which waited for: 4 -> 4; matrix products, arithmetic and copies ran while one was open for 0% -> 0% of each run, Pallas kernels for 13% -> 18%
where the time goes in v10:
time: 30.7 us; the launch traced here: 30.5 us
  starting transfers between devices  15.8 us (51%)
  waiting for transfers between devices  6.85 us (22%)
  Pallas kernels  6.31 us (21%)
  other arithmetic  0.78 us (3%)
  between operations  0.75 us (2%)
    ppermute x5, starting transfers between devices, swapped(): lax.ppermute(block, axis, [(i, partner(i, step, size)) for i in range(siz...  8.19 us
    pallas_call x16, Pallas kernels, call(): pl.pallas_call(kernel, out_shape=outs, in_specs=specs or [WHOLE] * len(ar...  6.31 us
    ppermute x3, starting transfers between devices, shifted(): lax.ppermute(block, axis, [((i - distance) % size, i) for i in range(size)])  5.9 us
    ppermute x5, waiting for transfers between devices, swapped(): lax.ppermute(block, axis, [(i, partner(i, step, size)) for i in range(siz...  4.55 us
    ppermute x1, starting transfers between devices, on_device(): lax.ppermute(block, 'tp', [(i, (i + 2 * (step + 1)) % peers) for i in ran...  1.59 us
    ppermute x3, waiting for transfers between devices, shifted(): lax.ppermute(block, axis, [((i - distance) % size, i) for i in range(size)])  1.43 us
    ppermute x1, waiting for transfers between devices, on_device(): got = lax.ppermute(give, 'tp', [(i, i ^ 1) for i in range(peers)])  0.87 us
    concatenate x1, other arithmetic, on_device(): pair_here = jnp.concatenate([key_vectors[0], value_vectors[0]], axis=1)  0.78 us
  transfers between devices with their start and end apart: 10, of which 4 were waited for; matrix products, arithmetic and copies ran while one was open for 0% of the time, Pallas kernels for 18%

profile of v10, /device:TPU:0, one launch (start us, length us, event | category | flops | bytes accessed | tf_op | source)
XLA Modules:
  0.0 30.5 jit_solution(9584118922485001475)
XLA Ops:
  0.6 0.8 %pad_maximum_fusion.here_ref.block_ref = bf16[128,256]{1,0:T(8,128)(2,1)S(1)} fusion(bf16[128,128]{1,0:T(8,128)(2,1)} %bitcast.5, bf16[128,128]{1,0:T(8,128)(2,1)} %bitcast.6), kind=kLoop, calls=%fused_computation | loop fusion | flops 131072 | bytes 131072 | tf_op jit(solution)/shard_map/concatenate | solution.py:268
  1.4 3.0 %collective-permute-start = (bf16[128,256]{1,0:T(8,128)(2,1)S(1)}, bf16[128,256]{1,0:T(8,128)(2,1)S(1)}, u32[]{:S(2)}, u32[]{:S(2)}) collective-permute-start(bf16[128,256]{1,0:T(8,128)(2,1)S(1)} %pad_maximum_fusion.here_ref.block_ref), channel_id=1, source_target_pairs={{16,0},{0,16},{17,1},{1,17},{18,2},{2,18},{19,3},{3,19},{20,4},{4,... | collective-permute-start | bytes 196616 | tf_op jit(solution)/shard_map/ppermute | solution.py:48
  4.5 1.0 %collective-permute-start.4 = (bf16[128,1024]{1,0:T(8,128)(2,1)S(1)}, bf16[128,1024]{1,0:T(8,128)(2,1)S(1)}, u32[]{:S(2)}, u32[]{:S(2)}) collective-permute-start(bf16[128,1024]{1,0:T(8,128)(2,1)S(1)} %take.2), channel_id=1, source_target_pairs={{16,0},{0,16},{17,1},{1,17},{18,2},{2,18},{19,3},{3,19},{20,4},{4,... | collective-permute-start | bytes 786440 | tf_op jit(solution)/shard_map/ppermute | solution.py:48
  5.5 1.4 %collective-permute-done.pair_ref = bf16[128,256]{1,0:T(8,128)(2,1)S(1)} collective-permute-done((bf16[128,256]{1,0:T(8,128)(2,1)S(1)}, bf16[128,256]{1,0:T(8,128)(2,1)S(1)}, u32[]{:S(2)}, u32[]{:S(2)}) %collective-permute-start) | collective-permute-done | bytes 65568 | tf_op jit(solution)/shard_map/ppermute | solution.py:48
  6.9 0.0 copy-start.2
  7.0 4.5 %collective-permute-start.1 = (bf16[128,384]{1,0:T(8,128)(2,1)S(1)}, bf16[128,384]{1,0:T(8,128)(2,1)S(1)}, u32[]{:S(2)}, u32[]{:S(2)}) collective-permute-start(bf16[128,384]{1,0:T(8,128)(2,1)S(1)} %join.1.refs_3_.after), channel_id=1, source_target_pairs={{0,12},{4,8},{8,4},{12,0},{1,13},{5,9},{9,5},{13,1},{2,14},{6,10},... | collective-permute-start | bytes 294920 | tf_op jit(solution)/shard_map/ppermute | solution.py:43
  11.4 0.6 %collective-permute-start.3 = (bf16[128,384]{1,0:T(8,128)(2,1)S(1)}, bf16[128,384]{1,0:T(8,128)(2,1)S(1)}, u32[]{:S(2)}, u32[]{:S(2)}) collective-permute-start(bf16[128,384]{1,0:T(8,128)(2,1)S(1)} %join.1.refs_3_.after), channel_id=1, source_target_pairs={{0,4},{4,0},{8,12},{12,8},{1,5},{5,1},{9,13},{13,9},{2,6},{6,2},{1... | collective-permute-start | bytes 294920 | tf_op jit(solution)/shard_map/ppermute | solution.py:43
  12.1 0.6 %prepare.1.feature_ref = bf16[2,128,512]{2,1,0:T(8,128)(2,1)S(1)} custom-call(s32[8]{0:T(128)S(1)} %copy-done.3, f32[8,128]{1,0:T(8,128)S(1)} %touch.1.after), custom_call_target="tpu_custom_call" | custom-call | flops 3000000000 | tf_op jit(solution)/shard_map/prepare/pallas_call | solution.py:24
  12.7 1.9 %collective-permute-start.7 = (bf16[128,1024]{1,0:T(8,128)(2,1)S(1)}, bf16[128,1024]{1,0:T(8,128)(2,1)S(1)}, u32[]{:S(2)}, u32[]{:S(2)}) collective-permute-start(bf16[128,1024]{1,0:T(8,128)(2,1)S(1)} %take.3), channel_id=1, source_target_pairs={{16,0},{0,16},{17,1},{1,17},{18,2},{2,18},{19,3},{3,19},{20,4},{4,... | collective-permute-start | bytes 786440 | tf_op jit(solution)/shard_map/ppermute | solution.py:48
  14.6 0.9 %weigh.1.after.w_ref = bf16[2048,1024]{1,0:T(8,128)(2,1)S(1)} custom-call(bf16[2048,1024]{1,0:T(8,128)(2,1)S(1)} %bitcast.4, bf16[1,2048]{1,0:T(2,128)(2,1)S(1)} %copy-done.2, bf16[128,384]{1,0:T(8,128)(2,1)S(1)} %collective-permute-done.1.after.refs_0_), custom_call_target="tpu_custom_call" | custom-call | flops 1000000000 | tf_op jit(solution)/shard_map/weigh/pallas_call | solution.py:24
  15.5 2.6 %collective-permute-done.2.refs_1_ = bf16[128,384]{1,0:T(8,128)(2,1)S(1)} collective-permute-done((bf16[128,384]{1,0:T(8,128)(2,1)S(1)}, bf16[128,384]{1,0:T(8,128)(2,1)S(1)}, u32[]{:S(2)}, u32[]{:S(2)}) %collective-permute-start.2) | collective-permute-done | bytes 98336 | tf_op jit(solution)/shard_map/ppermute | solution.py:43
  18.1 0.2 arrange.1
  18.3 0.8 %maxima.1.after.block_ref = f32[1,16]{1,0:T(1,128)S(1)} custom-call(bf16[1,128,2048]{2,1,0:T(8,128)(2,1)S(1)} %copy-done.1, bf16[1,2,256,512]{3,2,1,0:T(8,128)(2,1)S(1)} %get-tuple-element.11.own_ref), custom_call_target="tpu_custom_call" | custom-call | flops 700000000 | tf_op jit(solution)/shard_map/maxima/pallas_call | solution.py:24
  19.1 0.9 %attend.2.after.first_ref = bf16[128,1024]{1,0:T(8,128)(2,1)S(1)} custom-call(bf16[128,1024]{1,0:T(8,128)(2,1)S(1)} %collective-permute-done.4.q_ref, bf16[1,2,256,512]{3,2,1,0:T(8,128)(2,1)S(1)} %get-tuple-element.12.kt_ref, bf16[1,512,256]{2,1,0:T(8,128)(2,1)S(1)} %get-tuple-element.13.v_ref, f32[1,16]{1,0:T(1,128)S(1)} %maxima.1.after.block_ref), custom_call_target="tpu_custom_call" | custom-call | flops 960000000 | tf_op jit(solution)/shard_map/attend/pallas_call | solution.py:24
  20.0 1.5 %collective-permute-start.5 = (f32[1,16]{1,0:T(1,128)S(1)}, f32[1,16]{1,0:T(1,128)S(1)}, u32[]{:S(2)}, u32[]{:S(2)}) collective-permute-start(f32[1,16]{1,0:T(1,128)S(1)} %bind.1.left_ref), channel_id=1, source_target_pairs={{0,8},{4,12},{8,0},{12,4},{1,9},{5,13},{9,1},{13,5},{2,10},{6,14},... | collective-permute-start | bytes 200 | tf_op jit(solution)/shard_map/ppermute | solution.py:43
  21.5 0.9 %attend.3.last_ref = bf16[128,1024]{1,0:T(8,128)(2,1)S(1)} custom-call(bf16[128,1024]{1,0:T(8,128)(2,1)S(1)} %collective-permute-done.7.q_ref, bf16[1,2,256,512]{3,2,1,0:T(8,128)(2,1)S(1)} %get-tuple-element.12.kt_ref, bf16[1,512,256]{2,1,0:T(8,128)(2,1)S(1)} %get-tuple-element.13.v_ref, bf16[128,1024]{1,0:T(8,128)(2,1)S(1)} %attend.2.after.first_ref), custom_call_target="tpu_custom_call" | custom-call | flops 960000000 | tf_op jit(solution)/shard_map/attend/pallas_call | solution.py:24
  22.4 0.6 %project_give.1 = (bf16[2,144,256]{2,1,0:T(8,128)(2,1)S(1)}, f32[128,128]{1,0:T(8,128)S(1)}) custom-call(bf16[128,1024]{1,0:T(8,128)(2,1)S(1)} %attend.2.after.first_ref, bf16[128,1024]{1,0:T(8,128)(2,1)S(1)} %attend.3.last_ref, bf16[2048,1024]{1,0:T(8,128)(2,1)S(1)} %weigh.1.after.w_ref), custom_call_target="tpu_custom_call" | custom-call | flops 400000000 | tf_op jit(solution)/shard_map/project_give/pallas_call | solution.py:24
  23.0 0.1 collective-permute-start.8
  23.1 0.5 %project_keep.1.keep_ref = bf16[2,144,256]{2,1,0:T(8,128)(2,1)S(1)} custom-call(bf16[128,1024]{1,0:T(8,128)(2,1)S(1)} %attend.2.after.first_ref, bf16[128,1024]{1,0:T(8,128)(2,1)S(1)} %attend.3.last_ref, bf16[2048,1024]{1,0:T(8,128)(2,1)S(1)} %weigh.1.after.w_ref, f32[128,128]{1,0:T(8,128)S(1)} %get-tuple-element.14.square_ref), custom_call_target="tpu_custom_call" | custom-call | flops 3000000000 | tf_op jit(solution)/shard_map/project_keep/pallas_call | solution.py:24
  23.6 0.9 %collective-permute-done.8.got_ref = bf16[2,144,256]{2,1,0:T(8,128)(2,1)S(1)} collective-permute-done((bf16[2,144,256]{2,1,0:T(8,128)(2,1)S(1)}, bf16[2,144,256]{2,1,0:T(8,128)(2,1)S(1)}, u32[]{:S(2)}, u32[]{:S(2)}) %collective-permute-start.8) | collective-permute-done | bytes 147488 | tf_op jit(solution)/shard_map/ppermute | solution.py:341
  24.5 1.6 %collective-permute-start.9 = (bf16[144,256]{1,0:T(8,128)(2,1)S(1)}, bf16[144,256]{1,0:T(8,128)(2,1)S(1)}, u32[]{:S(2)}, u32[]{:S(2)}) collective-permute-start(bf16[144,256]{1,0:T(8,128)(2,1)S(1)} %get-tuple-element.17), channel_id=1, source_target_pairs={{0,2},{1,3},{2,0},{3,1},{4,6},{5,7},{6,4},{7,5},{8,10},{9,11},{10,... | collective-permute-start | bytes 221192 | tf_op jit(solution)/shard_map/ppermute | solution.py:356
  26.1 1.6 %collective-permute-start.6 = (f32[1,16]{1,0:T(1,128)S(1)}, f32[1,16]{1,0:T(1,128)S(1)}, u32[]{:S(2)}, u32[]{:S(2)}) collective-permute-start(f32[1,16]{1,0:T(1,128)S(1)} %larger.1.peak_ref), channel_id=1, source_target_pairs={{0,4},{4,0},{8,12},{12,8},{1,5},{5,1},{9,13},{13,9},{2,6},{6,2},{1... | collective-permute-start | bytes 200 | tf_op jit(solution)/shard_map/ppermute | solution.py:43
  27.7 1.9 %collective-permute-done.6.peak_got = f32[1,16]{1,0:T(1,128)S(1)} collective-permute-done((f32[1,16]{1,0:T(1,128)S(1)}, f32[1,16]{1,0:T(1,128)S(1)}, u32[]{:S(2)}, u32[]{:S(2)}) %collective-permute-start.6) | collective-permute-done | bytes 96 | tf_op jit(solution)/shard_map/ppermute | solution.py:43
  29.7 0.8 %finish.1 = (f32[1,16]{1,0:T(1,128)}, bf16[128,256]{1,0:T(8,128)(2,1)}) custom-call(f32[1,16]{1,0:T(1,128)S(1)} %larger.1.peak_ref, f32[1,16]{1,0:T(1,128)S(1)} %collective-permute-done.6.peak_got, f32[144,256]{1,0:T(8,128)S(1)} %get-tuple-element.16.keep_ref, bf16[144,256]{1,0:T(8,128)(2,1)S(1)} %collective-permute-done.9.refs_0_), custom_call_target="tpu_custom_call" | custom-call | tf_op jit(solution)/shard_map/finish/pallas_call | solution.py:24
  (21 shorter events, 0.1 us)
Async XLA Ops:
  1.4 3.0 %copy-start.1 = (bf16[1,128,2048]{2,1,0:T(8,128)(2,1)S(1)}, bf16[1,128,2048]{2,1,0:T(8,128)(2,1)}, u32[]{:S(2)}) copy-start(bf16[1,128,2048]{2,1,0:T(8,128)(2,1)} %q_ref.5) | copy-start | bytes 1572868
  1.4 5.5 %collective-permute-start = (bf16[128,256]{1,0:T(8,128)(2,1)S(1)}, bf16[128,256]{1,0:T(8,128)(2,1)S(1)}, u32[]{:S(2)}, u32[]{:S(2)}) collective-permute-start(bf16[128,256]{1,0:T(8,128)(2,1)S(1)} %pad_maximum_fusion.here_ref.block_ref), channel_id=1, source_target_pairs={{16,0},{0,16},{17,1},{1,17},{18,2},{2,18},{19,3},{3,19},{20,4},{4,... | collective-permute-start | bytes 196616 | tf_op jit(solution)/shard_map/ppermute | solution.py:48
  4.4 7.7 %copy-start.3 = (s32[8]{0:T(128)S(1)}, s32[8]{0:T(128)}, u32[]{:S(2)}) copy-start(s32[8]{0:T(128)} %order_ref.1) | copy-start | bytes 100
  4.5 14.6 %collective-permute-start.4 = (bf16[128,1024]{1,0:T(8,128)(2,1)S(1)}, bf16[128,1024]{1,0:T(8,128)(2,1)S(1)}, u32[]{:S(2)}, u32[]{:S(2)}) collective-permute-start(bf16[128,1024]{1,0:T(8,128)(2,1)S(1)} %take.2), channel_id=1, source_target_pairs={{16,0},{0,16},{17,1},{1,17},{18,2},{2,18},{19,3},{3,19},{20,4},{4,... | collective-permute-start | bytes 786440 | tf_op jit(solution)/shard_map/ppermute | solution.py:48
  6.9 7.7 %copy-start = (bf16[1,2048,1024]{2,1,0:T(8,128)(2,1)S(1)}, bf16[1,2048,1024]{2,1,0:T(8,128)(2,1)}, u32[]{:S(2)}) copy-start(bf16[1,2048,1024]{2,1,0:T(8,128)(2,1)} %param.11) | copy-start | bytes 12582916
  6.9 7.7 %copy-start.2 = (bf16[1,2048]{1,0:T(2,128)(2,1)S(1)}, bf16[1,2048]{1,0:T(2,128)(2,1)}, u32[]{:S(2)}) copy-start(bf16[1,2048]{1,0:T(2,128)(2,1)} %gain_ref.1) | copy-start | bytes 12292
  7.0 7.7 %collective-permute-start.1 = (bf16[128,384]{1,0:T(8,128)(2,1)S(1)}, bf16[128,384]{1,0:T(8,128)(2,1)S(1)}, u32[]{:S(2)}, u32[]{:S(2)}) collective-permute-start(bf16[128,384]{1,0:T(8,128)(2,1)S(1)} %join.1.refs_3_.after), channel_id=1, source_target_pairs={{0,12},{4,8},{8,4},{12,0},{1,13},{5,9},{9,5},{13,1},{2,14},{6,10},... | collective-permute-start | bytes 294920 | tf_op jit(solution)/shard_map/ppermute | solution.py:43
  11.4 6.7 %collective-permute-start.2 = (bf16[128,384]{1,0:T(8,128)(2,1)S(1)}, bf16[128,384]{1,0:T(8,128)(2,1)S(1)}, u32[]{:S(2)}, u32[]{:S(2)}) collective-permute-start(bf16[128,384]{1,0:T(8,128)(2,1)S(1)} %join.1.refs_3_.after), channel_id=1, source_target_pairs={{0,8},{4,12},{8,0},{12,4},{1,9},{5,13},{9,1},{13,5},{2,10},{6,14},... | collective-permute-start | bytes 294920 | tf_op jit(solution)/shard_map/ppermute | solution.py:43
  11.4 6.7 %collective-permute-start.3 = (bf16[128,384]{1,0:T(8,128)(2,1)S(1)}, bf16[128,384]{1,0:T(8,128)(2,1)S(1)}, u32[]{:S(2)}, u32[]{:S(2)}) collective-permute-start(bf16[128,384]{1,0:T(8,128)(2,1)S(1)} %join.1.refs_3_.after), channel_id=1, source_target_pairs={{0,4},{4,0},{8,12},{12,8},{1,5},{5,1},{9,13},{13,9},{2,6},{6,2},{1... | collective-permute-start | bytes 294920 | tf_op jit(solution)/shard_map/ppermute | solution.py:43
  12.7 8.8 %collective-permute-start.7 = (bf16[128,1024]{1,0:T(8,128)(2,1)S(1)}, bf16[128,1024]{1,0:T(8,128)(2,1)S(1)}, u32[]{:S(2)}, u32[]{:S(2)}) collective-permute-start(bf16[128,1024]{1,0:T(8,128)(2,1)S(1)} %take.3), channel_id=1, source_target_pairs={{16,0},{0,16},{17,1},{1,17},{18,2},{2,18},{19,3},{3,19},{20,4},{4,... | collective-permute-start | bytes 786440 | tf_op jit(solution)/shard_map/ppermute | solution.py:48
  20.0 6.1 %collective-permute-start.5 = (f32[1,16]{1,0:T(1,128)S(1)}, f32[1,16]{1,0:T(1,128)S(1)}, u32[]{:S(2)}, u32[]{:S(2)}) collective-permute-start(f32[1,16]{1,0:T(1,128)S(1)} %bind.1.left_ref), channel_id=1, source_target_pairs={{0,8},{4,12},{8,0},{12,4},{1,9},{5,13},{9,1},{13,5},{2,10},{6,14},... | collective-permute-start | bytes 200 | tf_op jit(solution)/shard_map/ppermute | solution.py:43
  23.0 1.4 %collective-permute-start.8 = (bf16[2,144,256]{2,1,0:T(8,128)(2,1)S(1)}, bf16[2,144,256]{2,1,0:T(8,128)(2,1)S(1)}, u32[]{:S(2)}, u32[]{:S(2)}) collective-permute-start(bf16[2,144,256]{2,1,0:T(8,128)(2,1)S(1)} %get-tuple-element.15), channel_id=1, source_target_pairs={{0,1},{1,0},{2,3},{3,2},{4,5},{5,4},{6,7},{7,6},{8,9},{9,8},{10,11... | collective-permute-start | bytes 442376 | tf_op jit(solution)/shard_map/ppermute | solution.py:341
  24.5 5.1 %collective-permute-start.9 = (bf16[144,256]{1,0:T(8,128)(2,1)S(1)}, bf16[144,256]{1,0:T(8,128)(2,1)S(1)}, u32[]{:S(2)}, u32[]{:S(2)}) collective-permute-start(bf16[144,256]{1,0:T(8,128)(2,1)S(1)} %get-tuple-element.17), channel_id=1, source_target_pairs={{0,2},{1,3},{2,0},{3,1},{4,6},{5,7},{6,4},{7,5},{8,10},{9,11},{10,... | collective-permute-start | bytes 221192 | tf_op jit(solution)/shard_map/ppermute | solution.py:356
  26.1 3.5 %collective-permute-start.6 = (f32[1,16]{1,0:T(1,128)S(1)}, f32[1,16]{1,0:T(1,128)S(1)}, u32[]{:S(2)}, u32[]{:S(2)}) collective-permute-start(f32[1,16]{1,0:T(1,128)S(1)} %larger.1.peak_ref), channel_id=1, source_target_pairs={{0,4},{4,0},{8,12},{12,8},{1,5},{5,1},{9,13},{13,9},{2,6},{6,2},{1... | collective-permute-start | bytes 200 | tf_op jit(solution)/shard_map/ppermute | solution.py:43

commit v11 on v10

--- a/solution.py
+++ b/solution.py
@@ -32,6 +32,20 @@
         cost_estimate=pl.CostEstimate(flops=int(micros * 1e9), bytes_accessed=0, transcendentals=0) if micros else None,
         compiler_params=pltpu.CompilerParams(vmem_limit_bytes=limit * 2**20),
     )(*args)
+
+
+def partner(index, step, size):
+    return (index + step) % size if size & (size - 1) else index ^ step
+
+
+def swapped(block, axis, step):
+    size = lax.axis_size(axis)
+    return lax.ppermute(block, axis, [(i, partner(i, step, size)) for i in range(size)])
+
+
+def shifted(block, axis, distance):
+    size = lax.axis_size(axis)
+    return lax.ppermute(block, axis, [((i - distance) % size, i) for i in range(size)])
 
 
 def partner(index, step, size):
@@ -132,8 +146,41 @@
     return jnp.concatenate([q, blocked], axis=1)
 
 
-def maxima(q_ref, own_ref, peak_ref):
-    q_ref = q_ref.at[0]
+def attention_units(first_head, heads, q_ref, kt_ref, v_ref, ctx_ref):
+    rows, width = q_ref.shape
+    keys = v_ref.shape[1]
+    block = rows // 2
+    factor = LOG2E / math.sqrt(DH)
+    units = [
+        (g, start, stop, side)
+        for g, start, stop in spans(first_head, width // DH, heads // v_ref.shape[0], max(1, 12 * 512 // keys))
+        for side in range(2)
+    ]
+
+    def scores(unit):
+        g, start, stop, side = unit
+        return jnp.dot(stacked(q_ref, start, stop, side), kt_ref[g, side], preferred_element_type=F32)
+
+    def finish_unit(unit, s):
+        g, start, stop, side = unit
+        m = jnp.max(s, axis=1, keepdims=True)
+        p = jnp.exp2((s - m) * factor).astype(BF16)
+        yield
+        o = jnp.dot(p, v_ref[g], preferred_element_type=F32)
+        o = (o[:, :DH] * (1.0 / o[:, DH:])).astype(BF16)
+        for j in range(stop - start):
+            ctx_ref[side * block:(side + 1) * block, (start + j) * DH:(start + j + 1) * DH] = o[
+                j * block:(j + 1) * block, :
+            ]
+
+    ahead = [scores(unit) for unit in units[:2]]
+    for n, unit in enumerate(units):
+        yield from finish_unit(unit, ahead.pop(0))
+        if n + 2 < len(units):
+            ahead.append(scores(units[n + 2]))
+
+
+def maxima_units(q_ref, own_ref, peak_ref):
     block = q_ref.shape[0] // 2
     heads = q_ref.shape[1] // DH
     keys = own_ref.shape[3]
@@ -141,6 +188,7 @@
         tops = []
         for side in range(2):
             s = jnp.dot(stacked(q_ref, start, stop, side), own_ref[g, side], preferred_element_type=F32)
+            yield
             top = s[:, :LANES]
             for c in range(LANES, keys, LANES):
                 top = jnp.maximum(top, s[:, c:c + LANES])
@@ -152,27 +200,26 @@
             peak_ref[:, h:h + 1] = jnp.max(one, axis=1, keepdims=True) * (1.0 / math.sqrt(DH))
 
 
-def attend(first_head, heads, q_ref, kt_ref, v_ref, after, ctx_ref):
-    rows, width = q_ref.shape
-    keys = v_ref.shape[1]
-    block = rows // 2
-    count = width // DH
-    scale = 1.0 / math.sqrt(DH)
-    for g, start, stop in spans(first_head, count, heads // v_ref.shape[0], max(1, 12 * 512 // keys)):
-        scores = [
-            jnp.dot(stacked(q_ref, start, stop, side), kt_ref[g, side], preferred_element_type=F32) for side in range(2)
-        ]
-        probs = []
-        for s in scores:
-            m = jnp.max(s, axis=1, keepdims=True)
-            probs.append(jnp.exp2((s - m) * (scale * LOG2E)).astype(BF16))
-        for side in range(2):
-            o = jnp.dot(probs[side], v_ref[g], preferred_element_type=F32)
-            o = (o[:, :DH] * (1.0 / o[:, DH:])).astype(BF16)
-            for j in range(stop - start):
-                ctx_ref[side * block:(side + 1) * block, (start + j) * DH:(start + j + 1) * DH] = o[
-                    j * block:(j + 1) * block, :
-                ]
+def interleave(*streams):
+    streams = list(streams)
+    while streams:
+        for stream in list(streams):
+            if next(stream, stream) is stream:
+                streams.remove(stream)
+
+
+def attend_first(heads, w_ref, feature_ref, *refs):
+    triples, refs = refs[:-7], refs[-7:]
+    mine_ref, q_ref, kt_ref, v_ref, ctx_ref, peak_ref, own_ref = refs
+    arrange(None, feature_ref, *triples, kt_ref, v_ref, own_ref)
+    interleave(
+        attention_units(0, heads, q_ref, kt_ref, v_ref, ctx_ref), maxima_units(mine_ref.at[0], own_ref, peak_ref)
+    )
+
+
+def attend_last(first_head, heads, q_ref, kt_ref, v_ref, first_ref, w_ref, ctx_ref, give_ref, square_ref):
+    interleave(attention_units(first_head, heads, q_ref, kt_ref, v_ref, ctx_ref))
+    project_give(first_ref, ctx_ref, w_ref, give_ref, square_ref)
 
 
 def weigh(w_ref, gain_ref, after, out_ref):
@@ -307,39 +354,33 @@
     )
     kv_local = kv_width // DH
     turned = shape((kv_local, 2, DH + LANES, sources * rows), BF16)
-    kt, v_all, own = call(
-        arrange,
-        (turned, shape((kv_local, sources * rows, 2 * DH), BF16), turned),
-        (w, features, *reversed(triples)),
-        [OUTSIDE] + [WHOLE] * (1 + sources),
-        name="arrange",
-        micros=0.2,
-    )
-    peak = call(maxima, shape((1, heads), F32), (queries, own), limit=32, name="maxima", micros=0.7)
-    contexts, after = [], peak
-    for start, count, part in zip(starts, counts, crossed):
-        context = call(
-            functools.partial(attend, start, heads),
-            shape((rows, count * DH), BF16),
-            (part, kt, v_all, after),
-            [WHOLE, WHOLE, WHOLE, OUTSIDE],
-            limit=32,
-            name="attend",
-            micros=count * 0.12,
-        )
-        contexts.append(context)
-        after = context
+    kt, v_all, first_context, peak = call(
+        functools.partial(attend_first, heads),
+        (
+            turned,
+            shape((kv_local, sources * rows, 2 * DH), BF16),
+            shape((rows, counts[0] * DH), BF16),
+            shape((1, heads), F32),
+        ),
+        (w, features, *reversed(triples), queries, crossed[0]),
+        [OUTSIDE] + [WHOLE] * (3 + sources),
+        scratch=[pltpu.VMEM(turned.shape, BF16)],
+        limit=36,
+        name="attend_first",
+        micros=2,
+    )
     slab = shape((peers // 2, rows + SQUARE_ROWS, out_cols), BF16)
-    give, squares = call(
-        project_give,
-        (slab, shape((rows, LANES), F32)),
-        (*contexts, w),
-        name="project_give",
-        micros=0.4,
-    )
+    last_context, give, squares = call(
+        functools.partial(attend_last, starts[1], heads),
+        (shape((rows, counts[1] * DH), BF16), slab, shape((rows, LANES), F32)),
+        (crossed[1], kt, v_all, first_context, w),
+        limit=32,
+        name="attend_last",
+        micros=1.5,
+    )
+    contexts = [first_context, last_context]
     keep = call(project_keep, slab, (*contexts, w, squares), name="project_keep", micros=3)
     got = lax.ppermute(give, "tp", [(i, i ^ 1) for i in range(peers)])
-    peak = bind(peak, contexts[0])
     for step in reversed(steps[1:]):
         peak = call(
             larger,

time: 30.7 us -> 30 us (0.977)
  Pallas kernels: 6.31 us -> 5.76 us
    pallas_call x16 -> x12, Pallas kernels: 6.31 us -> 5.76 us  [call(): pl.pallas_call(kernel, out_shape=outs, in_specs=specs or [WHOLE] * len(ar...]
  transfers between devices with their start and end apart: 10 -> 10, of which waited for: 4 -> 4; matrix products, arithmetic and copies ran while one was open for 0% -> 0% of each run, Pallas kernels for 18% -> 17%
where the time goes in v11:
time: 30 us; the launch traced here: 29.8 us
  starting transfers between devices  15.7 us (52%)
  waiting for transfers between devices  6.86 us (23%)
  Pallas kernels  5.76 us (19%)
  other arithmetic  0.78 us (3%)
  between operations  0.73 us (2%)
    ppermute x5, starting transfers between devices, swapped(): lax.ppermute(block, axis, [(i, partner(i, step, size)) for i in range(siz...  8.12 us
    ppermute x3, starting transfers between devices, shifted(): lax.ppermute(block, axis, [((i - distance) % size, i) for i in range(size)])  5.9 us
    pallas_call x12, Pallas kernels, call(): pl.pallas_call(kernel, out_shape=outs, in_specs=specs or [WHOLE] * len(ar...  5.76 us
    ppermute x5, waiting for transfers between devices, swapped(): lax.ppermute(block, axis, [(i, partner(i, step, size)) for i in range(siz...  4.56 us
    ppermute x1, starting transfers between devices, on_device(): lax.ppermute(block, 'tp', [(i, (i + 2 * (step + 1)) % peers) for i in ran...  1.58 us
    ppermute x3, waiting for transfers between devices, shifted(): lax.ppermute(block, axis, [((i - distance) % size, i) for i in range(size)])  1.43 us
    ppermute x1, waiting for transfers between devices, on_device(): got = lax.ppermute(give, 'tp', [(i, i ^ 1) for i in range(peers)])  0.86 us
    concatenate x1, other arithmetic, on_device(): pair_here = jnp.concatenate([key_vectors[0], value_vectors[0]], axis=1)  0.78 us
  transfers between devices with their start and end apart: 10, of which 4 were waited for; matrix products, arithmetic and copies ran while one was open for 0% of the time, Pallas kernels for 17%

profile of v11, /device:TPU:0, one launch (start us, length us, event | category | flops | bytes accessed | tf_op | source)
XLA Modules:
  0.0 29.8 jit_solution(10479150656214254582)
XLA Ops:
  0.6 0.8 %pad_maximum_fusion.here_ref.block_ref = bf16[128,256]{1,0:T(8,128)(2,1)S(1)} fusion(bf16[128,128]{1,0:T(8,128)(2,1)} %bitcast.5, bf16[128,128]{1,0:T(8,128)(2,1)} %bitcast.6), kind=kLoop, calls=%fused_computation | loop fusion | flops 131072 | bytes 131072 | tf_op jit(solution)/shard_map/concatenate | solution.py:315
  1.4 3.0 %collective-permute-start = (bf16[128,256]{1,0:T(8,128)(2,1)S(1)}, bf16[128,256]{1,0:T(8,128)(2,1)S(1)}, u32[]{:S(2)}, u32[]{:S(2)}) collective-permute-start(bf16[128,256]{1,0:T(8,128)(2,1)S(1)} %pad_maximum_fusion.here_ref.block_ref), channel_id=1, source_target_pairs={{16,0},{0,16},{17,1},{1,17},{18,2},{2,18},{19,3},{3,19},{20,4},{4,... | collective-permute-start | bytes 196616 | tf_op jit(solution)/shard_map/ppermute | solution.py:62
  4.5 1.0 %collective-permute-start.4 = (bf16[128,1024]{1,0:T(8,128)(2,1)S(1)}, bf16[128,1024]{1,0:T(8,128)(2,1)S(1)}, u32[]{:S(2)}, u32[]{:S(2)}) collective-permute-start(bf16[128,1024]{1,0:T(8,128)(2,1)S(1)} %take.2), channel_id=1, source_target_pairs={{16,0},{0,16},{17,1},{1,17},{18,2},{2,18},{19,3},{3,19},{20,4},{4,... | collective-permute-start | bytes 786440 | tf_op jit(solution)/shard_map/ppermute | solution.py:62
  5.5 1.4 %collective-permute-done.pair_ref = bf16[128,256]{1,0:T(8,128)(2,1)S(1)} collective-permute-done((bf16[128,256]{1,0:T(8,128)(2,1)S(1)}, bf16[128,256]{1,0:T(8,128)(2,1)S(1)}, u32[]{:S(2)}, u32[]{:S(2)}) %collective-permute-start) | collective-permute-done | bytes 65568 | tf_op jit(solution)/shard_map/ppermute | solution.py:62
  6.9 0.0 copy-start
  6.9 0.0 copy-start.2
  7.0 4.5 %collective-permute-start.1 = (bf16[128,384]{1,0:T(8,128)(2,1)S(1)}, bf16[128,384]{1,0:T(8,128)(2,1)S(1)}, u32[]{:S(2)}, u32[]{:S(2)}) collective-permute-start(bf16[128,384]{1,0:T(8,128)(2,1)S(1)} %join.1.refs_3_.after), channel_id=1, source_target_pairs={{0,12},{4,8},{8,4},{12,0},{1,13},{5,9},{9,5},{13,1},{2,14},{6,10},... | collective-permute-start | bytes 294920 | tf_op jit(solution)/shard_map/ppermute | solution.py:57
  11.4 0.6 %collective-permute-start.3 = (bf16[128,384]{1,0:T(8,128)(2,1)S(1)}, bf16[128,384]{1,0:T(8,128)(2,1)S(1)}, u32[]{:S(2)}, u32[]{:S(2)}) collective-permute-start(bf16[128,384]{1,0:T(8,128)(2,1)S(1)} %join.1.refs_3_.after), channel_id=1, source_target_pairs={{0,4},{4,0},{8,12},{12,8},{1,5},{5,1},{9,13},{13,9},{2,6},{6,2},{1... | collective-permute-start | bytes 294920 | tf_op jit(solution)/shard_map/ppermute | solution.py:57
  12.1 0.6 %prepare.1.feature_ref = bf16[2,128,512]{2,1,0:T(8,128)(2,1)S(1)} custom-call(s32[8]{0:T(128)S(1)} %copy-done.3, f32[8,128]{1,0:T(8,128)S(1)} %touch.1.after), custom_call_target="tpu_custom_call" | custom-call | flops 3000000000 | tf_op jit(solution)/shard_map/prepare/pallas_call | solution.py:24
  12.7 1.9 %collective-permute-start.7 = (bf16[128,1024]{1,0:T(8,128)(2,1)S(1)}, bf16[128,1024]{1,0:T(8,128)(2,1)S(1)}, u32[]{:S(2)}, u32[]{:S(2)}) collective-permute-start(bf16[128,1024]{1,0:T(8,128)(2,1)S(1)} %take.3), channel_id=1, source_target_pairs={{16,0},{0,16},{17,1},{1,17},{18,2},{2,18},{19,3},{3,19},{20,4},{4,... | collective-permute-start | bytes 786440 | tf_op jit(solution)/shard_map/ppermute | solution.py:62
  14.6 0.0 collective-permute-done.1.after.refs_0_
  14.6 0.9 %weigh.1.w_ref = bf16[2048,1024]{1,0:T(8,128)(2,1)S(1)} custom-call(bf16[2048,1024]{1,0:T(8,128)(2,1)S(1)} %bitcast.4, bf16[1,2048]{1,0:T(2,128)(2,1)S(1)} %copy-done.2, bf16[128,384]{1,0:T(8,128)(2,1)S(1)} %collective-permute-done.1.after.refs_0_), custom_call_target="tpu_custom_call" | custom-call | flops 1000000000 | tf_op jit(solution)/shard_map/weigh/pallas_call | solution.py:24
  15.5 2.6 %collective-permute-done.2.refs_1_ = bf16[128,384]{1,0:T(8,128)(2,1)S(1)} collective-permute-done((bf16[128,384]{1,0:T(8,128)(2,1)S(1)}, bf16[128,384]{1,0:T(8,128)(2,1)S(1)}, u32[]{:S(2)}, u32[]{:S(2)}) %collective-permute-start.2) | collective-permute-done | bytes 98336 | tf_op jit(solution)/shard_map/ppermute | solution.py:57
  18.1 0.0 collective-permute-done.4.refs_5_
  18.1 1.5 %attend_first.1 = (bf16[1,2,256,512]{3,2,1,0:T(8,128)(2,1)S(1)}, bf16[1,512,256]{2,1,0:T(8,128)(2,1)S(1)}, bf16[128,1024]{1,0:T(8,128)(2,1)S(1)}, f32[1,16]{1,0:T(1,128)S(1)}) custom-call(bf16[2048,1024]{1,0:T(8,128)(2,1)S(1)} %weigh.1.w_ref, bf16[2,128,512]{2,1,0:T(8,128)(2,1)S(1)} %prepare.1.feature_ref, ...), custom_call_target="tpu_custom_call" | custom-call | flops 2000000000 | tf_op jit(solution)/shard_map/attend_first/pallas_call | solution.py:24
  19.7 1.4 %collective-permute-start.5 = (f32[1,16]{1,0:T(1,128)S(1)}, f32[1,16]{1,0:T(1,128)S(1)}, u32[]{:S(2)}, u32[]{:S(2)}) collective-permute-start(f32[1,16]{1,0:T(1,128)S(1)} %get-tuple-element.13.left_ref), channel_id=1, source_target_pairs={{0,8},{4,12},{8,0},{12,4},{1,9},{5,13},{9,1},{13,5},{2,10},{6,14},... | collective-permute-start | bytes 200 | tf_op jit(solution)/shard_map/ppermute | solution.py:57
  21.1 1.3 %attend_last.1 = (bf16[128,1024]{1,0:T(8,128)(2,1)S(1)}, bf16[2,144,256]{2,1,0:T(8,128)(2,1)S(1)}, f32[128,128]{1,0:T(8,128)S(1)}) custom-call(bf16[128,1024]{1,0:T(8,128)(2,1)S(1)} %collective-permute-done.7.q_ref, bf16[1,2,256,512]{3,2,1,0:T(8,128)(2,1)S(1)} %get-tuple-element.15.kt_ref, bf16[1,512,256]{2,1,0:T(8,128)(2,1)S(1)} %get-tuple-element.16.v_ref, ...), custom_call_target="tpu_custom_call" | custom-call | flops 1500000000 | tf_op jit(solution)/shard_map/attend_last/pallas_call | solution.py:24
  22.4 0.1 collective-permute-start.8
  22.5 0.5 %project_keep.1.keep_ref = bf16[2,144,256]{2,1,0:T(8,128)(2,1)S(1)} custom-call(bf16[128,1024]{1,0:T(8,128)(2,1)S(1)} %get-tuple-element.14.first_ref, bf16[128,1024]{1,0:T(8,128)(2,1)S(1)} %get-tuple-element.17.last_ref, bf16[2048,1024]{1,0:T(8,128)(2,1)S(1)} %weigh.1.w_ref, f32[128,128]{1,0:T(8,128)S(1)} %get-tuple-element.18.square_ref), custom_call_target="tpu_custom_call" | custom-call | flops 3000000000 | tf_op jit(solution)/shard_map/project_keep/pallas_call | solution.py:24
  23.0 0.9 %collective-permute-done.8.got_ref = bf16[2,144,256]{2,1,0:T(8,128)(2,1)S(1)} collective-permute-done((bf16[2,144,256]{2,1,0:T(8,128)(2,1)S(1)}, bf16[2,144,256]{2,1,0:T(8,128)(2,1)S(1)}, u32[]{:S(2)}, u32[]{:S(2)}) %collective-permute-start.8) | collective-permute-done | bytes 147488 | tf_op jit(solution)/shard_map/ppermute | solution.py:383
  23.9 1.6 %collective-permute-start.9 = (bf16[144,256]{1,0:T(8,128)(2,1)S(1)}, bf16[144,256]{1,0:T(8,128)(2,1)S(1)}, u32[]{:S(2)}, u32[]{:S(2)}) collective-permute-start(bf16[144,256]{1,0:T(8,128)(2,1)S(1)} %get-tuple-element.21), channel_id=1, source_target_pairs={{0,2},{1,3},{2,0},{3,1},{4,6},{5,7},{6,4},{7,5},{8,10},{9,11},{10,... | collective-permute-start | bytes 221192 | tf_op jit(solution)/shard_map/ppermute | solution.py:397
  25.5 1.6 %collective-permute-start.6 = (f32[1,16]{1,0:T(1,128)S(1)}, f32[1,16]{1,0:T(1,128)S(1)}, u32[]{:S(2)}, u32[]{:S(2)}) collective-permute-start(f32[1,16]{1,0:T(1,128)S(1)} %larger.1.peak_ref), channel_id=1, source_target_pairs={{0,4},{4,0},{8,12},{12,8},{1,5},{5,1},{9,13},{13,9},{2,6},{6,2},{1... | collective-permute-start | bytes 200 | tf_op jit(solution)/shard_map/ppermute | solution.py:57
  27.1 1.9 %collective-permute-done.6.peak_got = f32[1,16]{1,0:T(1,128)S(1)} collective-permute-done((f32[1,16]{1,0:T(1,128)S(1)}, f32[1,16]{1,0:T(1,128)S(1)}, u32[]{:S(2)}, u32[]{:S(2)}) %collective-permute-start.6) | collective-permute-done | bytes 96 | tf_op jit(solution)/shard_map/ppermute | solution.py:57
  29.0 0.8 %finish.1 = (f32[1,16]{1,0:T(1,128)}, bf16[128,256]{1,0:T(8,128)(2,1)}) custom-call(f32[1,16]{1,0:T(1,128)S(1)} %larger.1.peak_ref, f32[1,16]{1,0:T(1,128)S(1)} %collective-permute-done.6.peak_got, f32[144,256]{1,0:T(8,128)S(1)} %get-tuple-element.20.keep_ref, bf16[144,256]{1,0:T(8,128)(2,1)S(1)} %collective-permute-done.9.refs_0_), custom_call_target="tpu_custom_call" | custom-call | tf_op jit(solution)/shard_map/finish/pallas_call | solution.py:24
  (17 shorter events, 0.1 us)
Async XLA Ops:
  1.4 3.0 %copy-start.1 = (bf16[1,128,2048]{2,1,0:T(8,128)(2,1)S(1)}, bf16[1,128,2048]{2,1,0:T(8,128)(2,1)}, u32[]{:S(2)}) copy-start(bf16[1,128,2048]{2,1,0:T(8,128)(2,1)} %q_ref.3) | copy-start | bytes 1572868
  1.4 5.5 %collective-permute-start = (bf16[128,256]{1,0:T(8,128)(2,1)S(1)}, bf16[128,256]{1,0:T(8,128)(2,1)S(1)}, u32[]{:S(2)}, u32[]{:S(2)}) collective-permute-start(bf16[128,256]{1,0:T(8,128)(2,1)S(1)} %pad_maximum_fusion.here_ref.block_ref), channel_id=1, source_target_pairs={{16,0},{0,16},{17,1},{1,17},{18,2},{2,18},{19,3},{3,19},{20,4},{4,... | collective-permute-start | bytes 196616 | tf_op jit(solution)/shard_map/ppermute | solution.py:62
  4.4 7.7 %copy-start.3 = (s32[8]{0:T(128)S(1)}, s32[8]{0:T(128)}, u32[]{:S(2)}) copy-start(s32[8]{0:T(128)} %order_ref.1) | copy-start | bytes 100
  4.5 13.7 %collective-permute-start.4 = (bf16[128,1024]{1,0:T(8,128)(2,1)S(1)}, bf16[128,1024]{1,0:T(8,128)(2,1)S(1)}, u32[]{:S(2)}, u32[]{:S(2)}) collective-permute-start(bf16[128,1024]{1,0:T(8,128)(2,1)S(1)} %take.2), channel_id=1, source_target_pairs={{16,0},{0,16},{17,1},{1,17},{18,2},{2,18},{19,3},{3,19},{20,4},{4,... | collective-permute-start | bytes 786440 | tf_op jit(solution)/shard_map/ppermute | solution.py:62
  6.9 7.7 %copy-start = (bf16[1,2048,1024]{2,1,0:T(8,128)(2,1)S(1)}, bf16[1,2048,1024]{2,1,0:T(8,128)(2,1)}, u32[]{:S(2)}) copy-start(bf16[1,2048,1024]{2,1,0:T(8,128)(2,1)} %param.11) | copy-start | bytes 12582916
  6.9 7.7 %copy-start.2 = (bf16[1,2048]{1,0:T(2,128)(2,1)S(1)}, bf16[1,2048]{1,0:T(2,128)(2,1)}, u32[]{:S(2)}) copy-start(bf16[1,2048]{1,0:T(2,128)(2,1)} %gain_ref.1) | copy-start | bytes 12292
  7.0 7.7 %collective-permute-start.1 = (bf16[128,384]{1,0:T(8,128)(2,1)S(1)}, bf16[128,384]{1,0:T(8,128)(2,1)S(1)}, u32[]{:S(2)}, u32[]{:S(2)}) collective-permute-start(bf16[128,384]{1,0:T(8,128)(2,1)S(1)} %join.1.refs_3_.after), channel_id=1, source_target_pairs={{0,12},{4,8},{8,4},{12,0},{1,13},{5,9},{9,5},{13,1},{2,14},{6,10},... | collective-permute-start | bytes 294920 | tf_op jit(solution)/shard_map/ppermute | solution.py:57
  11.4 6.7 %collective-permute-start.2 = (bf16[128,384]{1,0:T(8,128)(2,1)S(1)}, bf16[128,384]{1,0:T(8,128)(2,1)S(1)}, u32[]{:S(2)}, u32[]{:S(2)}) collective-permute-start(bf16[128,384]{1,0:T(8,128)(2,1)S(1)} %join.1.refs_3_.after), channel_id=1, source_target_pairs={{0,8},{4,12},{8,0},{12,4},{1,9},{5,13},{9,1},{13,5},{2,10},{6,14},... | collective-permute-start | bytes 294920 | tf_op jit(solution)/shard_map/ppermute | solution.py:57
  11.4 6.7 %collective-permute-start.3 = (bf16[128,384]{1,0:T(8,128)(2,1)S(1)}, bf16[128,384]{1,0:T(8,128)(2,1)S(1)}, u32[]{:S(2)}, u32[]{:S(2)}) collective-permute-start(bf16[128,384]{1,0:T(8,128)(2,1)S(1)} %join.1.refs_3_.after), channel_id=1, source_target_pairs={{0,4},{4,0},{8,12},{12,8},{1,5},{5,1},{9,13},{13,9},{2,6},{6,2},{1... | collective-permute-start | bytes 294920 | tf_op jit(solution)/shard_map/ppermute | solution.py:57
  12.7 8.3 %collective-permute-start.7 = (bf16[128,1024]{1,0:T(8,128)(2,1)S(1)}, bf16[128,1024]{1,0:T(8,128)(2,1)S(1)}, u32[]{:S(2)}, u32[]{:S(2)}) collective-permute-start(bf16[128,1024]{1,0:T(8,128)(2,1)S(1)} %take.3), channel_id=1, source_target_pairs={{16,0},{0,16},{17,1},{1,17},{18,2},{2,18},{19,3},{3,19},{20,4},{4,... | collective-permute-start | bytes 786440 | tf_op jit(solution)/shard_map/ppermute | solution.py:62
  19.7 5.8 %collective-permute-start.5 = (f32[1,16]{1,0:T(1,128)S(1)}, f32[1,16]{1,0:T(1,128)S(1)}, u32[]{:S(2)}, u32[]{:S(2)}) collective-permute-start(f32[1,16]{1,0:T(1,128)S(1)} %get-tuple-element.13.left_ref), channel_id=1, source_target_pairs={{0,8},{4,12},{8,0},{12,4},{1,9},{5,13},{9,1},{13,5},{2,10},{6,14},... | collective-permute-start | bytes 200 | tf_op jit(solution)/shard_map/ppermute | solution.py:57
  22.4 1.4 %collective-permute-start.8 = (bf16[2,144,256]{2,1,0:T(8,128)(2,1)S(1)}, bf16[2,144,256]{2,1,0:T(8,128)(2,1)S(1)}, u32[]{:S(2)}, u32[]{:S(2)}) collective-permute-start(bf16[2,144,256]{2,1,0:T(8,128)(2,1)S(1)} %get-tuple-element.19), channel_id=1, source_target_pairs={{0,1},{1,0},{2,3},{3,2},{4,5},{5,4},{6,7},{7,6},{8,9},{9,8},{10,11... | collective-permute-start | bytes 442376 | tf_op jit(solution)/shard_map/ppermute | solution.py:383
  23.9 5.1 %collective-permute-start.9 = (bf16[144,256]{1,0:T(8,128)(2,1)S(1)}, bf16[144,256]{1,0:T(8,128)(2,1)S(1)}, u32[]{:S(2)}, u32[]{:S(2)}) collective-permute-start(bf16[144,256]{1,0:T(8,128)(2,1)S(1)} %get-tuple-element.21), channel_id=1, source_target_pairs={{0,2},{1,3},{2,0},{3,1},{4,6},{5,7},{6,4},{7,5},{8,10},{9,11},{10,... | collective-permute-start | bytes 221192 | tf_op jit(solution)/shard_map/ppermute | solution.py:397
  25.5 3.5 %collective-permute-start.6 = (f32[1,16]{1,0:T(1,128)S(1)}, f32[1,16]{1,0:T(1,128)S(1)}, u32[]{:S(2)}, u32[]{:S(2)}) collective-permute-start(f32[1,16]{1,0:T(1,128)S(1)} %larger.1.peak_ref), channel_id=1, source_target_pairs={{0,4},{4,0},{8,12},{12,8},{1,5},{5,1},{9,13},{13,9},{2,6},{6,2},{1... | collective-permute-start | bytes 200 | tf_op jit(solution)/shard_map/ppermute | solution.py:57

commit v12 on v11

--- a/solution.py
+++ b/solution.py
@@ -217,9 +217,24 @@
     )
 
 
-def attend_last(first_head, heads, q_ref, kt_ref, v_ref, first_ref, w_ref, ctx_ref, give_ref, square_ref):
-    interleave(attention_units(first_head, heads, q_ref, kt_ref, v_ref, ctx_ref))
-    project_give(first_ref, ctx_ref, w_ref, give_ref, square_ref)
+def product_units(ctx_ref, w_ref, sums):
+    other = 1 - lax.rem(lax.axis_index("tp"), 2)
+    for y in range(sums.shape[0]):
+        w = w_ref[:ctx_ref.shape[1], columns_of(y, other, sums.shape[2])]
+        sums[y] = jnp.dot(ctx_ref[...], w, preferred_element_type=F32)
+        yield
+
+
+def attend_last(first_head, heads, q_ref, kt_ref, v_ref, first_ref, w_ref, ctx_ref, give_ref, square_ref, sums):
+    interleave(
+        attention_units(first_head, heads, q_ref, kt_ref, v_ref, ctx_ref), product_units(first_ref, w_ref, sums)
+    )
+    other = 1 - lax.rem(lax.axis_index("tp"), 2)
+    squares = square_sums(first_ref) + square_sums(ctx_ref)
+    square_ref[...] = squares
+    for y in range(give_ref.shape[0]):
+        w = w_ref[first_ref.shape[1]:, columns_of(y, other, give_ref.shape[2])]
+        fill(give_ref, y, sums[y] + jnp.dot(ctx_ref[...], w, preferred_element_type=F32), squares)
 
 
 def weigh(w_ref, gain_ref, after, out_ref):
@@ -258,14 +273,6 @@
     cut = first_ref.shape[1]
     part = jnp.dot(first_ref[...], w_ref[:cut, at], preferred_element_type=F32)
     return part + jnp.dot(last_ref[...], w_ref[cut:, at], preferred_element_type=F32)
-
-
-def project_give(first_ref, last_ref, w_ref, give_ref, square_ref):
-    other = 1 - lax.rem(lax.axis_index("tp"), 2)
-    squares = square_sums(first_ref) + square_sums(last_ref)
-    square_ref[...] = squares
-    for y in range(give_ref.shape[0]):
-        fill(give_ref, y, product(first_ref, last_ref, w_ref, columns_of(y, other, give_ref.shape[2])), squares)
 
 
 def project_keep(first_ref, last_ref, w_ref, square_ref, keep_ref):
@@ -374,6 +381,7 @@
         functools.partial(attend_last, starts[1], heads),
         (shape((rows, counts[1] * DH), BF16), slab, shape((rows, LANES), F32)),
         (crossed[1], kt, v_all, first_context, w),
+        scratch=[pltpu.VMEM((peers // 2, rows, out_cols), F32)],
         limit=32,
         name="attend_last",
         micros=1.5,
@@ -381,7 +389,7 @@
     contexts = [first_context, last_context]
     keep = call(project_keep, slab, (*contexts, w, squares), name="project_keep", micros=3)
     got = lax.ppermute(give, "tp", [(i, i ^ 1) for i in range(peers)])
-    for step in reversed(steps[1:]):
+    for step in steps[:-1]:
         peak = call(
             larger,
             shape((1, heads), F32),
@@ -400,7 +408,7 @@
     max_logits, kv_next = call(
         functools.partial(finish, width * peers),
         (shape((1, heads), F32), shape((rows, out_cols), BF16)),
-        (peak, swapped(peak, "cp", steps[0]), mine, *others),
+        (peak, swapped(peak, "cp", steps[-1]), mine, *others),
         name="finish",
     )
     return (max_logits, kv_next[None])

time: 30 us -> 30.2 us (level)
  no operation moved by 1% of the time
where the time goes in v12:
time: 30.2 us; the launch traced here: 30 us
  starting transfers between devices  15.7 us (52%)
  waiting for transfers between devices  6.84 us (23%)
  Pallas kernels  5.96 us (20%)
  other arithmetic  0.78 us (3%)
  between operations  0.73 us (2%)
    ppermute x5, starting transfers between devices, swapped(): lax.ppermute(block, axis, [(i, partner(i, step, size)) for i in range(siz...  8.12 us
    pallas_call x12, Pallas kernels, call(): pl.pallas_call(kernel, out_shape=outs, in_specs=specs or [WHOLE] * len(ar...  5.96 us
    ppermute x3, starting transfers between devices, shifted(): lax.ppermute(block, axis, [((i - distance) % size, i) for i in range(size)])  5.9 us
    ppermute x5, waiting for transfers between devices, swapped(): lax.ppermute(block, axis, [(i, partner(i, step, size)) for i in range(siz...  4.55 us
    ppermute x1, starting transfers between devices, on_device(): lax.ppermute(block, 'tp', [(i, (i + 2 * (step + 1)) % peers) for i in ran...  1.58 us
    ppermute x3, waiting for transfers between devices, shifted(): lax.ppermute(block, axis, [((i - distance) % size, i) for i in range(size)])  1.43 us
    ppermute x1, waiting for transfers between devices, on_device(): got = lax.ppermute(give, 'tp', [(i, i ^ 1) for i in range(peers)])  0.86 us
    concatenate x1, other arithmetic, on_device(): pair_here = jnp.concatenate([key_vectors[0], value_vectors[0]], axis=1)  0.78 us
  transfers between devices with their start and end apart: 10, of which 4 were waited for; matrix products, arithmetic and copies ran while one was open for 0% of the time, Pallas kernels for 17%

profile of v12, /device:TPU:0, one launch (start us, length us, event | category | flops | bytes accessed | tf_op | source)
XLA Modules:
  0.0 30.0 jit_solution(7074080021123521525)
XLA Ops:
  0.6 0.8 %pad_maximum_fusion.here_ref.block_ref = bf16[128,256]{1,0:T(8,128)(2,1)S(1)} fusion(bf16[128,128]{1,0:T(8,128)(2,1)} %bitcast.5, bf16[128,128]{1,0:T(8,128)(2,1)} %bitcast.6), kind=kLoop, calls=%fused_computation | loop fusion | flops 131072 | bytes 131072 | tf_op jit(solution)/shard_map/concatenate | solution.py:322
  1.4 3.0 %collective-permute-start = (bf16[128,256]{1,0:T(8,128)(2,1)S(1)}, bf16[128,256]{1,0:T(8,128)(2,1)S(1)}, u32[]{:S(2)}, u32[]{:S(2)}) collective-permute-start(bf16[128,256]{1,0:T(8,128)(2,1)S(1)} %pad_maximum_fusion.here_ref.block_ref), channel_id=1, source_target_pairs={{16,0},{0,16},{17,1},{1,17},{18,2},{2,18},{19,3},{3,19},{20,4},{4,... | collective-permute-start | bytes 196616 | tf_op jit(solution)/shard_map/ppermute | solution.py:62
  4.5 1.0 %collective-permute-start.4 = (bf16[128,1024]{1,0:T(8,128)(2,1)S(1)}, bf16[128,1024]{1,0:T(8,128)(2,1)S(1)}, u32[]{:S(2)}, u32[]{:S(2)}) collective-permute-start(bf16[128,1024]{1,0:T(8,128)(2,1)S(1)} %take.2), channel_id=1, source_target_pairs={{16,0},{0,16},{17,1},{1,17},{18,2},{2,18},{19,3},{3,19},{20,4},{4,... | collective-permute-start | bytes 786440 | tf_op jit(solution)/shard_map/ppermute | solution.py:62
  5.5 1.4 %collective-permute-done.pair_ref = bf16[128,256]{1,0:T(8,128)(2,1)S(1)} collective-permute-done((bf16[128,256]{1,0:T(8,128)(2,1)S(1)}, bf16[128,256]{1,0:T(8,128)(2,1)S(1)}, u32[]{:S(2)}, u32[]{:S(2)}) %collective-permute-start) | collective-permute-done | bytes 65568 | tf_op jit(solution)/shard_map/ppermute | solution.py:62
  6.9 0.0 copy-start
  6.9 0.0 copy-start.2
  7.0 4.5 %collective-permute-start.1 = (bf16[128,384]{1,0:T(8,128)(2,1)S(1)}, bf16[128,384]{1,0:T(8,128)(2,1)S(1)}, u32[]{:S(2)}, u32[]{:S(2)}) collective-permute-start(bf16[128,384]{1,0:T(8,128)(2,1)S(1)} %join.1.refs_3_.after), channel_id=1, source_target_pairs={{0,12},{4,8},{8,4},{12,0},{1,13},{5,9},{9,5},{13,1},{2,14},{6,10},... | collective-permute-start | bytes 294920 | tf_op jit(solution)/shard_map/ppermute | solution.py:57
  11.4 0.0 collective-permute-start.2
  11.4 0.6 %collective-permute-start.3 = (bf16[128,384]{1,0:T(8,128)(2,1)S(1)}, bf16[128,384]{1,0:T(8,128)(2,1)S(1)}, u32[]{:S(2)}, u32[]{:S(2)}) collective-permute-start(bf16[128,384]{1,0:T(8,128)(2,1)S(1)} %join.1.refs_3_.after), channel_id=1, source_target_pairs={{0,4},{4,0},{8,12},{12,8},{1,5},{5,1},{9,13},{13,9},{2,6},{6,2},{1... | collective-permute-start | bytes 294920 | tf_op jit(solution)/shard_map/ppermute | solution.py:57
  12.1 0.6 %prepare.1.feature_ref = bf16[2,128,512]{2,1,0:T(8,128)(2,1)S(1)} custom-call(s32[8]{0:T(128)S(1)} %copy-done.3, f32[8,128]{1,0:T(8,128)S(1)} %touch.1.after), custom_call_target="tpu_custom_call" | custom-call | flops 3000000000 | tf_op jit(solution)/shard_map/prepare/pallas_call | solution.py:24
  12.7 1.9 %collective-permute-start.7 = (bf16[128,1024]{1,0:T(8,128)(2,1)S(1)}, bf16[128,1024]{1,0:T(8,128)(2,1)S(1)}, u32[]{:S(2)}, u32[]{:S(2)}) collective-permute-start(bf16[128,1024]{1,0:T(8,128)(2,1)S(1)} %take.3), channel_id=1, source_target_pairs={{16,0},{0,16},{17,1},{1,17},{18,2},{2,18},{19,3},{3,19},{20,4},{4,... | collective-permute-start | bytes 786440 | tf_op jit(solution)/shard_map/ppermute | solution.py:62
  14.6 0.9 %weigh.1.w_ref = bf16[2048,1024]{1,0:T(8,128)(2,1)S(1)} custom-call(bf16[2048,1024]{1,0:T(8,128)(2,1)S(1)} %bitcast.4, bf16[1,2048]{1,0:T(2,128)(2,1)S(1)} %copy-done.2, bf16[128,384]{1,0:T(8,128)(2,1)S(1)} %collective-permute-done.1.after.refs_0_), custom_call_target="tpu_custom_call" | custom-call | flops 1000000000 | tf_op jit(solution)/shard_map/weigh/pallas_call | solution.py:24
  15.5 2.6 %collective-permute-done.2.refs_1_ = bf16[128,384]{1,0:T(8,128)(2,1)S(1)} collective-permute-done((bf16[128,384]{1,0:T(8,128)(2,1)S(1)}, bf16[128,384]{1,0:T(8,128)(2,1)S(1)}, u32[]{:S(2)}, u32[]{:S(2)}) %collective-permute-start.2) | collective-permute-done | bytes 98336 | tf_op jit(solution)/shard_map/ppermute | solution.py:57
  18.1 1.5 %attend_first.1 = (bf16[1,2,256,512]{3,2,1,0:T(8,128)(2,1)S(1)}, bf16[1,512,256]{2,1,0:T(8,128)(2,1)S(1)}, bf16[128,1024]{1,0:T(8,128)(2,1)S(1)}, f32[1,16]{1,0:T(1,128)S(1)}) custom-call(bf16[2048,1024]{1,0:T(8,128)(2,1)S(1)} %weigh.1.w_ref, bf16[2,128,512]{2,1,0:T(8,128)(2,1)S(1)} %prepare.1.feature_ref, ...), custom_call_target="tpu_custom_call" | custom-call | flops 2000000000 | tf_op jit(solution)/shard_map/attend_first/pallas_call | solution.py:24
  19.7 0.5 %collective-permute-start.5 = (f32[1,16]{1,0:T(1,128)S(1)}, f32[1,16]{1,0:T(1,128)S(1)}, u32[]{:S(2)}, u32[]{:S(2)}) collective-permute-start(f32[1,16]{1,0:T(1,128)S(1)} %get-tuple-element.13.left_ref), channel_id=1, source_target_pairs={{0,4},{4,0},{8,12},{12,8},{1,5},{5,1},{9,13},{13,9},{2,6},{6,2},{1... | collective-permute-start | bytes 200 | tf_op jit(solution)/shard_map/ppermute | solution.py:57
  20.1 1.5 %attend_last.1 = (bf16[128,1024]{1,0:T(8,128)(2,1)S(1)}, bf16[2,144,256]{2,1,0:T(8,128)(2,1)S(1)}, f32[128,128]{1,0:T(8,128)S(1)}) custom-call(bf16[128,1024]{1,0:T(8,128)(2,1)S(1)} %collective-permute-done.7.q_ref, bf16[1,2,256,512]{3,2,1,0:T(8,128)(2,1)S(1)} %get-tuple-element.15.kt_ref, bf16[1,512,256]{2,1,0:T(8,128)(2,1)S(1)} %get-tuple-element.16.v_ref, ...), custom_call_target="tpu_custom_call" | custom-call | flops 1500000000 | tf_op jit(solution)/shard_map/attend_last/pallas_call | solution.py:24
  21.7 0.1 collective-permute-start.8
  21.8 0.5 %project_keep.1.keep_ref = bf16[2,144,256]{2,1,0:T(8,128)(2,1)S(1)} custom-call(bf16[128,1024]{1,0:T(8,128)(2,1)S(1)} %get-tuple-element.14.first_ref, bf16[128,1024]{1,0:T(8,128)(2,1)S(1)} %get-tuple-element.17.last_ref, bf16[2048,1024]{1,0:T(8,128)(2,1)S(1)} %weigh.1.w_ref, f32[128,128]{1,0:T(8,128)S(1)} %get-tuple-element.18.square_ref), custom_call_target="tpu_custom_call" | custom-call | flops 3000000000 | tf_op jit(solution)/shard_map/project_keep/pallas_call | solution.py:24
  22.3 0.9 %collective-permute-done.8.got_ref = bf16[2,144,256]{2,1,0:T(8,128)(2,1)S(1)} collective-permute-done((bf16[2,144,256]{2,1,0:T(8,128)(2,1)S(1)}, bf16[2,144,256]{2,1,0:T(8,128)(2,1)S(1)}, u32[]{:S(2)}, u32[]{:S(2)}) %collective-permute-start.8) | collective-permute-done | bytes 147488 | tf_op jit(solution)/shard_map/ppermute | solution.py:391
  23.2 1.6 %collective-permute-start.9 = (bf16[144,256]{1,0:T(8,128)(2,1)S(1)}, bf16[144,256]{1,0:T(8,128)(2,1)S(1)}, u32[]{:S(2)}, u32[]{:S(2)}) collective-permute-start(bf16[144,256]{1,0:T(8,128)(2,1)S(1)} %get-tuple-element.21), channel_id=1, source_target_pairs={{0,2},{1,3},{2,0},{3,1},{4,6},{5,7},{6,4},{7,5},{8,10},{9,11},{10,... | collective-permute-start | bytes 221192 | tf_op jit(solution)/shard_map/ppermute | solution.py:405
  24.8 2.5 %collective-permute-start.6 = (f32[1,16]{1,0:T(1,128)S(1)}, f32[1,16]{1,0:T(1,128)S(1)}, u32[]{:S(2)}, u32[]{:S(2)}) collective-permute-start(f32[1,16]{1,0:T(1,128)S(1)} %larger.1.peak_ref), channel_id=1, source_target_pairs={{0,8},{4,12},{8,0},{12,4},{1,9},{5,13},{9,1},{13,5},{2,10},{6,14},... | collective-permute-start | bytes 200 | tf_op jit(solution)/shard_map/ppermute | solution.py:57
  27.3 1.9 %collective-permute-done.6.peak_got = f32[1,16]{1,0:T(1,128)S(1)} collective-permute-done((f32[1,16]{1,0:T(1,128)S(1)}, f32[1,16]{1,0:T(1,128)S(1)}, u32[]{:S(2)}, u32[]{:S(2)}) %collective-permute-start.6) | collective-permute-done | bytes 96 | tf_op jit(solution)/shard_map/ppermute | solution.py:57
  29.2 0.0 collective-permute-done.9.refs_0_
  29.2 0.8 %finish.1 = (f32[1,16]{1,0:T(1,128)}, bf16[128,256]{1,0:T(8,128)(2,1)}) custom-call(f32[1,16]{1,0:T(1,128)S(1)} %larger.1.peak_ref, f32[1,16]{1,0:T(1,128)S(1)} %collective-permute-done.6.peak_got, f32[144,256]{1,0:T(8,128)S(1)} %get-tuple-element.20.keep_ref, bf16[144,256]{1,0:T(8,128)(2,1)S(1)} %collective-permute-done.9.refs_0_), custom_call_target="tpu_custom_call" | custom-call | tf_op jit(solution)/shard_map/finish/pallas_call | solution.py:24
  (17 shorter events, 0.1 us)
Async XLA Ops:
  1.4 3.0 %copy-start.1 = (bf16[1,128,2048]{2,1,0:T(8,128)(2,1)S(1)}, bf16[1,128,2048]{2,1,0:T(8,128)(2,1)}, u32[]{:S(2)}) copy-start(bf16[1,128,2048]{2,1,0:T(8,128)(2,1)} %q_ref.3) | copy-start | bytes 1572868
  1.4 5.5 %collective-permute-start = (bf16[128,256]{1,0:T(8,128)(2,1)S(1)}, bf16[128,256]{1,0:T(8,128)(2,1)S(1)}, u32[]{:S(2)}, u32[]{:S(2)}) collective-permute-start(bf16[128,256]{1,0:T(8,128)(2,1)S(1)} %pad_maximum_fusion.here_ref.block_ref), channel_id=1, source_target_pairs={{16,0},{0,16},{17,1},{1,17},{18,2},{2,18},{19,3},{3,19},{20,4},{4,... | collective-permute-start | bytes 196616 | tf_op jit(solution)/shard_map/ppermute | solution.py:62
  4.4 7.7 %copy-start.3 = (s32[8]{0:T(128)S(1)}, s32[8]{0:T(128)}, u32[]{:S(2)}) copy-start(s32[8]{0:T(128)} %order_ref.1) | copy-start | bytes 100
  4.5 13.7 %collective-permute-start.4 = (bf16[128,1024]{1,0:T(8,128)(2,1)S(1)}, bf16[128,1024]{1,0:T(8,128)(2,1)S(1)}, u32[]{:S(2)}, u32[]{:S(2)}) collective-permute-start(bf16[128,1024]{1,0:T(8,128)(2,1)S(1)} %take.2), channel_id=1, source_target_pairs={{16,0},{0,16},{17,1},{1,17},{18,2},{2,18},{19,3},{3,19},{20,4},{4,... | collective-permute-start | bytes 786440 | tf_op jit(solution)/shard_map/ppermute | solution.py:62
  6.9 7.7 %copy-start = (bf16[1,2048,1024]{2,1,0:T(8,128)(2,1)S(1)}, bf16[1,2048,1024]{2,1,0:T(8,128)(2,1)}, u32[]{:S(2)}) copy-start(bf16[1,2048,1024]{2,1,0:T(8,128)(2,1)} %param.11) | copy-start | bytes 12582916
  6.9 7.7 %copy-start.2 = (bf16[1,2048]{1,0:T(2,128)(2,1)S(1)}, bf16[1,2048]{1,0:T(2,128)(2,1)}, u32[]{:S(2)}) copy-start(bf16[1,2048]{1,0:T(2,128)(2,1)} %gain_ref.1) | copy-start | bytes 12292
  7.0 7.7 %collective-permute-start.1 = (bf16[128,384]{1,0:T(8,128)(2,1)S(1)}, bf16[128,384]{1,0:T(8,128)(2,1)S(1)}, u32[]{:S(2)}, u32[]{:S(2)}) collective-permute-start(bf16[128,384]{1,0:T(8,128)(2,1)S(1)} %join.1.refs_3_.after), channel_id=1, source_target_pairs={{0,12},{4,8},{8,4},{12,0},{1,13},{5,9},{9,5},{13,1},{2,14},{6,10},... | collective-permute-start | bytes 294920 | tf_op jit(solution)/shard_map/ppermute | solution.py:57
  11.4 6.7 %collective-permute-start.2 = (bf16[128,384]{1,0:T(8,128)(2,1)S(1)}, bf16[128,384]{1,0:T(8,128)(2,1)S(1)}, u32[]{:S(2)}, u32[]{:S(2)}) collective-permute-start(bf16[128,384]{1,0:T(8,128)(2,1)S(1)} %join.1.refs_3_.after), channel_id=1, source_target_pairs={{0,8},{4,12},{8,0},{12,4},{1,9},{5,13},{9,1},{13,5},{2,10},{6,14},... | collective-permute-start | bytes 294920 | tf_op jit(solution)/shard_map/ppermute | solution.py:57
  11.4 6.7 %collective-permute-start.3 = (bf16[128,384]{1,0:T(8,128)(2,1)S(1)}, bf16[128,384]{1,0:T(8,128)(2,1)S(1)}, u32[]{:S(2)}, u32[]{:S(2)}) collective-permute-start(bf16[128,384]{1,0:T(8,128)(2,1)S(1)} %join.1.refs_3_.after), channel_id=1, source_target_pairs={{0,4},{4,0},{8,12},{12,8},{1,5},{5,1},{9,13},{13,9},{2,6},{6,2},{1... | collective-permute-start | bytes 294920 | tf_op jit(solution)/shard_map/ppermute | solution.py:57
  12.7 7.4 %collective-permute-start.7 = (bf16[128,1024]{1,0:T(8,128)(2,1)S(1)}, bf16[128,1024]{1,0:T(8,128)(2,1)S(1)}, u32[]{:S(2)}, u32[]{:S(2)}) collective-permute-start(bf16[128,1024]{1,0:T(8,128)(2,1)S(1)} %take.3), channel_id=1, source_target_pairs={{16,0},{0,16},{17,1},{1,17},{18,2},{2,18},{19,3},{3,19},{20,4},{4,... | collective-permute-start | bytes 786440 | tf_op jit(solution)/shard_map/ppermute | solution.py:62
  19.7 5.1 %collective-permute-start.5 = (f32[1,16]{1,0:T(1,128)S(1)}, f32[1,16]{1,0:T(1,128)S(1)}, u32[]{:S(2)}, u32[]{:S(2)}) collective-permute-start(f32[1,16]{1,0:T(1,128)S(1)} %get-tuple-element.13.left_ref), channel_id=1, source_target_pairs={{0,4},{4,0},{8,12},{12,8},{1,5},{5,1},{9,13},{13,9},{2,6},{6,2},{1... | collective-permute-start | bytes 200 | tf_op jit(solution)/shard_map/ppermute | solution.py:57
  21.7 1.4 %collective-permute-start.8 = (bf16[2,144,256]{2,1,0:T(8,128)(2,1)S(1)}, bf16[2,144,256]{2,1,0:T(8,128)(2,1)S(1)}, u32[]{:S(2)}, u32[]{:S(2)}) collective-permute-start(bf16[2,144,256]{2,1,0:T(8,128)(2,1)S(1)} %get-tuple-element.19), channel_id=1, source_target_pairs={{0,1},{1,0},{2,3},{3,2},{4,5},{5,4},{6,7},{7,6},{8,9},{9,8},{10,11... | collective-permute-start | bytes 442376 | tf_op jit(solution)/shard_map/ppermute | solution.py:391
  23.2 6.0 %collective-permute-start.9 = (bf16[144,256]{1,0:T(8,128)(2,1)S(1)}, bf16[144,256]{1,0:T(8,128)(2,1)S(1)}, u32[]{:S(2)}, u32[]{:S(2)}) collective-permute-start(bf16[144,256]{1,0:T(8,128)(2,1)S(1)} %get-tuple-element.21), channel_id=1, source_target_pairs={{0,2},{1,3},{2,0},{3,1},{4,6},{5,7},{6,4},{7,5},{8,10},{9,11},{10,... | collective-permute-start | bytes 221192 | tf_op jit(solution)/shard_map/ppermute | solution.py:405
  24.8 4.4 %collective-permute-start.6 = (f32[1,16]{1,0:T(1,128)S(1)}, f32[1,16]{1,0:T(1,128)S(1)}, u32[]{:S(2)}, u32[]{:S(2)}) collective-permute-start(f32[1,16]{1,0:T(1,128)S(1)} %larger.1.peak_ref), channel_id=1, source_target_pairs={{0,8},{4,12},{8,0},{12,4},{1,9},{5,13},{9,1},{13,5},{2,10},{6,14},... | collective-permute-start | bytes 200 | tf_op jit(solution)/shard_map/ppermute | solution.py:57

commit v13 on v11

--- a/solution.py
+++ b/solution.py
@@ -217,9 +217,15 @@
     )
 
 
-def attend_last(first_head, heads, q_ref, kt_ref, v_ref, first_ref, w_ref, ctx_ref, give_ref, square_ref):
+def attend_last(
+    first_head, heads, q_ref, kt_ref, v_ref, first_ref, w_ref, ctx_ref, far_ref, near_ref, square_ref
+):
     interleave(attention_units(first_head, heads, q_ref, kt_ref, v_ref, ctx_ref))
-    project_give(first_ref, ctx_ref, w_ref, give_ref, square_ref)
+    squares = square_sums(first_ref) + square_sums(ctx_ref)
+    square_ref[...] = squares
+    other = 1 - lax.rem(lax.axis_index("tp"), 2)
+    project(first_ref, ctx_ref, w_ref, other, 1, squares, far_ref)
+    project(first_ref, ctx_ref, w_ref, other, 0, squares, near_ref)
 
 
 def weigh(w_ref, gain_ref, after, out_ref):
@@ -260,39 +266,32 @@
     return part + jnp.dot(last_ref[...], w_ref[cut:, at], preferred_element_type=F32)
 
 
-def project_give(first_ref, last_ref, w_ref, give_ref, square_ref):
-    other = 1 - lax.rem(lax.axis_index("tp"), 2)
-    squares = square_sums(first_ref) + square_sums(last_ref)
-    square_ref[...] = squares
-    for y in range(give_ref.shape[0]):
-        fill(give_ref, y, product(first_ref, last_ref, w_ref, columns_of(y, other, give_ref.shape[2])), squares)
-
-
-def project_keep(first_ref, last_ref, w_ref, square_ref, keep_ref):
-    core = lax.rem(lax.axis_index("tp"), 2)
-    for y in range(keep_ref.shape[0]):
-        at = columns_of(y, core, keep_ref.shape[2])
-        fill(keep_ref, y, product(first_ref, last_ref, w_ref, at), square_ref[...])
-
-
-def larger(left_ref, right_ref, out_ref):
+def project(first_ref, last_ref, w_ref, side, step, squares, out_ref):
+    groups = w_ref.shape[1] // (2 * out_ref.shape[2])
+    mine = lax.axis_index("tp") // 2
+    for n in range(out_ref.shape[0]):
+        at = columns_of(lax.rem(mine + step + n, groups), side, out_ref.shape[2])
+        fill(out_ref, n, product(first_ref, last_ref, w_ref, at), squares)
+
+
+def project_keep(step, first_ref, last_ref, w_ref, square_ref, out_ref):
+    project(first_ref, last_ref, w_ref, lax.rem(lax.axis_index("tp"), 2), step, square_ref[...], out_ref)
+
+
+def larger(left_ref, right_ref, after, out_ref):
     out_ref[...] = jnp.maximum(left_ref[...], right_ref[...])
 
 
 def merge(keep_ref, got_ref, *give_refs):
-    groups = keep_ref.shape[0]
-    mine = lax.axis_index("tp") // 2
-    for step, ref in enumerate(give_refs):
-        y = lax.rem(mine + step, groups)
-        total = keep_ref[y].astype(F32) + got_ref[y].astype(F32)
-        ref[...] = total.astype(ref.dtype)
-
-
-def finish(features, peak_ref, peak_got, keep_ref, *refs):
+    for n, ref in enumerate(give_refs):
+        ref[...] = (keep_ref[n].astype(F32) + got_ref[n].astype(F32)).astype(ref.dtype)
+
+
+def finish(features, peak_ref, peak_got, keep_ref, got_ref, *refs):
     peak_out, out_ref = refs[-2:]
     peak_out[...] = jnp.maximum(peak_ref[...], peak_got[...])
     rows = out_ref.shape[0]
-    total = keep_ref[...]
+    total = keep_ref[0].astype(F32) + got_ref[0].astype(F32)
     for ref in refs[:-2]:
         total = total + ref[...].astype(F32)
     squares = total[rows:rows + 8, :rows] + total[rows:rows + 8, rows:2 * rows]
@@ -369,29 +368,45 @@
         name="attend_first",
         micros=2,
     )
-    slab = shape((peers // 2, rows + SQUARE_ROWS, out_cols), BF16)
-    last_context, give, squares = call(
+    def slabs(count):
+        return shape((count, rows + SQUARE_ROWS, out_cols), BF16)
+
+    def to_other_core(block):
+        return lax.ppermute(block, "tp", [(i, i ^ 1) for i in range(peers)])
+
+    last_context, give_far, give_near, squares = call(
         functools.partial(attend_last, starts[1], heads),
-        (shape((rows, counts[1] * DH), BF16), slab, shape((rows, LANES), F32)),
+        (shape((rows, counts[1] * DH), BF16), slabs(peers // 2 - 1), slabs(1), shape((rows, LANES), F32)),
         (crossed[1], kt, v_all, first_context, w),
         limit=32,
         name="attend_last",
         micros=1.5,
     )
-    contexts = [first_context, last_context]
-    keep = call(project_keep, slab, (*contexts, w, squares), name="project_keep", micros=3)
-    got = lax.ppermute(give, "tp", [(i, i ^ 1) for i in range(peers)])
-    for step in reversed(steps[1:]):
+    keep_far, keep_near = [
+        call(
+            functools.partial(project_keep, step),
+            slabs(count),
+            (first_context, last_context, w, squares),
+            name="project_keep",
+            micros=3 if step else 0,
+        )
+        for step, count in ((1, peers // 2 - 1), (0, 1))
+    ]
+    got_far, got_near = to_other_core(give_far), to_other_core(give_near)
+    for step in steps[:-1]:
         peak = call(
             larger,
             shape((1, heads), F32),
-            (peak, swapped(peak, "cp", step)),
+            (peak, swapped(peak, "cp", step), give_far),
+            [WHOLE, WHOLE, OUTSIDE],
             name="larger",
             micros=5,
         )
-    slab = (rows + SQUARE_ROWS, out_cols)
-    mine, *others = call(
-        merge, [shape(slab, F32)] + [shape(slab, BF16)] * (peers // 2 - 1), (keep, got), name="merge"
+    others = call(
+        merge,
+        [shape((rows + SQUARE_ROWS, out_cols), BF16)] * (peers // 2 - 1),
+        (keep_far, got_far),
+        name="merge",
     )
     others = [
         lax.ppermute(block, "tp", [(i, (i + 2 * (step + 1)) % peers) for i in range(peers)])
@@ -400,7 +415,7 @@
     max_logits, kv_next = call(
         functools.partial(finish, width * peers),
         (shape((1, heads), F32), shape((rows, out_cols), BF16)),
-        (peak, swapped(peak, "cp", steps[0]), mine, *others),
+        (peak, swapped(peak, "cp", steps[-1]), keep_near, got_near, *others),
         name="finish",
     )
     return (max_logits, kv_next[None])

time: 30 us -> 29.9 us (level)
  waiting for transfers between devices: 6.86 us -> 6.05 us
  starting transfers between devices: 15.7 us -> 16.2 us
    ppermute x1 -> x2, starting transfers between devices: 0.07 us -> 0.57 us  [to_other_core(): return lax.ppermute(block, 'tp', [(i, i ^ 1) for i in range(peers)])]
    ppermute x1 -> x2, waiting for transfers between devices: 0.86 us -> 0.41 us  [to_other_core(): return lax.ppermute(block, 'tp', [(i, i ^ 1) for i in range(peers)])]
    ppermute x5, waiting for transfers between devices: 4.56 us -> 4.21 us  [swapped(): lax.ppermute(block, axis, [(i, partner(i, step, size)) for i in range(siz...]
    pallas_call x12 -> x13, Pallas kernels: 5.76 us -> 5.93 us  [call(): pl.pallas_call(kernel, out_shape=outs, in_specs=specs or [WHOLE] * len(ar...]
  transfers between devices with their start and end apart: 10 -> 11, of which waited for: 4 -> 4; matrix products, arithmetic and copies ran while one was open for 0% -> 0% of each run, Pallas kernels for 17% -> 17%
where the time goes in v13:
time: 29.9 us; the launch traced here: 29.7 us
  starting transfers between devices  16.2 us (54%)
  waiting for transfers between devices  6.05 us (20%)
  Pallas kernels  5.93 us (20%)
  other arithmetic  0.78 us (3%)
  between operations  0.73 us (2%)
    ppermute x5, starting transfers between devices, swapped(): lax.ppermute(block, axis, [(i, partner(i, step, size)) for i in range(siz...  8.12 us
    pallas_call x13, Pallas kernels, call(): pl.pallas_call(kernel, out_shape=outs, in_specs=specs or [WHOLE] * len(ar...  5.93 us
    ppermute x3, starting transfers between devices, shifted(): lax.ppermute(block, axis, [((i - distance) % size, i) for i in range(size)])  5.9 us
    ppermute x5, waiting for transfers between devices, swapped(): lax.ppermute(block, axis, [(i, partner(i, step, size)) for i in range(siz...  4.21 us
    ppermute x1, starting transfers between devices, on_device(): lax.ppermute(block, 'tp', [(i, (i + 2 * (step + 1)) % peers) for i in ran...  1.58 us
    ppermute x3, waiting for transfers between devices, shifted(): lax.ppermute(block, axis, [((i - distance) % size, i) for i in range(size)])  1.43 us
    concatenate x1, other arithmetic, on_device(): pair_here = jnp.concatenate([key_vectors[0], value_vectors[0]], axis=1)  0.78 us
  transfers between devices with their start and end apart: 11, of which 4 were waited for; matrix products, arithmetic and copies ran while one was open for 0% of the time, Pallas kernels for 17%

profile of v13, /device:TPU:0, one launch (start us, length us, event | category | flops | bytes accessed | tf_op | source)
XLA Modules:
  0.0 29.7 jit_solution(9403805728583435196)
XLA Ops:
  0.6 0.8 %pad_maximum_fusion.here_ref.block_ref = bf16[128,256]{1,0:T(8,128)(2,1)S(1)} fusion(bf16[128,128]{1,0:T(8,128)(2,1)} %bitcast.5, bf16[128,128]{1,0:T(8,128)(2,1)} %bitcast.6), kind=kLoop, calls=%fused_computation | loop fusion | flops 131072 | bytes 131072 | tf_op jit(solution)/shard_map/concatenate | solution.py:314
  1.4 3.0 %collective-permute-start = (bf16[128,256]{1,0:T(8,128)(2,1)S(1)}, bf16[128,256]{1,0:T(8,128)(2,1)S(1)}, u32[]{:S(2)}, u32[]{:S(2)}) collective-permute-start(bf16[128,256]{1,0:T(8,128)(2,1)S(1)} %pad_maximum_fusion.here_ref.block_ref), channel_id=1, source_target_pairs={{16,0},{0,16},{17,1},{1,17},{18,2},{2,18},{19,3},{3,19},{20,4},{4,... | collective-permute-start | bytes 196616 | tf_op jit(solution)/shard_map/ppermute | solution.py:62
  4.5 1.0 %collective-permute-start.4 = (bf16[128,1024]{1,0:T(8,128)(2,1)S(1)}, bf16[128,1024]{1,0:T(8,128)(2,1)S(1)}, u32[]{:S(2)}, u32[]{:S(2)}) collective-permute-start(bf16[128,1024]{1,0:T(8,128)(2,1)S(1)} %take.2), channel_id=1, source_target_pairs={{16,0},{0,16},{17,1},{1,17},{18,2},{2,18},{19,3},{3,19},{20,4},{4,... | collective-permute-start | bytes 786440 | tf_op jit(solution)/shard_map/ppermute | solution.py:62
  5.5 1.4 %collective-permute-done.pair_ref = bf16[128,256]{1,0:T(8,128)(2,1)S(1)} collective-permute-done((bf16[128,256]{1,0:T(8,128)(2,1)S(1)}, bf16[128,256]{1,0:T(8,128)(2,1)S(1)}, u32[]{:S(2)}, u32[]{:S(2)}) %collective-permute-start) | collective-permute-done | bytes 65568 | tf_op jit(solution)/shard_map/ppermute | solution.py:62
  6.9 0.0 copy-start
  6.9 0.0 copy-start.2
  7.0 4.5 %collective-permute-start.1 = (bf16[128,384]{1,0:T(8,128)(2,1)S(1)}, bf16[128,384]{1,0:T(8,128)(2,1)S(1)}, u32[]{:S(2)}, u32[]{:S(2)}) collective-permute-start(bf16[128,384]{1,0:T(8,128)(2,1)S(1)} %join.1.refs_3_.after), channel_id=1, source_target_pairs={{0,12},{4,8},{8,4},{12,0},{1,13},{5,9},{9,5},{13,1},{2,14},{6,10},... | collective-permute-start | bytes 294920 | tf_op jit(solution)/shard_map/ppermute | solution.py:57
  11.4 0.6 %collective-permute-start.3 = (bf16[128,384]{1,0:T(8,128)(2,1)S(1)}, bf16[128,384]{1,0:T(8,128)(2,1)S(1)}, u32[]{:S(2)}, u32[]{:S(2)}) collective-permute-start(bf16[128,384]{1,0:T(8,128)(2,1)S(1)} %join.1.refs_3_.after), channel_id=1, source_target_pairs={{0,4},{4,0},{8,12},{12,8},{1,5},{5,1},{9,13},{13,9},{2,6},{6,2},{1... | collective-permute-start | bytes 294920 | tf_op jit(solution)/shard_map/ppermute | solution.py:57
  12.1 0.6 %prepare.1.feature_ref = bf16[2,128,512]{2,1,0:T(8,128)(2,1)S(1)} custom-call(s32[8]{0:T(128)S(1)} %copy-done.3, f32[8,128]{1,0:T(8,128)S(1)} %touch.1.after), custom_call_target="tpu_custom_call" | custom-call | flops 3000000000 | tf_op jit(solution)/shard_map/prepare/pallas_call | solution.py:24
  12.7 1.9 %collective-permute-start.6 = (bf16[128,1024]{1,0:T(8,128)(2,1)S(1)}, bf16[128,1024]{1,0:T(8,128)(2,1)S(1)}, u32[]{:S(2)}, u32[]{:S(2)}) collective-permute-start(bf16[128,1024]{1,0:T(8,128)(2,1)S(1)} %take.3), channel_id=1, source_target_pairs={{16,0},{0,16},{17,1},{1,17},{18,2},{2,18},{19,3},{3,19},{20,4},{4,... | collective-permute-start | bytes 786440 | tf_op jit(solution)/shard_map/ppermute | solution.py:62
  14.6 0.9 %weigh.1.w_ref = bf16[2048,1024]{1,0:T(8,128)(2,1)S(1)} custom-call(bf16[2048,1024]{1,0:T(8,128)(2,1)S(1)} %bitcast.4, bf16[1,2048]{1,0:T(2,128)(2,1)S(1)} %copy-done.2, bf16[128,384]{1,0:T(8,128)(2,1)S(1)} %collective-permute-done.1.after.refs_0_), custom_call_target="tpu_custom_call" | custom-call | flops 1000000000 | tf_op jit(solution)/shard_map/weigh/pallas_call | solution.py:24
  15.5 2.6 %collective-permute-done.2.refs_1_ = bf16[128,384]{1,0:T(8,128)(2,1)S(1)} collective-permute-done((bf16[128,384]{1,0:T(8,128)(2,1)S(1)}, bf16[128,384]{1,0:T(8,128)(2,1)S(1)}, u32[]{:S(2)}, u32[]{:S(2)}) %collective-permute-start.2) | collective-permute-done | bytes 98336 | tf_op jit(solution)/shard_map/ppermute | solution.py:57
  18.1 1.5 %attend_first.1 = (bf16[1,2,256,512]{3,2,1,0:T(8,128)(2,1)S(1)}, bf16[1,512,256]{2,1,0:T(8,128)(2,1)S(1)}, bf16[128,1024]{1,0:T(8,128)(2,1)S(1)}, f32[1,16]{1,0:T(1,128)S(1)}) custom-call(bf16[2048,1024]{1,0:T(8,128)(2,1)S(1)} %weigh.1.w_ref, bf16[2,128,512]{2,1,0:T(8,128)(2,1)S(1)} %prepare.1.feature_ref, ...), custom_call_target="tpu_custom_call" | custom-call | flops 2000000000 | tf_op jit(solution)/shard_map/attend_first/pallas_call | solution.py:24
  19.7 0.5 %collective-permute-start.5 = (f32[1,16]{1,0:T(1,128)S(1)}, f32[1,16]{1,0:T(1,128)S(1)}, u32[]{:S(2)}, u32[]{:S(2)}) collective-permute-start(f32[1,16]{1,0:T(1,128)S(1)} %get-tuple-element.12.left_ref), channel_id=1, source_target_pairs={{0,4},{4,0},{8,12},{12,8},{1,5},{5,1},{9,13},{13,9},{2,6},{6,2},{1... | collective-permute-start | bytes 200 | tf_op jit(solution)/shard_map/ppermute | solution.py:57
  20.1 1.3 %attend_last.1 = (bf16[128,1024]{1,0:T(8,128)(2,1)S(1)}, bf16[1,144,256]{2,1,0:T(8,128)(2,1)S(1)}, bf16[1,144,256]{2,1,0:T(8,128)(2,1)S(1)}, f32[128,128]{1,0:T(8,128)S(1)}) custom-call(bf16[128,1024]{1,0:T(8,128)(2,1)S(1)} %collective-permute-done.6.q_ref, bf16[1,2,256,512]{3,2,1,0:T(8,128)(2,1)S(1)} %get-tuple-element.13.kt_ref, ...), custom_call_target="tpu_custom_call" | custom-call | flops 1500000000 | tf_op jit(solution)/shard_map/attend_last/pallas_call | solution.py:24
  21.5 0.1 collective-permute-start.9
  21.6 0.5 %collective-permute-start.8 = (bf16[1,144,256]{2,1,0:T(8,128)(2,1)S(1)}, bf16[1,144,256]{2,1,0:T(8,128)(2,1)S(1)}, u32[]{:S(2)}, u32[]{:S(2)}) collective-permute-start(bf16[1,144,256]{2,1,0:T(8,128)(2,1)S(1)} %get-tuple-element.19), channel_id=1, source_target_pairs={{0,1},{1,0},{2,3},{3,2},{4,5},{5,4},{6,7},{7,6},{8,9},{9,8},{10,11... | collective-permute-start | bytes 221192 | tf_op jit(solution)/shard_map/ppermute | solution.py:375
  22.1 0.3 %project_keep.3.keep_ref = bf16[1,144,256]{2,1,0:T(8,128)(2,1)S(1)} custom-call(bf16[128,1024]{1,0:T(8,128)(2,1)S(1)} %get-tuple-element.15.first_ref, bf16[128,1024]{1,0:T(8,128)(2,1)S(1)} %get-tuple-element.17.last_ref, bf16[2048,1024]{1,0:T(8,128)(2,1)S(1)} %weigh.1.w_ref, f32[128,128]{1,0:T(8,128)S(1)} %get-tuple-element.18.square_ref), custom_call_target="tpu_custom_call" | custom-call | flops 3000000000 | tf_op jit(solution)/shard_map/project_keep/pallas_call | solution.py:24
  22.4 0.4 %collective-permute-done.9.got_ref = bf16[1,144,256]{2,1,0:T(8,128)(2,1)S(1)} collective-permute-done((bf16[1,144,256]{2,1,0:T(8,128)(2,1)S(1)}, bf16[1,144,256]{2,1,0:T(8,128)(2,1)S(1)}, u32[]{:S(2)}, u32[]{:S(2)}) %collective-permute-start.9) | collective-permute-done | bytes 73760 | tf_op jit(solution)/shard_map/ppermute | solution.py:375
  22.8 1.6 %collective-permute-start.10 = (bf16[144,256]{1,0:T(8,128)(2,1)S(1)}, bf16[144,256]{1,0:T(8,128)(2,1)S(1)}, u32[]{:S(2)}, u32[]{:S(2)}) collective-permute-start(bf16[144,256]{1,0:T(8,128)(2,1)S(1)} %merge.1), channel_id=1, source_target_pairs={{0,2},{1,3},{2,0},{3,1},{4,6},{5,7},{6,4},{7,5},{8,10},{9,11},{10,... | collective-permute-start | bytes 221192 | tf_op jit(solution)/shard_map/ppermute | solution.py:412
  24.4 2.5 %collective-permute-start.7 = (f32[1,16]{1,0:T(1,128)S(1)}, f32[1,16]{1,0:T(1,128)S(1)}, u32[]{:S(2)}, u32[]{:S(2)}) collective-permute-start(f32[1,16]{1,0:T(1,128)S(1)} %larger.1.peak_ref), channel_id=1, source_target_pairs={{0,8},{4,12},{8,0},{12,4},{1,9},{5,13},{9,1},{13,5},{2,10},{6,14},... | collective-permute-start | bytes 200 | tf_op jit(solution)/shard_map/ppermute | solution.py:57
  26.9 0.3 %project_keep.2.keep_ref = bf16[1,144,256]{2,1,0:T(8,128)(2,1)S(1)} custom-call(bf16[128,1024]{1,0:T(8,128)(2,1)S(1)} %get-tuple-element.15.first_ref, bf16[128,1024]{1,0:T(8,128)(2,1)S(1)} %get-tuple-element.17.last_ref, bf16[2048,1024]{1,0:T(8,128)(2,1)S(1)} %weigh.1.w_ref, f32[128,128]{1,0:T(8,128)S(1)} %get-tuple-element.18.square_ref), custom_call_target="tpu_custom_call" | custom-call | tf_op jit(solution)/shard_map/project_keep/pallas_call | solution.py:24
  27.3 1.6 %collective-permute-done.7.peak_got = f32[1,16]{1,0:T(1,128)S(1)} collective-permute-done((f32[1,16]{1,0:T(1,128)S(1)}, f32[1,16]{1,0:T(1,128)S(1)}, u32[]{:S(2)}, u32[]{:S(2)}) %collective-permute-start.7) | collective-permute-done | bytes 96 | tf_op jit(solution)/shard_map/ppermute | solution.py:57
  28.9 0.8 %finish.1 = (f32[1,16]{1,0:T(1,128)}, bf16[128,256]{1,0:T(8,128)(2,1)}) custom-call(f32[1,16]{1,0:T(1,128)S(1)} %larger.1.peak_ref, f32[1,16]{1,0:T(1,128)S(1)} %collective-permute-done.7.peak_got, bf16[1,144,256]{2,1,0:T(8,128)(2,1)S(1)} %project_keep.2.keep_ref, bf16[1,144,256]{2,1,0:T(8,128)(2,1)S(1)} %collective-permute-done.8.got_ref, ...), custom_call_target="tpu_custom_call" | custom-call | tf_op jit(solution)/shard_map/finish/pallas_call | solution.py:24
  (20 shorter events, 0.1 us)
Async XLA Ops:
  1.4 3.0 %copy-start.1 = (bf16[1,128,2048]{2,1,0:T(8,128)(2,1)S(1)}, bf16[1,128,2048]{2,1,0:T(8,128)(2,1)}, u32[]{:S(2)}) copy-start(bf16[1,128,2048]{2,1,0:T(8,128)(2,1)} %q_ref.3) | copy-start | bytes 1572868
  1.4 5.5 %collective-permute-start = (bf16[128,256]{1,0:T(8,128)(2,1)S(1)}, bf16[128,256]{1,0:T(8,128)(2,1)S(1)}, u32[]{:S(2)}, u32[]{:S(2)}) collective-permute-start(bf16[128,256]{1,0:T(8,128)(2,1)S(1)} %pad_maximum_fusion.here_ref.block_ref), channel_id=1, source_target_pairs={{16,0},{0,16},{17,1},{1,17},{18,2},{2,18},{19,3},{3,19},{20,4},{4,... | collective-permute-start | bytes 196616 | tf_op jit(solution)/shard_map/ppermute | solution.py:62
  4.4 7.7 %copy-start.3 = (s32[8]{0:T(128)S(1)}, s32[8]{0:T(128)}, u32[]{:S(2)}) copy-start(s32[8]{0:T(128)} %order_ref.1) | copy-start | bytes 100
  4.5 13.7 %collective-permute-start.4 = (bf16[128,1024]{1,0:T(8,128)(2,1)S(1)}, bf16[128,1024]{1,0:T(8,128)(2,1)S(1)}, u32[]{:S(2)}, u32[]{:S(2)}) collective-permute-start(bf16[128,1024]{1,0:T(8,128)(2,1)S(1)} %take.2), channel_id=1, source_target_pairs={{16,0},{0,16},{17,1},{1,17},{18,2},{2,18},{19,3},{3,19},{20,4},{4,... | collective-permute-start | bytes 786440 | tf_op jit(solution)/shard_map/ppermute | solution.py:62
  6.9 7.7 %copy-start = (bf16[1,2048,1024]{2,1,0:T(8,128)(2,1)S(1)}, bf16[1,2048,1024]{2,1,0:T(8,128)(2,1)}, u32[]{:S(2)}) copy-start(bf16[1,2048,1024]{2,1,0:T(8,128)(2,1)} %param.11) | copy-start | bytes 12582916
  6.9 7.7 %copy-start.2 = (bf16[1,2048]{1,0:T(2,128)(2,1)S(1)}, bf16[1,2048]{1,0:T(2,128)(2,1)}, u32[]{:S(2)}) copy-start(bf16[1,2048]{1,0:T(2,128)(2,1)} %gain_ref.1) | copy-start | bytes 12292
  7.0 7.7 %collective-permute-start.1 = (bf16[128,384]{1,0:T(8,128)(2,1)S(1)}, bf16[128,384]{1,0:T(8,128)(2,1)S(1)}, u32[]{:S(2)}, u32[]{:S(2)}) collective-permute-start(bf16[128,384]{1,0:T(8,128)(2,1)S(1)} %join.1.refs_3_.after), channel_id=1, source_target_pairs={{0,12},{4,8},{8,4},{12,0},{1,13},{5,9},{9,5},{13,1},{2,14},{6,10},... | collective-permute-start | bytes 294920 | tf_op jit(solution)/shard_map/ppermute | solution.py:57
  11.4 6.7 %collective-permute-start.2 = (bf16[128,384]{1,0:T(8,128)(2,1)S(1)}, bf16[128,384]{1,0:T(8,128)(2,1)S(1)}, u32[]{:S(2)}, u32[]{:S(2)}) collective-permute-start(bf16[128,384]{1,0:T(8,128)(2,1)S(1)} %join.1.refs_3_.after), channel_id=1, source_target_pairs={{0,8},{4,12},{8,0},{12,4},{1,9},{5,13},{9,1},{13,5},{2,10},{6,14},... | collective-permute-start | bytes 294920 | tf_op jit(solution)/shard_map/ppermute | solution.py:57
  11.4 6.7 %collective-permute-start.3 = (bf16[128,384]{1,0:T(8,128)(2,1)S(1)}, bf16[128,384]{1,0:T(8,128)(2,1)S(1)}, u32[]{:S(2)}, u32[]{:S(2)}) collective-permute-start(bf16[128,384]{1,0:T(8,128)(2,1)S(1)} %join.1.refs_3_.after), channel_id=1, source_target_pairs={{0,4},{4,0},{8,12},{12,8},{1,5},{5,1},{9,13},{13,9},{2,6},{6,2},{1... | collective-permute-start | bytes 294920 | tf_op jit(solution)/shard_map/ppermute | solution.py:57
  12.7 7.4 %collective-permute-start.6 = (bf16[128,1024]{1,0:T(8,128)(2,1)S(1)}, bf16[128,1024]{1,0:T(8,128)(2,1)S(1)}, u32[]{:S(2)}, u32[]{:S(2)}) collective-permute-start(bf16[128,1024]{1,0:T(8,128)(2,1)S(1)} %take.3), channel_id=1, source_target_pairs={{16,0},{0,16},{17,1},{1,17},{18,2},{2,18},{19,3},{3,19},{20,4},{4,... | collective-permute-start | bytes 786440 | tf_op jit(solution)/shard_map/ppermute | solution.py:62
  19.7 4.8 %collective-permute-start.5 = (f32[1,16]{1,0:T(1,128)S(1)}, f32[1,16]{1,0:T(1,128)S(1)}, u32[]{:S(2)}, u32[]{:S(2)}) collective-permute-start(f32[1,16]{1,0:T(1,128)S(1)} %get-tuple-element.12.left_ref), channel_id=1, source_target_pairs={{0,4},{4,0},{8,12},{12,8},{1,5},{5,1},{9,13},{13,9},{2,6},{6,2},{1... | collective-permute-start | bytes 200 | tf_op jit(solution)/shard_map/ppermute | solution.py:57
  21.5 1.3 %collective-permute-start.9 = (bf16[1,144,256]{2,1,0:T(8,128)(2,1)S(1)}, bf16[1,144,256]{2,1,0:T(8,128)(2,1)S(1)}, u32[]{:S(2)}, u32[]{:S(2)}) collective-permute-start(bf16[1,144,256]{2,1,0:T(8,128)(2,1)S(1)} %get-tuple-element.16.after), channel_id=1, source_target_pairs={{0,1},{1,0},{2,3},{3,2},{4,5},{5,4},{6,7},{7,6},{8,9},{9,8},{10,11... | collective-permute-start | bytes 221192 | tf_op jit(solution)/shard_map/ppermute | solution.py:375
  21.6 7.3 %collective-permute-start.8 = (bf16[1,144,256]{2,1,0:T(8,128)(2,1)S(1)}, bf16[1,144,256]{2,1,0:T(8,128)(2,1)S(1)}, u32[]{:S(2)}, u32[]{:S(2)}) collective-permute-start(bf16[1,144,256]{2,1,0:T(8,128)(2,1)S(1)} %get-tuple-element.19), channel_id=1, source_target_pairs={{0,1},{1,0},{2,3},{3,2},{4,5},{5,4},{6,7},{7,6},{8,9},{9,8},{10,11... | collective-permute-start | bytes 221192 | tf_op jit(solution)/shard_map/ppermute | solution.py:375
  22.8 6.0 %collective-permute-start.10 = (bf16[144,256]{1,0:T(8,128)(2,1)S(1)}, bf16[144,256]{1,0:T(8,128)(2,1)S(1)}, u32[]{:S(2)}, u32[]{:S(2)}) collective-permute-start(bf16[144,256]{1,0:T(8,128)(2,1)S(1)} %merge.1), channel_id=1, source_target_pairs={{0,2},{1,3},{2,0},{3,1},{4,6},{5,7},{6,4},{7,5},{8,10},{9,11},{10,... | collective-permute-start | bytes 221192 | tf_op jit(solution)/shard_map/ppermute | solution.py:412
  24.4 4.4 %collective-permute-start.7 = (f32[1,16]{1,0:T(1,128)S(1)}, f32[1,16]{1,0:T(1,128)S(1)}, u32[]{:S(2)}, u32[]{:S(2)}) collective-permute-start(f32[1,16]{1,0:T(1,128)S(1)} %larger.1.peak_ref), channel_id=1, source_target_pairs={{0,8},{4,12},{8,0},{12,4},{1,9},{5,13},{9,1},{13,5},{2,10},{6,14},... | collective-permute-start | bytes 200 | tf_op jit(solution)/shard_map/ppermute | solution.py:57

commit v14 on v13

--- a/solution.py
+++ b/solution.py
@@ -313,7 +313,7 @@
 
     pair_here = jnp.concatenate([key_vectors[0], value_vectors[0]], axis=1)
     pair = shifted(pair_here, "pp", 1)
-    cut = heads // 2
+    cut = heads * 3 // 8
     counts = [cut, heads - cut]
     starts = [0, cut]
     crossed = []

time: 29.9 us -> 29.8 us (level)
  no operation moved by 1% of the time
where the time goes in v14:
time: 29.8 us; the launch traced here: 29.6 us
  starting transfers between devices  16.2 us (54%)
  waiting for transfers between devices  6.02 us (20%)
  Pallas kernels  5.89 us (20%)
  other arithmetic  0.78 us (3%)
  between operations  0.75 us (3%)
    ppermute x5, starting transfers between devices, swapped(): lax.ppermute(block, axis, [(i, partner(i, step, size)) for i in range(siz...  8.13 us
    ppermute x3, starting transfers between devices, shifted(): lax.ppermute(block, axis, [((i - distance) % size, i) for i in range(size)])  5.9 us
    pallas_call x13, Pallas kernels, call(): pl.pallas_call(kernel, out_shape=outs, in_specs=specs or [WHOLE] * len(ar...  5.89 us
    ppermute x5, waiting for transfers between devices, swapped(): lax.ppermute(block, axis, [(i, partner(i, step, size)) for i in range(siz...  4.16 us
    ppermute x1, starting transfers between devices, on_device(): lax.ppermute(block, 'tp', [(i, (i + 2 * (step + 1)) % peers) for i in ran...  1.59 us
    ppermute x3, waiting for transfers between devices, shifted(): lax.ppermute(block, axis, [((i - distance) % size, i) for i in range(size)])  1.43 us
    concatenate x1, other arithmetic, on_device(): pair_here = jnp.concatenate([key_vectors[0], value_vectors[0]], axis=1)  0.78 us
  transfers between devices with their start and end apart: 11, of which 4 were waited for; matrix products, arithmetic and copies ran while one was open for 0% of the time, Pallas kernels for 17%

profile of v14, /device:TPU:0, one launch (start us, length us, event | category | flops | bytes accessed | tf_op | source)
XLA Modules:
  0.0 29.6 jit_solution(16591915215982405997)
XLA Ops:
  0.6 0.8 %pad_maximum_fusion.here_ref.block_ref = bf16[128,256]{1,0:T(8,128)(2,1)S(1)} fusion(bf16[128,128]{1,0:T(8,128)(2,1)} %bitcast.5, bf16[128,128]{1,0:T(8,128)(2,1)} %bitcast.6), kind=kLoop, calls=%fused_computation | loop fusion | flops 131072 | bytes 131072 | tf_op jit(solution)/shard_map/concatenate | solution.py:314
  1.4 3.0 %collective-permute-start = (bf16[128,256]{1,0:T(8,128)(2,1)S(1)}, bf16[128,256]{1,0:T(8,128)(2,1)S(1)}, u32[]{:S(2)}, u32[]{:S(2)}) collective-permute-start(bf16[128,256]{1,0:T(8,128)(2,1)S(1)} %pad_maximum_fusion.here_ref.block_ref), channel_id=1, source_target_pairs={{16,0},{0,16},{17,1},{1,17},{18,2},{2,18},{19,3},{3,19},{20,4},{4,... | collective-permute-start | bytes 196616 | tf_op jit(solution)/shard_map/ppermute | solution.py:62
  4.4 1.0 %collective-permute-start.4 = (bf16[128,768]{1,0:T(8,128)(2,1)S(1)}, bf16[128,768]{1,0:T(8,128)(2,1)S(1)}, u32[]{:S(2)}, u32[]{:S(2)}) collective-permute-start(bf16[128,768]{1,0:T(8,128)(2,1)S(1)} %take.2), channel_id=1, source_target_pairs={{16,0},{0,16},{17,1},{1,17},{18,2},{2,18},{19,3},{3,19},{20,4},{4,... | collective-permute-start | bytes 589832 | tf_op jit(solution)/shard_map/ppermute | solution.py:62
  5.5 1.4 %collective-permute-done.pair_ref = bf16[128,256]{1,0:T(8,128)(2,1)S(1)} collective-permute-done((bf16[128,256]{1,0:T(8,128)(2,1)S(1)}, bf16[128,256]{1,0:T(8,128)(2,1)S(1)}, u32[]{:S(2)}, u32[]{:S(2)}) %collective-permute-start) | collective-permute-done | bytes 65568 | tf_op jit(solution)/shard_map/ppermute | solution.py:62
  6.9 4.5 %collective-permute-start.1 = (bf16[128,384]{1,0:T(8,128)(2,1)S(1)}, bf16[128,384]{1,0:T(8,128)(2,1)S(1)}, u32[]{:S(2)}, u32[]{:S(2)}) collective-permute-start(bf16[128,384]{1,0:T(8,128)(2,1)S(1)} %join.1.refs_3_.after), channel_id=1, source_target_pairs={{0,12},{4,8},{8,4},{12,0},{1,13},{5,9},{9,5},{13,1},{2,14},{6,10},... | collective-permute-start | bytes 294920 | tf_op jit(solution)/shard_map/ppermute | solution.py:57
  11.4 0.6 %collective-permute-start.3 = (bf16[128,384]{1,0:T(8,128)(2,1)S(1)}, bf16[128,384]{1,0:T(8,128)(2,1)S(1)}, u32[]{:S(2)}, u32[]{:S(2)}) collective-permute-start(bf16[128,384]{1,0:T(8,128)(2,1)S(1)} %join.1.refs_3_.after), channel_id=1, source_target_pairs={{0,4},{4,0},{8,12},{12,8},{1,5},{5,1},{9,13},{13,9},{2,6},{6,2},{1... | collective-permute-start | bytes 294920 | tf_op jit(solution)/shard_map/ppermute | solution.py:57
  12.1 0.0 copy-start
  12.1 0.0 copy-start.2
  12.1 1.9 %collective-permute-start.6 = (bf16[128,1280]{1,0:T(8,128)(2,1)S(1)}, bf16[128,1280]{1,0:T(8,128)(2,1)S(1)}, u32[]{:S(2)}, u32[]{:S(2)}) collective-permute-start(bf16[128,1280]{1,0:T(8,128)(2,1)S(1)} %take.3), channel_id=1, source_target_pairs={{16,0},{0,16},{17,1},{1,17},{18,2},{2,18},{19,3},{3,19},{20,4},{4,... | collective-permute-start | bytes 983048 | tf_op jit(solution)/shard_map/ppermute | solution.py:62
  14.0 0.6 %prepare.1.feature_ref = bf16[2,128,512]{2,1,0:T(8,128)(2,1)S(1)} custom-call(s32[8]{0:T(128)S(1)} %copy-done.3, f32[8,128]{1,0:T(8,128)S(1)} %touch.1.after), custom_call_target="tpu_custom_call" | custom-call | flops 3000000000 | tf_op jit(solution)/shard_map/prepare/pallas_call | solution.py:24
  14.6 0.9 %weigh.1.w_ref = bf16[2048,1024]{1,0:T(8,128)(2,1)S(1)} custom-call(bf16[2048,1024]{1,0:T(8,128)(2,1)S(1)} %bitcast.4, bf16[1,2048]{1,0:T(2,128)(2,1)S(1)} %copy-done.2, bf16[128,384]{1,0:T(8,128)(2,1)S(1)} %collective-permute-done.1.after.refs_0_), custom_call_target="tpu_custom_call" | custom-call | flops 1000000000 | tf_op jit(solution)/shard_map/weigh/pallas_call | solution.py:24
  15.5 2.6 %collective-permute-done.2.refs_1_ = bf16[128,384]{1,0:T(8,128)(2,1)S(1)} collective-permute-done((bf16[128,384]{1,0:T(8,128)(2,1)S(1)}, bf16[128,384]{1,0:T(8,128)(2,1)S(1)}, u32[]{:S(2)}, u32[]{:S(2)}) %collective-permute-start.2) | collective-permute-done | bytes 98336 | tf_op jit(solution)/shard_map/ppermute | solution.py:57
  18.1 1.4 %attend_first.1 = (bf16[1,2,256,512]{3,2,1,0:T(8,128)(2,1)S(1)}, bf16[1,512,256]{2,1,0:T(8,128)(2,1)S(1)}, bf16[128,768]{1,0:T(8,128)(2,1)S(1)}, f32[1,16]{1,0:T(1,128)S(1)}) custom-call(bf16[2048,1024]{1,0:T(8,128)(2,1)S(1)} %weigh.1.w_ref, bf16[2,128,512]{2,1,0:T(8,128)(2,1)S(1)} %prepare.1.feature_ref, ...), custom_call_target="tpu_custom_call" | custom-call | flops 2000000000 | tf_op jit(solution)/shard_map/attend_first/pallas_call | solution.py:24
  19.5 0.5 %collective-permute-start.5 = (f32[1,16]{1,0:T(1,128)S(1)}, f32[1,16]{1,0:T(1,128)S(1)}, u32[]{:S(2)}, u32[]{:S(2)}) collective-permute-start(f32[1,16]{1,0:T(1,128)S(1)} %get-tuple-element.12.left_ref), channel_id=1, source_target_pairs={{0,4},{4,0},{8,12},{12,8},{1,5},{5,1},{9,13},{13,9},{2,6},{6,2},{1... | collective-permute-start | bytes 200 | tf_op jit(solution)/shard_map/ppermute | solution.py:57
  20.0 1.4 %attend_last.1 = (bf16[128,1280]{1,0:T(8,128)(2,1)S(1)}, bf16[1,144,256]{2,1,0:T(8,128)(2,1)S(1)}, bf16[1,144,256]{2,1,0:T(8,128)(2,1)S(1)}, f32[128,128]{1,0:T(8,128)S(1)}) custom-call(bf16[128,1280]{1,0:T(8,128)(2,1)S(1)} %collective-permute-done.6.q_ref, bf16[1,2,256,512]{3,2,1,0:T(8,128)(2,1)S(1)} %get-tuple-element.13.kt_ref, ...), custom_call_target="tpu_custom_call" | custom-call | flops 1500000000 | tf_op jit(solution)/shard_map/attend_last/pallas_call | solution.py:24
  21.4 0.1 collective-permute-start.9
  21.5 0.5 %collective-permute-start.8 = (bf16[1,144,256]{2,1,0:T(8,128)(2,1)S(1)}, bf16[1,144,256]{2,1,0:T(8,128)(2,1)S(1)}, u32[]{:S(2)}, u32[]{:S(2)}) collective-permute-start(bf16[1,144,256]{2,1,0:T(8,128)(2,1)S(1)} %get-tuple-element.19), channel_id=1, source_target_pairs={{0,1},{1,0},{2,3},{3,2},{4,5},{5,4},{6,7},{7,6},{8,9},{9,8},{10,11... | collective-permute-start | bytes 221192 | tf_op jit(solution)/shard_map/ppermute | solution.py:375
  22.0 0.3 %project_keep.3.keep_ref = bf16[1,144,256]{2,1,0:T(8,128)(2,1)S(1)} custom-call(bf16[128,768]{1,0:T(8,128)(2,1)S(1)} %get-tuple-element.15.first_ref, bf16[128,1280]{1,0:T(8,128)(2,1)S(1)} %get-tuple-element.17.last_ref, bf16[2048,1024]{1,0:T(8,128)(2,1)S(1)} %weigh.1.w_ref, f32[128,128]{1,0:T(8,128)S(1)} %get-tuple-element.18.square_ref), custom_call_target="tpu_custom_call" | custom-call | flops 3000000000 | tf_op jit(solution)/shard_map/project_keep/pallas_call | solution.py:24
  22.3 0.4 %collective-permute-done.9.got_ref = bf16[1,144,256]{2,1,0:T(8,128)(2,1)S(1)} collective-permute-done((bf16[1,144,256]{2,1,0:T(8,128)(2,1)S(1)}, bf16[1,144,256]{2,1,0:T(8,128)(2,1)S(1)}, u32[]{:S(2)}, u32[]{:S(2)}) %collective-permute-start.9) | collective-permute-done | bytes 73760 | tf_op jit(solution)/shard_map/ppermute | solution.py:375
  22.8 1.6 %collective-permute-start.10 = (bf16[144,256]{1,0:T(8,128)(2,1)S(1)}, bf16[144,256]{1,0:T(8,128)(2,1)S(1)}, u32[]{:S(2)}, u32[]{:S(2)}) collective-permute-start(bf16[144,256]{1,0:T(8,128)(2,1)S(1)} %merge.1), channel_id=1, source_target_pairs={{0,2},{1,3},{2,0},{3,1},{4,6},{5,7},{6,4},{7,5},{8,10},{9,11},{10,... | collective-permute-start | bytes 221192 | tf_op jit(solution)/shard_map/ppermute | solution.py:412
  24.4 2.5 %collective-permute-start.7 = (f32[1,16]{1,0:T(1,128)S(1)}, f32[1,16]{1,0:T(1,128)S(1)}, u32[]{:S(2)}, u32[]{:S(2)}) collective-permute-start(f32[1,16]{1,0:T(1,128)S(1)} %larger.1.peak_ref), channel_id=1, source_target_pairs={{0,8},{4,12},{8,0},{12,4},{1,9},{5,13},{9,1},{13,5},{2,10},{6,14},... | collective-permute-start | bytes 200 | tf_op jit(solution)/shard_map/ppermute | solution.py:57
  26.9 0.3 %project_keep.2.keep_ref = bf16[1,144,256]{2,1,0:T(8,128)(2,1)S(1)} custom-call(bf16[128,768]{1,0:T(8,128)(2,1)S(1)} %get-tuple-element.15.first_ref, bf16[128,1280]{1,0:T(8,128)(2,1)S(1)} %get-tuple-element.17.last_ref, bf16[2048,1024]{1,0:T(8,128)(2,1)S(1)} %weigh.1.w_ref, f32[128,128]{1,0:T(8,128)S(1)} %get-tuple-element.18.square_ref), custom_call_target="tpu_custom_call" | custom-call | tf_op jit(solution)/shard_map/project_keep/pallas_call | solution.py:24
  27.2 1.6 %collective-permute-done.7.peak_got = f32[1,16]{1,0:T(1,128)S(1)} collective-permute-done((f32[1,16]{1,0:T(1,128)S(1)}, f32[1,16]{1,0:T(1,128)S(1)}, u32[]{:S(2)}, u32[]{:S(2)}) %collective-permute-start.7) | collective-permute-done | bytes 96 | tf_op jit(solution)/shard_map/ppermute | solution.py:57
  28.8 0.8 %finish.1 = (f32[1,16]{1,0:T(1,128)}, bf16[128,256]{1,0:T(8,128)(2,1)}) custom-call(f32[1,16]{1,0:T(1,128)S(1)} %larger.1.peak_ref, f32[1,16]{1,0:T(1,128)S(1)} %collective-permute-done.7.peak_got, bf16[1,144,256]{2,1,0:T(8,128)(2,1)S(1)} %project_keep.2.keep_ref, bf16[1,144,256]{2,1,0:T(8,128)(2,1)S(1)} %collective-permute-done.8.got_ref, ...), custom_call_target="tpu_custom_call" | custom-call | tf_op jit(solution)/shard_map/finish/pallas_call | solution.py:24
  (20 shorter events, 0.1 us)
Async XLA Ops:
  1.4 3.0 %copy-start.1 = (bf16[1,128,2048]{2,1,0:T(8,128)(2,1)S(1)}, bf16[1,128,2048]{2,1,0:T(8,128)(2,1)}, u32[]{:S(2)}) copy-start(bf16[1,128,2048]{2,1,0:T(8,128)(2,1)} %q_ref.3) | copy-start | bytes 1572868
  1.4 5.5 %collective-permute-start = (bf16[128,256]{1,0:T(8,128)(2,1)S(1)}, bf16[128,256]{1,0:T(8,128)(2,1)S(1)}, u32[]{:S(2)}, u32[]{:S(2)}) collective-permute-start(bf16[128,256]{1,0:T(8,128)(2,1)S(1)} %pad_maximum_fusion.here_ref.block_ref), channel_id=1, source_target_pairs={{16,0},{0,16},{17,1},{1,17},{18,2},{2,18},{19,3},{3,19},{20,4},{4,... | collective-permute-start | bytes 196616 | tf_op jit(solution)/shard_map/ppermute | solution.py:62
  4.4 9.5 %copy-start.3 = (s32[8]{0:T(128)S(1)}, s32[8]{0:T(128)}, u32[]{:S(2)}) copy-start(s32[8]{0:T(128)} %order_ref.1) | copy-start | bytes 100
  4.4 13.6 %collective-permute-start.4 = (bf16[128,768]{1,0:T(8,128)(2,1)S(1)}, bf16[128,768]{1,0:T(8,128)(2,1)S(1)}, u32[]{:S(2)}, u32[]{:S(2)}) collective-permute-start(bf16[128,768]{1,0:T(8,128)(2,1)S(1)} %take.2), channel_id=1, source_target_pairs={{16,0},{0,16},{17,1},{1,17},{18,2},{2,18},{19,3},{3,19},{20,4},{4,... | collective-permute-start | bytes 589832 | tf_op jit(solution)/shard_map/ppermute | solution.py:62
  6.9 7.7 %collective-permute-start.1 = (bf16[128,384]{1,0:T(8,128)(2,1)S(1)}, bf16[128,384]{1,0:T(8,128)(2,1)S(1)}, u32[]{:S(2)}, u32[]{:S(2)}) collective-permute-start(bf16[128,384]{1,0:T(8,128)(2,1)S(1)} %join.1.refs_3_.after), channel_id=1, source_target_pairs={{0,12},{4,8},{8,4},{12,0},{1,13},{5,9},{9,5},{13,1},{2,14},{6,10},... | collective-permute-start | bytes 294920 | tf_op jit(solution)/shard_map/ppermute | solution.py:57
  11.4 6.7 %collective-permute-start.2 = (bf16[128,384]{1,0:T(8,128)(2,1)S(1)}, bf16[128,384]{1,0:T(8,128)(2,1)S(1)}, u32[]{:S(2)}, u32[]{:S(2)}) collective-permute-start(bf16[128,384]{1,0:T(8,128)(2,1)S(1)} %join.1.refs_3_.after), channel_id=1, source_target_pairs={{0,8},{4,12},{8,0},{12,4},{1,9},{5,13},{9,1},{13,5},{2,10},{6,14},... | collective-permute-start | bytes 294920 | tf_op jit(solution)/shard_map/ppermute | solution.py:57
  11.4 6.7 %collective-permute-start.3 = (bf16[128,384]{1,0:T(8,128)(2,1)S(1)}, bf16[128,384]{1,0:T(8,128)(2,1)S(1)}, u32[]{:S(2)}, u32[]{:S(2)}) collective-permute-start(bf16[128,384]{1,0:T(8,128)(2,1)S(1)} %join.1.refs_3_.after), channel_id=1, source_target_pairs={{0,4},{4,0},{8,12},{12,8},{1,5},{5,1},{9,13},{13,9},{2,6},{6,2},{1... | collective-permute-start | bytes 294920 | tf_op jit(solution)/shard_map/ppermute | solution.py:57
  12.1 2.5 %copy-start = (bf16[1,2048,1024]{2,1,0:T(8,128)(2,1)S(1)}, bf16[1,2048,1024]{2,1,0:T(8,128)(2,1)}, u32[]{:S(2)}) copy-start(bf16[1,2048,1024]{2,1,0:T(8,128)(2,1)} %param.11) | copy-start | bytes 12582916
  12.1 2.5 %copy-start.2 = (bf16[1,2048]{1,0:T(2,128)(2,1)S(1)}, bf16[1,2048]{1,0:T(2,128)(2,1)}, u32[]{:S(2)}) copy-start(bf16[1,2048]{1,0:T(2,128)(2,1)} %gain_ref.1) | copy-start | bytes 12292
  12.1 7.9 %collective-permute-start.6 = (bf16[128,1280]{1,0:T(8,128)(2,1)S(1)}, bf16[128,1280]{1,0:T(8,128)(2,1)S(1)}, u32[]{:S(2)}, u32[]{:S(2)}) collective-permute-start(bf16[128,1280]{1,0:T(8,128)(2,1)S(1)} %take.3), channel_id=1, source_target_pairs={{16,0},{0,16},{17,1},{1,17},{18,2},{2,18},{19,3},{3,19},{20,4},{4,... | collective-permute-start | bytes 983048 | tf_op jit(solution)/shard_map/ppermute | solution.py:62
  19.5 4.9 %collective-permute-start.5 = (f32[1,16]{1,0:T(1,128)S(1)}, f32[1,16]{1,0:T(1,128)S(1)}, u32[]{:S(2)}, u32[]{:S(2)}) collective-permute-start(f32[1,16]{1,0:T(1,128)S(1)} %get-tuple-element.12.left_ref), channel_id=1, source_target_pairs={{0,4},{4,0},{8,12},{12,8},{1,5},{5,1},{9,13},{13,9},{2,6},{6,2},{1... | collective-permute-start | bytes 200 | tf_op jit(solution)/shard_map/ppermute | solution.py:57
  21.4 1.3 %collective-permute-start.9 = (bf16[1,144,256]{2,1,0:T(8,128)(2,1)S(1)}, bf16[1,144,256]{2,1,0:T(8,128)(2,1)S(1)}, u32[]{:S(2)}, u32[]{:S(2)}) collective-permute-start(bf16[1,144,256]{2,1,0:T(8,128)(2,1)S(1)} %get-tuple-element.16.after), channel_id=1, source_target_pairs={{0,1},{1,0},{2,3},{3,2},{4,5},{5,4},{6,7},{7,6},{8,9},{9,8},{10,11... | collective-permute-start | bytes 221192 | tf_op jit(solution)/shard_map/ppermute | solution.py:375
  21.5 7.3 %collective-permute-start.8 = (bf16[1,144,256]{2,1,0:T(8,128)(2,1)S(1)}, bf16[1,144,256]{2,1,0:T(8,128)(2,1)S(1)}, u32[]{:S(2)}, u32[]{:S(2)}) collective-permute-start(bf16[1,144,256]{2,1,0:T(8,128)(2,1)S(1)} %get-tuple-element.19), channel_id=1, source_target_pairs={{0,1},{1,0},{2,3},{3,2},{4,5},{5,4},{6,7},{7,6},{8,9},{9,8},{10,11... | collective-permute-start | bytes 221192 | tf_op jit(solution)/shard_map/ppermute | solution.py:375
  22.8 6.0 %collective-permute-start.10 = (bf16[144,256]{1,0:T(8,128)(2,1)S(1)}, bf16[144,256]{1,0:T(8,128)(2,1)S(1)}, u32[]{:S(2)}, u32[]{:S(2)}) collective-permute-start(bf16[144,256]{1,0:T(8,128)(2,1)S(1)} %merge.1), channel_id=1, source_target_pairs={{0,2},{1,3},{2,0},{3,1},{4,6},{5,7},{6,4},{7,5},{8,10},{9,11},{10,... | collective-permute-start | bytes 221192 | tf_op jit(solution)/shard_map/ppermute | solution.py:412
  24.4 4.4 %collective-permute-start.7 = (f32[1,16]{1,0:T(1,128)S(1)}, f32[1,16]{1,0:T(1,128)S(1)}, u32[]{:S(2)}, u32[]{:S(2)}) collective-permute-start(f32[1,16]{1,0:T(1,128)S(1)} %larger.1.peak_ref), channel_id=1, source_target_pairs={{0,8},{4,12},{8,0},{12,4},{1,9},{5,13},{9,1},{13,5},{2,10},{6,14},... | collective-permute-start | bytes 200 | tf_op jit(solution)/shard_map/ppermute | solution.py:57

commit v15 on v14

--- a/solution.py
+++ b/solution.py
@@ -218,14 +218,13 @@
 
 
 def attend_last(
-    first_head, heads, q_ref, kt_ref, v_ref, first_ref, w_ref, ctx_ref, far_ref, near_ref, square_ref
+    first_head, heads, q_ref, kt_ref, v_ref, first_ref, w_ref, ctx_ref, far_ref, square_ref
 ):
     interleave(attention_units(first_head, heads, q_ref, kt_ref, v_ref, ctx_ref))
     squares = square_sums(first_ref) + square_sums(ctx_ref)
     square_ref[...] = squares
     other = 1 - lax.rem(lax.axis_index("tp"), 2)
     project(first_ref, ctx_ref, w_ref, other, 1, squares, far_ref)
-    project(first_ref, ctx_ref, w_ref, other, 0, squares, near_ref)
 
 
 def weigh(w_ref, gain_ref, after, out_ref):
@@ -274,8 +273,9 @@
         fill(out_ref, n, product(first_ref, last_ref, w_ref, at), squares)
 
 
-def project_keep(step, first_ref, last_ref, w_ref, square_ref, out_ref):
-    project(first_ref, last_ref, w_ref, lax.rem(lax.axis_index("tp"), 2), step, square_ref[...], out_ref)
+def project_more(shift, step, first_ref, last_ref, w_ref, square_ref, out_ref):
+    side = lax.rem(lax.axis_index("tp") + shift, 2)
+    project(first_ref, last_ref, w_ref, side, step, square_ref[...], out_ref)
 
 
 def larger(left_ref, right_ref, after, out_ref):
@@ -374,23 +374,23 @@
     def to_other_core(block):
         return lax.ppermute(block, "tp", [(i, i ^ 1) for i in range(peers)])
 
-    last_context, give_far, give_near, squares = call(
+    last_context, give_far, squares = call(
         functools.partial(attend_last, starts[1], heads),
-        (shape((rows, counts[1] * DH), BF16), slabs(peers // 2 - 1), slabs(1), shape((rows, LANES), F32)),
+        (shape((rows, counts[1] * DH), BF16), slabs(peers // 2 - 1), shape((rows, LANES), F32)),
         (crossed[1], kt, v_all, first_context, w),
         limit=32,
         name="attend_last",
         micros=1.5,
     )
-    keep_far, keep_near = [
+    give_near, keep_far, keep_near = [
         call(
-            functools.partial(project_keep, step),
+            functools.partial(project_more, shift, step),
             slabs(count),
             (first_context, last_context, w, squares),
-            name="project_keep",
-            micros=3 if step else 0,
+            name="project_more",
+            micros=micros,
         )
-        for step, count in ((1, peers // 2 - 1), (0, 1))
+        for shift, step, count, micros in ((1, 0, 1, 0.3), (0, 1, peers // 2 - 1, 3), (0, 0, 1, 0))
     ]
     got_far, got_near = to_other_core(give_far), to_other_core(give_near)
     for step in steps[:-1]:

time: 29.8 us -> 29.9 us (level)
  waiting for transfers between devices: 6.02 us -> 5.6 us
  Pallas kernels: 5.89 us -> 6.26 us
    ppermute x2, waiting for transfers between devices: 0.42 us -> 0.01 us  [to_other_core(): return lax.ppermute(block, 'tp', [(i, i ^ 1) for i in range(peers)])]
    pallas_call x13 -> x14, Pallas kernels: 5.89 us -> 6.26 us  [call(): pl.pallas_call(kernel, out_shape=outs, in_specs=specs or [WHOLE] * len(ar...]
  transfers between devices with their start and end apart: 11 -> 11, of which waited for: 4 -> 3; matrix products, arithmetic and copies ran while one was open for 0% -> 0% of each run, Pallas kernels for 17% -> 18%
where the time goes in v15:
time: 29.9 us; the launch traced here: 29.7 us
  starting transfers between devices  16.3 us (55%)
  Pallas kernels  6.26 us (21%)
  waiting for transfers between devices  5.6 us (19%)
  other arithmetic  0.78 us (3%)
  between operations  0.76 us (3%)
    ppermute x5, starting transfers between devices, swapped(): lax.ppermute(block, axis, [(i, partner(i, step, size)) for i in range(siz...  8.13 us
    pallas_call x14, Pallas kernels, call(): pl.pallas_call(kernel, out_shape=outs, in_specs=specs or [WHOLE] * len(ar...  6.26 us
    ppermute x3, starting transfers between devices, shifted(): lax.ppermute(block, axis, [((i - distance) % size, i) for i in range(size)])  5.9 us
    ppermute x5, waiting for transfers between devices, swapped(): lax.ppermute(block, axis, [(i, partner(i, step, size)) for i in range(siz...  4.16 us
    ppermute x1, starting transfers between devices, on_device(): lax.ppermute(block, 'tp', [(i, (i + 2 * (step + 1)) % peers) for i in ran...  1.64 us
    ppermute x3, waiting for transfers between devices, shifted(): lax.ppermute(block, axis, [((i - distance) % size, i) for i in range(size)])  1.43 us
    concatenate x1, other arithmetic, on_device(): pair_here = jnp.concatenate([key_vectors[0], value_vectors[0]], axis=1)  0.78 us
  transfers between devices with their start and end apart: 11, of which 3 were waited for; matrix products, arithmetic and copies ran while one was open for 0% of the time, Pallas kernels for 18%

profile of v15, /device:TPU:0, one launch (start us, length us, event | category | flops | bytes accessed | tf_op | source)
XLA Modules:
  0.0 29.7 jit_solution(4508861704128542911)
XLA Ops:
  0.6 0.8 %pad_maximum_fusion.here_ref.block_ref = bf16[128,256]{1,0:T(8,128)(2,1)S(1)} fusion(bf16[128,128]{1,0:T(8,128)(2,1)} %bitcast.5, bf16[128,128]{1,0:T(8,128)(2,1)} %bitcast.6), kind=kLoop, calls=%fused_computation | loop fusion | flops 131072 | bytes 131072 | tf_op jit(solution)/shard_map/concatenate | solution.py:314
  1.4 3.0 %collective-permute-start = (bf16[128,256]{1,0:T(8,128)(2,1)S(1)}, bf16[128,256]{1,0:T(8,128)(2,1)S(1)}, u32[]{:S(2)}, u32[]{:S(2)}) collective-permute-start(bf16[128,256]{1,0:T(8,128)(2,1)S(1)} %pad_maximum_fusion.here_ref.block_ref), channel_id=1, source_target_pairs={{16,0},{0,16},{17,1},{1,17},{18,2},{2,18},{19,3},{3,19},{20,4},{4,... | collective-permute-start | bytes 196616 | tf_op jit(solution)/shard_map/ppermute | solution.py:62
  4.4 1.0 %collective-permute-start.4 = (bf16[128,768]{1,0:T(8,128)(2,1)S(1)}, bf16[128,768]{1,0:T(8,128)(2,1)S(1)}, u32[]{:S(2)}, u32[]{:S(2)}) collective-permute-start(bf16[128,768]{1,0:T(8,128)(2,1)S(1)} %take.2), channel_id=1, source_target_pairs={{16,0},{0,16},{17,1},{1,17},{18,2},{2,18},{19,3},{3,19},{20,4},{4,... | collective-permute-start | bytes 589832 | tf_op jit(solution)/shard_map/ppermute | solution.py:62
  5.5 1.4 %collective-permute-done.pair_ref = bf16[128,256]{1,0:T(8,128)(2,1)S(1)} collective-permute-done((bf16[128,256]{1,0:T(8,128)(2,1)S(1)}, bf16[128,256]{1,0:T(8,128)(2,1)S(1)}, u32[]{:S(2)}, u32[]{:S(2)}) %collective-permute-start) | collective-permute-done | bytes 65568 | tf_op jit(solution)/shard_map/ppermute | solution.py:62
  6.9 4.5 %collective-permute-start.1 = (bf16[128,384]{1,0:T(8,128)(2,1)S(1)}, bf16[128,384]{1,0:T(8,128)(2,1)S(1)}, u32[]{:S(2)}, u32[]{:S(2)}) collective-permute-start(bf16[128,384]{1,0:T(8,128)(2,1)S(1)} %join.1.refs_3_.after), channel_id=1, source_target_pairs={{0,12},{4,8},{8,4},{12,0},{1,13},{5,9},{9,5},{13,1},{2,14},{6,10},... | collective-permute-start | bytes 294920 | tf_op jit(solution)/shard_map/ppermute | solution.py:57
  11.4 0.6 %collective-permute-start.3 = (bf16[128,384]{1,0:T(8,128)(2,1)S(1)}, bf16[128,384]{1,0:T(8,128)(2,1)S(1)}, u32[]{:S(2)}, u32[]{:S(2)}) collective-permute-start(bf16[128,384]{1,0:T(8,128)(2,1)S(1)} %join.1.refs_3_.after), channel_id=1, source_target_pairs={{0,4},{4,0},{8,12},{12,8},{1,5},{5,1},{9,13},{13,9},{2,6},{6,2},{1... | collective-permute-start | bytes 294920 | tf_op jit(solution)/shard_map/ppermute | solution.py:57
  12.1 0.0 copy-start
  12.1 0.0 copy-start.2
  12.1 1.9 %collective-permute-start.6 = (bf16[128,1280]{1,0:T(8,128)(2,1)S(1)}, bf16[128,1280]{1,0:T(8,128)(2,1)S(1)}, u32[]{:S(2)}, u32[]{:S(2)}) collective-permute-start(bf16[128,1280]{1,0:T(8,128)(2,1)S(1)} %take.3), channel_id=1, source_target_pairs={{16,0},{0,16},{17,1},{1,17},{18,2},{2,18},{19,3},{3,19},{20,4},{4,... | collective-permute-start | bytes 983048 | tf_op jit(solution)/shard_map/ppermute | solution.py:62
  14.0 0.6 %prepare.1.feature_ref = bf16[2,128,512]{2,1,0:T(8,128)(2,1)S(1)} custom-call(s32[8]{0:T(128)S(1)} %copy-done.3, f32[8,128]{1,0:T(8,128)S(1)} %touch.1.after), custom_call_target="tpu_custom_call" | custom-call | flops 3000000000 | tf_op jit(solution)/shard_map/prepare/pallas_call | solution.py:24
  14.6 0.9 %weigh.1.w_ref = bf16[2048,1024]{1,0:T(8,128)(2,1)S(1)} custom-call(bf16[2048,1024]{1,0:T(8,128)(2,1)S(1)} %bitcast.4, bf16[1,2048]{1,0:T(2,128)(2,1)S(1)} %copy-done.2, bf16[128,384]{1,0:T(8,128)(2,1)S(1)} %collective-permute-done.1.after.refs_0_), custom_call_target="tpu_custom_call" | custom-call | flops 1000000000 | tf_op jit(solution)/shard_map/weigh/pallas_call | solution.py:24
  15.5 2.6 %collective-permute-done.2.refs_1_ = bf16[128,384]{1,0:T(8,128)(2,1)S(1)} collective-permute-done((bf16[128,384]{1,0:T(8,128)(2,1)S(1)}, bf16[128,384]{1,0:T(8,128)(2,1)S(1)}, u32[]{:S(2)}, u32[]{:S(2)}) %collective-permute-start.2) | collective-permute-done | bytes 98336 | tf_op jit(solution)/shard_map/ppermute | solution.py:57
  18.1 1.4 %attend_first.1 = (bf16[1,2,256,512]{3,2,1,0:T(8,128)(2,1)S(1)}, bf16[1,512,256]{2,1,0:T(8,128)(2,1)S(1)}, bf16[128,768]{1,0:T(8,128)(2,1)S(1)}, f32[1,16]{1,0:T(1,128)S(1)}) custom-call(bf16[2048,1024]{1,0:T(8,128)(2,1)S(1)} %weigh.1.w_ref, bf16[2,128,512]{2,1,0:T(8,128)(2,1)S(1)} %prepare.1.feature_ref, ...), custom_call_target="tpu_custom_call" | custom-call | flops 2000000000 | tf_op jit(solution)/shard_map/attend_first/pallas_call | solution.py:24
  19.5 0.5 %collective-permute-start.5 = (f32[1,16]{1,0:T(1,128)S(1)}, f32[1,16]{1,0:T(1,128)S(1)}, u32[]{:S(2)}, u32[]{:S(2)}) collective-permute-start(f32[1,16]{1,0:T(1,128)S(1)} %get-tuple-element.11.left_ref), channel_id=1, source_target_pairs={{0,4},{4,0},{8,12},{12,8},{1,5},{5,1},{9,13},{13,9},{2,6},{6,2},{1... | collective-permute-start | bytes 200 | tf_op jit(solution)/shard_map/ppermute | solution.py:57
  20.0 1.4 %attend_last.1 = (bf16[128,1280]{1,0:T(8,128)(2,1)S(1)}, bf16[1,144,256]{2,1,0:T(8,128)(2,1)S(1)}, f32[128,128]{1,0:T(8,128)S(1)}) custom-call(bf16[128,1280]{1,0:T(8,128)(2,1)S(1)} %collective-permute-done.6.q_ref, bf16[1,2,256,512]{3,2,1,0:T(8,128)(2,1)S(1)} %get-tuple-element.12.kt_ref, bf16[1,512,256]{2,1,0:T(8,128)(2,1)S(1)} %get-tuple-element.13.v_ref, ...), custom_call_target="tpu_custom_call" | custom-call | flops 1500000000 | tf_op jit(solution)/shard_map/attend_last/pallas_call | solution.py:24
  21.4 0.1 collective-permute-start.9
  21.5 0.4 %project_more.5.keep_ref = bf16[1,144,256]{2,1,0:T(8,128)(2,1)S(1)} custom-call(bf16[128,768]{1,0:T(8,128)(2,1)S(1)} %get-tuple-element.14.first_ref, bf16[128,1280]{1,0:T(8,128)(2,1)S(1)} %get-tuple-element.16.last_ref, bf16[2048,1024]{1,0:T(8,128)(2,1)S(1)} %weigh.1.w_ref, f32[128,128]{1,0:T(8,128)S(1)} %get-tuple-element.17.square_ref), custom_call_target="tpu_custom_call" | custom-call | flops 3000000000 | tf_op jit(solution)/shard_map/project_more/pallas_call | solution.py:24
  21.9 0.4 %project_more.4 = bf16[1,144,256]{2,1,0:T(8,128)(2,1)S(1)} custom-call(bf16[128,768]{1,0:T(8,128)(2,1)S(1)} %get-tuple-element.14.first_ref, bf16[128,1280]{1,0:T(8,128)(2,1)S(1)} %get-tuple-element.16.last_ref, bf16[2048,1024]{1,0:T(8,128)(2,1)S(1)} %weigh.1.w_ref, f32[128,128]{1,0:T(8,128)S(1)} %get-tuple-element.17.square_ref), custom_call_target="tpu_custom_call" | custom-call | flops 300000000 | tf_op jit(solution)/shard_map/project_more/pallas_call | solution.py:24
  22.2 0.5 %collective-permute-start.8 = (bf16[1,144,256]{2,1,0:T(8,128)(2,1)S(1)}, bf16[1,144,256]{2,1,0:T(8,128)(2,1)S(1)}, u32[]{:S(2)}, u32[]{:S(2)}) collective-permute-start(bf16[1,144,256]{2,1,0:T(8,128)(2,1)S(1)} %project_more.4), channel_id=1, source_target_pairs={{0,1},{1,0},{2,3},{3,2},{4,5},{5,4},{6,7},{7,6},{8,9},{9,8},{10,11... | collective-permute-start | bytes 221192 | tf_op jit(solution)/shard_map/ppermute | solution.py:375
  22.8 1.6 %collective-permute-start.10 = (bf16[144,256]{1,0:T(8,128)(2,1)S(1)}, bf16[144,256]{1,0:T(8,128)(2,1)S(1)}, u32[]{:S(2)}, u32[]{:S(2)}) collective-permute-start(bf16[144,256]{1,0:T(8,128)(2,1)S(1)} %merge.1), channel_id=1, source_target_pairs={{0,2},{1,3},{2,0},{3,1},{4,6},{5,7},{6,4},{7,5},{8,10},{9,11},{10,... | collective-permute-start | bytes 221192 | tf_op jit(solution)/shard_map/ppermute | solution.py:412
  24.4 2.5 %collective-permute-start.7 = (f32[1,16]{1,0:T(1,128)S(1)}, f32[1,16]{1,0:T(1,128)S(1)}, u32[]{:S(2)}, u32[]{:S(2)}) collective-permute-start(f32[1,16]{1,0:T(1,128)S(1)} %larger.1.peak_ref), channel_id=1, source_target_pairs={{0,8},{4,12},{8,0},{12,4},{1,9},{5,13},{9,1},{13,5},{2,10},{6,14},... | collective-permute-start | bytes 200 | tf_op jit(solution)/shard_map/ppermute | solution.py:57
  26.9 0.3 %project_more.3.keep_ref = bf16[1,144,256]{2,1,0:T(8,128)(2,1)S(1)} custom-call(bf16[128,768]{1,0:T(8,128)(2,1)S(1)} %get-tuple-element.14.first_ref, bf16[128,1280]{1,0:T(8,128)(2,1)S(1)} %get-tuple-element.16.last_ref, bf16[2048,1024]{1,0:T(8,128)(2,1)S(1)} %weigh.1.w_ref, f32[128,128]{1,0:T(8,128)S(1)} %get-tuple-element.17.square_ref), custom_call_target="tpu_custom_call" | custom-call | tf_op jit(solution)/shard_map/project_more/pallas_call | solution.py:24
  27.3 1.6 %collective-permute-done.7.peak_got = f32[1,16]{1,0:T(1,128)S(1)} collective-permute-done((f32[1,16]{1,0:T(1,128)S(1)}, f32[1,16]{1,0:T(1,128)S(1)}, u32[]{:S(2)}, u32[]{:S(2)}) %collective-permute-start.7) | collective-permute-done | bytes 96 | tf_op jit(solution)/shard_map/ppermute | solution.py:57
  28.9 0.8 %finish.1 = (f32[1,16]{1,0:T(1,128)}, bf16[128,256]{1,0:T(8,128)(2,1)}) custom-call(f32[1,16]{1,0:T(1,128)S(1)} %larger.1.peak_ref, f32[1,16]{1,0:T(1,128)S(1)} %collective-permute-done.7.peak_got, bf16[1,144,256]{2,1,0:T(8,128)(2,1)S(1)} %project_more.3.keep_ref, bf16[1,144,256]{2,1,0:T(8,128)(2,1)S(1)} %collective-permute-done.8.got_ref, ...), custom_call_target="tpu_custom_call" | custom-call | tf_op jit(solution)/shard_map/finish/pallas_call | solution.py:24
  (21 shorter events, 0.1 us)
Async XLA Ops:
  1.4 3.0 %copy-start.1 = (bf16[1,128,2048]{2,1,0:T(8,128)(2,1)S(1)}, bf16[1,128,2048]{2,1,0:T(8,128)(2,1)}, u32[]{:S(2)}) copy-start(bf16[1,128,2048]{2,1,0:T(8,128)(2,1)} %q_ref.3) | copy-start | bytes 1572868
  1.4 5.5 %collective-permute-start = (bf16[128,256]{1,0:T(8,128)(2,1)S(1)}, bf16[128,256]{1,0:T(8,128)(2,1)S(1)}, u32[]{:S(2)}, u32[]{:S(2)}) collective-permute-start(bf16[128,256]{1,0:T(8,128)(2,1)S(1)} %pad_maximum_fusion.here_ref.block_ref), channel_id=1, source_target_pairs={{16,0},{0,16},{17,1},{1,17},{18,2},{2,18},{19,3},{3,19},{20,4},{4,... | collective-permute-start | bytes 196616 | tf_op jit(solution)/shard_map/ppermute | solution.py:62
  4.4 9.5 %copy-start.3 = (s32[8]{0:T(128)S(1)}, s32[8]{0:T(128)}, u32[]{:S(2)}) copy-start(s32[8]{0:T(128)} %order_ref.1) | copy-start | bytes 100
  4.4 13.6 %collective-permute-start.4 = (bf16[128,768]{1,0:T(8,128)(2,1)S(1)}, bf16[128,768]{1,0:T(8,128)(2,1)S(1)}, u32[]{:S(2)}, u32[]{:S(2)}) collective-permute-start(bf16[128,768]{1,0:T(8,128)(2,1)S(1)} %take.2), channel_id=1, source_target_pairs={{16,0},{0,16},{17,1},{1,17},{18,2},{2,18},{19,3},{3,19},{20,4},{4,... | collective-permute-start | bytes 589832 | tf_op jit(solution)/shard_map/ppermute | solution.py:62
  6.9 7.7 %collective-permute-start.1 = (bf16[128,384]{1,0:T(8,128)(2,1)S(1)}, bf16[128,384]{1,0:T(8,128)(2,1)S(1)}, u32[]{:S(2)}, u32[]{:S(2)}) collective-permute-start(bf16[128,384]{1,0:T(8,128)(2,1)S(1)} %join.1.refs_3_.after), channel_id=1, source_target_pairs={{0,12},{4,8},{8,4},{12,0},{1,13},{5,9},{9,5},{13,1},{2,14},{6,10},... | collective-permute-start | bytes 294920 | tf_op jit(solution)/shard_map/ppermute | solution.py:57
  11.4 6.7 %collective-permute-start.2 = (bf16[128,384]{1,0:T(8,128)(2,1)S(1)}, bf16[128,384]{1,0:T(8,128)(2,1)S(1)}, u32[]{:S(2)}, u32[]{:S(2)}) collective-permute-start(bf16[128,384]{1,0:T(8,128)(2,1)S(1)} %join.1.refs_3_.after), channel_id=1, source_target_pairs={{0,8},{4,12},{8,0},{12,4},{1,9},{5,13},{9,1},{13,5},{2,10},{6,14},... | collective-permute-start | bytes 294920 | tf_op jit(solution)/shard_map/ppermute | solution.py:57
  11.4 6.7 %collective-permute-start.3 = (bf16[128,384]{1,0:T(8,128)(2,1)S(1)}, bf16[128,384]{1,0:T(8,128)(2,1)S(1)}, u32[]{:S(2)}, u32[]{:S(2)}) collective-permute-start(bf16[128,384]{1,0:T(8,128)(2,1)S(1)} %join.1.refs_3_.after), channel_id=1, source_target_pairs={{0,4},{4,0},{8,12},{12,8},{1,5},{5,1},{9,13},{13,9},{2,6},{6,2},{1... | collective-permute-start | bytes 294920 | tf_op jit(solution)/shard_map/ppermute | solution.py:57
  12.1 2.5 %copy-start = (bf16[1,2048,1024]{2,1,0:T(8,128)(2,1)S(1)}, bf16[1,2048,1024]{2,1,0:T(8,128)(2,1)}, u32[]{:S(2)}) copy-start(bf16[1,2048,1024]{2,1,0:T(8,128)(2,1)} %param.11) | copy-start | bytes 12582916
  12.1 2.5 %copy-start.2 = (bf16[1,2048]{1,0:T(2,128)(2,1)S(1)}, bf16[1,2048]{1,0:T(2,128)(2,1)}, u32[]{:S(2)}) copy-start(bf16[1,2048]{1,0:T(2,128)(2,1)} %gain_ref.1) | copy-start | bytes 12292
  12.1 7.9 %collective-permute-start.6 = (bf16[128,1280]{1,0:T(8,128)(2,1)S(1)}, bf16[128,1280]{1,0:T(8,128)(2,1)S(1)}, u32[]{:S(2)}, u32[]{:S(2)}) collective-permute-start(bf16[128,1280]{1,0:T(8,128)(2,1)S(1)} %take.3), channel_id=1, source_target_pairs={{16,0},{0,16},{17,1},{1,17},{18,2},{2,18},{19,3},{3,19},{20,4},{4,... | collective-permute-start | bytes 983048 | tf_op jit(solution)/shard_map/ppermute | solution.py:62
  19.5 4.9 %collective-permute-start.5 = (f32[1,16]{1,0:T(1,128)S(1)}, f32[1,16]{1,0:T(1,128)S(1)}, u32[]{:S(2)}, u32[]{:S(2)}) collective-permute-start(f32[1,16]{1,0:T(1,128)S(1)} %get-tuple-element.11.left_ref), channel_id=1, source_target_pairs={{0,4},{4,0},{8,12},{12,8},{1,5},{5,1},{9,13},{13,9},{2,6},{6,2},{1... | collective-permute-start | bytes 200 | tf_op jit(solution)/shard_map/ppermute | solution.py:57
  21.4 1.3 %collective-permute-start.9 = (bf16[1,144,256]{2,1,0:T(8,128)(2,1)S(1)}, bf16[1,144,256]{2,1,0:T(8,128)(2,1)S(1)}, u32[]{:S(2)}, u32[]{:S(2)}) collective-permute-start(bf16[1,144,256]{2,1,0:T(8,128)(2,1)S(1)} %get-tuple-element.15.after), channel_id=1, source_target_pairs={{0,1},{1,0},{2,3},{3,2},{4,5},{5,4},{6,7},{7,6},{8,9},{9,8},{10,11... | collective-permute-start | bytes 221192 | tf_op jit(solution)/shard_map/ppermute | solution.py:375
  22.2 6.6 %collective-permute-start.8 = (bf16[1,144,256]{2,1,0:T(8,128)(2,1)S(1)}, bf16[1,144,256]{2,1,0:T(8,128)(2,1)S(1)}, u32[]{:S(2)}, u32[]{:S(2)}) collective-permute-start(bf16[1,144,256]{2,1,0:T(8,128)(2,1)S(1)} %project_more.4), channel_id=1, source_target_pairs={{0,1},{1,0},{2,3},{3,2},{4,5},{5,4},{6,7},{7,6},{8,9},{9,8},{10,11... | collective-permute-start | bytes 221192 | tf_op jit(solution)/shard_map/ppermute | solution.py:375
  22.8 6.1 %collective-permute-start.10 = (bf16[144,256]{1,0:T(8,128)(2,1)S(1)}, bf16[144,256]{1,0:T(8,128)(2,1)S(1)}, u32[]{:S(2)}, u32[]{:S(2)}) collective-permute-start(bf16[144,256]{1,0:T(8,128)(2,1)S(1)} %merge.1), channel_id=1, source_target_pairs={{0,2},{1,3},{2,0},{3,1},{4,6},{5,7},{6,4},{7,5},{8,10},{9,11},{10,... | collective-permute-start | bytes 221192 | tf_op jit(solution)/shard_map/ppermute | solution.py:412
  24.4 4.4 %collective-permute-start.7 = (f32[1,16]{1,0:T(1,128)S(1)}, f32[1,16]{1,0:T(1,128)S(1)}, u32[]{:S(2)}, u32[]{:S(2)}) collective-permute-start(f32[1,16]{1,0:T(1,128)S(1)} %larger.1.peak_ref), channel_id=1, source_target_pairs={{0,8},{4,12},{8,0},{12,4},{1,9},{5,13},{9,1},{13,5},{2,10},{6,14},... | collective-permute-start | bytes 200 | tf_op jit(solution)/shard_map/ppermute | solution.py:57

commit v16 on v14

--- a/solution.py
+++ b/solution.py
@@ -313,7 +313,7 @@
 
     pair_here = jnp.concatenate([key_vectors[0], value_vectors[0]], axis=1)
     pair = shifted(pair_here, "pp", 1)
-    cut = heads * 3 // 8
+    cut = heads // 4
     counts = [cut, heads - cut]
     starts = [0, cut]
     crossed = []

time: 29.8 us -> 30.8 us (1.034)
  waiting for transfers between devices: 6.02 us -> 7.19 us
    ppermute x3, waiting for transfers between devices: 1.43 us -> 2.42 us  [shifted(): lax.ppermute(block, axis, [((i - distance) % size, i) for i in range(size)])]
  transfers between devices with their start and end apart: 11 -> 11, of which waited for: 4 -> 5; matrix products, arithmetic and copies ran while one was open for 0% -> 0% of each run, Pallas kernels for 17% -> 16%
where the time goes in v16:
time: 30.8 us; the launch traced here: 30.6 us
  starting transfers between devices  16 us (52%)
  waiting for transfers between devices  7.19 us (23%)
  Pallas kernels  5.86 us (19%)
  other arithmetic  0.78 us (3%)
  between operations  0.76 us (2%)
    ppermute x5, starting transfers between devices, swapped(): lax.ppermute(block, axis, [(i, partner(i, step, size)) for i in range(siz...  7.92 us
    ppermute x3, starting transfers between devices, shifted(): lax.ppermute(block, axis, [((i - distance) % size, i) for i in range(size)])  5.89 us
    pallas_call x13, Pallas kernels, call(): pl.pallas_call(kernel, out_shape=outs, in_specs=specs or [WHOLE] * len(ar...  5.86 us
    ppermute x5, waiting for transfers between devices, swapped(): lax.ppermute(block, axis, [(i, partner(i, step, size)) for i in range(siz...  4.36 us
    ppermute x3, waiting for transfers between devices, shifted(): lax.ppermute(block, axis, [((i - distance) % size, i) for i in range(size)])  2.42 us
    ppermute x1, starting transfers between devices, on_device(): lax.ppermute(block, 'tp', [(i, (i + 2 * (step + 1)) % peers) for i in ran...  1.59 us
    concatenate x1, other arithmetic, on_device(): pair_here = jnp.concatenate([key_vectors[0], value_vectors[0]], axis=1)  0.78 us
  transfers between devices with their start and end apart: 11, of which 5 were waited for; matrix products, arithmetic and copies ran while one was open for 0% of the time, Pallas kernels for 16%

profile of v16, /device:TPU:0, one launch (start us, length us, event | category | flops | bytes accessed | tf_op | source)
XLA Modules:
  0.0 30.6 jit_solution(2935028098475677221)
XLA Ops:
  0.6 0.8 %pad_maximum_fusion.here_ref.block_ref = bf16[128,256]{1,0:T(8,128)(2,1)S(1)} fusion(bf16[128,128]{1,0:T(8,128)(2,1)} %bitcast.5, bf16[128,128]{1,0:T(8,128)(2,1)} %bitcast.6), kind=kLoop, calls=%fused_computation | loop fusion | flops 131072 | bytes 131072 | tf_op jit(solution)/shard_map/concatenate | solution.py:314
  1.4 3.0 %collective-permute-start = (bf16[128,256]{1,0:T(8,128)(2,1)S(1)}, bf16[128,256]{1,0:T(8,128)(2,1)S(1)}, u32[]{:S(2)}, u32[]{:S(2)}) collective-permute-start(bf16[128,256]{1,0:T(8,128)(2,1)S(1)} %pad_maximum_fusion.here_ref.block_ref), channel_id=1, source_target_pairs={{16,0},{0,16},{17,1},{1,17},{18,2},{2,18},{19,3},{3,19},{20,4},{4,... | collective-permute-start | bytes 196616 | tf_op jit(solution)/shard_map/ppermute | solution.py:62
  4.4 1.0 %collective-permute-start.4 = (bf16[128,512]{1,0:T(8,128)(2,1)S(1)}, bf16[128,512]{1,0:T(8,128)(2,1)S(1)}, u32[]{:S(2)}, u32[]{:S(2)}) collective-permute-start(bf16[128,512]{1,0:T(8,128)(2,1)S(1)} %take.2), channel_id=1, source_target_pairs={{16,0},{0,16},{17,1},{1,17},{18,2},{2,18},{19,3},{3,19},{20,4},{4,... | collective-permute-start | bytes 393224 | tf_op jit(solution)/shard_map/ppermute | solution.py:62
  5.5 1.4 %collective-permute-done.pair_ref = bf16[128,256]{1,0:T(8,128)(2,1)S(1)} collective-permute-done((bf16[128,256]{1,0:T(8,128)(2,1)S(1)}, bf16[128,256]{1,0:T(8,128)(2,1)S(1)}, u32[]{:S(2)}, u32[]{:S(2)}) %collective-permute-start) | collective-permute-done | bytes 65568 | tf_op jit(solution)/shard_map/ppermute | solution.py:62
  6.9 4.5 %collective-permute-start.1 = (bf16[128,384]{1,0:T(8,128)(2,1)S(1)}, bf16[128,384]{1,0:T(8,128)(2,1)S(1)}, u32[]{:S(2)}, u32[]{:S(2)}) collective-permute-start(bf16[128,384]{1,0:T(8,128)(2,1)S(1)} %join.1.refs_3_.after), channel_id=1, source_target_pairs={{0,12},{4,8},{8,4},{12,0},{1,13},{5,9},{9,5},{13,1},{2,14},{6,10},... | collective-permute-start | bytes 294920 | tf_op jit(solution)/shard_map/ppermute | solution.py:57
  11.4 0.6 %collective-permute-start.3 = (bf16[128,384]{1,0:T(8,128)(2,1)S(1)}, bf16[128,384]{1,0:T(8,128)(2,1)S(1)}, u32[]{:S(2)}, u32[]{:S(2)}) collective-permute-start(bf16[128,384]{1,0:T(8,128)(2,1)S(1)} %join.1.refs_3_.after), channel_id=1, source_target_pairs={{0,4},{4,0},{8,12},{12,8},{1,5},{5,1},{9,13},{13,9},{2,6},{6,2},{1... | collective-permute-start | bytes 294920 | tf_op jit(solution)/shard_map/ppermute | solution.py:57
  12.1 0.0 copy-start
  12.1 1.9 %collective-permute-start.6 = (bf16[128,1536]{1,0:T(8,128)(2,1)S(1)}, bf16[128,1536]{1,0:T(8,128)(2,1)S(1)}, u32[]{:S(2)}, u32[]{:S(2)}) collective-permute-start(bf16[128,1536]{1,0:T(8,128)(2,1)S(1)} %take.3), channel_id=1, source_target_pairs={{16,0},{0,16},{17,1},{1,17},{18,2},{2,18},{19,3},{3,19},{20,4},{4,... | collective-permute-start | bytes 1179656 | tf_op jit(solution)/shard_map/ppermute | solution.py:62
  14.0 0.6 %prepare.1.feature_ref = bf16[2,128,512]{2,1,0:T(8,128)(2,1)S(1)} custom-call(s32[8]{0:T(128)S(1)} %copy-done.3, f32[8,128]{1,0:T(8,128)S(1)} %touch.1.after), custom_call_target="tpu_custom_call" | custom-call | flops 3000000000 | tf_op jit(solution)/shard_map/prepare/pallas_call | solution.py:24
  14.6 0.9 %weigh.1.w_ref = bf16[2048,1024]{1,0:T(8,128)(2,1)S(1)} custom-call(bf16[2048,1024]{1,0:T(8,128)(2,1)S(1)} %bitcast.4, bf16[1,2048]{1,0:T(2,128)(2,1)S(1)} %copy-done.2, bf16[128,384]{1,0:T(8,128)(2,1)S(1)} %collective-permute-done.1.after.refs_0_), custom_call_target="tpu_custom_call" | custom-call | flops 1000000000 | tf_op jit(solution)/shard_map/weigh/pallas_call | solution.py:24
  15.5 2.6 %collective-permute-done.2.refs_1_ = bf16[128,384]{1,0:T(8,128)(2,1)S(1)} collective-permute-done((bf16[128,384]{1,0:T(8,128)(2,1)S(1)}, bf16[128,384]{1,0:T(8,128)(2,1)S(1)}, u32[]{:S(2)}, u32[]{:S(2)}) %collective-permute-start.2) | collective-permute-done | bytes 98336 | tf_op jit(solution)/shard_map/ppermute | solution.py:57
  18.1 1.2 %attend_first.1 = (bf16[1,2,256,512]{3,2,1,0:T(8,128)(2,1)S(1)}, bf16[1,512,256]{2,1,0:T(8,128)(2,1)S(1)}, bf16[128,512]{1,0:T(8,128)(2,1)S(1)}, f32[1,16]{1,0:T(1,128)S(1)}) custom-call(bf16[2048,1024]{1,0:T(8,128)(2,1)S(1)} %weigh.1.w_ref, bf16[2,128,512]{2,1,0:T(8,128)(2,1)S(1)} %prepare.1.feature_ref, ...), custom_call_target="tpu_custom_call" | custom-call | flops 2000000000 | tf_op jit(solution)/shard_map/attend_first/pallas_call | solution.py:24
  19.3 0.5 %collective-permute-start.5 = (f32[1,16]{1,0:T(1,128)S(1)}, f32[1,16]{1,0:T(1,128)S(1)}, u32[]{:S(2)}, u32[]{:S(2)}) collective-permute-start(f32[1,16]{1,0:T(1,128)S(1)} %get-tuple-element.12.left_ref), channel_id=1, source_target_pairs={{0,4},{4,0},{8,12},{12,8},{1,5},{5,1},{9,13},{13,9},{2,6},{6,2},{1... | collective-permute-start | bytes 200 | tf_op jit(solution)/shard_map/ppermute | solution.py:57
  19.8 1.0 %collective-permute-done.6.q_ref = bf16[128,1536]{1,0:T(8,128)(2,1)S(1)} collective-permute-done((bf16[128,1536]{1,0:T(8,128)(2,1)S(1)}, bf16[128,1536]{1,0:T(8,128)(2,1)S(1)}, u32[]{:S(2)}, u32[]{:S(2)}) %collective-permute-start.6) | collective-permute-done | bytes 393248 | tf_op jit(solution)/shard_map/ppermute | solution.py:62
  20.8 1.6 %attend_last.1 = (bf16[128,1536]{1,0:T(8,128)(2,1)S(1)}, bf16[1,144,256]{2,1,0:T(8,128)(2,1)S(1)}, bf16[1,144,256]{2,1,0:T(8,128)(2,1)S(1)}, f32[128,128]{1,0:T(8,128)S(1)}) custom-call(bf16[128,1536]{1,0:T(8,128)(2,1)S(1)} %collective-permute-done.6.q_ref, bf16[1,2,256,512]{3,2,1,0:T(8,128)(2,1)S(1)} %get-tuple-element.13.kt_ref, ...), custom_call_target="tpu_custom_call" | custom-call | flops 1500000000 | tf_op jit(solution)/shard_map/attend_last/pallas_call | solution.py:24
  22.4 0.1 collective-permute-start.9
  22.4 0.5 %collective-permute-start.8 = (bf16[1,144,256]{2,1,0:T(8,128)(2,1)S(1)}, bf16[1,144,256]{2,1,0:T(8,128)(2,1)S(1)}, u32[]{:S(2)}, u32[]{:S(2)}) collective-permute-start(bf16[1,144,256]{2,1,0:T(8,128)(2,1)S(1)} %get-tuple-element.19), channel_id=1, source_target_pairs={{0,1},{1,0},{2,3},{3,2},{4,5},{5,4},{6,7},{7,6},{8,9},{9,8},{10,11... | collective-permute-start | bytes 221192 | tf_op jit(solution)/shard_map/ppermute | solution.py:375
  22.9 0.3 %project_keep.3.keep_ref = bf16[1,144,256]{2,1,0:T(8,128)(2,1)S(1)} custom-call(bf16[128,512]{1,0:T(8,128)(2,1)S(1)} %get-tuple-element.15.first_ref, bf16[128,1536]{1,0:T(8,128)(2,1)S(1)} %get-tuple-element.17.last_ref, bf16[2048,1024]{1,0:T(8,128)(2,1)S(1)} %weigh.1.w_ref, f32[128,128]{1,0:T(8,128)S(1)} %get-tuple-element.18.square_ref), custom_call_target="tpu_custom_call" | custom-call | flops 3000000000 | tf_op jit(solution)/shard_map/project_keep/pallas_call | solution.py:24
  23.3 0.4 %collective-permute-done.9.got_ref = bf16[1,144,256]{2,1,0:T(8,128)(2,1)S(1)} collective-permute-done((bf16[1,144,256]{2,1,0:T(8,128)(2,1)S(1)}, bf16[1,144,256]{2,1,0:T(8,128)(2,1)S(1)}, u32[]{:S(2)}, u32[]{:S(2)}) %collective-permute-start.9) | collective-permute-done | bytes 73760 | tf_op jit(solution)/shard_map/ppermute | solution.py:375
  23.7 1.6 %collective-permute-start.10 = (bf16[144,256]{1,0:T(8,128)(2,1)S(1)}, bf16[144,256]{1,0:T(8,128)(2,1)S(1)}, u32[]{:S(2)}, u32[]{:S(2)}) collective-permute-start(bf16[144,256]{1,0:T(8,128)(2,1)S(1)} %merge.1), channel_id=1, source_target_pairs={{0,2},{1,3},{2,0},{3,1},{4,6},{5,7},{6,4},{7,5},{8,10},{9,11},{10,... | collective-permute-start | bytes 221192 | tf_op jit(solution)/shard_map/ppermute | solution.py:412
  25.3 2.3 %collective-permute-start.7 = (f32[1,16]{1,0:T(1,128)S(1)}, f32[1,16]{1,0:T(1,128)S(1)}, u32[]{:S(2)}, u32[]{:S(2)}) collective-permute-start(f32[1,16]{1,0:T(1,128)S(1)} %larger.1.peak_ref), channel_id=1, source_target_pairs={{0,8},{4,12},{8,0},{12,4},{1,9},{5,13},{9,1},{13,5},{2,10},{6,14},... | collective-permute-start | bytes 200 | tf_op jit(solution)/shard_map/ppermute | solution.py:57
  27.6 0.3 %project_keep.2.keep_ref = bf16[1,144,256]{2,1,0:T(8,128)(2,1)S(1)} custom-call(bf16[128,512]{1,0:T(8,128)(2,1)S(1)} %get-tuple-element.15.first_ref, bf16[128,1536]{1,0:T(8,128)(2,1)S(1)} %get-tuple-element.17.last_ref, bf16[2048,1024]{1,0:T(8,128)(2,1)S(1)} %weigh.1.w_ref, f32[128,128]{1,0:T(8,128)S(1)} %get-tuple-element.18.square_ref), custom_call_target="tpu_custom_call" | custom-call | tf_op jit(solution)/shard_map/project_keep/pallas_call | solution.py:24
  28.0 1.8 %collective-permute-done.7.peak_got = f32[1,16]{1,0:T(1,128)S(1)} collective-permute-done((f32[1,16]{1,0:T(1,128)S(1)}, f32[1,16]{1,0:T(1,128)S(1)}, u32[]{:S(2)}, u32[]{:S(2)}) %collective-permute-start.7) | collective-permute-done | bytes 96 | tf_op jit(solution)/shard_map/ppermute | solution.py:57
  29.8 0.8 %finish.1 = (f32[1,16]{1,0:T(1,128)}, bf16[128,256]{1,0:T(8,128)(2,1)}) custom-call(f32[1,16]{1,0:T(1,128)S(1)} %larger.1.peak_ref, f32[1,16]{1,0:T(1,128)S(1)} %collective-permute-done.7.peak_got, bf16[1,144,256]{2,1,0:T(8,128)(2,1)S(1)} %project_keep.2.keep_ref, bf16[1,144,256]{2,1,0:T(8,128)(2,1)S(1)} %collective-permute-done.8.got_ref, ...), custom_call_target="tpu_custom_call" | custom-call | tf_op jit(solution)/shard_map/finish/pallas_call | solution.py:24
  (20 shorter events, 0.1 us)
Async XLA Ops:
  1.4 3.0 %copy-start.1 = (bf16[1,128,2048]{2,1,0:T(8,128)(2,1)S(1)}, bf16[1,128,2048]{2,1,0:T(8,128)(2,1)}, u32[]{:S(2)}) copy-start(bf16[1,128,2048]{2,1,0:T(8,128)(2,1)} %q_ref.3) | copy-start | bytes 1572868
  1.4 5.5 %collective-permute-start = (bf16[128,256]{1,0:T(8,128)(2,1)S(1)}, bf16[128,256]{1,0:T(8,128)(2,1)S(1)}, u32[]{:S(2)}, u32[]{:S(2)}) collective-permute-start(bf16[128,256]{1,0:T(8,128)(2,1)S(1)} %pad_maximum_fusion.here_ref.block_ref), channel_id=1, source_target_pairs={{16,0},{0,16},{17,1},{1,17},{18,2},{2,18},{19,3},{3,19},{20,4},{4,... | collective-permute-start | bytes 196616 | tf_op jit(solution)/shard_map/ppermute | solution.py:62
  4.4 9.6 %copy-start.3 = (s32[8]{0:T(128)S(1)}, s32[8]{0:T(128)}, u32[]{:S(2)}) copy-start(s32[8]{0:T(128)} %order_ref.1) | copy-start | bytes 100
  4.4 11.1 %collective-permute-start.4 = (bf16[128,512]{1,0:T(8,128)(2,1)S(1)}, bf16[128,512]{1,0:T(8,128)(2,1)S(1)}, u32[]{:S(2)}, u32[]{:S(2)}) collective-permute-start(bf16[128,512]{1,0:T(8,128)(2,1)S(1)} %take.2), channel_id=1, source_target_pairs={{16,0},{0,16},{17,1},{1,17},{18,2},{2,18},{19,3},{3,19},{20,4},{4,... | collective-permute-start | bytes 393224 | tf_op jit(solution)/shard_map/ppermute | solution.py:62
  6.9 7.7 %collective-permute-start.1 = (bf16[128,384]{1,0:T(8,128)(2,1)S(1)}, bf16[128,384]{1,0:T(8,128)(2,1)S(1)}, u32[]{:S(2)}, u32[]{:S(2)}) collective-permute-start(bf16[128,384]{1,0:T(8,128)(2,1)S(1)} %join.1.refs_3_.after), channel_id=1, source_target_pairs={{0,12},{4,8},{8,4},{12,0},{1,13},{5,9},{9,5},{13,1},{2,14},{6,10},... | collective-permute-start | bytes 294920 | tf_op jit(solution)/shard_map/ppermute | solution.py:57
  11.4 6.7 %collective-permute-start.2 = (bf16[128,384]{1,0:T(8,128)(2,1)S(1)}, bf16[128,384]{1,0:T(8,128)(2,1)S(1)}, u32[]{:S(2)}, u32[]{:S(2)}) collective-permute-start(bf16[128,384]{1,0:T(8,128)(2,1)S(1)} %join.1.refs_3_.after), channel_id=1, source_target_pairs={{0,8},{4,12},{8,0},{12,4},{1,9},{5,13},{9,1},{13,5},{2,10},{6,14},... | collective-permute-start | bytes 294920 | tf_op jit(solution)/shard_map/ppermute | solution.py:57
  11.4 6.7 %collective-permute-start.3 = (bf16[128,384]{1,0:T(8,128)(2,1)S(1)}, bf16[128,384]{1,0:T(8,128)(2,1)S(1)}, u32[]{:S(2)}, u32[]{:S(2)}) collective-permute-start(bf16[128,384]{1,0:T(8,128)(2,1)S(1)} %join.1.refs_3_.after), channel_id=1, source_target_pairs={{0,4},{4,0},{8,12},{12,8},{1,5},{5,1},{9,13},{13,9},{2,6},{6,2},{1... | collective-permute-start | bytes 294920 | tf_op jit(solution)/shard_map/ppermute | solution.py:57
  12.1 2.5 %copy-start = (bf16[1,2048,1024]{2,1,0:T(8,128)(2,1)S(1)}, bf16[1,2048,1024]{2,1,0:T(8,128)(2,1)}, u32[]{:S(2)}) copy-start(bf16[1,2048,1024]{2,1,0:T(8,128)(2,1)} %param.11) | copy-start | bytes 12582916
  12.1 2.5 %copy-start.2 = (bf16[1,2048]{1,0:T(2,128)(2,1)S(1)}, bf16[1,2048]{1,0:T(2,128)(2,1)}, u32[]{:S(2)}) copy-start(bf16[1,2048]{1,0:T(2,128)(2,1)} %gain_ref.1) | copy-start | bytes 12292
  12.1 8.7 %collective-permute-start.6 = (bf16[128,1536]{1,0:T(8,128)(2,1)S(1)}, bf16[128,1536]{1,0:T(8,128)(2,1)S(1)}, u32[]{:S(2)}, u32[]{:S(2)}) collective-permute-start(bf16[128,1536]{1,0:T(8,128)(2,1)S(1)} %take.3), channel_id=1, source_target_pairs={{16,0},{0,16},{17,1},{1,17},{18,2},{2,18},{19,3},{3,19},{20,4},{4,... | collective-permute-start | bytes 1179656 | tf_op jit(solution)/shard_map/ppermute | solution.py:62
  19.3 6.0 %collective-permute-start.5 = (f32[1,16]{1,0:T(1,128)S(1)}, f32[1,16]{1,0:T(1,128)S(1)}, u32[]{:S(2)}, u32[]{:S(2)}) collective-permute-start(f32[1,16]{1,0:T(1,128)S(1)} %get-tuple-element.12.left_ref), channel_id=1, source_target_pairs={{0,4},{4,0},{8,12},{12,8},{1,5},{5,1},{9,13},{13,9},{2,6},{6,2},{1... | collective-permute-start | bytes 200 | tf_op jit(solution)/shard_map/ppermute | solution.py:57
  22.4 1.3 %collective-permute-start.9 = (bf16[1,144,256]{2,1,0:T(8,128)(2,1)S(1)}, bf16[1,144,256]{2,1,0:T(8,128)(2,1)S(1)}, u32[]{:S(2)}, u32[]{:S(2)}) collective-permute-start(bf16[1,144,256]{2,1,0:T(8,128)(2,1)S(1)} %get-tuple-element.16.after), channel_id=1, source_target_pairs={{0,1},{1,0},{2,3},{3,2},{4,5},{5,4},{6,7},{7,6},{8,9},{9,8},{10,11... | collective-permute-start | bytes 221192 | tf_op jit(solution)/shard_map/ppermute | solution.py:375
  22.4 7.3 %collective-permute-start.8 = (bf16[1,144,256]{2,1,0:T(8,128)(2,1)S(1)}, bf16[1,144,256]{2,1,0:T(8,128)(2,1)S(1)}, u32[]{:S(2)}, u32[]{:S(2)}) collective-permute-start(bf16[1,144,256]{2,1,0:T(8,128)(2,1)S(1)} %get-tuple-element.19), channel_id=1, source_target_pairs={{0,1},{1,0},{2,3},{3,2},{4,5},{5,4},{6,7},{7,6},{8,9},{9,8},{10,11... | collective-permute-start | bytes 221192 | tf_op jit(solution)/shard_map/ppermute | solution.py:375
  23.7 6.0 %collective-permute-start.10 = (bf16[144,256]{1,0:T(8,128)(2,1)S(1)}, bf16[144,256]{1,0:T(8,128)(2,1)S(1)}, u32[]{:S(2)}, u32[]{:S(2)}) collective-permute-start(bf16[144,256]{1,0:T(8,128)(2,1)S(1)} %merge.1), channel_id=1, source_target_pairs={{0,2},{1,3},{2,0},{3,1},{4,6},{5,7},{6,4},{7,5},{8,10},{9,11},{10,... | collective-permute-start | bytes 221192 | tf_op jit(solution)/shard_map/ppermute | solution.py:412
  25.3 4.4 %collective-permute-start.7 = (f32[1,16]{1,0:T(1,128)S(1)}, f32[1,16]{1,0:T(1,128)S(1)}, u32[]{:S(2)}, u32[]{:S(2)}) collective-permute-start(f32[1,16]{1,0:T(1,128)S(1)} %larger.1.peak_ref), channel_id=1, source_target_pairs={{0,8},{4,12},{8,0},{12,4},{1,9},{5,13},{9,1},{13,5},{2,10},{6,14},... | collective-permute-start | bytes 200 | tf_op jit(solution)/shard_map/ppermute | solution.py:57

commit v17 on v14

--- a/solution.py
+++ b/solution.py
@@ -184,7 +184,7 @@
     block = q_ref.shape[0] // 2
     heads = q_ref.shape[1] // DH
     keys = own_ref.shape[3]
-    for g, start, stop in spans(0, heads, heads // own_ref.shape[0], max(1, 8 * 512 // keys)):
+    for g, start, stop in spans(0, heads, heads // own_ref.shape[0], max(1, 16 * 512 // keys)):
         tops = []
         for side in range(2):
             s = jnp.dot(stacked(q_ref, start, stop, side), own_ref[g, side], preferred_element_type=F32)

time: 29.8 us -> 29.8 us (level)
  no operation moved by 1% of the time
where the time goes in v17:
time: 29.8 us; the launch traced here: 29.7 us
  starting transfers between devices  16.2 us (54%)
  waiting for transfers between devices  6.01 us (20%)
  Pallas kernels  5.91 us (20%)
  other arithmetic  0.78 us (3%)
  between operations  0.75 us (3%)
    ppermute x5, starting transfers between devices, swapped(): lax.ppermute(block, axis, [(i, partner(i, step, size)) for i in range(siz...  8.13 us
    pallas_call x13, Pallas kernels, call(): pl.pallas_call(kernel, out_shape=outs, in_specs=specs or [WHOLE] * len(ar...  5.91 us
    ppermute x3, starting transfers between devices, shifted(): lax.ppermute(block, axis, [((i - distance) % size, i) for i in range(size)])  5.9 us
    ppermute x5, waiting for transfers between devices, swapped(): lax.ppermute(block, axis, [(i, partner(i, step, size)) for i in range(siz...  4.16 us
    ppermute x1, starting transfers between devices, on_device(): lax.ppermute(block, 'tp', [(i, (i + 2 * (step + 1)) % peers) for i in ran...  1.59 us
    ppermute x3, waiting for transfers between devices, shifted(): lax.ppermute(block, axis, [((i - distance) % size, i) for i in range(size)])  1.43 us
    concatenate x1, other arithmetic, on_device(): pair_here = jnp.concatenate([key_vectors[0], value_vectors[0]], axis=1)  0.78 us
  transfers between devices with their start and end apart: 11, of which 4 were waited for; matrix products, arithmetic and copies ran while one was open for 0% of the time, Pallas kernels for 17%

profile of v17, /device:TPU:0, one launch (start us, length us, event | category | flops | bytes accessed | tf_op | source)
XLA Modules:
  0.0 29.7 jit_solution(1957212379048885226)
XLA Ops:
  0.6 0.8 %pad_maximum_fusion.here_ref.block_ref = bf16[128,256]{1,0:T(8,128)(2,1)S(1)} fusion(bf16[128,128]{1,0:T(8,128)(2,1)} %bitcast.5, bf16[128,128]{1,0:T(8,128)(2,1)} %bitcast.6), kind=kLoop, calls=%fused_computation | loop fusion | flops 131072 | bytes 131072 | tf_op jit(solution)/shard_map/concatenate | solution.py:314
  1.4 3.0 %collective-permute-start = (bf16[128,256]{1,0:T(8,128)(2,1)S(1)}, bf16[128,256]{1,0:T(8,128)(2,1)S(1)}, u32[]{:S(2)}, u32[]{:S(2)}) collective-permute-start(bf16[128,256]{1,0:T(8,128)(2,1)S(1)} %pad_maximum_fusion.here_ref.block_ref), channel_id=1, source_target_pairs={{16,0},{0,16},{17,1},{1,17},{18,2},{2,18},{19,3},{3,19},{20,4},{4,... | collective-permute-start | bytes 196616 | tf_op jit(solution)/shard_map/ppermute | solution.py:62
  4.4 1.0 %collective-permute-start.4 = (bf16[128,768]{1,0:T(8,128)(2,1)S(1)}, bf16[128,768]{1,0:T(8,128)(2,1)S(1)}, u32[]{:S(2)}, u32[]{:S(2)}) collective-permute-start(bf16[128,768]{1,0:T(8,128)(2,1)S(1)} %take.2), channel_id=1, source_target_pairs={{16,0},{0,16},{17,1},{1,17},{18,2},{2,18},{19,3},{3,19},{20,4},{4,... | collective-permute-start | bytes 589832 | tf_op jit(solution)/shard_map/ppermute | solution.py:62
  5.5 1.4 %collective-permute-done.pair_ref = bf16[128,256]{1,0:T(8,128)(2,1)S(1)} collective-permute-done((bf16[128,256]{1,0:T(8,128)(2,1)S(1)}, bf16[128,256]{1,0:T(8,128)(2,1)S(1)}, u32[]{:S(2)}, u32[]{:S(2)}) %collective-permute-start) | collective-permute-done | bytes 65568 | tf_op jit(solution)/shard_map/ppermute | solution.py:62
  6.9 4.5 %collective-permute-start.1 = (bf16[128,384]{1,0:T(8,128)(2,1)S(1)}, bf16[128,384]{1,0:T(8,128)(2,1)S(1)}, u32[]{:S(2)}, u32[]{:S(2)}) collective-permute-start(bf16[128,384]{1,0:T(8,128)(2,1)S(1)} %join.1.refs_3_.after), channel_id=1, source_target_pairs={{0,12},{4,8},{8,4},{12,0},{1,13},{5,9},{9,5},{13,1},{2,14},{6,10},... | collective-permute-start | bytes 294920 | tf_op jit(solution)/shard_map/ppermute | solution.py:57
  11.4 0.6 %collective-permute-start.3 = (bf16[128,384]{1,0:T(8,128)(2,1)S(1)}, bf16[128,384]{1,0:T(8,128)(2,1)S(1)}, u32[]{:S(2)}, u32[]{:S(2)}) collective-permute-start(bf16[128,384]{1,0:T(8,128)(2,1)S(1)} %join.1.refs_3_.after), channel_id=1, source_target_pairs={{0,4},{4,0},{8,12},{12,8},{1,5},{5,1},{9,13},{13,9},{2,6},{6,2},{1... | collective-permute-start | bytes 294920 | tf_op jit(solution)/shard_map/ppermute | solution.py:57
  12.1 0.0 copy-start
  12.1 0.0 copy-start.2
  12.1 1.9 %collective-permute-start.6 = (bf16[128,1280]{1,0:T(8,128)(2,1)S(1)}, bf16[128,1280]{1,0:T(8,128)(2,1)S(1)}, u32[]{:S(2)}, u32[]{:S(2)}) collective-permute-start(bf16[128,1280]{1,0:T(8,128)(2,1)S(1)} %take.3), channel_id=1, source_target_pairs={{16,0},{0,16},{17,1},{1,17},{18,2},{2,18},{19,3},{3,19},{20,4},{4,... | collective-permute-start | bytes 983048 | tf_op jit(solution)/shard_map/ppermute | solution.py:62
  14.0 0.6 %prepare.1.feature_ref = bf16[2,128,512]{2,1,0:T(8,128)(2,1)S(1)} custom-call(s32[8]{0:T(128)S(1)} %copy-done.3, f32[8,128]{1,0:T(8,128)S(1)} %touch.1.after), custom_call_target="tpu_custom_call" | custom-call | flops 3000000000 | tf_op jit(solution)/shard_map/prepare/pallas_call | solution.py:24
  14.6 0.9 %weigh.1.w_ref = bf16[2048,1024]{1,0:T(8,128)(2,1)S(1)} custom-call(bf16[2048,1024]{1,0:T(8,128)(2,1)S(1)} %bitcast.4, bf16[1,2048]{1,0:T(2,128)(2,1)S(1)} %copy-done.2, bf16[128,384]{1,0:T(8,128)(2,1)S(1)} %collective-permute-done.1.after.refs_0_), custom_call_target="tpu_custom_call" | custom-call | flops 1000000000 | tf_op jit(solution)/shard_map/weigh/pallas_call | solution.py:24
  15.5 2.6 %collective-permute-done.2.refs_1_ = bf16[128,384]{1,0:T(8,128)(2,1)S(1)} collective-permute-done((bf16[128,384]{1,0:T(8,128)(2,1)S(1)}, bf16[128,384]{1,0:T(8,128)(2,1)S(1)}, u32[]{:S(2)}, u32[]{:S(2)}) %collective-permute-start.2) | collective-permute-done | bytes 98336 | tf_op jit(solution)/shard_map/ppermute | solution.py:57
  18.1 1.4 %attend_first.1 = (bf16[1,2,256,512]{3,2,1,0:T(8,128)(2,1)S(1)}, bf16[1,512,256]{2,1,0:T(8,128)(2,1)S(1)}, bf16[128,768]{1,0:T(8,128)(2,1)S(1)}, f32[1,16]{1,0:T(1,128)S(1)}) custom-call(bf16[2048,1024]{1,0:T(8,128)(2,1)S(1)} %weigh.1.w_ref, bf16[2,128,512]{2,1,0:T(8,128)(2,1)S(1)} %prepare.1.feature_ref, ...), custom_call_target="tpu_custom_call" | custom-call | flops 2000000000 | tf_op jit(solution)/shard_map/attend_first/pallas_call | solution.py:24
  19.5 0.5 %collective-permute-start.5 = (f32[1,16]{1,0:T(1,128)S(1)}, f32[1,16]{1,0:T(1,128)S(1)}, u32[]{:S(2)}, u32[]{:S(2)}) collective-permute-start(f32[1,16]{1,0:T(1,128)S(1)} %get-tuple-element.12.left_ref), channel_id=1, source_target_pairs={{0,4},{4,0},{8,12},{12,8},{1,5},{5,1},{9,13},{13,9},{2,6},{6,2},{1... | collective-permute-start | bytes 200 | tf_op jit(solution)/shard_map/ppermute | solution.py:57
  20.0 1.4 %attend_last.1 = (bf16[128,1280]{1,0:T(8,128)(2,1)S(1)}, bf16[1,144,256]{2,1,0:T(8,128)(2,1)S(1)}, bf16[1,144,256]{2,1,0:T(8,128)(2,1)S(1)}, f32[128,128]{1,0:T(8,128)S(1)}) custom-call(bf16[128,1280]{1,0:T(8,128)(2,1)S(1)} %collective-permute-done.6.q_ref, bf16[1,2,256,512]{3,2,1,0:T(8,128)(2,1)S(1)} %get-tuple-element.13.kt_ref, ...), custom_call_target="tpu_custom_call" | custom-call | flops 1500000000 | tf_op jit(solution)/shard_map/attend_last/pallas_call | solution.py:24
  21.4 0.1 collective-permute-start.9
  21.5 0.5 %collective-permute-start.8 = (bf16[1,144,256]{2,1,0:T(8,128)(2,1)S(1)}, bf16[1,144,256]{2,1,0:T(8,128)(2,1)S(1)}, u32[]{:S(2)}, u32[]{:S(2)}) collective-permute-start(bf16[1,144,256]{2,1,0:T(8,128)(2,1)S(1)} %get-tuple-element.19), channel_id=1, source_target_pairs={{0,1},{1,0},{2,3},{3,2},{4,5},{5,4},{6,7},{7,6},{8,9},{9,8},{10,11... | collective-permute-start | bytes 221192 | tf_op jit(solution)/shard_map/ppermute | solution.py:375
  22.0 0.3 %project_keep.3.keep_ref = bf16[1,144,256]{2,1,0:T(8,128)(2,1)S(1)} custom-call(bf16[128,768]{1,0:T(8,128)(2,1)S(1)} %get-tuple-element.15.first_ref, bf16[128,1280]{1,0:T(8,128)(2,1)S(1)} %get-tuple-element.17.last_ref, bf16[2048,1024]{1,0:T(8,128)(2,1)S(1)} %weigh.1.w_ref, f32[128,128]{1,0:T(8,128)S(1)} %get-tuple-element.18.square_ref), custom_call_target="tpu_custom_call" | custom-call | flops 3000000000 | tf_op jit(solution)/shard_map/project_keep/pallas_call | solution.py:24
  22.4 0.4 %collective-permute-done.9.got_ref = bf16[1,144,256]{2,1,0:T(8,128)(2,1)S(1)} collective-permute-done((bf16[1,144,256]{2,1,0:T(8,128)(2,1)S(1)}, bf16[1,144,256]{2,1,0:T(8,128)(2,1)S(1)}, u32[]{:S(2)}, u32[]{:S(2)}) %collective-permute-start.9) | collective-permute-done | bytes 73760 | tf_op jit(solution)/shard_map/ppermute | solution.py:375
  22.8 1.6 %collective-permute-start.10 = (bf16[144,256]{1,0:T(8,128)(2,1)S(1)}, bf16[144,256]{1,0:T(8,128)(2,1)S(1)}, u32[]{:S(2)}, u32[]{:S(2)}) collective-permute-start(bf16[144,256]{1,0:T(8,128)(2,1)S(1)} %merge.1), channel_id=1, source_target_pairs={{0,2},{1,3},{2,0},{3,1},{4,6},{5,7},{6,4},{7,5},{8,10},{9,11},{10,... | collective-permute-start | bytes 221192 | tf_op jit(solution)/shard_map/ppermute | solution.py:412
  24.4 2.5 %collective-permute-start.7 = (f32[1,16]{1,0:T(1,128)S(1)}, f32[1,16]{1,0:T(1,128)S(1)}, u32[]{:S(2)}, u32[]{:S(2)}) collective-permute-start(f32[1,16]{1,0:T(1,128)S(1)} %larger.1.peak_ref), channel_id=1, source_target_pairs={{0,8},{4,12},{8,0},{12,4},{1,9},{5,13},{9,1},{13,5},{2,10},{6,14},... | collective-permute-start | bytes 200 | tf_op jit(solution)/shard_map/ppermute | solution.py:57
  26.9 0.3 %project_keep.2.keep_ref = bf16[1,144,256]{2,1,0:T(8,128)(2,1)S(1)} custom-call(bf16[128,768]{1,0:T(8,128)(2,1)S(1)} %get-tuple-element.15.first_ref, bf16[128,1280]{1,0:T(8,128)(2,1)S(1)} %get-tuple-element.17.last_ref, bf16[2048,1024]{1,0:T(8,128)(2,1)S(1)} %weigh.1.w_ref, f32[128,128]{1,0:T(8,128)S(1)} %get-tuple-element.18.square_ref), custom_call_target="tpu_custom_call" | custom-call | tf_op jit(solution)/shard_map/project_keep/pallas_call | solution.py:24
  27.2 1.6 %collective-permute-done.7.peak_got = f32[1,16]{1,0:T(1,128)S(1)} collective-permute-done((f32[1,16]{1,0:T(1,128)S(1)}, f32[1,16]{1,0:T(1,128)S(1)}, u32[]{:S(2)}, u32[]{:S(2)}) %collective-permute-start.7) | collective-permute-done | bytes 96 | tf_op jit(solution)/shard_map/ppermute | solution.py:57
  28.8 0.8 %finish.1 = (f32[1,16]{1,0:T(1,128)}, bf16[128,256]{1,0:T(8,128)(2,1)}) custom-call(f32[1,16]{1,0:T(1,128)S(1)} %larger.1.peak_ref, f32[1,16]{1,0:T(1,128)S(1)} %collective-permute-done.7.peak_got, bf16[1,144,256]{2,1,0:T(8,128)(2,1)S(1)} %project_keep.2.keep_ref, bf16[1,144,256]{2,1,0:T(8,128)(2,1)S(1)} %collective-permute-done.8.got_ref, ...), custom_call_target="tpu_custom_call" | custom-call | tf_op jit(solution)/shard_map/finish/pallas_call | solution.py:24
  (20 shorter events, 0.1 us)
Async XLA Ops:
  1.4 3.0 %copy-start.1 = (bf16[1,128,2048]{2,1,0:T(8,128)(2,1)S(1)}, bf16[1,128,2048]{2,1,0:T(8,128)(2,1)}, u32[]{:S(2)}) copy-start(bf16[1,128,2048]{2,1,0:T(8,128)(2,1)} %q_ref.3) | copy-start | bytes 1572868
  1.4 5.5 %collective-permute-start = (bf16[128,256]{1,0:T(8,128)(2,1)S(1)}, bf16[128,256]{1,0:T(8,128)(2,1)S(1)}, u32[]{:S(2)}, u32[]{:S(2)}) collective-permute-start(bf16[128,256]{1,0:T(8,128)(2,1)S(1)} %pad_maximum_fusion.here_ref.block_ref), channel_id=1, source_target_pairs={{16,0},{0,16},{17,1},{1,17},{18,2},{2,18},{19,3},{3,19},{20,4},{4,... | collective-permute-start | bytes 196616 | tf_op jit(solution)/shard_map/ppermute | solution.py:62
  4.4 9.5 %copy-start.3 = (s32[8]{0:T(128)S(1)}, s32[8]{0:T(128)}, u32[]{:S(2)}) copy-start(s32[8]{0:T(128)} %order_ref.1) | copy-start | bytes 100
  4.4 13.6 %collective-permute-start.4 = (bf16[128,768]{1,0:T(8,128)(2,1)S(1)}, bf16[128,768]{1,0:T(8,128)(2,1)S(1)}, u32[]{:S(2)}, u32[]{:S(2)}) collective-permute-start(bf16[128,768]{1,0:T(8,128)(2,1)S(1)} %take.2), channel_id=1, source_target_pairs={{16,0},{0,16},{17,1},{1,17},{18,2},{2,18},{19,3},{3,19},{20,4},{4,... | collective-permute-start | bytes 589832 | tf_op jit(solution)/shard_map/ppermute | solution.py:62
  6.9 7.7 %collective-permute-start.1 = (bf16[128,384]{1,0:T(8,128)(2,1)S(1)}, bf16[128,384]{1,0:T(8,128)(2,1)S(1)}, u32[]{:S(2)}, u32[]{:S(2)}) collective-permute-start(bf16[128,384]{1,0:T(8,128)(2,1)S(1)} %join.1.refs_3_.after), channel_id=1, source_target_pairs={{0,12},{4,8},{8,4},{12,0},{1,13},{5,9},{9,5},{13,1},{2,14},{6,10},... | collective-permute-start | bytes 294920 | tf_op jit(solution)/shard_map/ppermute | solution.py:57
  11.4 6.7 %collective-permute-start.2 = (bf16[128,384]{1,0:T(8,128)(2,1)S(1)}, bf16[128,384]{1,0:T(8,128)(2,1)S(1)}, u32[]{:S(2)}, u32[]{:S(2)}) collective-permute-start(bf16[128,384]{1,0:T(8,128)(2,1)S(1)} %join.1.refs_3_.after), channel_id=1, source_target_pairs={{0,8},{4,12},{8,0},{12,4},{1,9},{5,13},{9,1},{13,5},{2,10},{6,14},... | collective-permute-start | bytes 294920 | tf_op jit(solution)/shard_map/ppermute | solution.py:57
  11.4 6.7 %collective-permute-start.3 = (bf16[128,384]{1,0:T(8,128)(2,1)S(1)}, bf16[128,384]{1,0:T(8,128)(2,1)S(1)}, u32[]{:S(2)}, u32[]{:S(2)}) collective-permute-start(bf16[128,384]{1,0:T(8,128)(2,1)S(1)} %join.1.refs_3_.after), channel_id=1, source_target_pairs={{0,4},{4,0},{8,12},{12,8},{1,5},{5,1},{9,13},{13,9},{2,6},{6,2},{1... | collective-permute-start | bytes 294920 | tf_op jit(solution)/shard_map/ppermute | solution.py:57
  12.1 2.5 %copy-start = (bf16[1,2048,1024]{2,1,0:T(8,128)(2,1)S(1)}, bf16[1,2048,1024]{2,1,0:T(8,128)(2,1)}, u32[]{:S(2)}) copy-start(bf16[1,2048,1024]{2,1,0:T(8,128)(2,1)} %param.11) | copy-start | bytes 12582916
  12.1 2.5 %copy-start.2 = (bf16[1,2048]{1,0:T(2,128)(2,1)S(1)}, bf16[1,2048]{1,0:T(2,128)(2,1)}, u32[]{:S(2)}) copy-start(bf16[1,2048]{1,0:T(2,128)(2,1)} %gain_ref.1) | copy-start | bytes 12292
  12.1 7.9 %collective-permute-start.6 = (bf16[128,1280]{1,0:T(8,128)(2,1)S(1)}, bf16[128,1280]{1,0:T(8,128)(2,1)S(1)}, u32[]{:S(2)}, u32[]{:S(2)}) collective-permute-start(bf16[128,1280]{1,0:T(8,128)(2,1)S(1)} %take.3), channel_id=1, source_target_pairs={{16,0},{0,16},{17,1},{1,17},{18,2},{2,18},{19,3},{3,19},{20,4},{4,... | collective-permute-start | bytes 983048 | tf_op jit(solution)/shard_map/ppermute | solution.py:62
  19.5 4.9 %collective-permute-start.5 = (f32[1,16]{1,0:T(1,128)S(1)}, f32[1,16]{1,0:T(1,128)S(1)}, u32[]{:S(2)}, u32[]{:S(2)}) collective-permute-start(f32[1,16]{1,0:T(1,128)S(1)} %get-tuple-element.12.left_ref), channel_id=1, source_target_pairs={{0,4},{4,0},{8,12},{12,8},{1,5},{5,1},{9,13},{13,9},{2,6},{6,2},{1... | collective-permute-start | bytes 200 | tf_op jit(solution)/shard_map/ppermute | solution.py:57
  21.4 1.3 %collective-permute-start.9 = (bf16[1,144,256]{2,1,0:T(8,128)(2,1)S(1)}, bf16[1,144,256]{2,1,0:T(8,128)(2,1)S(1)}, u32[]{:S(2)}, u32[]{:S(2)}) collective-permute-start(bf16[1,144,256]{2,1,0:T(8,128)(2,1)S(1)} %get-tuple-element.16.after), channel_id=1, source_target_pairs={{0,1},{1,0},{2,3},{3,2},{4,5},{5,4},{6,7},{7,6},{8,9},{9,8},{10,11... | collective-permute-start | bytes 221192 | tf_op jit(solution)/shard_map/ppermute | solution.py:375
  21.5 7.3 %collective-permute-start.8 = (bf16[1,144,256]{2,1,0:T(8,128)(2,1)S(1)}, bf16[1,144,256]{2,1,0:T(8,128)(2,1)S(1)}, u32[]{:S(2)}, u32[]{:S(2)}) collective-permute-start(bf16[1,144,256]{2,1,0:T(8,128)(2,1)S(1)} %get-tuple-element.19), channel_id=1, source_target_pairs={{0,1},{1,0},{2,3},{3,2},{4,5},{5,4},{6,7},{7,6},{8,9},{9,8},{10,11... | collective-permute-start | bytes 221192 | tf_op jit(solution)/shard_map/ppermute | solution.py:375
  22.8 6.0 %collective-permute-start.10 = (bf16[144,256]{1,0:T(8,128)(2,1)S(1)}, bf16[144,256]{1,0:T(8,128)(2,1)S(1)}, u32[]{:S(2)}, u32[]{:S(2)}) collective-permute-start(bf16[144,256]{1,0:T(8,128)(2,1)S(1)} %merge.1), channel_id=1, source_target_pairs={{0,2},{1,3},{2,0},{3,1},{4,6},{5,7},{6,4},{7,5},{8,10},{9,11},{10,... | collective-permute-start | bytes 221192 | tf_op jit(solution)/shard_map/ppermute | solution.py:412
  24.4 4.4 %collective-permute-start.7 = (f32[1,16]{1,0:T(1,128)S(1)}, f32[1,16]{1,0:T(1,128)S(1)}, u32[]{:S(2)}, u32[]{:S(2)}) collective-permute-start(f32[1,16]{1,0:T(1,128)S(1)} %larger.1.peak_ref), channel_id=1, source_target_pairs={{0,8},{4,12},{8,0},{12,4},{1,9},{5,13},{9,1},{13,5},{2,10},{6,14},... | collective-permute-start | bytes 200 | tf_op jit(solution)/shard_map/ppermute | solution.py:57

commit v18 on v14

--- a/solution.py
+++ b/solution.py
@@ -220,8 +220,9 @@
 def attend_last(
     first_head, heads, q_ref, kt_ref, v_ref, first_ref, w_ref, ctx_ref, far_ref, near_ref, square_ref
 ):
+    square_ref[...] = square_sums(first_ref)
     interleave(attention_units(first_head, heads, q_ref, kt_ref, v_ref, ctx_ref))
-    squares = square_sums(first_ref) + square_sums(ctx_ref)
+    squares = square_ref[...] + square_sums(ctx_ref)
     square_ref[...] = squares
     other = 1 - lax.rem(lax.axis_index("tp"), 2)
     project(first_ref, ctx_ref, w_ref, other, 1, squares, far_ref)

time: 29.8 us -> 29.8 us (level)
  no operation moved by 1% of the time
where the time goes in v18:
time: 29.8 us; the launch traced here: 29.6 us
  starting transfers between devices  16.2 us (54%)
  waiting for transfers between devices  6.01 us (20%)
  Pallas kernels  5.89 us (20%)
  other arithmetic  0.78 us (3%)
  between operations  0.75 us (3%)
    ppermute x5, starting transfers between devices, swapped(): lax.ppermute(block, axis, [(i, partner(i, step, size)) for i in range(siz...  8.13 us
    ppermute x3, starting transfers between devices, shifted(): lax.ppermute(block, axis, [((i - distance) % size, i) for i in range(size)])  5.9 us
    pallas_call x13, Pallas kernels, call(): pl.pallas_call(kernel, out_shape=outs, in_specs=specs or [WHOLE] * len(ar...  5.89 us
    ppermute x5, waiting for transfers between devices, swapped(): lax.ppermute(block, axis, [(i, partner(i, step, size)) for i in range(siz...  4.16 us
    ppermute x1, starting transfers between devices, on_device(): lax.ppermute(block, 'tp', [(i, (i + 2 * (step + 1)) % peers) for i in ran...  1.59 us
    ppermute x3, waiting for transfers between devices, shifted(): lax.ppermute(block, axis, [((i - distance) % size, i) for i in range(size)])  1.43 us
    concatenate x1, other arithmetic, on_device(): pair_here = jnp.concatenate([key_vectors[0], value_vectors[0]], axis=1)  0.78 us
  transfers between devices with their start and end apart: 11, of which 4 were waited for; matrix products, arithmetic and copies ran while one was open for 0% of the time, Pallas kernels for 17%

profile of v18, /device:TPU:0, one launch (start us, length us, event | category | flops | bytes accessed | tf_op | source)
XLA Modules:
  0.0 29.6 jit_solution(3162277150079672624)
XLA Ops:
  0.6 0.8 %pad_maximum_fusion.here_ref.block_ref = bf16[128,256]{1,0:T(8,128)(2,1)S(1)} fusion(bf16[128,128]{1,0:T(8,128)(2,1)} %bitcast.5, bf16[128,128]{1,0:T(8,128)(2,1)} %bitcast.6), kind=kLoop, calls=%fused_computation | loop fusion | flops 131072 | bytes 131072 | tf_op jit(solution)/shard_map/concatenate | solution.py:315
  1.4 3.0 %collective-permute-start = (bf16[128,256]{1,0:T(8,128)(2,1)S(1)}, bf16[128,256]{1,0:T(8,128)(2,1)S(1)}, u32[]{:S(2)}, u32[]{:S(2)}) collective-permute-start(bf16[128,256]{1,0:T(8,128)(2,1)S(1)} %pad_maximum_fusion.here_ref.block_ref), channel_id=1, source_target_pairs={{16,0},{0,16},{17,1},{1,17},{18,2},{2,18},{19,3},{3,19},{20,4},{4,... | collective-permute-start | bytes 196616 | tf_op jit(solution)/shard_map/ppermute | solution.py:62
  4.4 1.0 %collective-permute-start.4 = (bf16[128,768]{1,0:T(8,128)(2,1)S(1)}, bf16[128,768]{1,0:T(8,128)(2,1)S(1)}, u32[]{:S(2)}, u32[]{:S(2)}) collective-permute-start(bf16[128,768]{1,0:T(8,128)(2,1)S(1)} %take.2), channel_id=1, source_target_pairs={{16,0},{0,16},{17,1},{1,17},{18,2},{2,18},{19,3},{3,19},{20,4},{4,... | collective-permute-start | bytes 589832 | tf_op jit(solution)/shard_map/ppermute | solution.py:62
  5.5 1.4 %collective-permute-done.pair_ref = bf16[128,256]{1,0:T(8,128)(2,1)S(1)} collective-permute-done((bf16[128,256]{1,0:T(8,128)(2,1)S(1)}, bf16[128,256]{1,0:T(8,128)(2,1)S(1)}, u32[]{:S(2)}, u32[]{:S(2)}) %collective-permute-start) | collective-permute-done | bytes 65568 | tf_op jit(solution)/shard_map/ppermute | solution.py:62
  6.9 4.5 %collective-permute-start.1 = (bf16[128,384]{1,0:T(8,128)(2,1)S(1)}, bf16[128,384]{1,0:T(8,128)(2,1)S(1)}, u32[]{:S(2)}, u32[]{:S(2)}) collective-permute-start(bf16[128,384]{1,0:T(8,128)(2,1)S(1)} %join.1.refs_3_.after), channel_id=1, source_target_pairs={{0,12},{4,8},{8,4},{12,0},{1,13},{5,9},{9,5},{13,1},{2,14},{6,10},... | collective-permute-start | bytes 294920 | tf_op jit(solution)/shard_map/ppermute | solution.py:57
  11.4 0.6 %collective-permute-start.3 = (bf16[128,384]{1,0:T(8,128)(2,1)S(1)}, bf16[128,384]{1,0:T(8,128)(2,1)S(1)}, u32[]{:S(2)}, u32[]{:S(2)}) collective-permute-start(bf16[128,384]{1,0:T(8,128)(2,1)S(1)} %join.1.refs_3_.after), channel_id=1, source_target_pairs={{0,4},{4,0},{8,12},{12,8},{1,5},{5,1},{9,13},{13,9},{2,6},{6,2},{1... | collective-permute-start | bytes 294920 | tf_op jit(solution)/shard_map/ppermute | solution.py:57
  12.1 0.0 copy-start
  12.1 0.0 copy-start.2
  12.1 1.9 %collective-permute-start.6 = (bf16[128,1280]{1,0:T(8,128)(2,1)S(1)}, bf16[128,1280]{1,0:T(8,128)(2,1)S(1)}, u32[]{:S(2)}, u32[]{:S(2)}) collective-permute-start(bf16[128,1280]{1,0:T(8,128)(2,1)S(1)} %take.3), channel_id=1, source_target_pairs={{16,0},{0,16},{17,1},{1,17},{18,2},{2,18},{19,3},{3,19},{20,4},{4,... | collective-permute-start | bytes 983048 | tf_op jit(solution)/shard_map/ppermute | solution.py:62
  14.0 0.6 %prepare.1.feature_ref = bf16[2,128,512]{2,1,0:T(8,128)(2,1)S(1)} custom-call(s32[8]{0:T(128)S(1)} %copy-done.3, f32[8,128]{1,0:T(8,128)S(1)} %touch.1.after), custom_call_target="tpu_custom_call" | custom-call | flops 3000000000 | tf_op jit(solution)/shard_map/prepare/pallas_call | solution.py:24
  14.6 0.9 %weigh.1.w_ref = bf16[2048,1024]{1,0:T(8,128)(2,1)S(1)} custom-call(bf16[2048,1024]{1,0:T(8,128)(2,1)S(1)} %bitcast.4, bf16[1,2048]{1,0:T(2,128)(2,1)S(1)} %copy-done.2, bf16[128,384]{1,0:T(8,128)(2,1)S(1)} %collective-permute-done.1.after.refs_0_), custom_call_target="tpu_custom_call" | custom-call | flops 1000000000 | tf_op jit(solution)/shard_map/weigh/pallas_call | solution.py:24
  15.5 2.6 %collective-permute-done.2.refs_1_ = bf16[128,384]{1,0:T(8,128)(2,1)S(1)} collective-permute-done((bf16[128,384]{1,0:T(8,128)(2,1)S(1)}, bf16[128,384]{1,0:T(8,128)(2,1)S(1)}, u32[]{:S(2)}, u32[]{:S(2)}) %collective-permute-start.2) | collective-permute-done | bytes 98336 | tf_op jit(solution)/shard_map/ppermute | solution.py:57
  18.1 1.4 %attend_first.1 = (bf16[1,2,256,512]{3,2,1,0:T(8,128)(2,1)S(1)}, bf16[1,512,256]{2,1,0:T(8,128)(2,1)S(1)}, bf16[128,768]{1,0:T(8,128)(2,1)S(1)}, f32[1,16]{1,0:T(1,128)S(1)}) custom-call(bf16[2048,1024]{1,0:T(8,128)(2,1)S(1)} %weigh.1.w_ref, bf16[2,128,512]{2,1,0:T(8,128)(2,1)S(1)} %prepare.1.feature_ref, ...), custom_call_target="tpu_custom_call" | custom-call | flops 2000000000 | tf_op jit(solution)/shard_map/attend_first/pallas_call | solution.py:24
  19.5 0.5 %collective-permute-start.5 = (f32[1,16]{1,0:T(1,128)S(1)}, f32[1,16]{1,0:T(1,128)S(1)}, u32[]{:S(2)}, u32[]{:S(2)}) collective-permute-start(f32[1,16]{1,0:T(1,128)S(1)} %get-tuple-element.12.left_ref), channel_id=1, source_target_pairs={{0,4},{4,0},{8,12},{12,8},{1,5},{5,1},{9,13},{13,9},{2,6},{6,2},{1... | collective-permute-start | bytes 200 | tf_op jit(solution)/shard_map/ppermute | solution.py:57
  20.0 1.5 %attend_last.1 = (bf16[128,1280]{1,0:T(8,128)(2,1)S(1)}, bf16[1,144,256]{2,1,0:T(8,128)(2,1)S(1)}, bf16[1,144,256]{2,1,0:T(8,128)(2,1)S(1)}, f32[128,128]{1,0:T(8,128)S(1)}) custom-call(bf16[128,1280]{1,0:T(8,128)(2,1)S(1)} %collective-permute-done.6.q_ref, bf16[1,2,256,512]{3,2,1,0:T(8,128)(2,1)S(1)} %get-tuple-element.13.kt_ref, ...), custom_call_target="tpu_custom_call" | custom-call | flops 1500000000 | tf_op jit(solution)/shard_map/attend_last/pallas_call | solution.py:24
  21.4 0.1 collective-permute-start.9
  21.5 0.5 %collective-permute-start.8 = (bf16[1,144,256]{2,1,0:T(8,128)(2,1)S(1)}, bf16[1,144,256]{2,1,0:T(8,128)(2,1)S(1)}, u32[]{:S(2)}, u32[]{:S(2)}) collective-permute-start(bf16[1,144,256]{2,1,0:T(8,128)(2,1)S(1)} %get-tuple-element.19), channel_id=1, source_target_pairs={{0,1},{1,0},{2,3},{3,2},{4,5},{5,4},{6,7},{7,6},{8,9},{9,8},{10,11... | collective-permute-start | bytes 221192 | tf_op jit(solution)/shard_map/ppermute | solution.py:376
  22.0 0.3 %project_keep.3.keep_ref = bf16[1,144,256]{2,1,0:T(8,128)(2,1)S(1)} custom-call(bf16[128,768]{1,0:T(8,128)(2,1)S(1)} %get-tuple-element.15.first_ref, bf16[128,1280]{1,0:T(8,128)(2,1)S(1)} %get-tuple-element.17.last_ref, bf16[2048,1024]{1,0:T(8,128)(2,1)S(1)} %weigh.1.w_ref, f32[128,128]{1,0:T(8,128)S(1)} %get-tuple-element.18.square_ref), custom_call_target="tpu_custom_call" | custom-call | flops 3000000000 | tf_op jit(solution)/shard_map/project_keep/pallas_call | solution.py:24
  22.3 0.4 %collective-permute-done.9.got_ref = bf16[1,144,256]{2,1,0:T(8,128)(2,1)S(1)} collective-permute-done((bf16[1,144,256]{2,1,0:T(8,128)(2,1)S(1)}, bf16[1,144,256]{2,1,0:T(8,128)(2,1)S(1)}, u32[]{:S(2)}, u32[]{:S(2)}) %collective-permute-start.9) | collective-permute-done | bytes 73760 | tf_op jit(solution)/shard_map/ppermute | solution.py:376
  22.8 1.6 %collective-permute-start.10 = (bf16[144,256]{1,0:T(8,128)(2,1)S(1)}, bf16[144,256]{1,0:T(8,128)(2,1)S(1)}, u32[]{:S(2)}, u32[]{:S(2)}) collective-permute-start(bf16[144,256]{1,0:T(8,128)(2,1)S(1)} %merge.1), channel_id=1, source_target_pairs={{0,2},{1,3},{2,0},{3,1},{4,6},{5,7},{6,4},{7,5},{8,10},{9,11},{10,... | collective-permute-start | bytes 221192 | tf_op jit(solution)/shard_map/ppermute | solution.py:413
  24.4 2.5 %collective-permute-start.7 = (f32[1,16]{1,0:T(1,128)S(1)}, f32[1,16]{1,0:T(1,128)S(1)}, u32[]{:S(2)}, u32[]{:S(2)}) collective-permute-start(f32[1,16]{1,0:T(1,128)S(1)} %larger.1.peak_ref), channel_id=1, source_target_pairs={{0,8},{4,12},{8,0},{12,4},{1,9},{5,13},{9,1},{13,5},{2,10},{6,14},... | collective-permute-start | bytes 200 | tf_op jit(solution)/shard_map/ppermute | solution.py:57
  26.9 0.3 %project_keep.2.keep_ref = bf16[1,144,256]{2,1,0:T(8,128)(2,1)S(1)} custom-call(bf16[128,768]{1,0:T(8,128)(2,1)S(1)} %get-tuple-element.15.first_ref, bf16[128,1280]{1,0:T(8,128)(2,1)S(1)} %get-tuple-element.17.last_ref, bf16[2048,1024]{1,0:T(8,128)(2,1)S(1)} %weigh.1.w_ref, f32[128,128]{1,0:T(8,128)S(1)} %get-tuple-element.18.square_ref), custom_call_target="tpu_custom_call" | custom-call | tf_op jit(solution)/shard_map/project_keep/pallas_call | solution.py:24
  27.2 1.6 %collective-permute-done.7.peak_got = f32[1,16]{1,0:T(1,128)S(1)} collective-permute-done((f32[1,16]{1,0:T(1,128)S(1)}, f32[1,16]{1,0:T(1,128)S(1)}, u32[]{:S(2)}, u32[]{:S(2)}) %collective-permute-start.7) | collective-permute-done | bytes 96 | tf_op jit(solution)/shard_map/ppermute | solution.py:57
  28.8 0.8 %finish.1 = (f32[1,16]{1,0:T(1,128)}, bf16[128,256]{1,0:T(8,128)(2,1)}) custom-call(f32[1,16]{1,0:T(1,128)S(1)} %larger.1.peak_ref, f32[1,16]{1,0:T(1,128)S(1)} %collective-permute-done.7.peak_got, bf16[1,144,256]{2,1,0:T(8,128)(2,1)S(1)} %project_keep.2.keep_ref, bf16[1,144,256]{2,1,0:T(8,128)(2,1)S(1)} %collective-permute-done.8.got_ref, ...), custom_call_target="tpu_custom_call" | custom-call | tf_op jit(solution)/shard_map/finish/pallas_call | solution.py:24
  (20 shorter events, 0.1 us)
Async XLA Ops:
  1.4 3.0 %copy-start.1 = (bf16[1,128,2048]{2,1,0:T(8,128)(2,1)S(1)}, bf16[1,128,2048]{2,1,0:T(8,128)(2,1)}, u32[]{:S(2)}) copy-start(bf16[1,128,2048]{2,1,0:T(8,128)(2,1)} %q_ref.3) | copy-start | bytes 1572868
  1.4 5.5 %collective-permute-start = (bf16[128,256]{1,0:T(8,128)(2,1)S(1)}, bf16[128,256]{1,0:T(8,128)(2,1)S(1)}, u32[]{:S(2)}, u32[]{:S(2)}) collective-permute-start(bf16[128,256]{1,0:T(8,128)(2,1)S(1)} %pad_maximum_fusion.here_ref.block_ref), channel_id=1, source_target_pairs={{16,0},{0,16},{17,1},{1,17},{18,2},{2,18},{19,3},{3,19},{20,4},{4,... | collective-permute-start | bytes 196616 | tf_op jit(solution)/shard_map/ppermute | solution.py:62
  4.4 9.5 %copy-start.3 = (s32[8]{0:T(128)S(1)}, s32[8]{0:T(128)}, u32[]{:S(2)}) copy-start(s32[8]{0:T(128)} %order_ref.1) | copy-start | bytes 100
  4.4 13.6 %collective-permute-start.4 = (bf16[128,768]{1,0:T(8,128)(2,1)S(1)}, bf16[128,768]{1,0:T(8,128)(2,1)S(1)}, u32[]{:S(2)}, u32[]{:S(2)}) collective-permute-start(bf16[128,768]{1,0:T(8,128)(2,1)S(1)} %take.2), channel_id=1, source_target_pairs={{16,0},{0,16},{17,1},{1,17},{18,2},{2,18},{19,3},{3,19},{20,4},{4,... | collective-permute-start | bytes 589832 | tf_op jit(solution)/shard_map/ppermute | solution.py:62
  6.9 7.7 %collective-permute-start.1 = (bf16[128,384]{1,0:T(8,128)(2,1)S(1)}, bf16[128,384]{1,0:T(8,128)(2,1)S(1)}, u32[]{:S(2)}, u32[]{:S(2)}) collective-permute-start(bf16[128,384]{1,0:T(8,128)(2,1)S(1)} %join.1.refs_3_.after), channel_id=1, source_target_pairs={{0,12},{4,8},{8,4},{12,0},{1,13},{5,9},{9,5},{13,1},{2,14},{6,10},... | collective-permute-start | bytes 294920 | tf_op jit(solution)/shard_map/ppermute | solution.py:57
  11.4 6.7 %collective-permute-start.2 = (bf16[128,384]{1,0:T(8,128)(2,1)S(1)}, bf16[128,384]{1,0:T(8,128)(2,1)S(1)}, u32[]{:S(2)}, u32[]{:S(2)}) collective-permute-start(bf16[128,384]{1,0:T(8,128)(2,1)S(1)} %join.1.refs_3_.after), channel_id=1, source_target_pairs={{0,8},{4,12},{8,0},{12,4},{1,9},{5,13},{9,1},{13,5},{2,10},{6,14},... | collective-permute-start | bytes 294920 | tf_op jit(solution)/shard_map/ppermute | solution.py:57
  11.4 6.7 %collective-permute-start.3 = (bf16[128,384]{1,0:T(8,128)(2,1)S(1)}, bf16[128,384]{1,0:T(8,128)(2,1)S(1)}, u32[]{:S(2)}, u32[]{:S(2)}) collective-permute-start(bf16[128,384]{1,0:T(8,128)(2,1)S(1)} %join.1.refs_3_.after), channel_id=1, source_target_pairs={{0,4},{4,0},{8,12},{12,8},{1,5},{5,1},{9,13},{13,9},{2,6},{6,2},{1... | collective-permute-start | bytes 294920 | tf_op jit(solution)/shard_map/ppermute | solution.py:57
  12.1 2.5 %copy-start = (bf16[1,2048,1024]{2,1,0:T(8,128)(2,1)S(1)}, bf16[1,2048,1024]{2,1,0:T(8,128)(2,1)}, u32[]{:S(2)}) copy-start(bf16[1,2048,1024]{2,1,0:T(8,128)(2,1)} %param.11) | copy-start | bytes 12582916
  12.1 2.5 %copy-start.2 = (bf16[1,2048]{1,0:T(2,128)(2,1)S(1)}, bf16[1,2048]{1,0:T(2,128)(2,1)}, u32[]{:S(2)}) copy-start(bf16[1,2048]{1,0:T(2,128)(2,1)} %gain_ref.1) | copy-start | bytes 12292
  12.1 7.9 %collective-permute-start.6 = (bf16[128,1280]{1,0:T(8,128)(2,1)S(1)}, bf16[128,1280]{1,0:T(8,128)(2,1)S(1)}, u32[]{:S(2)}, u32[]{:S(2)}) collective-permute-start(bf16[128,1280]{1,0:T(8,128)(2,1)S(1)} %take.3), channel_id=1, source_target_pairs={{16,0},{0,16},{17,1},{1,17},{18,2},{2,18},{19,3},{3,19},{20,4},{4,... | collective-permute-start | bytes 983048 | tf_op jit(solution)/shard_map/ppermute | solution.py:62
  19.5 4.9 %collective-permute-start.5 = (f32[1,16]{1,0:T(1,128)S(1)}, f32[1,16]{1,0:T(1,128)S(1)}, u32[]{:S(2)}, u32[]{:S(2)}) collective-permute-start(f32[1,16]{1,0:T(1,128)S(1)} %get-tuple-element.12.left_ref), channel_id=1, source_target_pairs={{0,4},{4,0},{8,12},{12,8},{1,5},{5,1},{9,13},{13,9},{2,6},{6,2},{1... | collective-permute-start | bytes 200 | tf_op jit(solution)/shard_map/ppermute | solution.py:57
  21.4 1.3 %collective-permute-start.9 = (bf16[1,144,256]{2,1,0:T(8,128)(2,1)S(1)}, bf16[1,144,256]{2,1,0:T(8,128)(2,1)S(1)}, u32[]{:S(2)}, u32[]{:S(2)}) collective-permute-start(bf16[1,144,256]{2,1,0:T(8,128)(2,1)S(1)} %get-tuple-element.16.after), channel_id=1, source_target_pairs={{0,1},{1,0},{2,3},{3,2},{4,5},{5,4},{6,7},{7,6},{8,9},{9,8},{10,11... | collective-permute-start | bytes 221192 | tf_op jit(solution)/shard_map/ppermute | solution.py:376
  21.5 7.3 %collective-permute-start.8 = (bf16[1,144,256]{2,1,0:T(8,128)(2,1)S(1)}, bf16[1,144,256]{2,1,0:T(8,128)(2,1)S(1)}, u32[]{:S(2)}, u32[]{:S(2)}) collective-permute-start(bf16[1,144,256]{2,1,0:T(8,128)(2,1)S(1)} %get-tuple-element.19), channel_id=1, source_target_pairs={{0,1},{1,0},{2,3},{3,2},{4,5},{5,4},{6,7},{7,6},{8,9},{9,8},{10,11... | collective-permute-start | bytes 221192 | tf_op jit(solution)/shard_map/ppermute | solution.py:376
  22.8 6.0 %collective-permute-start.10 = (bf16[144,256]{1,0:T(8,128)(2,1)S(1)}, bf16[144,256]{1,0:T(8,128)(2,1)S(1)}, u32[]{:S(2)}, u32[]{:S(2)}) collective-permute-start(bf16[144,256]{1,0:T(8,128)(2,1)S(1)} %merge.1), channel_id=1, source_target_pairs={{0,2},{1,3},{2,0},{3,1},{4,6},{5,7},{6,4},{7,5},{8,10},{9,11},{10,... | collective-permute-start | bytes 221192 | tf_op jit(solution)/shard_map/ppermute | solution.py:413
  24.4 4.4 %collective-permute-start.7 = (f32[1,16]{1,0:T(1,128)S(1)}, f32[1,16]{1,0:T(1,128)S(1)}, u32[]{:S(2)}, u32[]{:S(2)}) collective-permute-start(f32[1,16]{1,0:T(1,128)S(1)} %larger.1.peak_ref), channel_id=1, source_target_pairs={{0,8},{4,12},{8,0},{12,4},{1,9},{5,13},{9,1},{13,5},{2,10},{6,14},... | collective-permute-start | bytes 200 | tf_op jit(solution)/shard_map/ppermute | solution.py:57

commit v19 on v18

--- a/solution.py
+++ b/solution.py
@@ -314,7 +314,7 @@
 
     pair_here = jnp.concatenate([key_vectors[0], value_vectors[0]], axis=1)
     pair = shifted(pair_here, "pp", 1)
-    cut = heads * 3 // 8
+    cut = heads * 7 // 16
     counts = [cut, heads - cut]
     starts = [0, cut]
     crossed = []

time: 29.8 us -> 30 us (level)
  transfers between devices with their start and end apart: 11 -> 11, of which waited for: 4 -> 4; matrix products, arithmetic and copies ran while one was open for 0% -> 0% of each run, Pallas kernels for 17% -> 18%
where the time goes in v19:
time: 30 us; the launch traced here: 29.8 us
  starting transfers between devices  16.2 us (54%)
  Pallas kernels  6.04 us (20%)
  waiting for transfers between devices  6.04 us (20%)
  other arithmetic  0.78 us (3%)
  between operations  0.75 us (2%)
    ppermute x5, starting transfers between devices, swapped(): lax.ppermute(block, axis, [(i, partner(i, step, size)) for i in range(siz...  8.12 us
    pallas_call x13, Pallas kernels, call(): pl.pallas_call(kernel, out_shape=outs, in_specs=specs or [WHOLE] * len(ar...  6.04 us
    ppermute x3, starting transfers between devices, shifted(): lax.ppermute(block, axis, [((i - distance) % size, i) for i in range(size)])  5.9 us
    ppermute x5, waiting for transfers between devices, swapped(): lax.ppermute(block, axis, [(i, partner(i, step, size)) for i in range(siz...  4.17 us
    ppermute x1, starting transfers between devices, on_device(): lax.ppermute(block, 'tp', [(i, (i + 2 * (step + 1)) % peers) for i in ran...  1.57 us
    ppermute x3, waiting for transfers between devices, shifted(): lax.ppermute(block, axis, [((i - distance) % size, i) for i in range(size)])  1.43 us
    concatenate x1, other arithmetic, on_device(): pair_here = jnp.concatenate([key_vectors[0], value_vectors[0]], axis=1)  0.78 us
  transfers between devices with their start and end apart: 11, of which 4 were waited for; matrix products, arithmetic and copies ran while one was open for 0% of the time, Pallas kernels for 18%

profile of v19, /device:TPU:0, one launch (start us, length us, event | category | flops | bytes accessed | tf_op | source)
XLA Modules:
  0.0 29.8 jit_solution(17147506363648968611)
XLA Ops:
  0.6 0.8 %pad_maximum_fusion.here_ref.block_ref = bf16[128,256]{1,0:T(8,128)(2,1)S(1)} fusion(bf16[128,128]{1,0:T(8,128)(2,1)} %bitcast.5, bf16[128,128]{1,0:T(8,128)(2,1)} %bitcast.6), kind=kLoop, calls=%fused_computation | loop fusion | flops 131072 | bytes 131072 | tf_op jit(solution)/shard_map/concatenate | solution.py:315
  1.4 3.0 %collective-permute-start = (bf16[128,256]{1,0:T(8,128)(2,1)S(1)}, bf16[128,256]{1,0:T(8,128)(2,1)S(1)}, u32[]{:S(2)}, u32[]{:S(2)}) collective-permute-start(bf16[128,256]{1,0:T(8,128)(2,1)S(1)} %pad_maximum_fusion.here_ref.block_ref), channel_id=1, source_target_pairs={{16,0},{0,16},{17,1},{1,17},{18,2},{2,18},{19,3},{3,19},{20,4},{4,... | collective-permute-start | bytes 196616 | tf_op jit(solution)/shard_map/ppermute | solution.py:62
  4.5 1.0 %collective-permute-start.4 = (bf16[128,896]{1,0:T(8,128)(2,1)S(1)}, bf16[128,896]{1,0:T(8,128)(2,1)S(1)}, u32[]{:S(2)}, u32[]{:S(2)}) collective-permute-start(bf16[128,896]{1,0:T(8,128)(2,1)S(1)} %take.2), channel_id=1, source_target_pairs={{16,0},{0,16},{17,1},{1,17},{18,2},{2,18},{19,3},{3,19},{20,4},{4,... | collective-permute-start | bytes 688136 | tf_op jit(solution)/shard_map/ppermute | solution.py:62
  5.5 1.4 %collective-permute-done.pair_ref = bf16[128,256]{1,0:T(8,128)(2,1)S(1)} collective-permute-done((bf16[128,256]{1,0:T(8,128)(2,1)S(1)}, bf16[128,256]{1,0:T(8,128)(2,1)S(1)}, u32[]{:S(2)}, u32[]{:S(2)}) %collective-permute-start) | collective-permute-done | bytes 65568 | tf_op jit(solution)/shard_map/ppermute | solution.py:62
  6.9 4.5 %collective-permute-start.1 = (bf16[128,384]{1,0:T(8,128)(2,1)S(1)}, bf16[128,384]{1,0:T(8,128)(2,1)S(1)}, u32[]{:S(2)}, u32[]{:S(2)}) collective-permute-start(bf16[128,384]{1,0:T(8,128)(2,1)S(1)} %join.1.refs_3_.after), channel_id=1, source_target_pairs={{0,12},{4,8},{8,4},{12,0},{1,13},{5,9},{9,5},{13,1},{2,14},{6,10},... | collective-permute-start | bytes 294920 | tf_op jit(solution)/shard_map/ppermute | solution.py:57
  11.4 0.6 %collective-permute-start.3 = (bf16[128,384]{1,0:T(8,128)(2,1)S(1)}, bf16[128,384]{1,0:T(8,128)(2,1)S(1)}, u32[]{:S(2)}, u32[]{:S(2)}) collective-permute-start(bf16[128,384]{1,0:T(8,128)(2,1)S(1)} %join.1.refs_3_.after), channel_id=1, source_target_pairs={{0,4},{4,0},{8,12},{12,8},{1,5},{5,1},{9,13},{13,9},{2,6},{6,2},{1... | collective-permute-start | bytes 294920 | tf_op jit(solution)/shard_map/ppermute | solution.py:57
  12.1 0.0 copy-start
  12.1 0.0 copy-start.2
  12.1 1.9 %collective-permute-start.6 = (bf16[128,1152]{1,0:T(8,128)(2,1)S(1)}, bf16[128,1152]{1,0:T(8,128)(2,1)S(1)}, u32[]{:S(2)}, u32[]{:S(2)}) collective-permute-start(bf16[128,1152]{1,0:T(8,128)(2,1)S(1)} %take.3), channel_id=1, source_target_pairs={{16,0},{0,16},{17,1},{1,17},{18,2},{2,18},{19,3},{3,19},{20,4},{4,... | collective-permute-start | bytes 884744 | tf_op jit(solution)/shard_map/ppermute | solution.py:62
  14.0 0.6 %prepare.1.feature_ref = bf16[2,128,512]{2,1,0:T(8,128)(2,1)S(1)} custom-call(s32[8]{0:T(128)S(1)} %copy-done.3, f32[8,128]{1,0:T(8,128)S(1)} %touch.1.after), custom_call_target="tpu_custom_call" | custom-call | flops 3000000000 | tf_op jit(solution)/shard_map/prepare/pallas_call | solution.py:24
  14.6 0.9 %weigh.1.w_ref = bf16[2048,1024]{1,0:T(8,128)(2,1)S(1)} custom-call(bf16[2048,1024]{1,0:T(8,128)(2,1)S(1)} %bitcast.4, bf16[1,2048]{1,0:T(2,128)(2,1)S(1)} %copy-done.2, bf16[128,384]{1,0:T(8,128)(2,1)S(1)} %collective-permute-done.1.after.refs_0_), custom_call_target="tpu_custom_call" | custom-call | flops 1000000000 | tf_op jit(solution)/shard_map/weigh/pallas_call | solution.py:24
  15.5 2.6 %collective-permute-done.2.refs_1_ = bf16[128,384]{1,0:T(8,128)(2,1)S(1)} collective-permute-done((bf16[128,384]{1,0:T(8,128)(2,1)S(1)}, bf16[128,384]{1,0:T(8,128)(2,1)S(1)}, u32[]{:S(2)}, u32[]{:S(2)}) %collective-permute-start.2) | collective-permute-done | bytes 98336 | tf_op jit(solution)/shard_map/ppermute | solution.py:57
  18.1 1.6 %attend_first.1 = (bf16[1,2,256,512]{3,2,1,0:T(8,128)(2,1)S(1)}, bf16[1,512,256]{2,1,0:T(8,128)(2,1)S(1)}, bf16[128,896]{1,0:T(8,128)(2,1)S(1)}, f32[1,16]{1,0:T(1,128)S(1)}) custom-call(bf16[2048,1024]{1,0:T(8,128)(2,1)S(1)} %weigh.1.w_ref, bf16[2,128,512]{2,1,0:T(8,128)(2,1)S(1)} %prepare.1.feature_ref, ...), custom_call_target="tpu_custom_call" | custom-call | flops 2000000000 | tf_op jit(solution)/shard_map/attend_first/pallas_call | solution.py:24
  19.7 0.5 %collective-permute-start.5 = (f32[1,16]{1,0:T(1,128)S(1)}, f32[1,16]{1,0:T(1,128)S(1)}, u32[]{:S(2)}, u32[]{:S(2)}) collective-permute-start(f32[1,16]{1,0:T(1,128)S(1)} %get-tuple-element.12.left_ref), channel_id=1, source_target_pairs={{0,4},{4,0},{8,12},{12,8},{1,5},{5,1},{9,13},{13,9},{2,6},{6,2},{1... | collective-permute-start | bytes 200 | tf_op jit(solution)/shard_map/ppermute | solution.py:57
  20.2 1.4 %attend_last.1 = (bf16[128,1152]{1,0:T(8,128)(2,1)S(1)}, bf16[1,144,256]{2,1,0:T(8,128)(2,1)S(1)}, bf16[1,144,256]{2,1,0:T(8,128)(2,1)S(1)}, f32[128,128]{1,0:T(8,128)S(1)}) custom-call(bf16[128,1152]{1,0:T(8,128)(2,1)S(1)} %collective-permute-done.6.q_ref, bf16[1,2,256,512]{3,2,1,0:T(8,128)(2,1)S(1)} %get-tuple-element.13.kt_ref, ...), custom_call_target="tpu_custom_call" | custom-call | flops 1500000000 | tf_op jit(solution)/shard_map/attend_last/pallas_call | solution.py:24
  21.6 0.1 collective-permute-start.9
  21.7 0.5 %collective-permute-start.8 = (bf16[1,144,256]{2,1,0:T(8,128)(2,1)S(1)}, bf16[1,144,256]{2,1,0:T(8,128)(2,1)S(1)}, u32[]{:S(2)}, u32[]{:S(2)}) collective-permute-start(bf16[1,144,256]{2,1,0:T(8,128)(2,1)S(1)} %get-tuple-element.19), channel_id=1, source_target_pairs={{0,1},{1,0},{2,3},{3,2},{4,5},{5,4},{6,7},{7,6},{8,9},{9,8},{10,11... | collective-permute-start | bytes 221192 | tf_op jit(solution)/shard_map/ppermute | solution.py:376
  22.2 0.3 %project_keep.3.keep_ref = bf16[1,144,256]{2,1,0:T(8,128)(2,1)S(1)} custom-call(bf16[128,896]{1,0:T(8,128)(2,1)S(1)} %get-tuple-element.15.first_ref, bf16[128,1152]{1,0:T(8,128)(2,1)S(1)} %get-tuple-element.17.last_ref, bf16[2048,1024]{1,0:T(8,128)(2,1)S(1)} %weigh.1.w_ref, f32[128,128]{1,0:T(8,128)S(1)} %get-tuple-element.18.square_ref), custom_call_target="tpu_custom_call" | custom-call | flops 3000000000 | tf_op jit(solution)/shard_map/project_keep/pallas_call | solution.py:24
  22.5 0.4 %collective-permute-done.9.got_ref = bf16[1,144,256]{2,1,0:T(8,128)(2,1)S(1)} collective-permute-done((bf16[1,144,256]{2,1,0:T(8,128)(2,1)S(1)}, bf16[1,144,256]{2,1,0:T(8,128)(2,1)S(1)}, u32[]{:S(2)}, u32[]{:S(2)}) %collective-permute-start.9) | collective-permute-done | bytes 73760 | tf_op jit(solution)/shard_map/ppermute | solution.py:376
  22.9 1.6 %collective-permute-start.10 = (bf16[144,256]{1,0:T(8,128)(2,1)S(1)}, bf16[144,256]{1,0:T(8,128)(2,1)S(1)}, u32[]{:S(2)}, u32[]{:S(2)}) collective-permute-start(bf16[144,256]{1,0:T(8,128)(2,1)S(1)} %merge.1), channel_id=1, source_target_pairs={{0,2},{1,3},{2,0},{3,1},{4,6},{5,7},{6,4},{7,5},{8,10},{9,11},{10,... | collective-permute-start | bytes 221192 | tf_op jit(solution)/shard_map/ppermute | solution.py:413
  24.5 2.5 %collective-permute-start.7 = (f32[1,16]{1,0:T(1,128)S(1)}, f32[1,16]{1,0:T(1,128)S(1)}, u32[]{:S(2)}, u32[]{:S(2)}) collective-permute-start(f32[1,16]{1,0:T(1,128)S(1)} %larger.1.peak_ref), channel_id=1, source_target_pairs={{0,8},{4,12},{8,0},{12,4},{1,9},{5,13},{9,1},{13,5},{2,10},{6,14},... | collective-permute-start | bytes 200 | tf_op jit(solution)/shard_map/ppermute | solution.py:57
  27.0 0.3 %project_keep.2.keep_ref = bf16[1,144,256]{2,1,0:T(8,128)(2,1)S(1)} custom-call(bf16[128,896]{1,0:T(8,128)(2,1)S(1)} %get-tuple-element.15.first_ref, bf16[128,1152]{1,0:T(8,128)(2,1)S(1)} %get-tuple-element.17.last_ref, bf16[2048,1024]{1,0:T(8,128)(2,1)S(1)} %weigh.1.w_ref, f32[128,128]{1,0:T(8,128)S(1)} %get-tuple-element.18.square_ref), custom_call_target="tpu_custom_call" | custom-call | tf_op jit(solution)/shard_map/project_keep/pallas_call | solution.py:24
  27.4 1.6 %collective-permute-done.7.peak_got = f32[1,16]{1,0:T(1,128)S(1)} collective-permute-done((f32[1,16]{1,0:T(1,128)S(1)}, f32[1,16]{1,0:T(1,128)S(1)}, u32[]{:S(2)}, u32[]{:S(2)}) %collective-permute-start.7) | collective-permute-done | bytes 96 | tf_op jit(solution)/shard_map/ppermute | solution.py:57
  29.0 0.8 %finish.1 = (f32[1,16]{1,0:T(1,128)}, bf16[128,256]{1,0:T(8,128)(2,1)}) custom-call(f32[1,16]{1,0:T(1,128)S(1)} %larger.1.peak_ref, f32[1,16]{1,0:T(1,128)S(1)} %collective-permute-done.7.peak_got, bf16[1,144,256]{2,1,0:T(8,128)(2,1)S(1)} %project_keep.2.keep_ref, bf16[1,144,256]{2,1,0:T(8,128)(2,1)S(1)} %collective-permute-done.8.got_ref, ...), custom_call_target="tpu_custom_call" | custom-call | tf_op jit(solution)/shard_map/finish/pallas_call | solution.py:24
  (20 shorter events, 0.1 us)
Async XLA Ops:
  1.4 3.0 %copy-start.1 = (bf16[1,128,2048]{2,1,0:T(8,128)(2,1)S(1)}, bf16[1,128,2048]{2,1,0:T(8,128)(2,1)}, u32[]{:S(2)}) copy-start(bf16[1,128,2048]{2,1,0:T(8,128)(2,1)} %q_ref.3) | copy-start | bytes 1572868
  1.4 5.5 %collective-permute-start = (bf16[128,256]{1,0:T(8,128)(2,1)S(1)}, bf16[128,256]{1,0:T(8,128)(2,1)S(1)}, u32[]{:S(2)}, u32[]{:S(2)}) collective-permute-start(bf16[128,256]{1,0:T(8,128)(2,1)S(1)} %pad_maximum_fusion.here_ref.block_ref), channel_id=1, source_target_pairs={{16,0},{0,16},{17,1},{1,17},{18,2},{2,18},{19,3},{3,19},{20,4},{4,... | collective-permute-start | bytes 196616 | tf_op jit(solution)/shard_map/ppermute | solution.py:62
  4.4 9.5 %copy-start.3 = (s32[8]{0:T(128)S(1)}, s32[8]{0:T(128)}, u32[]{:S(2)}) copy-start(s32[8]{0:T(128)} %order_ref.1) | copy-start | bytes 100
  4.5 13.6 %collective-permute-start.4 = (bf16[128,896]{1,0:T(8,128)(2,1)S(1)}, bf16[128,896]{1,0:T(8,128)(2,1)S(1)}, u32[]{:S(2)}, u32[]{:S(2)}) collective-permute-start(bf16[128,896]{1,0:T(8,128)(2,1)S(1)} %take.2), channel_id=1, source_target_pairs={{16,0},{0,16},{17,1},{1,17},{18,2},{2,18},{19,3},{3,19},{20,4},{4,... | collective-permute-start | bytes 688136 | tf_op jit(solution)/shard_map/ppermute | solution.py:62
  6.9 7.7 %collective-permute-start.1 = (bf16[128,384]{1,0:T(8,128)(2,1)S(1)}, bf16[128,384]{1,0:T(8,128)(2,1)S(1)}, u32[]{:S(2)}, u32[]{:S(2)}) collective-permute-start(bf16[128,384]{1,0:T(8,128)(2,1)S(1)} %join.1.refs_3_.after), channel_id=1, source_target_pairs={{0,12},{4,8},{8,4},{12,0},{1,13},{5,9},{9,5},{13,1},{2,14},{6,10},... | collective-permute-start | bytes 294920 | tf_op jit(solution)/shard_map/ppermute | solution.py:57
  11.4 6.7 %collective-permute-start.2 = (bf16[128,384]{1,0:T(8,128)(2,1)S(1)}, bf16[128,384]{1,0:T(8,128)(2,1)S(1)}, u32[]{:S(2)}, u32[]{:S(2)}) collective-permute-start(bf16[128,384]{1,0:T(8,128)(2,1)S(1)} %join.1.refs_3_.after), channel_id=1, source_target_pairs={{0,8},{4,12},{8,0},{12,4},{1,9},{5,13},{9,1},{13,5},{2,10},{6,14},... | collective-permute-start | bytes 294920 | tf_op jit(solution)/shard_map/ppermute | solution.py:57
  11.4 6.7 %collective-permute-start.3 = (bf16[128,384]{1,0:T(8,128)(2,1)S(1)}, bf16[128,384]{1,0:T(8,128)(2,1)S(1)}, u32[]{:S(2)}, u32[]{:S(2)}) collective-permute-start(bf16[128,384]{1,0:T(8,128)(2,1)S(1)} %join.1.refs_3_.after), channel_id=1, source_target_pairs={{0,4},{4,0},{8,12},{12,8},{1,5},{5,1},{9,13},{13,9},{2,6},{6,2},{1... | collective-permute-start | bytes 294920 | tf_op jit(solution)/shard_map/ppermute | solution.py:57
  12.1 2.5 %copy-start = (bf16[1,2048,1024]{2,1,0:T(8,128)(2,1)S(1)}, bf16[1,2048,1024]{2,1,0:T(8,128)(2,1)}, u32[]{:S(2)}) copy-start(bf16[1,2048,1024]{2,1,0:T(8,128)(2,1)} %param.11) | copy-start | bytes 12582916
  12.1 2.5 %copy-start.2 = (bf16[1,2048]{1,0:T(2,128)(2,1)S(1)}, bf16[1,2048]{1,0:T(2,128)(2,1)}, u32[]{:S(2)}) copy-start(bf16[1,2048]{1,0:T(2,128)(2,1)} %gain_ref.1) | copy-start | bytes 12292
  12.1 8.1 %collective-permute-start.6 = (bf16[128,1152]{1,0:T(8,128)(2,1)S(1)}, bf16[128,1152]{1,0:T(8,128)(2,1)S(1)}, u32[]{:S(2)}, u32[]{:S(2)}) collective-permute-start(bf16[128,1152]{1,0:T(8,128)(2,1)S(1)} %take.3), channel_id=1, source_target_pairs={{16,0},{0,16},{17,1},{1,17},{18,2},{2,18},{19,3},{3,19},{20,4},{4,... | collective-permute-start | bytes 884744 | tf_op jit(solution)/shard_map/ppermute | solution.py:62
  19.7 4.8 %collective-permute-start.5 = (f32[1,16]{1,0:T(1,128)S(1)}, f32[1,16]{1,0:T(1,128)S(1)}, u32[]{:S(2)}, u32[]{:S(2)}) collective-permute-start(f32[1,16]{1,0:T(1,128)S(1)} %get-tuple-element.12.left_ref), channel_id=1, source_target_pairs={{0,4},{4,0},{8,12},{12,8},{1,5},{5,1},{9,13},{13,9},{2,6},{6,2},{1... | collective-permute-start | bytes 200 | tf_op jit(solution)/shard_map/ppermute | solution.py:57
  21.6 1.3 %collective-permute-start.9 = (bf16[1,144,256]{2,1,0:T(8,128)(2,1)S(1)}, bf16[1,144,256]{2,1,0:T(8,128)(2,1)S(1)}, u32[]{:S(2)}, u32[]{:S(2)}) collective-permute-start(bf16[1,144,256]{2,1,0:T(8,128)(2,1)S(1)} %get-tuple-element.16.after), channel_id=1, source_target_pairs={{0,1},{1,0},{2,3},{3,2},{4,5},{5,4},{6,7},{7,6},{8,9},{9,8},{10,11... | collective-permute-start | bytes 221192 | tf_op jit(solution)/shard_map/ppermute | solution.py:376
  21.7 7.3 %collective-permute-start.8 = (bf16[1,144,256]{2,1,0:T(8,128)(2,1)S(1)}, bf16[1,144,256]{2,1,0:T(8,128)(2,1)S(1)}, u32[]{:S(2)}, u32[]{:S(2)}) collective-permute-start(bf16[1,144,256]{2,1,0:T(8,128)(2,1)S(1)} %get-tuple-element.19), channel_id=1, source_target_pairs={{0,1},{1,0},{2,3},{3,2},{4,5},{5,4},{6,7},{7,6},{8,9},{9,8},{10,11... | collective-permute-start | bytes 221192 | tf_op jit(solution)/shard_map/ppermute | solution.py:376
  22.9 6.0 %collective-permute-start.10 = (bf16[144,256]{1,0:T(8,128)(2,1)S(1)}, bf16[144,256]{1,0:T(8,128)(2,1)S(1)}, u32[]{:S(2)}, u32[]{:S(2)}) collective-permute-start(bf16[144,256]{1,0:T(8,128)(2,1)S(1)} %merge.1), channel_id=1, source_target_pairs={{0,2},{1,3},{2,0},{3,1},{4,6},{5,7},{6,4},{7,5},{8,10},{9,11},{10,... | collective-permute-start | bytes 221192 | tf_op jit(solution)/shard_map/ppermute | solution.py:413
  24.5 4.4 %collective-permute-start.7 = (f32[1,16]{1,0:T(1,128)S(1)}, f32[1,16]{1,0:T(1,128)S(1)}, u32[]{:S(2)}, u32[]{:S(2)}) collective-permute-start(f32[1,16]{1,0:T(1,128)S(1)} %larger.1.peak_ref), channel_id=1, source_target_pairs={{0,8},{4,12},{8,0},{12,4},{1,9},{5,13},{9,1},{13,5},{2,10},{6,14},... | collective-permute-start | bytes 200 | tf_op jit(solution)/shard_map/ppermute | solution.py:57
